TPU v7x, 32 devices: a whole 2x2x4 slice. The times are simulated.
32 devices in a mesh: dp: 2 (over y), fsdp: 16 (over z, x, core).
Axes of the slice: x: 2, y: 2, z: 4, core: 2. Of those that a mesh axis runs over, the one named last changes fastest.
Arguments:
- video: bfloat16 [32, 512, 3072], P(('dp', 'fsdp'))
- audio: bfloat16 [32, 1024, 128], P(('dp', 'fsdp'))
- word_ids: int32 [32, 3, 32], P(('dp', 'fsdp')), may hold values from 0 to 65535
- word_counts: int32 [32, 3], P(('dp', 'fsdp')), may hold values from 4 to 32
- caption_counts: int32 [32], P(('dp', 'fsdp')), may hold values from 1 to 3, as said below
- caption_clips: int32 [32, 3], P(('dp', 'fsdp')), may hold values from 0 to 31, as said below
- mixing_in: float32 [3, 768, 6144], P(None, 'fsdp')
- mixing_in_first: float32 [3, 768, 6144], P(None, 'fsdp'), may hold values from -5.0755807e-07 to 5.0755807e-07
- mixing_in_second: float32 [3, 768, 6144], P(None, 'fsdp'), may hold values from 7.052482e-14 to 2.7943796e-13
- mixing_out: float32 [3, 3072, 768], P(None, 'fsdp'), may hold values from -0.109375 to 0.109375
- mixing_out_first: float32 [3, 3072, 768], P(None, 'fsdp'), may hold values from -5.0755807e-07 to 5.0755807e-07
- mixing_out_second: float32 [3, 3072, 768], P(None, 'fsdp'), may hold values from 7.052482e-14 to 2.7943796e-13
- norm_params: float32 [3, 6, 768], P(None, None, 'fsdp')
- norm_params_first: float32 [3, 6, 768], P(None, None, 'fsdp'), may hold values from -2.5377904e-06 to 2.5377904e-06
- norm_params_second: float32 [3, 6, 768], P(None, None, 'fsdp'), may hold values from 1.7298541e-12 to 7.052482e-12
- input_embed: float32 [3200, 768], P('fsdp')
- input_embed_first: float32 [3200, 768], P('fsdp'), may hold values from -5.0755807e-07 to 5.0755807e-07
- input_embed_second: float32 [3200, 768], P('fsdp'), may hold values from 7.052482e-14 to 2.7943796e-13
- word_table: float32 [65536, 768], P('fsdp'), may hold values from -1.8 to 1.8
- word_table_first: float32 [65536, 768], P('fsdp'), may hold values from -5.0755807e-07 to 5.0755807e-07
- word_table_second: float32 [65536, 768], P('fsdp'), may hold values from 7.052482e-14 to 2.7943796e-13
- head_proj: float32 [768, 1280], P('fsdp'), may hold values from -0.21875 to 0.21875
- head_proj_first: float32 [768, 1280], P('fsdp'), may hold values from -5.0755807e-07 to 5.0755807e-07
- head_proj_second: float32 [768, 1280], P('fsdp'), may hold values from 7.052482e-14 to 2.7943796e-13
- video_text_proj: float32 [512, 256], P('fsdp'), may hold values from -0.25 to 0.25
- video_text_proj_first: float32 [512, 256], P('fsdp'), may hold values from -5.0755807e-07 to 5.0755807e-07
- video_text_proj_second: float32 [512, 256], P('fsdp'), may hold values from 7.052482e-14 to 2.7943796e-13
Outputs:
- loss: float32 [], replicated
- grad_norm: float32 [], replicated
- mixing_in_new: float32 [3, 768, 6144], P(None, 'fsdp')
- mixing_in_first_new: float32 [3, 768, 6144], P(None, 'fsdp')
- mixing_in_second_new: float32 [3, 768, 6144], P(None, 'fsdp')
- mixing_out_new: float32 [3, 3072, 768], P(None, 'fsdp')
- mixing_out_first_new: float32 [3, 3072, 768], P(None, 'fsdp')
- mixing_out_second_new: float32 [3, 3072, 768], P(None, 'fsdp')
- norm_params_new: float32 [3, 6, 768], P(None, None, 'fsdp')
- norm_params_first_new: float32 [3, 6, 768], P(None, None, 'fsdp')
- norm_params_second_new: float32 [3, 6, 768], P(None, None, 'fsdp')
- input_embed_new: float32 [3200, 768], P('fsdp')
- input_embed_first_new: float32 [3200, 768], P('fsdp')
- input_embed_second_new: float32 [3200, 768], P('fsdp')
- word_table_new: float32 [65536, 768], P('fsdp')
- word_table_grad: float32 [65536, 768], P('fsdp')
- word_table_second_new: float32 [65536, 768], P('fsdp')
- head_proj_new: float32 [768, 1280], P('fsdp')
- head_proj_first_new: float32 [768, 1280], P('fsdp')
- head_proj_second_new: float32 [768, 1280], P('fsdp')
- video_text_proj_new: float32 [512, 256], P('fsdp')
- video_text_proj_first_new: float32 [512, 256], P('fsdp')
- video_text_proj_second_new: float32 [512, 256], P('fsdp')
Inputs may be any that keep to these rules, and one draw needn't show every extreme that they name: `caption_clips`: slot 0 of a clip names that clip; every other slot names a clip at most two away from its own, counted cyclically over the 32 clips. `caption_counts`: clip c has (c * 3) // 32 plus one or two live slots, at most 3.
All inputs are finite; a program needn't handle non-finite values.
Results may differ from a plain program's by a relative error of at most 0.015.
The roundings to bfloat16 on the way count: a program that leaves them out, or rounds other values in their place, can miss the bound.
Values may be sent and summed in bfloat16 or wider, within the bound.
A program may use at most 384 MiB of HBM per device.

v0:
```python
import jax
import jax.numpy as jnp
from jax import lax
from jax.sharding import PartitionSpec as P

HEAD = 64
ADAM_STEP = 10


FULL_PRECISION = lax.Precision.HIGHEST
SOFTMAX_WARMTH = 0.03
CLIP_NORM = 0.01
RATES = (0.1, 0.05, 0.3, 0.1, 0.2, 0.1, 0.1)
BETA_ONE = 0.9
BETA_TWO = 0.95
EPSILON = 1e-08
WEIGHT_DECAY = 0.1


def norm_rows(values, gain_row, shift_row):
    centred = values - jnp.mean(values, -1, keepdims=True)
    return (
        centred * lax.rsqrt(jnp.mean(centred * centred, -1, keepdims=True) + 1e-06) * gain_row
        + shift_row
    )


def unit_rows(values):
    return values * lax.rsqrt(jnp.sum(values * values, -1, keepdims=True) + 1e-06)


def log_sum(similarity_scores):
    highest = jnp.max(similarity_scores, -1, keepdims=True)
    return highest[..., 0] + jnp.log(jnp.sum(jnp.exp(similarity_scores - highest), -1))


def word_bias(valid):
    captions, slots = valid.shape
    caption_of = jnp.arange(captions * slots) // slots
    allowed = (caption_of[:, None] == caption_of[None, :]) & (valid.reshape(-1)[None, :] > 0.5)
    return jnp.where(allowed, 0.0, -1000000000.0).astype(jnp.float32)


def pool_plain(stream, gain_row, shift_row):
    return norm_rows(jnp.mean(stream, 0), gain_row, shift_row)


def pool_words(stream, valid, gain_row, shift_row):
    captions, slots = valid.shape
    summed = jnp.sum(stream.reshape(captions, slots, -1) * valid[:, :, None], 1)
    return norm_rows(summed / jnp.sum(valid, 1)[:, None], gain_row, shift_row)


def project(video_pool, audio_pool, text_pool, heads, video_to_text_embed):
    joint = video_to_text_embed.shape[0]
    video_to_audio_embed = jnp.dot(video_pool, heads[:, :joint], precision=FULL_PRECISION)
    return (
        unit_rows(video_to_audio_embed),
        unit_rows(jnp.dot(video_to_audio_embed, video_to_text_embed, precision=FULL_PRECISION)),
        unit_rows(jnp.dot(audio_pool, heads[:, joint : 2 * joint], precision=FULL_PRECISION)),
        unit_rows(jnp.dot(text_pool, heads[:, 2 * joint :], precision=FULL_PRECISION)),
    )


def contrast(
    video_to_audio_embed,
    video_to_text_embed,
    gathered_audio_rows,
    gathered_text_rows,
    live,
    positive,
    own_clip,
):
    similarity_scores = (
        jnp.dot(video_to_audio_embed, gathered_audio_rows.T, precision=FULL_PRECISION)
        / SOFTMAX_WARMTH
    )
    matched = log_sum(similarity_scores) - jnp.sum(similarity_scores * own_clip, -1)
    caption_embeddings = (
        jnp.dot(video_to_text_embed, gathered_text_rows.T, precision=FULL_PRECISION)
        / SOFTMAX_WARMTH
    )
    every_text = log_sum(jnp.where(live[None, :], caption_embeddings, -1e30))
    chosen_text = log_sum(jnp.where(positive, caption_embeddings, -1e30))
    weight_rows = jnp.sum(positive.astype(jnp.float32), -1)
    live_total = jnp.sum(live.astype(jnp.float32))
    return (
        jnp.sum(matched) / gathered_audio_rows.shape[0]
        + jnp.sum(weight_rows * (every_text - chosen_text)) / live_total
    )


def adam_update(master, first, second, gradient, rate):
    first_new = BETA_ONE * first + (1.0 - BETA_ONE) * gradient
    second_new = BETA_TWO * second + (1.0 - BETA_TWO) * gradient * gradient
    first_hat = first_new / (1.0 - BETA_ONE**ADAM_STEP)
    second_hat = second_new / (1.0 - BETA_TWO**ADAM_STEP)
    master_new = master - rate * (
        first_hat / (jnp.sqrt(second_hat) + EPSILON) + WEIGHT_DECAY * master
    )
    return (master_new, first_new, second_new)


def block_scores(query_block, keys, bias_block):
    scaling = keys.shape[-1] ** (-0.5)
    return (
        jnp.einsum("qhe,khe->hqk", query_block, keys, preferred_element_type=jnp.float32) * scaling
        + bias_block[None]
    )


def split_blocks(values, block_rows):
    return values.reshape((values.shape[0] // block_rows, block_rows) + values.shape[1:])


def attend(queries, keys, values, bias):
    row_count = queries.shape[0]
    block_rows = min(512, row_count)

    def one_block(inputs):
        query_block, bias_block = inputs
        similarity_scores = block_scores(query_block, keys, bias_block)
        highest = jnp.max(similarity_scores, -1, keepdims=True)
        exponent = jnp.exp(similarity_scores - highest)
        summed = jnp.sum(exponent, -1, keepdims=True)
        mixed = jnp.einsum(
            "hqk,khe->qhe",
            (exponent / summed).astype(jnp.bfloat16),
            values,
            preferred_element_type=jnp.float32,
        )
        return (mixed.astype(jnp.bfloat16), highest[..., 0] + jnp.log(summed[..., 0]))

    mixed, log_totals = lax.map(
        one_block, (split_blocks(queries, block_rows), split_blocks(bias, block_rows))
    )
    return (mixed.reshape(queries.shape), log_totals)


def attend_back(queries, keys, values, bias, log_totals, grad_mixed):
    row_count = queries.shape[0]
    block_rows = min(512, row_count)
    scaling = keys.shape[-1] ** (-0.5)

    def one_block(carry, inputs):
        query_block, bias_block, total_block, grad_block = inputs
        similarity_scores = block_scores(query_block, keys, bias_block)
        weights_now = jnp.exp(similarity_scores - total_block[..., None])
        grad_weights = jnp.einsum(
            "qhe,khe->hqk", grad_block, values, preferred_element_type=jnp.float32
        )
        grad_scores = (
            weights_now * (grad_weights - jnp.sum(weights_now * grad_weights, -1, keepdims=True))
        ).astype(jnp.bfloat16)
        grad_query = (
            jnp.einsum("hqk,khe->qhe", grad_scores, keys, preferred_element_type=jnp.float32)
            * scaling
        )
        grad_keys = (
            carry[0]
            + jnp.einsum(
                "hqk,qhe->khe", grad_scores, query_block, preferred_element_type=jnp.float32
            )
            * scaling
        )
        grad_values = carry[1] + jnp.einsum(
            "hqk,qhe->khe",
            weights_now.astype(jnp.bfloat16),
            grad_block,
            preferred_element_type=jnp.float32,
        )
        return ((grad_keys, grad_values), grad_query)

    zeros_keys = jnp.zeros(keys.shape, jnp.float32)
    carried, grad_query = lax.scan(
        one_block,
        (zeros_keys, zeros_keys),
        (
            split_blocks(queries, block_rows),
            split_blocks(bias, block_rows),
            log_totals,
            split_blocks(grad_mixed, block_rows),
        ),
    )
    return (grad_query.reshape(queries.shape), carried[0], carried[1])


def layer_forward(stream, bias, mixing, mixing_back, gains_low):
    row_count, features = stream.shape
    gains = gains_low.astype(jnp.float32)
    normed = norm_rows(stream, gains[0], gains[1]).astype(jnp.bfloat16)
    joined = jnp.dot(normed, mixing[:, : 3 * features], preferred_element_type=jnp.float32).astype(
        jnp.bfloat16
    )
    joined = joined.reshape(row_count, 3, -1, HEAD)
    mixed, log_totals = attend(joined[:, 0], joined[:, 1], joined[:, 2], bias)
    mixed = mixed.reshape(row_count, features)
    middle = stream + jnp.dot(
        mixed, mixing[:, 3 * features : 4 * features], preferred_element_type=jnp.float32
    )
    normed_two = norm_rows(middle, gains[2], gains[3]).astype(jnp.bfloat16)
    hidden = jnp.dot(normed_two, mixing[:, 4 * features :], preferred_element_type=jnp.float32)
    activated = jax.nn.gelu(hidden).astype(jnp.bfloat16)
    result = middle + jnp.dot(activated, mixing_back, preferred_element_type=jnp.float32)
    return (
        result,
        (stream, normed, joined, log_totals, mixed, middle, normed_two, hidden, activated),
    )


def layer_backward(grad_result, saved, bias, mixing, mixing_back, gains_low):
    stream, normed, joined, log_totals, mixed, middle, normed_two, hidden, activated = saved
    row_count, features = stream.shape
    gains = gains_low.astype(jnp.float32)
    grad_branch = grad_result.astype(jnp.bfloat16)
    grad_back = jnp.dot(activated.T, grad_branch, preferred_element_type=jnp.float32)
    grad_activated = jnp.dot(grad_branch, mixing_back.T, preferred_element_type=jnp.float32)
    grad_hidden = jax.vjp(jax.nn.gelu, hidden)[1](grad_activated)[0].astype(jnp.bfloat16)
    grad_up = jnp.dot(normed_two.T, grad_hidden, preferred_element_type=jnp.float32)
    grad_normed_two = jnp.dot(
        grad_hidden, mixing[:, 4 * features :].T, preferred_element_type=jnp.float32
    )
    grad_middle_norm, grad_gain_three, grad_shift_three = jax.vjp(
        norm_rows, middle, gains[2], gains[3]
    )[1](grad_normed_two)
    grad_middle = grad_result + grad_middle_norm
    grad_attention = grad_middle.astype(jnp.bfloat16)
    grad_output = jnp.dot(mixed.T, grad_attention, preferred_element_type=jnp.float32)
    grad_mixed = jnp.dot(
        grad_attention, mixing[:, 3 * features : 4 * features].T, preferred_element_type=jnp.float32
    )
    grad_mixed = grad_mixed.astype(jnp.bfloat16).reshape(row_count, -1, HEAD)
    grad_query, grad_keys, grad_values = attend_back(
        joined[:, 0], joined[:, 1], joined[:, 2], bias, log_totals, grad_mixed
    )
    grad_joined = (
        jnp.stack([grad_query, grad_keys, grad_values], 1)
        .reshape(row_count, 3 * features)
        .astype(jnp.bfloat16)
    )
    grad_inward = jnp.dot(normed.T, grad_joined, preferred_element_type=jnp.float32)
    grad_normed = jnp.dot(
        grad_joined, mixing[:, : 3 * features].T, preferred_element_type=jnp.float32
    )
    grad_stream_norm, grad_gain_one, grad_shift_one = jax.vjp(
        norm_rows, stream, gains[0], gains[1]
    )[1](grad_normed)
    grad_mixing = jnp.concatenate([grad_inward, grad_output, grad_up], 1)
    grad_gains = jnp.stack([grad_gain_one, grad_shift_one, grad_gain_three, grad_shift_three])
    return (grad_middle + grad_stream_norm, grad_mixing, grad_back, grad_gains)


def body(
    video,
    audio,
    word_ids,
    word_counts,
    caption_counts,
    caption_clips,
    mixing_in,
    mixing_in_first,
    mixing_in_second,
    mixing_out,
    mixing_out_first,
    mixing_out_second,
    norm_params,
    norm_params_first,
    norm_params_second,
    input_embed,
    input_embed_first,
    input_embed_second,
    word_table,
    word_table_first,
    word_table_second,
    head_proj,
    head_proj_first,
    head_proj_second,
    video_text_proj,
    video_text_proj_first,
    video_text_proj_second,
):
    group_size = lax.axis_size("fsdp")
    member = lax.axis_index("fsdp")
    replica = lax.axis_index("dp")
    clip_index = replica * group_size + member
    captions = word_ids.shape[1]
    slots = word_ids.shape[2]
    word_rows_own = captions * slots
    all_ids, all_word_counts, all_caption_counts, all_caption_clips = (
        lax.all_gather(word_ids, ("dp", "fsdp"), axis=0, tiled=True),
        lax.all_gather(word_counts, ("dp", "fsdp"), axis=0, tiled=True),
        lax.all_gather(caption_counts, ("dp", "fsdp"), axis=0, tiled=True),
        lax.all_gather(caption_clips, ("dp", "fsdp"), axis=0, tiled=True),
    )
    group_ids = lax.dynamic_slice_in_dim(
        all_ids.reshape(-1), replica * (group_size * word_rows_own), group_size * word_rows_own
    )
    table_rows = word_table.shape[0]
    first_row = member * table_rows

    def owned_rows():
        local_ids = group_ids - first_row
        owned = (local_ids >= 0) & (local_ids < table_rows)
        return (jnp.clip(local_ids, 0, table_rows - 1), owned)

    local_ids, owned = owned_rows()
    words_in = lax.psum_scatter(
        jnp.where(owned[:, None], word_table[local_ids], 0.0),
        "fsdp",
        scatter_dimension=0,
        tiled=True,
    )
    embed, heads, video_to_text_embed = (
        lax.all_gather(input_embed.astype(jnp.bfloat16), "fsdp", axis=0, tiled=True),
        lax.all_gather(head_proj.astype(jnp.bfloat16), "fsdp", axis=0, tiled=True),
        lax.all_gather(video_text_proj.astype(jnp.bfloat16), "fsdp", axis=0, tiled=True),
    )
    patch_width = video.shape[2]
    video_rows = jnp.dot(video[0], embed[:patch_width], preferred_element_type=jnp.float32)
    audio_rows = jnp.dot(audio[0], embed[patch_width:], preferred_element_type=jnp.float32)
    valid = (jnp.arange(slots)[None, :] < word_counts[0][:, None]).astype(jnp.float32)
    inputs = (video_rows, audio_rows, words_in)
    biases = (
        jnp.zeros((video_rows.shape[0], video_rows.shape[0]), jnp.float32),
        jnp.zeros((audio_rows.shape[0], audio_rows.shape[0]), jnp.float32),
        word_bias(valid),
    )

    def pool_text(stream, gain_row, shift_row):
        return pool_words(stream, valid, gain_row, shift_row)

    poolers = (pool_plain, pool_plain, pool_text)
    kept, caches, outputs, pooled = ([], [], [], [])
    for towers in range(3):
        weights = (
            lax.all_gather(mixing_in[towers].astype(jnp.bfloat16), "fsdp", axis=0, tiled=True),
            lax.all_gather(mixing_out[towers].astype(jnp.bfloat16), "fsdp", axis=0, tiled=True),
            lax.all_gather(norm_params[towers].astype(jnp.bfloat16), "fsdp", axis=1, tiled=True),
        )
        kept.append(None)
        result, cache = layer_forward(
            inputs[towers], biases[towers], weights[0], weights[1], weights[2]
        )
        caches.append(cache)
        outputs.append(result)
        gains = weights[2].astype(jnp.float32)
        pooled.append(poolers[towers](result, gains[4], gains[5]))
    heads_f = heads.astype(jnp.float32)
    video_text_f = video_to_text_embed.astype(jnp.float32)
    projected, head_pull = jax.vjp(
        project, pooled[0][None], pooled[1][None], pooled[2], heads_f, video_text_f
    )
    gathered_audio_rows, gathered_text_rows = (
        lax.all_gather(projected[2], ("dp", "fsdp"), axis=0, tiled=True),
        lax.all_gather(projected[3], ("dp", "fsdp"), axis=0, tiled=True),
    )
    clip_total = gathered_audio_rows.shape[0]
    live = (jnp.arange(captions)[None, :] < all_caption_counts[:, None]).reshape(-1)
    positive = (live & (all_caption_clips.reshape(-1) == clip_index))[None, :]
    own_clip = (jnp.arange(clip_total) == clip_index).astype(jnp.float32)[None, :]

    def local_loss(video_to_audio_embed, video_textual, audio_every, text_every):
        return contrast(
            video_to_audio_embed, video_textual, audio_every, text_every, live, positive, own_clip
        )

    loss_part, loss_pull = jax.vjp(
        local_loss, projected[0], projected[1], gathered_audio_rows, gathered_text_rows
    )
    grad_video_audio, grad_video_text, grad_audio_all, grad_text_all = loss_pull(jnp.float32(1.0))
    grad_audio, grad_text = (
        lax.psum_scatter(grad_audio_all, ("dp", "fsdp"), scatter_dimension=0, tiled=True),
        lax.psum_scatter(grad_text_all, ("dp", "fsdp"), scatter_dimension=0, tiled=True),
    )
    grad_pools = head_pull((grad_video_audio, grad_video_text, grad_audio, grad_text))
    pool_grads = (grad_pools[0][0], grad_pools[1][0], grad_pools[2])
    grad_inputs, mixing_shards, back_shards, gain_shards = ([], [], [], [])
    for towers in range(3):
        weights = (
            lax.all_gather(mixing_in[towers].astype(jnp.bfloat16), "fsdp", axis=0, tiled=True),
            lax.all_gather(mixing_out[towers].astype(jnp.bfloat16), "fsdp", axis=0, tiled=True),
            lax.all_gather(norm_params[towers].astype(jnp.bfloat16), "fsdp", axis=1, tiled=True),
        )
        gains = weights[2].astype(jnp.float32)
        grad_stream, grad_pool_gain, grad_pool_shift = jax.vjp(
            poolers[towers], outputs[towers], gains[4], gains[5]
        )[1](pool_grads[towers])
        grad_entry, grad_mixing, grad_back, grad_gains = layer_backward(
            grad_stream, caches[towers], biases[towers], weights[0], weights[1], weights[2]
        )
        grad_gains = jnp.concatenate([grad_gains, grad_pool_gain[None], grad_pool_shift[None]], 0)
        shares = (
            lax.psum_scatter(grad_mixing, "fsdp", scatter_dimension=0, tiled=True),
            lax.psum_scatter(grad_back, "fsdp", scatter_dimension=0, tiled=True),
            lax.psum_scatter(grad_gains, "fsdp", scatter_dimension=1, tiled=True),
        )
        grad_inputs.append(grad_entry)
        mixing_shards.append(shares[0])
        back_shards.append(shares[1])
        gain_shards.append(shares[2])
    grad_video_rows = grad_inputs[0].astype(jnp.bfloat16)
    grad_audio_rows = grad_inputs[1].astype(jnp.bfloat16)
    grad_embed = jnp.concatenate(
        [
            jnp.dot(video[0].T, grad_video_rows, preferred_element_type=jnp.float32),
            jnp.dot(audio[0].T, grad_audio_rows, preferred_element_type=jnp.float32),
        ],
        0,
    )
    embed_share, heads_share, video_text_share = (
        lax.psum_scatter(grad_embed, "fsdp", scatter_dimension=0, tiled=True),
        lax.psum_scatter(grad_pools[3], "fsdp", scatter_dimension=0, tiled=True),
        lax.psum_scatter(grad_pools[4], "fsdp", scatter_dimension=0, tiled=True),
    )
    local_ids, owned = owned_rows()
    table_share = jax.ops.segment_sum(
        jnp.where(
            owned[:, None],
            lax.all_gather(grad_inputs[2].astype(jnp.bfloat16), "fsdp", axis=0, tiled=True).astype(
                jnp.float32
            ),
            0.0,
        ),
        local_ids,
        num_segments=table_rows,
    )
    grads = (
        lax.psum(jnp.stack(mixing_shards).astype(jnp.bfloat16), "dp").astype(jnp.float32),
        lax.psum(jnp.stack(back_shards).astype(jnp.bfloat16), "dp").astype(jnp.float32),
        lax.psum(jnp.stack(gain_shards).astype(jnp.bfloat16), "dp").astype(jnp.float32),
        lax.psum(embed_share.astype(jnp.bfloat16), "dp").astype(jnp.float32),
        lax.psum(table_share.astype(jnp.bfloat16), "dp").astype(jnp.float32),
        lax.psum(heads_share.astype(jnp.bfloat16), "dp").astype(jnp.float32),
        lax.psum(video_text_share.astype(jnp.bfloat16), "dp").astype(jnp.float32),
    )
    local_square = sum((jnp.sum(g * g) for g in grads))
    loss = lax.psum(loss_part, ("dp", "fsdp"))
    square = lax.psum(local_square, "fsdp")
    grad_norm = jnp.sqrt(square)
    factor = CLIP_NORM / jnp.maximum(grad_norm, CLIP_NORM)
    clipped = [g * factor for g in grads]
    masters = (
        mixing_in,
        mixing_out,
        norm_params,
        input_embed,
        word_table,
        head_proj,
        video_text_proj,
    )
    firsts = (
        mixing_in_first,
        mixing_out_first,
        norm_params_first,
        input_embed_first,
        word_table_first,
        head_proj_first,
        video_text_proj_first,
    )
    seconds = (
        mixing_in_second,
        mixing_out_second,
        norm_params_second,
        input_embed_second,
        word_table_second,
        head_proj_second,
        video_text_proj_second,
    )
    new = [adam_update(masters[i], firsts[i], seconds[i], clipped[i], RATES[i]) for i in range(7)]
    return (
        loss,
        grad_norm,
        new[0][0],
        new[0][1],
        new[0][2],
        new[1][0],
        new[1][1],
        new[1][2],
        new[2][0],
        new[2][1],
        new[2][2],
        new[3][0],
        new[3][1],
        new[3][2],
        new[4][0],
        clipped[4],
        new[4][2],
        new[5][0],
        new[5][1],
        new[5][2],
        new[6][0],
        new[6][1],
        new[6][2],
    )


def solution(mesh):
    return jax.shard_map(
        body,
        mesh=mesh,
        in_specs=(
            P(("dp", "fsdp"), None, None),
            P(("dp", "fsdp"), None, None),
            P(("dp", "fsdp"), None, None),
            P(("dp", "fsdp"), None),
            P(("dp", "fsdp")),
            P(("dp", "fsdp"), None),
            P(None, "fsdp", None),
            P(None, "fsdp", None),
            P(None, "fsdp", None),
            P(None, "fsdp", None),
            P(None, "fsdp", None),
            P(None, "fsdp", None),
            P(None, None, "fsdp"),
            P(None, None, "fsdp"),
            P(None, None, "fsdp"),
            P("fsdp", None),
            P("fsdp", None),
            P("fsdp", None),
            P("fsdp", None),
            P("fsdp", None),
            P("fsdp", None),
            P("fsdp", None),
            P("fsdp", None),
            P("fsdp", None),
            P("fsdp", None),
            P("fsdp", None),
            P("fsdp", None),
        ),
        out_specs=(
            P(),
            P(),
            P(None, "fsdp", None),
            P(None, "fsdp", None),
            P(None, "fsdp", None),
            P(None, "fsdp", None),
            P(None, "fsdp", None),
            P(None, "fsdp", None),
            P(None, None, "fsdp"),
            P(None, None, "fsdp"),
            P(None, None, "fsdp"),
            P("fsdp", None),
            P("fsdp", None),
            P("fsdp", None),
            P("fsdp", None),
            P("fsdp", None),
            P("fsdp", None),
            P("fsdp", None),
            P("fsdp", None),
            P("fsdp", None),
            P("fsdp", None),
            P("fsdp", None),
            P("fsdp", None),
        ),
        check_vma=False,
    )
```

profile of v0, /device:TPU:0, one launch (start us, length us, event | category | flops | bytes accessed | tf_op | source)
XLA Modules:
  0.0 2672.1 jit_solution(3576937631281071720)
XLA Ops:
  8.1 43.5 %all_gather.75 = s32[32,3,32]{2,1,0:T(4,128)S(1)} all-gather(s32[1,3,32]{2,1,0:T(4,128)S(1)} %copy.175), channel_id=1, replica_groups=mesh['dp'=2,'fsdp'=16] {'dp','fsdp'}, dimensions={0}, use_global_device_ids=true | all-gather | bytes 12672 | tf_op jit(solution)/shard_map/all_gather | solution.py:290
  52.5 11.3 gather_fusion
  82.7 38.4 %all-reduce.3 = s32[32]{0:T(128)S(1)} all-reduce(s32[32]{0:T(128)S(1)} %dynamic-update-slice), channel_id=1, replica_groups=mesh['dp'=2,'fsdp'=16] {'dp','fsdp'}, use_global_device_ids=true, to_apply=%add.3 | all-reduce | flops 32 | bytes 256
  123.0 39.8 %all-gather.11 = s32[32,1,3]{2,1,0:T(1,128)S(1)} all-gather(s32[1,1,3]{2,1,0:T(1,128)S(1)} %bitcast.465), channel_id=1, replica_groups=mesh['dp'=2,'fsdp'=16] {'dp','fsdp'}, dimensions={0}, use_global_device_ids=true | all-gather | bytes 396 | tf_op jit(solution)/shard_map/all_gather | solution.py:293
  165.6 20.4 all_gather.74
  186.0 20.8 all-gather.7
  207.3 13.4 slice_reduce_fusion.3
  220.7 20.0 all-gather.3
  241.2 13.4 slice_reduce_fusion.7
  254.6 21.4 all-gather
  276.4 13.6 slice_reduce_fusion.13
  320.6 21.8 all-gather.39.cloned.1.call-done
  347.8 77.7 %all-gather.33.cloned.1.call-done = bf16[1,768,6144]{2,1,0:T(8,128)(2,1)} async-done(((bf16[1,48,6144]{2,1,0:T(8,128)(2,1)}), bf16[1,768,6144]{2,1,0:T(8,128)(2,1)}) %all-gather.33.cloned.1.call-update) | async-done | bytes 9437200 | tf_op jit(solution)/shard_map/all_gather | solution.py:336
  425.5 9.3 convolution_convert_fusion
  453.0 75.4 %while.5 = (s32[]{:T(128)}, bf16[2,512,12,64]{1,3,2,0:T(8,128)(2,1)}, f32[2,12,512]{2,1,0:T(8,128)S(1)}, bf16[2,512,12,64]{1,3,2,0:T(8,128)(2,1)}, bf16[1024,12,...) while((s32[]{:T(128)}, bf16[2,512,12,64]{1,3,2,0:T(8,128)(2,1)}, ...), condition=%wide.region_15.16_spmd, body=%wide.region_12.15_spmd.sunk | while | flops 1667622912 | bytes 99328176 | solution.py:134
  453.0 14.6 multiply_reduce_fusion.46
  467.6 11.4 fusion.377
  479.0 10.8 fusion.378
  491.0 14.0 multiply_reduce_fusion.46
  505.0 11.3 fusion.377
  516.3 10.9 fusion.378
  537.5 9.2 fusion.80
  558.6 39.7 %all-gather.12 = f32[32,3,256]{2,1,0:T(4,128)S(1)} all-gather(f32[1,3,256]{2,1,0:T(4,128)S(1)} %multiply_bitcast_fusion), channel_id=1, replica_groups=mesh['dp'=2,'fsdp'=16] {'dp','fsdp'}, dimensions={0}, use_global_device_ids=true | all-gather | bytes 101376 | tf_op jit(solution)/shard_map/all_gather | solution.py:355
  598.3 7.5 all-gather.35.cloned.1.call-done
  605.8 11.2 add_reduce_fusion
  623.0 42.6 %all-gather.10 = f32[32,1,512]{2,1,0:T(1,128)} all-gather(f32[1,1,512]{2,1,0:T(1,128)S(1)} %bitcast.459), channel_id=8, replica_groups=mesh['dp'=2,'fsdp'=16] {'dp','fsdp'}, dimensions={0}, use_global_device_ids=true | all-gather | bytes 67584 | tf_op jit(solution)/shard_map/all_gather | solution.py:354
  688.5 8.4 add_reduce_fusion.1
  726.9 117.3 %all-reduce.12.cloned.1.call-done = (f32[96,256]{1,0:T(8,128)}, f32[32,512]{1,0:T(8,128)}) async-done(((f32[96,256]{1,0:T(8,128)}, f32[32,512]{1,0:T(8,128)}), (f32[96,256]{1,0:T(8,128)}, f32[32,512]{1,0:T(8,128)})) %all-reduce.12.cloned.1.call-update) | async-done | bytes 163856
  899.2 9.6 fusion.175
  909.1 8.7 fusion.51
  932.3 12.7 fusion.158
  950.9 13.8 multiply_reduce_fusion.2
  991.5 13.7 fusion.39
  1037.1 166.8 %while.6 = (s32[]{:T(128)}, f32[1024,12,64]{0,2,1:T(8,128)}, f32[1024,12,64]{0,2,1:T(8,128)}, bf16[2,512,12,64]{1,3,2,0:T(8,128)(2,1)}, bf16[2,512,12,64]{1,3,2,...) while((s32[]{:T(128)}, f32[1024,12,64]{0,2,1:T(8,128)}, ...), condition=%wide.region_67.68_spmd.clone, body=%wide.region_65.67_spmd.clone.sunk | while | flops 4106348544 | bytes 217235632 | solution.py:175
  1037.3 10.2 fusion.388
  1047.5 12.9 bitcast_add_fusion.5
  1060.4 17.2 multiply_reduce_fusion.47
  1077.6 22.1 multiply_convert_fusion.15
  1099.7 9.5 bitcast_dynamic-update-slice_fusion.5
  1109.2 8.5 bitcast_add_fusion.4
  1117.7 12.8 fusion.388
  1130.5 14.8 bitcast_add_fusion.5
  1145.3 17.0 multiply_reduce_fusion.47
  1162.3 22.0 multiply_convert_fusion.15
  1184.3 9.6 bitcast_dynamic-update-slice_fusion.5
  1193.9 9.6 bitcast_add_fusion.4
  1215.2 9.3 fusion.310
  1240.7 11.1 copy.224
  1278.2 7.5 fusion.265
  1310.7 17.8 scatter_custom_fusion
  1328.6 8.1 convert_element_type.371
  1342.6 116.2 %reduce-scatter.46.cloned.1.call-done = f32[200,768]{1,0:T(8,128)} async-done(((f32[3200,768]{1,0:T(8,128)}), f32[200,768]{1,0:T(8,128)}) %reduce-scatter.46.cloned.1.call-update) | async-done | bytes 614416
  1460.8 197.1 %reduce-scatter.24.cloned.1.call-done = f32[48,6144]{1,0:T(8,128)} async-done(((f32[768,6144]{1,0:T(8,128)}), f32[48,6144]{1,0:T(8,128)}) %reduce-scatter.24.cloned.1.call-update) | async-done | bytes 1179664 | tf_op jit(solution)/shard_map/reduce_scatter | solution.py:393
  1659.2 197.1 %reduce-scatter.26.cloned.1.call-done = f32[48,6144]{1,0:T(8,128)} async-done(((f32[768,6144]{1,0:T(8,128)}), f32[48,6144]{1,0:T(8,128)}) %reduce-scatter.26.cloned.1.call-update) | async-done | bytes 1179664 | tf_op jit(solution)/shard_map/reduce_scatter | solution.py:393
  1857.6 197.2 %reduce-scatter.28.cloned.1.call-done = f32[48,6144]{1,0:T(8,128)} async-done(((f32[768,6144]{1,0:T(8,128)}), f32[48,6144]{1,0:T(8,128)}) %reduce-scatter.28.cloned.1.call-update) | async-done | bytes 1179664 | tf_op jit(solution)/shard_map/reduce_scatter | solution.py:393
  2066.8 47.2 %reduce-scatter.40.cloned.1.call-done = f32[48,6]{1,0:T(8,128)} async-done(((f32[768,6]{1,0:T(8,128)}), f32[48,6]{1,0:T(8,128)}) %reduce-scatter.40.cloned.1.call-update) | async-done | bytes 1168
  2114.8 57.9 %reduce-scatter.44.cloned.1.call-done = f32[48,6]{1,0:T(8,128)} async-done(((f32[768,6]{1,0:T(8,128)}), f32[48,6]{1,0:T(8,128)}) %reduce-scatter.44.cloned.1.call-update) | async-done | bytes 1168
  2173.5 58.3 %reduce-scatter.42.cloned.1.call-done = f32[48,6]{1,0:T(8,128)} async-done(((f32[768,6]{1,0:T(8,128)}), f32[48,6]{1,0:T(8,128)}) %reduce-scatter.42.cloned.1.call-update) | async-done | bytes 1168
  2232.6 58.2 %reduce-scatter.38.cloned.1.call-done = f32[32,256]{1,0:T(8,128)} async-done(((f32[512,256]{1,0:T(8,128)}), f32[32,256]{1,0:T(8,128)}) %reduce-scatter.38.cloned.1.call-update) | async-done | bytes 32784 | tf_op jit(solution)/shard_map/reduce_scatter | solution.py:413
  2291.5 8.3 all-reduce.7
  2301.0 216.7 %all-reduce.14.cloned.1.call-done = (bf16[3,48,6144]{2,1,0:T(8,128)(2,1)}, bf16[3,192,768]{2,1,0:T(8,128)(2,1)}, bf16[200,768]{0,1:T(8,128)(2,1)}, bf16[4096,768]{1,0:T(8,128)(2,1)}, bf16[48,1280]{1,0:T(8,128)(2,1)}) async-done(((bf16[3,48,6144]{2,1,0:T(8,128)(2,1)}, bf16[3,192,768]{2,1,0:T(8,128)(2,1)}, bf16[200,768]{0,1:T(8,128)(2,1)}, bf16[4096,768]{1,0:T(8,128)(2,1)}, bf16[48,1280]{1,0:T(8,128)(2,1)}), ...) | async-done | bytes 9375760 | tf_op jit(solution)/shard_map/psum | solution.py:428
  2536.1 39.8 %psum.63 = f32[]{:T(128)} all-reduce(f32[]{:T(128)S(6)} %add.630), channel_id=1, replica_groups=mesh['dp'=2,'fsdp'=16] {'dp','fsdp'}, use_global_device_ids=true, to_apply=%region_44.45 | all-reduce | flops 1 | bytes 8 | tf_op jit(solution)/shard_map/psum | solution.py:437
  2576.0 32.4 %psum.71 = f32[]{:T(128)} all-reduce(f32[]{:T(128)S(6)} %add.646), channel_id=1, replica_groups=mesh['dp'=2,'fsdp'=16] {'fsdp'}, use_global_device_ids=true, to_apply=%region_121.122 | all-reduce | flops 1 | bytes 8 | tf_op jit(solution)/shard_map/psum | solution.py:438
  2635.6 28.3 %multiply_subtract_fusion = (f32[4096,768]{1,0:T(8,128)}, f32[4096,768]{1,0:T(8,128)}, f32[4096,768]{1,0:T(8,128)}) fusion(f32[4096,768]{1,0:T(8,128)} %param.49, f32[4096,768]{1,0:T(8,128)} %param.50, f32[4096,768]{1,0:T(8,128)} %param.51, f32[]{:T(128)S(6)} %div.497, bf16[4096,768]{1,0:T(8,128)(2,1)} %get-tuple-element.465), kind=kLoop, calls=%fused_computation.59 | loop fusion | flops 53477376 | bytes 81788928 | tf_op jit(solution)/shard_map/sub | solution.py:98
  (850 shorter events, 417.3 us)
Async XLA Ops:
  7.2 287.4 %copy-start = (bf16[1,512,3072]{2,1,0:T(8,128)(2,1)S(1)}, bf16[1,512,3072]{2,1,0:T(8,128)(2,1)}, u32[]{:S(2)}) copy-start(bf16[1,512,3072]{2,1,0:T(8,128)(2,1)} %param.31) | copy-start | bytes 9437188
  7.2 282.9 %reduce-scatter.22.cloned.1.call-start = ((), (), s32[]{:S(2)}) async-start(), calls=%async_computation.15 | async-start | bytes 5013504 | tf_op jit(solution)/shard_map/reduce_scatter | solution.py:307
  68.7 224.2 %all-gather.23.cloned.1.call-start = ((), (), s32[]{:S(2)}) async-start(), calls=%async_computation.13 | async-start | bytes 5222400 | tf_op jit(solution)/shard_map/all_gather | solution.py:314
  70.6 232.9 %all-gather.37.cloned.1.call-start = ((), (), s32[]{:S(2)}) async-start(), calls=%async_computation.29 | async-start | bytes 10027008 | tf_op jit(solution)/shard_map/all_gather | solution.py:336
  74.3 48.7 %copy-start.227 = (s32[1,3]{1,0:T(1,128)S(1)}, s32[1,3]{1,0:T(1,128)}, u32[]{:S(2)}) copy-start(s32[1,3]{1,0:T(1,128)} %param.36) | copy-start | bytes 40
  74.3 91.1 %copy-start.84 = (f32[32,256]{1,0:T(8,128)S(1)}, f32[32,256]{1,0:T(8,128)}, u32[]{:S(2)}) copy-start(f32[32,256]{1,0:T(8,128)} %param.55) | copy-start | bytes 98308
  74.3 91.1 %copy-start.107 = (f32[3,6,48]{2,1,0:T(8,128)S(1)}, f32[3,6,48]{2,1,0:T(8,128)}, u32[]{:S(2)}) copy-start(f32[3,6,48]{2,1,0:T(8,128)} %param.43) | copy-start | bytes 10372
  74.3 268.1 %all-gather.39.cloned.1.call-start = ((), (), s32[]{:S(2)}) async-start(), calls=%async_computation.30 | async-start | bytes 5013504 | tf_op jit(solution)/shard_map/all_gather | solution.py:337
  77.1 348.4 %all-gather.33.cloned.1.call-start = ((), (), s32[]{:S(2)}) async-start(), calls=%async_computation.27 | async-start | bytes 10027008 | tf_op jit(solution)/shard_map/all_gather | solution.py:336
  77.7 469.0 %all-gather.29.cloned.1.call-start = ((), (), s32[]{:S(2)}) async-start(), calls=%async_computation.25 | async-start | bytes 10027008 | tf_op jit(solution)/shard_map/all_gather | solution.py:336
  78.2 474.5 %all-gather.25.cloned.1.call-start = ((), (), s32[]{:S(2)}) async-start(), calls=%async_computation.14 | async-start | bytes 2088960 | tf_op jit(solution)/shard_map/all_gather | solution.py:315
  79.0 526.8 %all-gather.35.cloned.1.call-start = ((), (), s32[]{:S(2)}) async-start(), calls=%async_computation.28 | async-start | bytes 5013504 | tf_op jit(solution)/shard_map/all_gather | solution.py:337
  79.7 608.8 %all-gather.31.cloned.1.call-start = ((), (), s32[]{:S(2)}) async-start(), calls=%async_computation.26 | async-start | bytes 5013504 | tf_op jit(solution)/shard_map/all_gather | solution.py:337
  80.5 763.7 %all-reduce.12.cloned.1.call-start = ((), (), s32[]{:S(2)}) async-start(), calls=%async_computation.35 | async-start | bytes 327680
  81.9 41.1 %copy-start.143 = (f32[3,32]{1,0:T(4,128)}, f32[3,32]{1,0:T(4,128)S(1)}, u32[]{:S(2)}) copy-start(f32[3,32]{1,0:T(4,128)S(1)} %fusion.226) | copy-start | bytes 1156
  241.1 48.9 %copy-start.216 = (s32[96]{0:T(128)S(1)}, s32[96]{0:T(128)}, u32[]{:S(2)}) copy-start(s32[96]{0:T(128)} %and_select_fusion.1) | copy-start | bytes 1156
  241.1 48.8 %copy-start.225 = (pred[96]{0:T(512)(128)(4,1)S(1)}, pred[96]{0:T(512)(128)(4,1)}, u32[]{:S(2)}) copy-start(pred[96]{0:T(512)(128)(4,1)} %broadcast_compare_fusion.1) | copy-start | bytes 292
  241.2 51.8 %copy-start.70 = (bf16[1,1024,128]{2,1,0:T(8,128)(2,1)S(1)}, bf16[1,1024,128]{2,1,0:T(8,128)(2,1)}, u32[]{:S(2)}) copy-start(bf16[1,1024,128]{2,1,0:T(8,128)(2,1)} %param.32) | copy-start | bytes 786436
  320.6 25.6 copy-start.144
  320.6 25.7 copy-start.215
  320.6 104.9 %copy-start.101 = (f32[1024]{0:T(1024)S(1)}, f32[1024]{0:T(1024)}, u32[]{:S(2)}) copy-start(f32[1024]{0:T(1024)} %copy-done.100) | copy-start | bytes 12292
  320.6 104.9 %copy-start.122 = (f32[768]{0:T(1024)S(1)}, f32[768]{0:T(1024)}, u32[]{:S(2)}) copy-start(f32[768]{0:T(1024)} %get-tuple-element.406) | copy-start | bytes 9220
  320.6 104.9 %copy-start.146 = (f32[1024]{0:T(1024)S(1)}, f32[1024]{0:T(1024)}, u32[]{:S(2)}) copy-start(f32[1024]{0:T(1024)} %fusion.217) | copy-start | bytes 12292
  320.6 104.9 %copy-start.190 = (f32[768]{0:T(1024)S(1)}, f32[768]{0:T(1024)}, u32[]{:S(2)}) copy-start(f32[768]{0:T(1024)} %get-tuple-element.405) | copy-start | bytes 9220
  346.5 88.2 %copy-start.184 = (f32[3]{0:T(128)}, f32[3]{0:T(128)S(1)}, u32[]{:S(2)}) copy-start(f32[3]{0:T(128)S(1)} %broadcast_multiply_fusion.13) | copy-start | bytes 40
  347.3 87.5 %copy-start.228 = (f32[3]{0:T(128)}, f32[3]{0:T(128)S(1)}, u32[]{:S(2)}) copy-start(f32[3]{0:T(128)S(1)} %multiply_reduce_fusion.26) | copy-start | bytes 40
  554.2 291.4 %copy-start.114 = (f32[3,256]{1,0:T(4,128)}, f32[3,256]{1,0:T(4,128)S(1)}, u32[]{:S(2)}) copy-start(f32[3,256]{1,0:T(4,128)S(1)} %get-tuple-element.562) | copy-start | bytes 9220
  554.3 62.7 %copy-start.220 = (f32[3]{0:T(128)}, f32[3]{0:T(128)S(1)}, u32[]{:S(2)}) copy-start(f32[3]{0:T(128)S(1)} %add_rsqrt_fusion) | copy-start | bytes 40
  598.3 21.2 copy-start.89
  598.3 21.2 copy-start.115
  617.0 51.9 %copy-start.92 = (f32[768]{0:T(1024)}, f32[768]{0:T(1024)S(1)}, u32[]{:S(2)}) copy-start(f32[768]{0:T(1024)S(1)} %add_reduce_fusion) | copy-start | bytes 9220
  621.7 47.2 %copy-start.106 = (f32[1,512]{1,0:T(1,128)}, f32[1,512]{1,0:T(1,128)S(1)}, u32[]{:S(2)}) copy-start(f32[1,512]{1,0:T(1,128)S(1)} %fusion.167) | copy-start | bytes 6148
  688.5 14.5 copy-start.46
  688.5 37.1 %copy-start.99 = (f32[12,96]{1,0:T(8,128)S(1)}, f32[12,96]{1,0:T(8,128)}, u32[]{:S(2)}) copy-start(f32[12,96]{1,0:T(8,128)} %copy-done.98) | copy-start | bytes 13828
  697.0 158.3 %copy-start.94 = (f32[768]{0:T(1024)}, f32[768]{0:T(1024)S(1)}, u32[]{:S(2)}) copy-start(f32[768]{0:T(1024)S(1)} %add_reduce_fusion.1) | copy-start | bytes 9220
  701.7 153.6 %copy-start.96 = (f32[1,512]{1,0:T(1,128)}, f32[1,512]{1,0:T(1,128)S(1)}, u32[]{:S(2)}) copy-start(f32[1,512]{1,0:T(1,128)S(1)} %fusion.171) | copy-start | bytes 6148
  711.7 143.6 %copy-start.182 = (f32[32]{0:T(128)}, f32[32]{0:T(128)S(1)}, u32[]{:S(2)}) copy-start(f32[32]{0:T(128)S(1)} %fusion.242) | copy-start | bytes 388
  724.4 130.9 %copy-start.183 = (f32[96]{0:T(128)}, f32[96]{0:T(128)S(1)}, u32[]{:S(2)}) copy-start(f32[96]{0:T(128)S(1)} %add_multiply_fusion.2) | copy-start | bytes 1156
  725.2 585.5 %all-gather.27.cloned.1.call-start = ((), (), s32[]{:S(2)}) async-start(), calls=%async_computation.22 | async-start | bytes 2506752 | tf_op jit(solution)/shard_map/all_gather | solution.py:419
  876.1 460.6 %reduce-scatter.36.cloned.1.call-start = ((), (), s32[]{:S(2)}) async-start(), calls=%async_computation.23 | async-start | bytes 4177920 | tf_op jit(solution)/shard_map/reduce_scatter | solution.py:412
  893.5 444.7 %reduce-scatter.30.cloned.1.call-start = ((), (), s32[]{:S(2)}) async-start(), calls=%async_computation.19 | async-start | bytes 10027008 | tf_op jit(solution)/shard_map/reduce_scatter | solution.py:394
  899.2 86.1 %copy-start.207 = (f32[768]{0:T(1024)}, f32[768]{0:T(1024)S(1)}, u32[]{:S(2)}) copy-start(f32[768]{0:T(1024)S(1)} %get-tuple-element.495) | copy-start | bytes 9220
  908.8 430.6 %reduce-scatter.32.cloned.1.call-start = ((), (), s32[]{:S(2)}) async-start(), calls=%async_computation.20 | async-start | bytes 10027008 | tf_op jit(solution)/shard_map/reduce_scatter | solution.py:394
  926.7 58.6 %copy-start.217 = (f32[512]{0:T(512)}, f32[512]{0:T(512)S(1)}, u32[]{:S(2)}) copy-start(f32[512]{0:T(512)S(1)} %negate_multiply_fusion.3) | copy-start | bytes 6148
  932.3 89.3 %copy-start.209 = (f32[768]{0:T(1024)}, f32[768]{0:T(1024)S(1)}, u32[]{:S(2)}) copy-start(f32[768]{0:T(1024)S(1)} %get-tuple-element.501) | copy-start | bytes 9220
  945.0 395.6 %reduce-scatter.34.cloned.1.call-start = ((), (), s32[]{:S(2)}) async-start(), calls=%async_computation.21 | async-start | bytes 10027008 | tf_op jit(solution)/shard_map/reduce_scatter | solution.py:394
  950.8 13.8 slice-start
  950.8 13.8 slice-start.1
  950.9 13.8 slice-start.2
  979.4 12.1 slice-start.12
  986.0 19.1 slice-start.9
  991.5 13.7 slice-start.10
  991.5 13.7 slice-start.11
  1035.2 423.6 %reduce-scatter.46.cloned.1.call-start = ((), (), s32[]{:S(2)}) async-start(), calls=%async_computation.34 | async-start | bytes 10444800
  1117.7 12.8 copy-start.7
  1251.8 406.0 %reduce-scatter.24.cloned.1.call-start = ((), (), s32[]{:S(2)}) async-start(), calls=%async_computation.16 | async-start | bytes 20054016 | tf_op jit(solution)/shard_map/reduce_scatter | solution.py:393
  1267.6 588.7 %reduce-scatter.26.cloned.1.call-start = ((), (), s32[]{:S(2)}) async-start(), calls=%async_computation.17 | async-start | bytes 20054016 | tf_op jit(solution)/shard_map/reduce_scatter | solution.py:393
  1292.8 762.1 %reduce-scatter.28.cloned.1.call-start = ((), (), s32[]{:S(2)}) async-start(), calls=%async_computation.18 | async-start | bytes 20054016 | tf_op jit(solution)/shard_map/reduce_scatter | solution.py:393
  1305.3 808.7 %reduce-scatter.40.cloned.1.call-start = ((), (), s32[]{:S(2)}) async-start(), calls=%async_computation.31 | async-start | bytes 417792
  1306.9 865.8 %reduce-scatter.44.cloned.1.call-start = ((), (), s32[]{:S(2)}) async-start(), calls=%async_computation.33 | async-start | bytes 417792
  1308.1 923.7 %reduce-scatter.42.cloned.1.call-start = ((), (), s32[]{:S(2)}) async-start(), calls=%async_computation.32 | async-start | bytes 417792
  1309.2 981.5 %reduce-scatter.38.cloned.1.call-start = ((), (), s32[]{:S(2)}) async-start(), calls=%async_computation.24 | async-start | bytes 557056 | tf_op jit(solution)/shard_map/reduce_scatter | solution.py:413
  1310.2 1207.4 %all-reduce.14.cloned.1.call-start = ((), (), s32[]{:S(2)}) async-start(), calls=%async_computation.36 | async-start | bytes 18923520 | tf_op jit(solution)/shard_map/psum | solution.py:428
  2635.6 28.3 %copy-start.1 = (bf16[1,512,3072]{2,1,0:T(8,128)(2,1)S(1)}, bf16[1,512,3072]{2,1,0:T(8,128)(2,1)}, u32[]{:S(2)}) copy-start(bf16[1,512,3072]{2,1,0:T(8,128)(2,1)} %param.31) | copy-start | bytes 9437188
  (212 other events, 884.0 us)
Sparse Core Ops, SparseCore 0:
  68.9 71.9 reduce-scatter.21
  143.8 55.1 all-gather.22
  202.1 85.4 all-gather.36
  290.6 51.8 all-gather.38
  345.4 79.9 all-gather.32
  428.4 79.5 all-gather.28
  511.1 38.9 all-gather.24
  553.2 52.5 all-gather.34
  608.4 52.1 all-gather.30
  725.3 118.8 all-reduce.11
  876.2 44.1 all-gather.26
  924.7 69.0 reduce-scatter.35
  997.8 110.2 reduce-scatter.29
  1112.6 111.1 reduce-scatter.31
  1228.3 111.0 reduce-scatter.33
  1344.6 114.1 reduce-scatter.45
  1463.3 194.5 reduce-scatter.23
  1662.4 193.8 reduce-scatter.25
  1861.0 193.8 reduce-scatter.27
  2059.2 54.7 reduce-scatter.39
  2118.0 54.6 reduce-scatter.43
  2177.1 54.5 reduce-scatter.41
  2235.9 54.8 reduce-scatter.37
  2295.3 222.2 all-reduce.13
where the time goes:
time: 2680 us; the launch traced here: 2670 us
  waiting for transfers between devices  1370 us (51%)
  matrix products  441 us (16%)
  blocking collectives  367 us (14%)
  other arithmetic  277 us (10%)
  local copies, waits for them, and re-layouts  163 us (6%)
  between operations  47.4 us (2%)
    reduce_scatter x3, waiting for transfers between devices, body(): lax.psum_scatter(grad_mixing, 'fsdp', scatter_dimension=0, tiled=True)  591 us
    unnamed x29, waiting for transfers between devices  400 us
    psum x1, waiting for transfers between devices, body(): lax.psum(jnp.stack(mixing_shards).astype(jnp.bfloat16), 'dp')  217 us
    all_gather x3, waiting for transfers between devices, body(): lax.all_gather(mixing_in[towers].astype(jnp.bfloat16), 'fsdp', axis=0, ti...  77.7 us
    all_gather x3, blocking collectives, body(): lax.all_gather(norm_params[towers].astype(jnp.bfloat16), 'fsdp', axis=1,...  62.3 us
    reduce_scatter x1, waiting for transfers between devices, body(): lax.psum_scatter(grad_pools[4], 'fsdp', scatter_dimension=0, tiled=True)  58.2 us
    dot_general x6, matrix products, block_scores(): jnp.einsum('qhe,khe->hqk', query_block, keys, preferred_element_type=jnp....  56.1 us
    unnamed x509, local copies, waits for them, and re-layouts  55.7 us
  transfers between devices with their start and end apart: 24, of which 13 were waited for; matrix products, arithmetic and copies ran while one was open for 27% of the time, Pallas kernels for 0%

commit v1 on v0

v1 whole, which is shorter than its diff:
```python
import functools

import jax
import jax.numpy as jnp
from jax import lax
from jax.experimental import pallas as pl
from jax.experimental.pallas import tpu as pltpu
from jax.sharding import PartitionSpec as P

ADAM_STEP = 10
FULL_PRECISION = lax.Precision.HIGHEST
SOFTMAX_WARMTH = 0.03
CLIP_NORM = 0.01
RATES = (0.1, 0.05, 0.3, 0.1, 0.2, 0.1, 0.1)
BETA_ONE = 0.9
BETA_TWO = 0.95
EPSILON = 1e-08
WEIGHT_DECAY = 0.1
F32 = jnp.float32
BF16 = jnp.bfloat16
MESH_ID = pl.DeviceIdType.MESH
VMEM_LIMIT = 56 * 1024 * 1024
NT = (((1,), (1,)), ((), ()))


def dot(a, b):
    return jnp.dot(a, b, preferred_element_type=F32)


def dot_nt(a, b):
    return lax.dot_general(a, b, NT, preferred_element_type=F32)


def dot_tn(a, b):
    return lax.dot_general(a, b, (((0,), (0,)), ((), ())), preferred_element_type=F32)


def full(a, b):
    return jnp.dot(a, b, precision=FULL_PRECISION)


def norm_rows(values, gain_row, shift_row):
    centred = values - jnp.mean(values, -1, keepdims=True)
    return (
        centred * lax.rsqrt(jnp.mean(centred * centred, -1, keepdims=True) + 1e-06) * gain_row
        + shift_row
    )


def unit_rows(values):
    return values * lax.rsqrt(jnp.sum(values * values, -1, keepdims=True) + 1e-06)


def log_sum(scores):
    highest = jnp.max(scores, -1, keepdims=True)
    return highest[..., 0] + jnp.log(jnp.sum(jnp.exp(scores - highest), -1))


def adam_update(master, first, second, gradient, rate):
    first_new = BETA_ONE * first + (1.0 - BETA_ONE) * gradient
    second_new = BETA_TWO * second + (1.0 - BETA_TWO) * gradient * gradient
    first_hat = first_new / (1.0 - BETA_ONE**ADAM_STEP)
    second_hat = second_new / (1.0 - BETA_TWO**ADAM_STEP)
    master_new = master - rate * (
        first_hat / (jnp.sqrt(second_hat) + EPSILON) + WEIGHT_DECAY * master
    )
    return (master_new, first_new, second_new)


def everyone_kernel(x_ref, o_ref, send, recv, local):
    group = lax.axis_size("fsdp")
    count = lax.axis_size("dp") * group
    me = lax.axis_index("dp") * group + lax.axis_index("fsdp")
    barrier = pltpu.get_barrier_semaphore()

    def place(step):
        peer = lax.rem(me + step, count)
        return (peer // group, lax.rem(peer, group))

    def greet(step, carry):
        pl.semaphore_signal(barrier, inc=1, device_id=place(step), device_id_type=MESH_ID)
        return carry

    lax.fori_loop(1, count, greet, 0)
    mine = pltpu.make_async_copy(x_ref, o_ref.at[me], local)
    mine.start()
    pl.semaphore_wait(barrier, count - 1)

    def copy(step):
        return pltpu.make_async_remote_copy(
            src_ref=x_ref,
            dst_ref=o_ref.at[me],
            send_sem=send.at[step],
            recv_sem=recv.at[step],
            device_id=place(step),
            device_id_type=MESH_ID,
        )

    def begin(step, carry):
        copy(step).start()
        return carry

    def finish(step, carry):
        copy(step).wait()
        return carry

    lax.fori_loop(1, count, begin, 0)
    mine.wait()
    lax.fori_loop(1, count, finish, 0)


def everyone(x, collective):
    count = lax.axis_size("dp") * lax.axis_size("fsdp")
    return pl.pallas_call(
        everyone_kernel,
        out_shape=jax.ShapeDtypeStruct((count,) + x.shape, x.dtype),
        in_specs=[pl.BlockSpec(memory_space=pltpu.VMEM)],
        out_specs=pl.BlockSpec(memory_space=pltpu.VMEM),
        scratch_shapes=[
            pltpu.SemaphoreType.DMA((count,)),
            pltpu.SemaphoreType.DMA((count,)),
            pltpu.SemaphoreType.DMA,
        ],
        compiler_params=pltpu.CompilerParams(collective_id=collective, has_side_effects=True),
        name=f"everyone_{collective}",
    )(x)


def attend_kernel(rows, block, masked, *refs):
    if masked:
        qkv_ref, bias_ref, o_ref, l_ref = refs
    else:
        qkv_ref, o_ref, l_ref = refs
    lane = lax.broadcasted_iota(jnp.int32, (1, 128), 1)
    low = lane < 64
    keys = qkv_ref[:, 128:256]
    values = qkv_ref[:, 256:384]
    for at in range(0, rows, block):
        queries = qkv_ref[at : at + block, :128]
        outs, totals = [], []
        for head in range(2):
            picked = jnp.where(low if head == 0 else ~low, queries, 0) * jnp.array(0.125, BF16)
            scores = dot_nt(picked, keys)
            if masked:
                scores = scores + bias_ref[at : at + block, :]
            highest = jnp.max(scores, -1, keepdims=True)
            exponent = jnp.exp(scores - highest)
            summed = jnp.sum(exponent, -1, keepdims=True)
            outs.append(dot(exponent.astype(BF16), values) * (1.0 / summed))
            totals.append(highest + jnp.log(summed))
        o_ref[at : at + block, :] = jnp.where(low, outs[0], outs[1]).astype(BF16)
        l_ref[at : at + block, :] = jnp.where(low, totals[0], totals[1])


def attend(qkv, bias, block):
    rows, width = qkv.shape
    pairs = width // 384
    specs = [pl.BlockSpec((rows, 384), lambda j: (0, j))]
    args = [qkv]
    if bias is not None:
        specs.append(pl.BlockSpec(bias.shape, lambda j: (0, 0)))
        args.append(bias)
    return pl.pallas_call(
        functools.partial(attend_kernel, rows, block, bias is not None),
        grid=(pairs,),
        out_shape=(
            jax.ShapeDtypeStruct((rows, pairs * 128), BF16),
            jax.ShapeDtypeStruct((rows, pairs * 128), F32),
        ),
        in_specs=specs,
        out_specs=(
            pl.BlockSpec((rows, 128), lambda j: (0, j)),
            pl.BlockSpec((rows, 128), lambda j: (0, j)),
        ),
        compiler_params=pltpu.CompilerParams(vmem_limit_bytes=VMEM_LIMIT),
        cost_estimate=pl.CostEstimate(
            flops=16 * rows * rows * 256 * pairs,
            bytes_accessed=rows * pairs * 128 * 12,
            transcendentals=2 * pairs * rows * rows,
        ),
        name=f"attend_{rows}",
    )(*args)


def attend_back_kernel(rows, block, masked, *refs):
    if masked:
        qkv_ref, do_ref, o_ref, l_ref, bias_ref, g_ref, dk_ref, dv_ref = refs
    else:
        qkv_ref, do_ref, o_ref, l_ref, g_ref, dk_ref, dv_ref = refs
    lane = lax.broadcasted_iota(jnp.int32, (1, 128), 1)
    low = lane < 64
    keys = qkv_ref[:, 128:256]
    values = qkv_ref[:, 256:384]
    keys_t = keys.astype(F32).T.astype(BF16)
    row = lax.broadcasted_iota(jnp.int32, (128, 1), 0)
    keys_of = [jnp.where(row < 64, keys_t, 0), jnp.where(row < 64, 0, keys_t)]
    eighth = jnp.array(0.125, BF16)
    for at in range(0, rows, block):
        queries = qkv_ref[at : at + block, :128]
        grads = do_ref[at : at + block, :]
        totals_t = l_ref[at : at + block, :].T
        product_t = (grads.astype(F32) * o_ref[at : at + block, :].astype(F32)).T
        grad_q = None
        for head in range(2):
            mask = low if head == 0 else ~low
            picked = jnp.where(mask, queries, 0) * eighth
            picked_grad = jnp.where(mask, grads, 0)
            total = totals_t[64 * head : 64 * head + 1, :]
            delta = jnp.sum(product_t[64 * head : 64 * head + 64, :], 0, keepdims=True)
            scores = dot_nt(keys, picked)
            if masked:
                scores = scores + bias_ref[:, at : at + block]
            weights = jnp.exp(scores - total)
            grad_weights = dot_nt(values, picked_grad)
            grad_scores = (weights * (grad_weights - delta)).astype(BF16)
            part_v = dot(weights.astype(BF16), picked_grad)
            part_k = dot(grad_scores, picked)
            if at == 0 and head == 0:
                dv_ref[...] = part_v
                dk_ref[...] = part_k
            else:
                dv_ref[...] += part_v
                dk_ref[...] += part_k
            part_q = dot(keys_of[head], grad_scores)
            grad_q = part_q if grad_q is None else grad_q + part_q
        g_ref[at : at + block, :128] = (grad_q.T * 0.125).astype(BF16)
    g_ref[:, 128:256] = dk_ref[...].astype(BF16)
    g_ref[:, 256:384] = dv_ref[...].astype(BF16)


def attend_back(qkv, grad_out, out, totals, bias, block):
    rows, width = qkv.shape
    pairs = width // 384
    specs = [
        pl.BlockSpec((rows, 384), lambda j: (0, j)),
        pl.BlockSpec((rows, 128), lambda j: (0, j)),
        pl.BlockSpec((rows, 128), lambda j: (0, j)),
        pl.BlockSpec((rows, 128), lambda j: (0, j)),
    ]
    args = [qkv, grad_out, out, totals]
    if bias is not None:
        specs.append(pl.BlockSpec(bias.shape, lambda j: (0, 0)))
        args.append(bias)
    return pl.pallas_call(
        functools.partial(attend_back_kernel, rows, block, bias is not None),
        grid=(pairs,),
        out_shape=jax.ShapeDtypeStruct(qkv.shape, BF16),
        in_specs=specs,
        out_specs=pl.BlockSpec((rows, 384), lambda j: (0, j)),
        scratch_shapes=[pltpu.VMEM((rows, 128), F32), pltpu.VMEM((rows, 128), F32)],
        compiler_params=pltpu.CompilerParams(vmem_limit_bytes=VMEM_LIMIT),
        cost_estimate=pl.CostEstimate(
            flops=40 * rows * rows * 256 * pairs,
            bytes_accessed=rows * pairs * 128 * 20,
            transcendentals=2 * pairs * rows * rows,
        ),
        name=f"attend_back_{rows}",
    )(*args)


def feed_kernel(with_product, h_ref, w_ref, sel_ref, slope_ref, sums_ref, *rest):
    hidden = dot(h_ref[...], w_ref[...])
    root = 0.7978845608028654
    square = hidden * hidden
    tang = jnp.tanh(root * hidden * (1.0 + 0.044715 * square))
    half = 0.5 * (1.0 + tang)
    active = (hidden * half).astype(BF16)
    slope = half + (0.5 * root) * hidden * (1.0 - tang * tang) * (1.0 + (3 * 0.044715) * square)
    slope = slope.astype(BF16)
    slope_ref[...] = slope
    if with_product:
        sums_ref[...] = jnp.broadcast_to(
            jnp.sum(active.astype(F32), 0, keepdims=True), sums_ref.shape
        )
        rest[0][...] = dot_tn(h_ref[...], slope).astype(BF16)
    else:
        sums_ref[...] = dot(sel_ref[...], active)


def feed(normed, weight, select, column, tile, with_product):
    rows, features = normed.shape
    width = weight.shape[1] - column
    first = column // tile
    shapes = [
        jax.ShapeDtypeStruct((rows, width), BF16),
        jax.ShapeDtypeStruct((8, width), F32),
    ]
    outs = [
        pl.BlockSpec((rows, tile), lambda j: (0, j)),
        pl.BlockSpec((8, tile), lambda j: (0, j)),
    ]
    if with_product:
        shapes.append(jax.ShapeDtypeStruct((features, width), BF16))
        outs.append(pl.BlockSpec((features, tile), lambda j: (0, j)))
    return pl.pallas_call(
        functools.partial(feed_kernel, with_product),
        grid=(width // tile,),
        out_shape=tuple(shapes),
        in_specs=[
            pl.BlockSpec((rows, features), lambda j: (0, 0)),
            pl.BlockSpec((features, tile), lambda j: (0, first + j)),
            pl.BlockSpec(select.shape, lambda j: (0, 0)),
        ],
        out_specs=tuple(outs),
        compiler_params=pltpu.CompilerParams(vmem_limit_bytes=VMEM_LIMIT),
        cost_estimate=pl.CostEstimate(
            flops=4 * rows * features * width,
            bytes_accessed=2 * features * width * 2 + 2 * rows * width,
            transcendentals=rows * width,
        ),
        name=f"feed_{rows}",
    )(normed, weight, select)


def layer_forward(stream, bias, mixing, gains, select, block, with_product):
    features = stream.shape[1]
    normed = norm_rows(stream, gains[0], gains[1]).astype(BF16)
    joined = dot(normed, mixing[:, : 3 * features]).astype(BF16)
    mixed, totals = attend(joined, bias, block)
    middle = stream + dot(mixed, mixing[:, 3 * features : 4 * features])
    normed_two = norm_rows(middle, gains[2], gains[3]).astype(BF16)
    fed = feed(normed_two, mixing, select, 4 * features, 512, with_product)
    return middle, fed, (stream, normed, joined, totals, mixed, middle, normed_two)


def layer_backward(grad_rows, grad_normed_two, saved, bias, mixing, gains, block):
    stream, normed, joined, totals, mixed, middle, normed_two = saved
    features = stream.shape[1]
    grad_middle_norm, grad_gain_three, grad_shift_three = jax.vjp(
        norm_rows, middle, gains[2], gains[3]
    )[1](grad_normed_two)
    grad_middle = grad_rows + grad_middle_norm
    grad_attention = grad_middle.astype(BF16)
    grad_output = dot_tn(mixed, grad_attention)
    grad_mixed = dot_nt(grad_attention, mixing[:, 3 * features : 4 * features]).astype(BF16)
    grad_joined = attend_back(
        joined, grad_mixed, mixed, totals, None if bias is None else bias.T, block
    )
    grad_inward = dot_tn(normed, grad_joined)
    grad_normed = dot_nt(grad_joined, mixing[:, : 3 * features])
    grad_stream_norm, grad_gain_one, grad_shift_one = jax.vjp(
        norm_rows, stream, gains[0], gains[1]
    )[1](grad_normed)
    grad_gains = jnp.stack([grad_gain_one, grad_shift_one, grad_gain_three, grad_shift_three])
    return (grad_middle + grad_stream_norm, grad_inward, grad_output, grad_gains)


def body(
    video,
    audio,
    word_ids,
    word_counts,
    caption_counts,
    caption_clips,
    mixing_in,
    mixing_in_first,
    mixing_in_second,
    mixing_out,
    mixing_out_first,
    mixing_out_second,
    norm_params,
    norm_params_first,
    norm_params_second,
    input_embed,
    input_embed_first,
    input_embed_second,
    word_table,
    word_table_first,
    word_table_second,
    head_proj,
    head_proj_first,
    head_proj_second,
    video_text_proj,
    video_text_proj_first,
    video_text_proj_second,
):
    group = lax.axis_size("fsdp")
    replicas = lax.axis_size("dp")
    clips = group * replicas
    member = lax.axis_index("fsdp")
    replica = lax.axis_index("dp")
    clip = replica * group + member
    captions, slots = word_ids.shape[1:]
    words = captions * slots
    patch = video.shape[2]
    video_count, audio_count = video.shape[1], audio.shape[1]
    features = mixing_in.shape[1] * group
    pairs = features // 128
    shard = mixing_in.shape[1]
    qkv = 3 * features

    gain_part = norm_params.shape[2]
    packed = jnp.concatenate(
        [
            word_ids.reshape(-1).astype(F32),
            word_counts.reshape(-1).astype(F32),
            caption_counts.reshape(-1).astype(F32),
            caption_clips.reshape(-1).astype(F32),
            norm_params.reshape(-1),
        ]
    )
    size = packed.shape[0]
    packed = jnp.pad(packed, (0, -size % 1024)).reshape(-1, 128)
    every = everyone(packed, 0).reshape(clips, -1)
    all_ids = every[:, :words].astype(jnp.int32)
    at = words + captions
    all_caption_counts = every[:, at].astype(jnp.int32)
    all_counts = every[:, words : words + captions]
    all_caption_clips = every[:, at + 1 : at + 1 + captions].astype(jnp.int32)
    at = at + 1 + captions
    gains_all = (
        every[:group, at : at + 18 * gain_part]
        .reshape(group, 3, 6, gain_part)
        .transpose(1, 2, 0, 3)
        .reshape(3, 6, features)
        .astype(BF16)
        .astype(F32)
    )

    def gather(values, axis=0):
        return lax.all_gather(values, "fsdp", axis=axis, tiled=True)

    def regroup(values):
        inward = values[:, :qkv].reshape(shard, 3, pairs, 128).transpose(0, 2, 1, 3)
        return jnp.concatenate([inward.reshape(shard, qkv), values[:, qkv:]], 1)

    embed = gather(input_embed.astype(BF16))
    mixings = [gather(regroup(mixing_in[tower].astype(BF16))) for tower in range(3)]
    backs = gather(mixing_out.astype(BF16), 1)
    heads = gather(head_proj.astype(BF16)).astype(F32)
    video_text = gather(video_text_proj.astype(BF16)).astype(F32)

    table_rows = word_table.shape[0]

    def owned_rows(ids):
        local_ids = ids - member * table_rows
        owned = (local_ids >= 0) & (local_ids < table_rows)
        return jnp.clip(local_ids, 0, table_rows - 1), owned

    group_ids = lax.dynamic_slice_in_dim(all_ids, replica * group, group, 0).reshape(-1)
    local_ids, owned = owned_rows(group_ids)
    words_in = lax.psum_scatter(
        jnp.where(owned[:, None], word_table[local_ids], 0.0).astype(BF16),
        "fsdp",
        scatter_dimension=0,
        tiled=True,
    ).astype(F32)

    valid = jnp.arange(slots)[None, :] < word_counts[0][:, None]
    flat_valid = valid.reshape(-1)
    caption_of = jnp.arange(words) // slots
    allowed = (caption_of[:, None] == caption_of[None, :]) & flat_valid[None, :]
    word_bias = jnp.where(allowed, 0.0, -1000000000.0).astype(F32)
    select = ((jnp.arange(8)[:, None] == caption_of[None, :]) & flat_valid[None, :]).astype(BF16)
    unused = jnp.zeros((8, 128), BF16)

    streams = (
        dot(video[0], embed[:patch]),
        dot(audio[0], embed[patch:]),
        words_in,
    )
    biases = (None, None, word_bias)
    selects = (unused, unused, select)
    forward_block = (512, 512, words)
    backward_block = (512, 256, words)
    caches, slopes, sums, products = [], [], [], []
    tokens = []
    counts = word_counts[0].astype(F32)
    for tower in range(3):
        middle, fed, cache = layer_forward(
            streams[tower],
            biases[tower],
            mixings[tower],
            gains_all[tower],
            selects[tower],
            forward_block[tower],
            tower < 2,
        )
        caches.append(cache)
        slopes.append(fed[0])
        if tower < 2:
            products.append(fed[2])
            summed = fed[1][:1]
            base = jnp.sum(middle, 0, keepdims=True)
            scale = 1.0 / middle.shape[0]
        else:
            summed = fed[1][:captions]
            base = full(select[:captions].astype(F32), middle)
            scale = 1.0 / counts[:, None]
        upper = summed.astype(BF16)
        lower = (summed - upper.astype(F32)).astype(BF16)
        through = dot(upper, backs[tower]) + dot(lower, backs[tower])
        tokens.append((base + through) * scale)
        sums.append(summed)

    token_count = 2 + captions
    mine = jnp.concatenate(tokens, 0)
    pooled = everyone(jnp.pad(mine, ((0, -token_count % 8), (0, 0))), 1)
    pooled_rows = (pooled[:, 0], pooled[:, 1], pooled[:, 2:token_count].reshape(-1, features))
    live = (jnp.arange(captions)[None, :] < all_caption_counts[:, None]).reshape(-1)
    positive = live[None, :] & (all_caption_clips.reshape(-1)[None, :] == jnp.arange(clips)[:, None])
    joint = video_text.shape[0]
    heads_of = (heads[:, :joint], heads[:, joint : 2 * joint], heads[:, 2 * joint :])

    normed_pull = [
        jax.vjp(norm_rows, pooled_rows[t], gains_all[t, 4], gains_all[t, 5]) for t in range(3)
    ]
    z = [entry[0] for entry in normed_pull]
    embed_video = full(z[0], heads_of[0])
    embed_video_text = full(embed_video, video_text)
    embed_audio = full(z[1], heads_of[1])
    embed_text = full(z[2], heads_of[2])

    def contrast(e_video, e_video_text, e_audio, e_text):
        scores = full(unit_rows(e_video), unit_rows(e_audio).T) / SOFTMAX_WARMTH
        own = jnp.eye(clips, dtype=F32)
        matched = log_sum(scores) - jnp.sum(scores * own, -1)
        text_scores = full(unit_rows(e_video_text), unit_rows(e_text).T) / SOFTMAX_WARMTH
        every_text = log_sum(jnp.where(live[None, :], text_scores, -1e30))
        chosen_text = log_sum(jnp.where(positive, text_scores, -1e30))
        weight_rows = jnp.sum(positive.astype(F32), -1)
        live_total = jnp.sum(live.astype(F32))
        return (
            jnp.sum(matched) / clips
            + jnp.sum(weight_rows * (every_text - chosen_text)) / live_total
        )

    loss, pull = jax.vjp(contrast, embed_video, embed_video_text, embed_audio, embed_text)
    d_video, d_video_text, d_audio, d_text = pull(F32(1.0))
    d_video = d_video + full(d_video_text, video_text.T)
    d_heads = (d_video, d_audio, d_text)
    grad_pooled, grad_pool_gains = [], []
    for t in range(3):
        d_rows, d_gain, d_shift = normed_pull[t][1](full(d_heads[t], heads_of[t].T))
        grad_pooled.append(d_rows)
        grad_pool_gains.append(jnp.stack([d_gain, d_shift]))

    def own_columns(values):
        return lax.dynamic_slice_in_dim(values, member * shard, shard, 1)

    heads_grad = jnp.concatenate([full(own_columns(z[t]).T, d_heads[t]) for t in range(3)], 1)
    joint_part = video_text_proj.shape[0]
    video_text_grad = full(
        lax.dynamic_slice_in_dim(embed_video, member * joint_part, joint_part, 1).T, d_video_text
    )
    grad_rows_all = [
        grad_pooled[0] / video_count,
        grad_pooled[1] / audio_count,
        grad_pooled[2] / all_counts.reshape(-1, 1),
    ]
    branch_all = [rows.astype(BF16) for rows in grad_rows_all]

    every_sum = lax.all_gather(jnp.concatenate(sums, 0), ("dp", "fsdp"), axis=0, tiled=False)
    back_part = mixing_out.shape[1]
    own_sums = lax.dynamic_slice_in_dim(every_sum, member * back_part, back_part, 2)
    own_sums = (own_sums[:, 0], own_sums[:, 1], own_sums[:, 2:].reshape(-1, back_part))
    back_grad = jnp.stack([full(own_sums[t].T, branch_all[t].astype(F32)) for t in range(3)])

    def own_rows(values, per_clip):
        return lax.dynamic_slice_in_dim(values, clip * per_clip, per_clip, 0)

    own_grads = [own_rows(grad_rows_all[t], 1 if t < 2 else captions) for t in range(3)]
    own_slopes = [
        dot_nt(own_grads[t].astype(BF16), backs[t]) for t in range(3)
    ]

    def over_replicas(part):
        part = part.astype(BF16)
        if replicas == 2:
            other = lax.ppermute(part, "dp", [(0, 1), (1, 0)])
            return part.astype(F32) + other.astype(F32)
        return lax.psum(part, "dp").astype(F32)

    def scatter(values):
        part = lax.psum_scatter(values.astype(BF16), "fsdp", scatter_dimension=0, tiled=True)
        return over_replicas(part)

    up_grads = scatter(
        jnp.concatenate(
            [(products[t].astype(F32) * own_slopes[t]).astype(BF16) for t in (1, 0)], 1
        )
    )
    hidden = products[0].shape[1]

    grad_inputs, gains_grads, shares = [None] * 3, [None] * 3, [None] * 3
    for tower in (2, 0, 1):
        weights = mixings[tower]
        if tower == 2:
            spread = select[:captions].astype(F32).T
            rows_grad = full(spread, own_grads[tower])
            slope_rows = full(spread, own_slopes[tower])
            grad_hidden = (slopes[tower].astype(F32) * slope_rows).astype(BF16)
            up = dot_tn(caches[tower][6], grad_hidden)
            grad_normed_two = dot_nt(grad_hidden, weights[:, 4 * features :])
        else:
            rows_grad = own_grads[tower]
            scaled = (weights[:, 4 * features :].astype(F32) * own_slopes[tower]).astype(BF16)
            grad_normed_two = dot_nt(slopes[tower], scaled)
        grad_inputs[tower], inward, outward, gains_grads[tower] = layer_backward(
            rows_grad,
            grad_normed_two,
            caches[tower],
            biases[tower],
            weights,
            gains_all[tower],
            backward_block[tower],
        )
        if tower == 2:
            shares[2] = scatter(
                jnp.concatenate([inward.astype(BF16), outward.astype(BF16), up.astype(BF16)], 1)
            )
            every_word = lax.all_gather(
                grad_inputs[2].astype(BF16), ("dp", "fsdp"), axis=0, tiled=True
            )
            local_ids, owned = owned_rows(all_ids.reshape(-1))
            table_grad = jax.ops.segment_sum(
                jnp.where(owned[:, None], every_word.astype(F32), 0.0),
                local_ids,
                num_segments=table_rows,
            )
        elif tower == 0:
            shares[0] = scatter(jnp.concatenate([inward.astype(BF16), outward.astype(BF16)], 1))
        else:
            gain_columns = jnp.concatenate(gains_grads, 0)
            gain_columns = jnp.pad(gain_columns, ((0, 128 - gain_columns.shape[0]), (0, 0))).T
            shares[1] = scatter(
                jnp.concatenate(
                    [inward.astype(BF16), outward.astype(BF16), gain_columns.astype(BF16)], 1
                )
            )
    embed_grad = scatter(
        jnp.concatenate(
            [
                dot_tn(video[0], grad_inputs[0].astype(BF16)).astype(BF16),
                dot_tn(audio[0], grad_inputs[1].astype(BF16)).astype(BF16),
            ],
            0,
        )
    )

    def ungroup(part):
        inward = part[:, :qkv].reshape(shard, pairs, 3, 128).transpose(0, 2, 1, 3)
        return jnp.concatenate([inward.reshape(shard, qkv), part[:, qkv:]], 1)

    mixing_grad = jnp.stack(
        [
            ungroup(jnp.concatenate([shares[0], up_grads[:, hidden:]], 1)),
            ungroup(jnp.concatenate([shares[1][:, : 4 * features], up_grads[:, :hidden]], 1)),
            ungroup(shares[2]),
        ]
    )
    inner_gains = shares[1][:, 4 * features : 4 * features + 12].T.reshape(3, 4, gain_part)
    outer_gains = lax.dynamic_slice_in_dim(
        jnp.stack(grad_pool_gains), member * gain_part, gain_part, 2
    )
    gains_grad = jnp.concatenate([inner_gains, outer_gains], 1)

    grads = (
        mixing_grad,
        back_grad,
        gains_grad,
        embed_grad,
        table_grad,
        heads_grad,
        video_text_grad,
    )
    local_square = sum((jnp.sum(g * g) for g in grads))
    squares = everyone(jnp.full((8, 128), local_square, F32), 2)
    square = jnp.sum(squares[:group, 0, 0])
    grad_norm = jnp.sqrt(square)
    factor = CLIP_NORM / jnp.maximum(grad_norm, CLIP_NORM)
    clipped = [g * factor for g in grads]
    masters = (
        mixing_in,
        mixing_out,
        norm_params,
        input_embed,
        word_table,
        head_proj,
        video_text_proj,
    )
    firsts = (
        mixing_in_first,
        mixing_out_first,
        norm_params_first,
        input_embed_first,
        word_table_first,
        head_proj_first,
        video_text_proj_first,
    )
    seconds = (
        mixing_in_second,
        mixing_out_second,
        norm_params_second,
        input_embed_second,
        word_table_second,
        head_proj_second,
        video_text_proj_second,
    )
    new = [adam_update(masters[i], firsts[i], seconds[i], clipped[i], RATES[i]) for i in range(7)]
    outputs = [loss, grad_norm]
    for i in range(7):
        outputs += [new[i][0], clipped[4] if i == 4 else new[i][1], new[i][2]]
    return tuple(outputs)


def solution(mesh):
    both = ("dp", "fsdp")
    weight_specs = (
        P(None, "fsdp", None),
        P(None, "fsdp", None),
        P(None, None, "fsdp"),
        P("fsdp", None),
        P("fsdp", None),
        P("fsdp", None),
        P("fsdp", None),
    )
    tripled = tuple(spec for spec in weight_specs for _ in range(3))
    return jax.shard_map(
        body,
        mesh=mesh,
        in_specs=(
            P(both, None, None),
            P(both, None, None),
            P(both, None, None),
            P(both, None),
            P(both),
            P(both, None),
        )
        + tripled,
        out_specs=(P(), P()) + tripled,
        check_vma=False,
    )
```

time: 2680 us -> 1350 us (0.50)
  waiting for transfers between devices: 1370 us -> 625 us
  blocking collectives: 367 us -> 23.5 us
  matrix products: 441 us -> 161 us
  Pallas kernels: 0 us -> 172 us
  other arithmetic: 277 us -> 197 us
  local copies, waits for them, and re-layouts: 163 us -> 124 us
    reduce_scatter x9 -> x5, waiting for transfers between devices: 650 us -> 208 us  [the longest x4 208 us: scatter(): lax.psum_scatter(values.astype(BF16), 'fsdp', scatter_dimension=0, tiled=...]
    unnamed x29 -> x15, waiting for transfers between devices: 400 us -> 71 us
    dot_general x79 -> x59, matrix products: 441 us -> 161 us  [the longest x12 56 us: dot_nt(): return lax.dot_general(a, b, NT, preferred_element_type=F32)]
    all_gather x9 -> x8, waiting for transfers between devices: 107 us -> 334 us  [the longest x6 279 us: gather(): return lax.all_gather(values, 'fsdp', axis=axis, tiled=True)]
    all_gather x8 -> x1, blocking collectives: 248 us -> 23.5 us  [gather(): return lax.all_gather(values, 'fsdp', axis=axis, tiled=True)]
    psum x1 -> x0, waiting for transfers between devices: 217 us -> none  [body(): lax.psum(jnp.stack(mixing_shards).astype(jnp.bfloat16), 'dp')]
    pallas_call x0 -> x12, Pallas kernels: none -> 172 us  [the longest x3 51.7 us: attend_back(): pl.pallas_call(functools.partial(attend_back_kernel, rows, block, bias is...]
    psum x3 -> x0, blocking collectives: 80.5 us -> none  [the longest x1 39.8 us: body(): loss = lax.psum(loss_part, ('dp', 'fsdp'))]
  transfers between devices with their start and end apart: 24 -> 19, of which waited for: 13 -> 11; matrix products, arithmetic and copies ran while one was open for 27% -> 28% of each run, Pallas kernels for 0% -> 11%
where the time goes in v1:
time: 1350 us; the launch traced here: 1340 us
  waiting for transfers between devices  625 us (46%)
  other arithmetic  197 us (15%)
  Pallas kernels  172 us (13%)
  matrix products  161 us (12%)
  local copies, waits for them, and re-layouts  124 us (9%)
  between operations  27.9 us (2%)
  blocking collectives  23.5 us (2%)
    all_gather x6, waiting for transfers between devices, gather(): return lax.all_gather(values, 'fsdp', axis=axis, tiled=True)  279 us
    reduce_scatter x4, waiting for transfers between devices, scatter(): lax.psum_scatter(values.astype(BF16), 'fsdp', scatter_dimension=0, tiled=...  208 us
    unnamed x15, waiting for transfers between devices  71 us
    dot_general x12, matrix products, dot_nt(): return lax.dot_general(a, b, NT, preferred_element_type=F32)  56 us
    all_gather x1, waiting for transfers between devices, body(): lax.all_gather(grad_inputs[2].astype(BF16), ('dp', 'fsdp'), axis=0, tiled...  54.6 us
    pallas_call x3, Pallas kernels, attend_back(): pl.pallas_call(functools.partial(attend_back_kernel, rows, block, bias is...  51.7 us
    sub x7, other arithmetic, adam_update(): master - rate * (first_hat / (jnp.sqrt(second_hat) + EPSILON) + WEIGHT_DE...  51 us
    dot_general x14, matrix products, dot(): return jnp.dot(a, b, preferred_element_type=F32)  47.5 us
  transfers between devices with their start and end apart: 19, of which 11 were waited for; matrix products, arithmetic and copies ran while one was open for 28% of the time, Pallas kernels for 11%

profile of v1, /device:TPU:0, one launch (start us, length us, event | category | flops | bytes accessed | tf_op | source)
XLA Modules:
  0.0 1338.3 jit_solution(12517145283576194030)
XLA Ops:
  11.1 12.8 everyone_0.1
  25.7 11.3 gather_fusion
  37.0 3.5 select_convert_fusion
  86.5 23.5 %all_gather.36 = bf16[512,256]{1,0:T(8,128)(2,1)} all-gather(bf16[32,256]{1,0:T(8,128)(2,1)S(1)} %convert_element_type.352), channel_id=1, replica_groups=mesh['dp'=2,'fsdp'=16] {'fsdp'}, dimensions={0}, use_global_device_ids=true | all-gather | bytes 278528 | tf_op jit(solution)/shard_map/all_gather | solution.py:421
  113.4 47.4 %all-gather.11.cloned.1.call-done = bf16[3200,768]{1,0:T(8,128)(2,1)} async-done(((bf16[200,768]{1,0:T(8,128)(2,1)}), bf16[3200,768]{1,0:T(8,128)(2,1)}) %all-gather.11.cloned.1.call-update) | async-done | bytes 4915216 | tf_op jit(solution)/shard_map/all_gather | solution.py:421
  160.9 5.0 fusion.229
  165.9 3.4 fusion.227
  170.3 3.9 copy.109
  176.6 67.5 %all-gather.19.cloned.1.call-done.w_ref = bf16[768,6144]{1,0:T(8,128)(2,1)} async-done(((bf16[48,6144]{1,0:T(8,128)(2,1)}), bf16[768,6144]{1,0:T(8,128)(2,1)}) %all-gather.19.cloned.1.call-update) | async-done | bytes 9437200 | tf_op jit(solution)/shard_map/all_gather | solution.py:421
  244.0 3.5 convolution_convert_fusion.7.refs_0_
  247.6 5.7 attend_96.1
  256.1 6.2 feed_96.1
  263.8 63.0 %all-gather.13.cloned.1.call-done.w_ref = bf16[768,6144]{1,0:T(8,128)(2,1)} async-done(((bf16[48,6144]{1,0:T(8,128)(2,1)}), bf16[768,6144]{1,0:T(8,128)(2,1)}) %all-gather.13.cloned.1.call-update) | async-done | bytes 9437200 | tf_op jit(solution)/shard_map/all_gather | solution.py:421
  326.7 6.0 convolution_convert_fusion.6.refs_0_
  332.8 8.4 attend_512.1
  341.1 3.4 fusion.230
  344.6 64.7 %all-gather.17.cloned.1.call-done.w_ref = bf16[768,6144]{1,0:T(8,128)(2,1)} async-done(((bf16[48,6144]{1,0:T(8,128)(2,1)}), bf16[768,6144]{1,0:T(8,128)(2,1)}) %all-gather.17.cloned.1.call-update) | async-done | bytes 9437200 | tf_op jit(solution)/shard_map/all_gather | solution.py:421
  409.3 9.2 convolution_convert_fusion.refs_0_
  418.5 22.4 %attend_1024.1 = (bf16[1024,768]{1,0:T(8,128)(2,1)}, f32[1024,768]{1,0:T(8,128)}) custom-call(bf16[1024,2304]{1,0:T(8,128)(2,1)} %convolution_convert_fusion.refs_0_), custom_call_target="tpu_custom_call" | custom-call | flops 25769803776 | bytes 9437184 | tf_op jit(solution)/shard_map/attend_1024/pallas_call | solution.py:163
  443.1 12.2 feed_512.1
  456.2 2.9 fusion.228
  462.5 19.6 %feed_1024.1 = (bf16[1024,3072]{1,0:T(8,128)(2,1)}, f32[8,3072]{1,0:T(8,128)}, bf16[768,3072]{1,0:T(8,128)(2,1)}) custom-call(bf16[1024,768]{1,0:T(8,128)(2,1)} %add_convert_fusion.1.h_ref, bf16[768,6144]{1,0:T(8,128)(2,1)} %all-gather.17.cloned.1.call-done.w_ref, bf16[8,128]{1,0:T(8,128)(2,1)} %broadcast_in_dim.118.sel_ref), custom_call_target="tpu_custom_call" | custom-call | flops 9663676416 | bytes 15728640 | tf_op jit(solution)/shard_map/feed_1024/pallas_call | solution.py:295
  483.8 36.7 %all-gather.15.cloned.1.call-done = bf16[3,3072,768]{2,1,0:T(8,128)(2,1)} async-done(((bf16[3,192,768]{2,1,0:T(8,128)(2,1)}), bf16[3,3072,768]{2,1,0:T(8,128)(2,1)}) %all-gather.15.cloned.1.call-update) | async-done | bytes 14155792 | tf_op jit(solution)/shard_map/all_gather | solution.py:421
  520.5 3.2 fusion.54
  523.7 3.6 fusion.55
  527.4 3.2 fusion.52
  533.8 22.7 %everyone_1.1 = f32[32,8,768]{2,1,0:T(8,128)} custom-call(f32[8,768]{1,0:T(8,128)} %select_maximum_fusion.x_ref), custom_call_target="tpu_custom_call" | custom-call | tf_op jit(solution)/shard_map/everyone_1/pallas_call | solution.py:114
  557.8 2.8 slice_reduce_fusion.20
  561.2 2.7 multiply_reduce_fusion.16
  597.3 2.8 multiply_reduce_fusion.23
  601.7 3.8 fusion.21
  605.7 12.0 multiply_reduce_fusion.3
  622.0 6.6 multiply_reduce_fusion.10
  638.4 5.8 attend_back_96.1
  644.2 3.6 fusion.89
  648.6 3.0 convolution_convert_fusion.12.refs_1_
  651.7 11.3 attend_back_512.1
  663.0 6.8 multiply_reduce_fusion.9
  677.1 2.8 pad_maximum_fusion.4
  680.0 4.8 convolution_convert_fusion.8.refs_1_
  684.8 34.6 %attend_back_1024.1 = bf16[1024,2304]{1,0:T(8,128)(2,1)} custom-call(bf16[1024,2304]{1,0:T(8,128)(2,1)} %convolution_convert_fusion.refs_0_, bf16[1024,768]{1,0:T(8,128)(2,1)} %convolution_convert_fusion.8.refs_1_, bf16[1024,768]{1,0:T(8,128)(2,1)} %get-tuple-element.39.refs_2_, f32[1024,768]{1,0:T(8,128)} %get-tuple-element.48.refs_3_), custom_call_target="tpu_custom_call" | custom-call | flops 64424509440 | bytes 15728640 | tf_op jit(solution)/shard_map/attend_back_1024/pallas_call | solution.py:244
  719.5 9.9 multiply_reduce_fusion.2
  731.3 4.1 convolution_convert_fusion.10
  735.4 6.9 convolution_convert_fusion.4
  745.5 2.6 fusion.215
  748.2 3.2 fusion.216
  752.8 3.4 fusion.17
  758.8 7.5 copy.133
  771.6 4.1 pad_maximum_fusion.1
  778.6 4.0 multiply_convert_fusion.2
  784.1 4.0 pad_maximum_fusion
  823.6 21.4 %reduce-scatter.15.cloned.1.call-done = bf16[48,3200]{1,0:T(8,128)(2,1)} async-done(((bf16[768,3200]{1,0:T(8,128)(2,1)}), bf16[48,3200]{1,0:T(8,128)(2,1)}) %reduce-scatter.15.cloned.1.call-update) | async-done | bytes 307216 | tf_op jit(solution)/shard_map/reduce_scatter | solution.py:575
  855.2 70.7 %reduce-scatter.19.cloned.1.call-done = bf16[200,768]{1,0:T(8,128)(2,1)} async-done(((bf16[3200,768]{1,0:T(8,128)(2,1)}), bf16[200,768]{1,0:T(8,128)(2,1)}) %reduce-scatter.19.cloned.1.call-update) | async-done | bytes 307216
  931.2 109.5 %reduce-scatter.17.cloned.1.call-done = bf16[48,6144]{1,0:T(8,128)(2,1)} async-done(((bf16[768,6144]{1,0:T(8,128)(2,1)}), bf16[48,6144]{1,0:T(8,128)(2,1)}) %reduce-scatter.17.cloned.1.call-update) | async-done | bytes 589840 | tf_op jit(solution)/shard_map/reduce_scatter | solution.py:575
  1053.2 54.6 %all-gather.23.cloned.1.call-done = bf16[3072,768]{1,0:T(8,128)(2,1)} async-done(((bf16[96,768]{1,0:T(8,128)(2,1)}), bf16[3072,768]{1,0:T(8,128)(2,1)}) %all-gather.23.cloned.1.call-update) | async-done | bytes 4718608 | tf_op jit(solution)/shard_map/all_gather | solution.py:612
  1107.8 29.3 %scatter_custom_fusion = f32[4096,768]{1,0:T(8,128)} fusion(s32[3072]{0:T(1024)} %reshape.773, bf16[3072,768]{1,0:T(8,128)(2,1)} %all-gather.23.cloned.1.call-done, f32[]{:T(128)} %constant.81.clone.1, pred[3072]{0:T(1024)(128)(4,1)S(1)} %copy-done.136), kind=kCustom, calls=%fused_computation.8 | custom fusion | flops 7077888 | bytes 17305600 | tf_op jit(solution)/shard_map/scatter-add | solution.py:616
  1137.1 8.4 multiply_reduce_fusion
  1145.5 77.5 %reduce-scatter.13.cloned.1.call-done = bf16[48,6144]{1,0:T(8,128)(2,1)} async-done(((bf16[768,6144]{1,0:T(8,128)(2,1)}), bf16[48,6144]{1,0:T(8,128)(2,1)}) %reduce-scatter.13.cloned.1.call-update) | async-done | bytes 589840 | tf_op jit(solution)/shard_map/reduce_scatter | solution.py:575
  1227.1 11.2 collective-permute-done.1
  1257.2 10.5 everyone_2.1
  1269.9 3.6 multiply_subtract_fusion.3
  1283.7 6.5 multiply_subtract_fusion.2
  1291.8 6.9 multiply_subtract_fusion.1
  1298.7 29.9 %multiply_subtract_fusion = (f32[4096,768]{1,0:T(8,128)}, f32[4096,768]{1,0:T(8,128)}, f32[4096,768]{1,0:T(8,128)}) fusion(f32[4096,768]{1,0:T(8,128)} %param.45, f32[4096,768]{1,0:T(8,128)} %param.46, f32[4096,768]{1,0:T(8,128)} %param.47, f32[4096,768]{1,0:T(8,128)} %scatter_custom_fusion, f32[]{:T(128)S(6)} %div.462), kind=kLoop, calls=%fused_computation.4 | loop fusion | flops 50331648 | bytes 88080384 | tf_op jit(solution)/shard_map/sub | solution.py:64
  (723 shorter events, 242.4 us)
Async XLA Ops:
  7.2 153.7 %copy-start = (bf16[1,512,3072]{2,1,0:T(8,128)(2,1)S(1)}, bf16[1,512,3072]{2,1,0:T(8,128)(2,1)}, u32[]{:S(2)}) copy-start(bf16[1,512,3072]{2,1,0:T(8,128)(2,1)} %param.27) | copy-start | bytes 9437188
  7.2 103.5 %reduce-scatter.9.cloned.1.call-start = ((), (), s32[]{:S(2)}) async-start(), calls=%async_computation.10 | async-start | bytes 2506752 | tf_op jit(solution)/shard_map/reduce_scatter | solution.py:442
  40.6 120.3 %all-gather.11.cloned.1.call-start = ((), (), s32[]{:S(2)}) async-start(), calls=%async_computation.6 | async-start | bytes 5222400 | tf_op jit(solution)/shard_map/all_gather | solution.py:421
  42.5 201.6 %all-gather.19.cloned.1.call-start = ((), (), s32[]{:S(2)}) async-start(), calls=%async_computation.11 | async-start | bytes 10027008 | tf_op jit(solution)/shard_map/all_gather | solution.py:421
  54.0 272.7 %all-gather.13.cloned.1.call-start = ((), (), s32[]{:S(2)}) async-start(), calls=%async_computation.7 | async-start | bytes 10027008 | tf_op jit(solution)/shard_map/all_gather | solution.py:421
  64.1 345.2 %all-gather.17.cloned.1.call-start = ((), (), s32[]{:S(2)}) async-start(), calls=%async_computation.9 | async-start | bytes 10027008 | tf_op jit(solution)/shard_map/all_gather | solution.py:421
  74.2 446.3 %all-gather.15.cloned.1.call-start = ((), (), s32[]{:S(2)}) async-start(), calls=%async_computation.8 | async-start | bytes 15040512 | tf_op jit(solution)/shard_map/all_gather | solution.py:421
  76.9 492.2 %all-gather.21.cloned.1.call-start = ((), (), s32[]{:S(2)}) async-start(), calls=%async_computation.12 | async-start | bytes 2088960 | tf_op jit(solution)/shard_map/all_gather | solution.py:421
  77.7 720.0 %all-gather.25.cloned.1.call-start = ((), (), s32[]{:S(2)}) async-start(), calls=%async_computation.18 | async-start | bytes 3244032 | tf_op jit(solution)/shard_map/all_gather | solution.py:553
  86.4 157.6 %copy-start.79 = (f32[768]{0:T(1024)}, f32[768]{0:T(1024)S(1)}, u32[]{:S(2)}) copy-start(f32[768]{0:T(1024)S(1)} %get-tuple-element.162) | copy-start | bytes 9220
  86.4 157.6 %copy-start.122 = (f32[768]{0:T(1024)}, f32[768]{0:T(1024)S(1)}, u32[]{:S(2)}) copy-start(f32[768]{0:T(1024)S(1)} %get-tuple-element.161) | copy-start | bytes 9220
  86.4 168.8 %copy-start.91 = (f32[768]{0:T(1024)}, f32[768]{0:T(1024)S(1)}, u32[]{:S(2)}) copy-start(f32[768]{0:T(1024)S(1)} %get-tuple-element.160) | copy-start | bytes 9220
  86.4 240.3 %copy-start.134 = (f32[768]{0:T(1024)}, f32[768]{0:T(1024)S(1)}, u32[]{:S(2)}) copy-start(f32[768]{0:T(1024)S(1)} %get-tuple-element.170) | copy-start | bytes 9220
  86.4 240.3 %copy-start.158 = (f32[768]{0:T(1024)}, f32[768]{0:T(1024)S(1)}, u32[]{:S(2)}) copy-start(f32[768]{0:T(1024)S(1)} %get-tuple-element.169) | copy-start | bytes 9220
  86.4 322.9 %copy-start.124 = (f32[768]{0:T(1024)}, f32[768]{0:T(1024)S(1)}, u32[]{:S(2)}) copy-start(f32[768]{0:T(1024)S(1)} %get-tuple-element.166) | copy-start | bytes 9220
  86.4 322.9 %copy-start.156 = (f32[768]{0:T(1024)}, f32[768]{0:T(1024)S(1)}, u32[]{:S(2)}) copy-start(f32[768]{0:T(1024)S(1)} %get-tuple-element.165) | copy-start | bytes 9220
  86.4 354.8 %copy-start.102 = (f32[768]{0:T(1024)}, f32[768]{0:T(1024)S(1)}, u32[]{:S(2)}) copy-start(f32[768]{0:T(1024)S(1)} %get-tuple-element.168) | copy-start | bytes 9220
  86.5 373.4 %copy-start.89 = (f32[768]{0:T(1024)}, f32[768]{0:T(1024)S(1)}, u32[]{:S(2)}) copy-start(f32[768]{0:T(1024)S(1)} %get-tuple-element.164) | copy-start | bytes 9220
  111.8 132.3 %copy-start.137 = (f32[96]{0:T(128)}, f32[96]{0:T(128)S(1)}, u32[]{:S(2)}) copy-start(f32[96]{0:T(128)S(1)} %broadcast_multiply_fusion.10) | copy-start | bytes 1156
  113.4 130.6 %copy-start.144 = (f32[96]{0:T(128)}, f32[96]{0:T(128)S(1)}, u32[]{:S(2)}) copy-start(f32[96]{0:T(128)S(1)} %fusion.184) | copy-start | bytes 1156
  113.4 52.5 %copy-start.74 = (bf16[1,1024,128]{2,1,0:T(8,128)(2,1)S(1)}, bf16[1,1024,128]{2,1,0:T(8,128)(2,1)}, u32[]{:S(2)}) copy-start(bf16[1,1024,128]{2,1,0:T(8,128)(2,1)} %param.28) | copy-start | bytes 786436
  165.9 160.8 %copy-start.112 = (f32[512]{0:T(512)}, f32[512]{0:T(512)S(1)}, u32[]{:S(2)}) copy-start(f32[512]{0:T(512)S(1)} %broadcast_multiply_fusion.5) | copy-start | bytes 6148
  169.4 239.9 %copy-start.93 = (f32[1024]{0:T(1024)}, f32[1024]{0:T(1024)S(1)}, u32[]{:S(2)}) copy-start(f32[1024]{0:T(1024)S(1)} %broadcast_multiply_fusion.3) | copy-start | bytes 12292
  169.7 157.1 %copy-start.142 = (f32[512]{0:T(512)}, f32[512]{0:T(512)S(1)}, u32[]{:S(2)}) copy-start(f32[512]{0:T(512)S(1)} %fusion.177) | copy-start | bytes 6148
  174.1 69.9 %copy-start.25 = (bf16[96,768]{1,0:T(8,128)(2,1)S(1)}, bf16[96,768]{1,0:T(8,128)(2,1)}, u32[]{:S(2)}) copy-start(bf16[96,768]{1,0:T(8,128)(2,1)} %reduce-scatter.9.cloned.1.call-done) | copy-start | bytes 442372
  176.5 76.7 %copy-start.98 = (f32[1024]{0:T(1024)}, f32[1024]{0:T(1024)S(1)}, u32[]{:S(2)}) copy-start(f32[1024]{0:T(1024)S(1)} %multiply_reduce_fusion.7) | copy-start | bytes 12292
  176.6 232.7 %copy-start.130 = (f32[1024]{0:T(1024)}, f32[1024]{0:T(1024)S(1)}, u32[]{:S(2)}) copy-start(f32[1024]{0:T(1024)S(1)} %fusion.163) | copy-start | bytes 12292
  344.6 96.7 %copy-start.104 = (f32[512]{0:T(512)}, f32[512]{0:T(512)S(1)}, u32[]{:S(2)}) copy-start(f32[512]{0:T(512)S(1)} %broadcast_multiply_fusion.4) | copy-start | bytes 6148
  418.5 22.4 %copy-start.8 = (f32[512,768]{1,0:T(8,128)S(1)}, f32[512,768]{1,0:T(8,128)}, u32[]{:S(2)}) copy-start(f32[512,768]{1,0:T(8,128)} %get-tuple-element.253) | copy-start | bytes 4718596
  459.8 22.3 %copy-start.100 = (f32[1024]{0:T(1024)}, f32[1024]{0:T(1024)S(1)}, u32[]{:S(2)}) copy-start(f32[1024]{0:T(1024)S(1)} %get-tuple-element.130) | copy-start | bytes 12292
  459.9 22.3 %copy-start.95 = (f32[1024]{0:T(1024)}, f32[1024]{0:T(1024)S(1)}, u32[]{:S(2)}) copy-start(f32[1024]{0:T(1024)S(1)} %fusion.164) | copy-start | bytes 12292
  462.5 58.0 %copy-start.64 = (f32[8,3072]{1,0:T(8,128)S(1)}, f32[8,3072]{1,0:T(8,128)}, u32[]{:S(2)}) copy-start(f32[8,3072]{1,0:T(8,128)} %get-tuple-element.38) | copy-start | bytes 294916
  483.7 334.3 %reduce-scatter.11.cloned.1.call-start = ((), (), s32[]{:S(2)}) async-start(), calls=%async_computation.13 | async-start | bytes 5013504 | tf_op jit(solution)/shard_map/reduce_scatter | solution.py:575
  563.9 23.2 %copy-start.81 = (f32[768]{0:T(1024)S(1)}, f32[768]{0:T(1024)}, u32[]{:S(2)}) copy-start(f32[768]{0:T(1024)} %get-tuple-element.153) | copy-start | bytes 9220
  563.9 23.2 %copy-start.126 = (f32[768]{0:T(1024)S(1)}, f32[768]{0:T(1024)}, u32[]{:S(2)}) copy-start(f32[768]{0:T(1024)} %get-tuple-element.154) | copy-start | bytes 9220
  563.9 23.2 %copy-start.139 = (f32[96]{0:T(128)S(1)}, f32[96]{0:T(128)}, u32[]{:S(2)}) copy-start(f32[96]{0:T(128)} %div.411) | copy-start | bytes 1156
  569.1 28.1 %copy-start.97 = (f32[768]{0:T(1024)S(1)}, f32[768]{0:T(1024)}, u32[]{:S(2)}) copy-start(f32[768]{0:T(1024)} %get-tuple-element.156) | copy-start | bytes 9220
  589.9 40.5 %copy-start.44 = (f32[96,256]{1,0:T(8,128)}, f32[96,256]{1,0:T(8,128)S(1)}, u32[]{:S(2)}) copy-start(f32[96,256]{1,0:T(8,128)S(1)} %get-tuple-element.261) | copy-start | bytes 294916
  589.9 40.5 %copy-start.150 = (f32[96]{0:T(128)}, f32[96]{0:T(128)S(1)}, u32[]{:S(2)}) copy-start(f32[96]{0:T(128)S(1)} %add_rsqrt_fusion) | copy-start | bytes 1156
  594.6 23.2 %copy-start.108 = (f32[32,256]{1,0:T(8,128)}, f32[32,256]{1,0:T(8,128)S(1)}, u32[]{:S(2)}) copy-start(f32[32,256]{1,0:T(8,128)S(1)} %get-tuple-element.272) | copy-start | bytes 98308
  595.9 34.5 %copy-start.70 = (f32[96,256]{1,0:T(8,128)}, f32[96,256]{1,0:T(8,128)S(1)}, u32[]{:S(2)}) copy-start(f32[96,256]{1,0:T(8,128)S(1)} %get-tuple-element.266) | copy-start | bytes 294916
  620.6 52.5 %copy-start.164 = (f32[768]{0:T(1024)}, f32[768]{0:T(1024)S(1)}, u32[]{:S(2)}) copy-start(f32[768]{0:T(1024)S(1)} %fusion.179) | copy-start | bytes 9220
  630.3 42.8 %copy-start.175 = (f32[512]{0:T(512)}, f32[512]{0:T(512)S(1)}, u32[]{:S(2)}) copy-start(f32[512]{0:T(512)S(1)} %negate_multiply_fusion.3) | copy-start | bytes 6148
  679.9 165.1 %reduce-scatter.15.cloned.1.call-start = ((), (), s32[]{:S(2)}) async-start(), calls=%async_computation.15 | async-start | bytes 5222400 | tf_op jit(solution)/shard_map/reduce_scatter | solution.py:575
  684.8 34.7 %copy-start.3 = (f32[1024,768]{1,0:T(8,128)S(1)}, f32[1024,768]{1,0:T(8,128)}, u32[]{:S(2)}) copy-start(f32[1024,768]{1,0:T(8,128)} %copy.109) | copy-start | bytes 9437188
  684.8 34.7 %copy-start.94 = (f32[1024]{0:T(1024)S(1)}, f32[1024]{0:T(1024)}, u32[]{:S(2)}) copy-start(f32[1024]{0:T(1024)} %copy-done.93) | copy-start | bytes 12292
  684.8 34.7 %copy-start.125 = (f32[768]{0:T(1024)S(1)}, f32[768]{0:T(1024)}, u32[]{:S(2)}) copy-start(f32[768]{0:T(1024)} %copy-done.124) | copy-start | bytes 9220
  684.8 34.7 %copy-start.131 = (f32[1024]{0:T(1024)S(1)}, f32[1024]{0:T(1024)}, u32[]{:S(2)}) copy-start(f32[1024]{0:T(1024)} %copy-done.130) | copy-start | bytes 12292
  744.8 181.1 %reduce-scatter.19.cloned.1.call-start = ((), (), s32[]{:S(2)}) async-start(), calls=%async_computation.19 | async-start | bytes 5222400
  766.3 274.3 %reduce-scatter.17.cloned.1.call-start = ((), (), s32[]{:S(2)}) async-start(), calls=%async_computation.16 | async-start | bytes 10027008 | tf_op jit(solution)/shard_map/reduce_scatter | solution.py:575
  775.7 332.1 %all-gather.23.cloned.1.call-start = ((), (), s32[]{:S(2)}) async-start(), calls=%async_computation.17 | async-start | bytes 4866048 | tf_op jit(solution)/shard_map/all_gather | solution.py:612
  778.3 444.8 %reduce-scatter.13.cloned.1.call-start = ((), (), s32[]{:S(2)}) async-start(), calls=%async_computation.14 | async-start | bytes 10027008 | tf_op jit(solution)/shard_map/reduce_scatter | solution.py:575
  797.6 23.7 %copy-start.72 = (f32[32,256]{1,0:T(8,128)S(1)}, f32[32,256]{1,0:T(8,128)}, u32[]{:S(2)}) copy-start(f32[32,256]{1,0:T(8,128)} %get-tuple-element.263) | copy-start | bytes 98308
  799.5 21.9 %copy-start.109 = (f32[32,256]{1,0:T(8,128)S(1)}, f32[32,256]{1,0:T(8,128)}, u32[]{:S(2)}) copy-start(f32[32,256]{1,0:T(8,128)} %copy-done.108) | copy-start | bytes 98308
  818.1 28.5 %collective-permute-start = (bf16[48,3072]{1,0:T(8,128)(2,1)}, bf16[48,3072]{1,0:T(8,128)(2,1)S(1)}, u32[]{:S(2)}, u32[]{:S(2)}) collective-permute-start(bf16[48,3072]{1,0:T(8,128)(2,1)} %reduce-scatter.11.cloned.1.call-done), channel_id=1, source_target_pairs={{0,16},{16,0},{1,17},{17,1},{2,18},{18,2},{3,19},{19,3},{4,20},{20... | collective-permute-start | bytes 884744 | tf_op jit(solution)/shard_map/ppermute | solution.py:570
  845.0 83.6 %collective-permute-start.2 = (bf16[48,3200]{1,0:T(8,128)(2,1)}, bf16[48,3200]{1,0:T(8,128)(2,1)}, u32[]{:S(2)}, u32[]{:S(2)}) collective-permute-start(bf16[48,3200]{1,0:T(8,128)(2,1)} %reduce-scatter.15.cloned.1.call-done), channel_id=1, source_target_pairs={{0,16},{16,0},{1,17},{17,1},{2,18},{18,2},{3,19},{19,3},{4,20},{20... | collective-permute-start | bytes 921608 | tf_op jit(solution)/shard_map/ppermute | solution.py:570
  927.0 115.2 %collective-permute-start.4 = (bf16[200,768]{0,1:T(8,128)(2,1)S(1)}, bf16[200,768]{0,1:T(8,128)(2,1)}, u32[]{:S(2)}, u32[]{:S(2)}) collective-permute-start(bf16[200,768]{0,1:T(8,128)(2,1)S(1)} %copy.134), channel_id=1, source_target_pairs={{0,16},{16,0},{1,17},{17,1},{2,18},{18,2},{3,19},{19,3},{4,20},{20... | collective-permute-start | bytes 921608 | tf_op jit(solution)/shard_map/ppermute | solution.py:570
  1040.7 183.9 %collective-permute-start.3 = (bf16[48,6144]{1,0:T(8,128)(2,1)}, bf16[48,6144]{1,0:T(8,128)(2,1)}, u32[]{:S(2)}, u32[]{:S(2)}) collective-permute-start(bf16[48,6144]{1,0:T(8,128)(2,1)} %reduce-scatter.17.cloned.1.call-done), channel_id=1, source_target_pairs={{0,16},{16,0},{1,17},{17,1},{2,18},{18,2},{3,19},{19,3},{4,20},{20... | collective-permute-start | bytes 1769480 | tf_op jit(solution)/shard_map/ppermute | solution.py:570
  1046.6 61.2 %copy-start.136 = (pred[3072]{0:T(1024)(128)(4,1)S(1)}, pred[3072]{0:T(1024)(128)(4,1)}, u32[]{:S(2)}) copy-start(pred[3072]{0:T(1024)(128)(4,1)} %and.88) | copy-start | bytes 9220
  1223.1 15.2 %collective-permute-start.1 = (bf16[48,6144]{1,0:T(8,128)(2,1)}, bf16[48,6144]{1,0:T(8,128)(2,1)S(1)}, u32[]{:S(2)}, u32[]{:S(2)}) collective-permute-start(bf16[48,6144]{1,0:T(8,128)(2,1)} %reduce-scatter.13.cloned.1.call-done), channel_id=1, source_target_pairs={{0,16},{16,0},{1,17},{17,1},{2,18},{18,2},{3,19},{19,3},{4,20},{20... | collective-permute-start | bytes 1769480 | tf_op jit(solution)/shard_map/ppermute | solution.py:570
  1298.7 30.0 %copy-start.78 = (f32[32,256]{1,0:T(8,128)S(1)}, f32[32,256]{1,0:T(8,128)}, u32[]{:S(2)}) copy-start(f32[32,256]{1,0:T(8,128)} %param.51) | copy-start | bytes 98308
  1298.7 30.0 %copy-start.106 = (f32[32,256]{1,0:T(8,128)S(1)}, f32[32,256]{1,0:T(8,128)}, u32[]{:S(2)}) copy-start(f32[32,256]{1,0:T(8,128)} %param.52) | copy-start | bytes 98308
  1298.7 30.0 %copy-start.107 = (f32[32,256]{1,0:T(8,128)S(1)}, f32[32,256]{1,0:T(8,128)}, u32[]{:S(2)}) copy-start(f32[32,256]{1,0:T(8,128)} %param.53) | copy-start | bytes 98308
  1298.7 30.0 %copy-start.110 = (f32[32,256]{1,0:T(8,128)S(1)}, f32[32,256]{1,0:T(8,128)}, u32[]{:S(2)}) copy-start(f32[32,256]{1,0:T(8,128)} %get-tuple-element.284) | copy-start | bytes 98308
  (162 other events, 1036.0 us)
Sparse Core Ops, SparseCore 0:
  40.7 63.4 reduce-scatter.8
  107.2 53.6 all-gather.10
  164.0 79.9 all-gather.18
  247.0 79.6 all-gather.12
  329.7 79.5 all-gather.16
  411.7 108.7 all-gather.14
  523.6 43.5 all-gather.20
  570.4 58.3 all-gather.24
  680.1 84.0 reduce-scatter.10
  768.6 76.3 reduce-scatter.14
  849.5 76.2 reduce-scatter.18
  930.4 110.2 reduce-scatter.16
  1044.5 63.2 all-gather.22
  1112.9 110.1 reduce-scatter.12

commit v2 on v1

v2 whole, which is shorter than its diff:
```python
import functools

import jax
import jax.numpy as jnp
from jax import lax
from jax.experimental import pallas as pl
from jax.experimental.pallas import tpu as pltpu
from jax.sharding import PartitionSpec as P

ADAM_STEP = 10
FULL_PRECISION = lax.Precision.HIGHEST
SOFTMAX_WARMTH = 0.03
CLIP_NORM = 0.01
RATES = (0.1, 0.05, 0.3, 0.1, 0.2, 0.1, 0.1)
BETA_ONE = 0.9
BETA_TWO = 0.95
EPSILON = 1e-08
WEIGHT_DECAY = 0.1
F32 = jnp.float32
BF16 = jnp.bfloat16
MESH_ID = pl.DeviceIdType.MESH
VMEM_LIMIT = 56 * 1024 * 1024
NT = (((1,), (1,)), ((), ()))


def dot(a, b):
    return jnp.dot(a, b, preferred_element_type=F32)


def dot_nt(a, b):
    return lax.dot_general(a, b, NT, preferred_element_type=F32)


def dot_tn(a, b):
    return lax.dot_general(a, b, (((0,), (0,)), ((), ())), preferred_element_type=F32)


def full(a, b):
    return jnp.dot(a, b, precision=FULL_PRECISION)


def dot_nt_full(a, b):
    return lax.dot_general(a, b, NT, precision=FULL_PRECISION, preferred_element_type=F32)


def norm_rows(values, gain_row, shift_row):
    centred = values - jnp.mean(values, -1, keepdims=True)
    return (
        centred * lax.rsqrt(jnp.mean(centred * centred, -1, keepdims=True) + 1e-06) * gain_row
        + shift_row
    )


def unit_rows(values):
    return values * lax.rsqrt(jnp.sum(values * values, -1, keepdims=True) + 1e-06)


def log_sum(scores):
    highest = jnp.max(scores, -1, keepdims=True)
    return highest[..., 0] + jnp.log(jnp.sum(jnp.exp(scores - highest), -1))


def adam_update(master, first, second, gradient, rate):
    first_new = BETA_ONE * first + (1.0 - BETA_ONE) * gradient
    second_new = BETA_TWO * second + (1.0 - BETA_TWO) * gradient * gradient
    first_hat = first_new / (1.0 - BETA_ONE**ADAM_STEP)
    second_hat = second_new / (1.0 - BETA_TWO**ADAM_STEP)
    master_new = master - rate * (
        first_hat / (jnp.sqrt(second_hat) + EPSILON) + WEIGHT_DECAY * master
    )
    return (master_new, first_new, second_new)


def exchange_kernel(within, parts, x_ref, o_ref, send, recv, local):
    group = lax.axis_size("fsdp")
    member = lax.axis_index("fsdp")
    replica = lax.axis_index("dp")
    count = group if within else lax.axis_size("dp") * group
    me = member if within else replica * group + member
    barrier = pltpu.get_barrier_semaphore()

    def place(step):
        peer = lax.rem(me + step, count)
        if within:
            return peer, (replica, peer)
        return peer, (peer // group, lax.rem(peer, group))

    def part(peer):
        return x_ref.at[lax.rem(peer, group)] if parts else x_ref

    def greet(step, carry):
        pl.semaphore_signal(barrier, inc=1, device_id=place(step)[1], device_id_type=MESH_ID)
        return carry

    lax.fori_loop(1, count, greet, 0)
    mine = pltpu.make_async_copy(part(me), o_ref.at[me], local)
    mine.start()
    pl.semaphore_wait(barrier, count - 1)

    def copy(step):
        peer, device = place(step)
        return pltpu.make_async_remote_copy(
            src_ref=part(peer),
            dst_ref=o_ref.at[me],
            send_sem=send.at[step],
            recv_sem=recv.at[step],
            device_id=device,
            device_id_type=MESH_ID,
        )

    def begin(step, carry):
        copy(step).start()
        return carry

    def finish(step, carry):
        copy(step).wait()
        return carry

    lax.fori_loop(1, count, begin, 0)
    mine.wait()
    lax.fori_loop(1, count, finish, 0)


def everyone(x, collective, within=False, parts=False):
    group = lax.axis_size("fsdp")
    count = group if within else lax.axis_size("dp") * group
    return pl.pallas_call(
        functools.partial(exchange_kernel, within, parts),
        out_shape=jax.ShapeDtypeStruct((count,) + x.shape[1 if parts else 0 :], x.dtype),
        in_specs=[pl.BlockSpec(memory_space=pltpu.VMEM)],
        out_specs=pl.BlockSpec(memory_space=pltpu.VMEM),
        scratch_shapes=[
            pltpu.SemaphoreType.DMA((count,)),
            pltpu.SemaphoreType.DMA((count,)),
            pltpu.SemaphoreType.DMA,
        ],
        compiler_params=pltpu.CompilerParams(collective_id=collective, has_side_effects=True),
        name=f"everyone_{collective}",
    )(x)


def pack(values):
    rows = values.reshape(values.shape[0], -1)
    return jnp.pad(rows, ((0, 0), (0, -rows.shape[1] % 1024))).reshape(rows.shape[0], -1, 128)


def unpack(values, shape):
    size = 1
    for length in shape:
        size *= length
    return values.reshape(values.shape[0], -1)[:, :size].reshape((values.shape[0],) + shape)


def attend_kernel(rows, block, masked, *refs):
    if masked:
        qkv_ref, bias_ref, o_ref, l_ref = refs
    else:
        qkv_ref, o_ref, l_ref = refs
    lane = lax.broadcasted_iota(jnp.int32, (1, 128), 1)
    low = lane < 64
    keys = qkv_ref[:, 128:256]
    values = qkv_ref[:, 256:384]
    for at in range(0, rows, block):
        queries = qkv_ref[at : at + block, :128]
        outs, totals = [], []
        for head in range(2):
            picked = jnp.where(low if head == 0 else ~low, queries, 0) * jnp.array(0.125, BF16)
            scores = dot_nt(picked, keys)
            if masked:
                scores = scores + bias_ref[at : at + block, :]
            highest = jnp.max(scores, -1, keepdims=True)
            exponent = jnp.exp(scores - highest)
            summed = jnp.sum(exponent, -1, keepdims=True)
            outs.append(dot(exponent.astype(BF16), values) * (1.0 / summed))
            totals.append(highest + jnp.log(summed))
        o_ref[at : at + block, :] = jnp.where(low, outs[0], outs[1]).astype(BF16)
        l_ref[at : at + block, :] = jnp.where(low, totals[0], totals[1])


def attend(qkv, bias, block):
    rows, width = qkv.shape
    pairs = width // 384
    specs = [pl.BlockSpec((rows, 384), lambda j: (0, j))]
    args = [qkv]
    if bias is not None:
        specs.append(pl.BlockSpec(bias.shape, lambda j: (0, 0)))
        args.append(bias)
    return pl.pallas_call(
        functools.partial(attend_kernel, rows, block, bias is not None),
        grid=(pairs,),
        out_shape=(
            jax.ShapeDtypeStruct((rows, pairs * 128), BF16),
            jax.ShapeDtypeStruct((rows, pairs * 128), F32),
        ),
        in_specs=specs,
        out_specs=(
            pl.BlockSpec((rows, 128), lambda j: (0, j)),
            pl.BlockSpec((rows, 128), lambda j: (0, j)),
        ),
        compiler_params=pltpu.CompilerParams(vmem_limit_bytes=VMEM_LIMIT),
        cost_estimate=pl.CostEstimate(
            flops=16 * rows * rows * 256 * pairs,
            bytes_accessed=rows * pairs * 128 * 12,
            transcendentals=2 * pairs * rows * rows,
        ),
        name=f"attend_{rows}",
    )(*args)


def attend_back_kernel(rows, block, masked, *refs):
    if masked:
        qkv_ref, do_ref, o_ref, l_ref, bias_ref, g_ref, dk_ref, dv_ref = refs
    else:
        qkv_ref, do_ref, o_ref, l_ref, g_ref, dk_ref, dv_ref = refs
    lane = lax.broadcasted_iota(jnp.int32, (1, 128), 1)
    low = lane < 64
    keys = qkv_ref[:, 128:256]
    values = qkv_ref[:, 256:384]
    keys_t = keys.astype(F32).T.astype(BF16)
    row = lax.broadcasted_iota(jnp.int32, (128, 1), 0)
    keys_of = [jnp.where(row < 64, keys_t, 0), jnp.where(row < 64, 0, keys_t)]
    eighth = jnp.array(0.125, BF16)
    for at in range(0, rows, block):
        queries = qkv_ref[at : at + block, :128]
        grads = do_ref[at : at + block, :]
        totals_t = l_ref[at : at + block, :].T
        product_t = (grads.astype(F32) * o_ref[at : at + block, :].astype(F32)).T
        grad_q = None
        for head in range(2):
            mask = low if head == 0 else ~low
            picked = jnp.where(mask, queries, 0) * eighth
            picked_grad = jnp.where(mask, grads, 0)
            total = totals_t[64 * head : 64 * head + 1, :]
            delta = jnp.sum(product_t[64 * head : 64 * head + 64, :], 0, keepdims=True)
            scores = dot_nt(keys, picked)
            if masked:
                scores = scores + bias_ref[:, at : at + block]
            weights = jnp.exp(scores - total)
            grad_weights = dot_nt(values, picked_grad)
            grad_scores = (weights * (grad_weights - delta)).astype(BF16)
            part_v = dot(weights.astype(BF16), picked_grad)
            part_k = dot(grad_scores, picked)
            if at == 0 and head == 0:
                dv_ref[...] = part_v
                dk_ref[...] = part_k
            else:
                dv_ref[...] += part_v
                dk_ref[...] += part_k
            part_q = dot(keys_of[head], grad_scores)
            grad_q = part_q if grad_q is None else grad_q + part_q
        g_ref[at : at + block, :128] = (grad_q.T * 0.125).astype(BF16)
    g_ref[:, 128:256] = dk_ref[...].astype(BF16)
    g_ref[:, 256:384] = dv_ref[...].astype(BF16)


def attend_back(qkv, grad_out, out, totals, bias, block):
    rows, width = qkv.shape
    pairs = width // 384
    specs = [
        pl.BlockSpec((rows, 384), lambda j: (0, j)),
        pl.BlockSpec((rows, 128), lambda j: (0, j)),
        pl.BlockSpec((rows, 128), lambda j: (0, j)),
        pl.BlockSpec((rows, 128), lambda j: (0, j)),
    ]
    args = [qkv, grad_out, out, totals]
    if bias is not None:
        specs.append(pl.BlockSpec(bias.shape, lambda j: (0, 0)))
        args.append(bias)
    return pl.pallas_call(
        functools.partial(attend_back_kernel, rows, block, bias is not None),
        grid=(pairs,),
        out_shape=jax.ShapeDtypeStruct(qkv.shape, BF16),
        in_specs=specs,
        out_specs=pl.BlockSpec((rows, 384), lambda j: (0, j)),
        scratch_shapes=[pltpu.VMEM((rows, 128), F32), pltpu.VMEM((rows, 128), F32)],
        compiler_params=pltpu.CompilerParams(vmem_limit_bytes=VMEM_LIMIT),
        cost_estimate=pl.CostEstimate(
            flops=40 * rows * rows * 256 * pairs,
            bytes_accessed=rows * pairs * 128 * 20,
            transcendentals=2 * pairs * rows * rows,
        ),
        name=f"attend_back_{rows}",
    )(*args)


def column_runs(features, width):
    runs = [
        (kind * features + pair * 128, (3 * pair + kind) * 128, 128)
        for pair in range(features // 128)
        for kind in range(3)
    ]
    return runs + [(3 * features, 3 * features, width - 3 * features)]


def gradient_runs(features, width):
    half = features // 2
    upper = width - 4 * features
    runs = column_runs(features, width)[:-1]
    towers = []
    for piece, upper_at in ((2, upper), (3, 0)):
        tower = []
        for begin, at, size in runs:
            side, local = divmod(at, 3 * half)
            spots = [4 * half * (side ^ core) + local for core in range(2)]
            tower.append((piece, *spots, begin, size))
        for side in range(2):
            spots = [4 * half * (side ^ core) + 3 * half for core in range(2)]
            tower.append((piece, *spots, 3 * features + side * half, half))
        tower.append((0, upper_at, upper_at, 4 * features, upper))
        towers.append(tower)
    tower = [(1, at, at, begin, size) for begin, at, size in runs]
    tower.append((1, 3 * features, 3 * features, 3 * features, width - 3 * features))
    return towers + [tower]


def regroup_kernel(runs, w_ref, low_ref):
    for begin, at, size in runs:
        low_ref[0, :, at : at + size] = w_ref[0, :, begin : begin + size].astype(BF16)


def regroup(mixing, features):
    towers, rows, width = mixing.shape
    spec = pl.BlockSpec((1, rows, width), lambda t: (t, 0, 0))
    return pl.pallas_call(
        functools.partial(regroup_kernel, column_runs(features, width)),
        grid=(towers,),
        out_shape=jax.ShapeDtypeStruct((towers, rows, width), BF16),
        in_specs=[spec],
        out_specs=spec,
        compiler_params=pltpu.CompilerParams(vmem_limit_bytes=VMEM_LIMIT),
        name="regroup",
    )(mixing)


def adam_kernel(towers, scal_ref, core_ref, *refs):
    pieces, (w_ref, first_ref, second_ref), outs = refs[:4], refs[4:7], refs[7:]
    factor = scal_ref[0]
    for tower, runs in enumerate(towers):
        for core in range(2):

            @pl.when((pl.program_id(0) == tower) & (core_ref[0] == core))
            def _():
                for run in runs:
                    piece, begin, size = run[0], run[3], run[4]
                    at = run[1 + core]
                    new = adam_update(
                        w_ref[0, :, begin : begin + size],
                        first_ref[0, :, begin : begin + size],
                        second_ref[0, :, begin : begin + size],
                        pieces[piece][:, at : at + size] * factor,
                        RATES[0],
                    )
                    for out, value in zip(outs, new):
                        out[0, :, begin : begin + size] = value


def adam_mixing(factor, core, pieces, master, first, second, features):
    towers, rows, width = master.shape
    spec = pl.BlockSpec((1, rows, width), lambda t: (t, 0, 0))
    scalar = pl.BlockSpec(memory_space=pltpu.SMEM)
    return pl.pallas_call(
        functools.partial(adam_kernel, gradient_runs(features, width)),
        grid=(towers,),
        out_shape=(jax.ShapeDtypeStruct(master.shape, F32),) * 3,
        in_specs=[scalar, scalar]
        + [pl.BlockSpec(piece.shape, lambda t: (0, 0)) for piece in pieces]
        + [spec] * 3,
        out_specs=(spec,) * 3,
        compiler_params=pltpu.CompilerParams(vmem_limit_bytes=VMEM_LIMIT),
        name="adam_mixing",
    )(factor.reshape(1), core.reshape(1).astype(jnp.int32), *pieces, master, first, second)


def scale_kernel(first_ref, second_ref, slopes_ref, out_ref):
    width = first_ref.shape[1]
    for at, ref in enumerate((first_ref, second_ref)):
        part = ref[...].astype(F32) * slopes_ref[at : at + 1, :]
        out_ref[:, at * width : (at + 1) * width] = part.astype(BF16)


def scale_columns(first, second, slopes):
    rows, width = first.shape
    block = rows // 6
    spec = pl.BlockSpec((block, width), lambda j: (j, 0))
    return pl.pallas_call(
        scale_kernel,
        grid=(rows // block,),
        out_shape=jax.ShapeDtypeStruct((rows, 2 * width), BF16),
        in_specs=[spec, spec, pl.BlockSpec(slopes.shape, lambda j: (0, 0))],
        out_specs=pl.BlockSpec((block, 2 * width), lambda j: (j, 0)),
        compiler_params=pltpu.CompilerParams(vmem_limit_bytes=VMEM_LIMIT),
        name="scale_columns",
    )(first, second, slopes)


def patch_kernel(tile, video_ref, entry_ref, out_ref):
    patch = video_ref.shape[2]
    for at in range(0, patch, tile):
        out_ref[at : at + tile, :] = dot_tn(video_ref[0, :, at : at + tile], entry_ref[...]).astype(
            BF16
        )
    out_ref[patch:, :] = jnp.zeros((out_ref.shape[0] - patch, out_ref.shape[1]), BF16)


def patch_grads(video, entry, rows):
    return pl.pallas_call(
        functools.partial(patch_kernel, 512),
        out_shape=jax.ShapeDtypeStruct((rows, entry.shape[1]), BF16),
        in_specs=[pl.BlockSpec(memory_space=pltpu.VMEM)] * 2,
        out_specs=pl.BlockSpec(memory_space=pltpu.VMEM),
        compiler_params=pltpu.CompilerParams(vmem_limit_bytes=VMEM_LIMIT),
        name="patch_grads",
    )(video, entry)


def middle_kernel(
    scales, yv_ref, ya_ref, yt_ref, gains_ref, heads_ref, vt_ref, live_ref, pos_ref, count_ref,
    loss_ref, dv_ref, da_ref, dt_ref, gg_ref, z_ref, zt_ref, de_ref, dt_e_ref, ev_ref, dvt_ref,
):
    clips = yv_ref.shape[0]
    joint = vt_ref.shape[0]

    def times(a, b, dims):
        return lax.dot_general(
            a, b, (dims, ((), ())), precision=FULL_PRECISION, preferred_element_type=F32
        )

    plain, right, left = ((1,), (0,)), ((1,), (1,)), ((0,), (0,))

    def normalise(values):
        centred = values - jnp.mean(values, -1, keepdims=True)
        inverse = lax.rsqrt(jnp.mean(centred * centred, -1, keepdims=True) + 1e-06)
        return centred * inverse, inverse

    def unit(values):
        scale = lax.rsqrt(jnp.sum(values * values, -1, keepdims=True) + 1e-06)
        return values * scale, scale

    def unit_back(values, scale, grads):
        along = jnp.sum(values * grads, -1, keepdims=True)
        return scale * grads - values * (scale * scale * scale * along)

    def soft(scores):
        highest = jnp.max(scores, -1, keepdims=True)
        exponent = jnp.exp(scores - highest)
        total = jnp.sum(exponent, -1, keepdims=True)
        return highest + jnp.log(total), exponent * (1.0 / total)

    hats, z = [], []
    for t, ref in enumerate((yv_ref, ya_ref, yt_ref)):
        hat, inverse = normalise(ref[...])
        hats.append((hat, inverse))
        z.append(hat * gains_ref[2 * t : 2 * t + 1, :] + gains_ref[2 * t + 1 : 2 * t + 2, :])
    heads = heads_ref[...]
    parts = (heads[:, :joint], heads[:, joint : 2 * joint], heads[:, 2 * joint :])
    video_text = vt_ref[...]
    e_video = times(z[0], parts[0], plain)
    e_both = times(e_video, video_text, plain)
    e_audio = times(z[1], parts[1], plain)
    e_text = times(z[2], parts[2], plain)
    (n_video, s_video), (n_both, s_both) = unit(e_video), unit(e_both)
    (n_audio, s_audio), (n_text, s_text) = unit(e_audio), unit(e_text)
    scores = times(n_video, n_audio, right) / SOFTMAX_WARMTH
    own = lax.broadcasted_iota(jnp.int32, scores.shape, 0) == lax.broadcasted_iota(
        jnp.int32, scores.shape, 1
    )
    total, share = soft(scores)
    matched = total - jnp.sum(jnp.where(own, scores, 0.0), -1, keepdims=True)
    d_scores = (share - jnp.where(own, 1.0, 0.0)) * (1.0 / (clips * SOFTMAX_WARMTH))
    live = live_ref[...]
    positive = pos_ref[...]
    text_scores = times(n_both, n_text, right) / SOFTMAX_WARMTH
    every, every_share = soft(jnp.where(live > 0.5, text_scores, -1e30))
    chosen, chosen_share = soft(jnp.where(positive > 0.5, text_scores, -1e30))
    weight = jnp.sum(positive, -1, keepdims=True) / jnp.sum(live)
    loss = jnp.sum(matched) / clips + jnp.sum(weight * (every - chosen))
    loss_ref[...] = jnp.broadcast_to(loss, loss_ref.shape)
    d_text_scores = (every_share * live - chosen_share * positive) * (weight / SOFTMAX_WARMTH)
    d_video = unit_back(e_video, s_video, times(d_scores, n_audio, plain))
    d_audio = unit_back(e_audio, s_audio, times(d_scores, n_video, left))
    d_both = unit_back(e_both, s_both, times(d_text_scores, n_text, plain))
    d_text = unit_back(e_text, s_text, times(d_text_scores, n_both, left))
    d_video = d_video + times(d_both, video_text, right)
    for t, (grad, out) in enumerate(((d_video, dv_ref), (d_audio, da_ref), (d_text, dt_ref))):
        d_z = times(grad, parts[t], right)
        hat, inverse = hats[t]
        gg_ref[2 * t : 2 * t + 1, :] = jnp.sum(d_z * hat, 0, keepdims=True)
        gg_ref[2 * t + 1 : 2 * t + 2, :] = jnp.sum(d_z, 0, keepdims=True)
        d_hat = d_z * gains_ref[2 * t : 2 * t + 1, :]
        inner = d_hat - jnp.mean(d_hat, -1, keepdims=True)
        rows = inverse * (inner - hat * jnp.mean(d_hat * hat, -1, keepdims=True))
        out[...] = rows * scales[t] if t < 2 else rows / count_ref[...]
    z_ref[0] = z[0]
    z_ref[1] = z[1]
    zt_ref[...] = z[2]
    de_ref[0] = d_video
    de_ref[1] = d_audio
    dt_e_ref[...] = d_text
    ev_ref[...] = e_video
    dvt_ref[...] = d_both


def contrast(scales, rows, gains, heads, video_text, live, positive, counts):
    clips, features = rows[0].shape
    texts = rows[2].shape[0]
    joint, width = video_text.shape
    shapes = [
        (8, 128),
        (clips, features),
        (clips, features),
        (texts, features),
        (8, features),
        (2, clips, features),
        (texts, features),
        (2, clips, joint),
        (texts, width),
        (clips, joint),
        (clips, width),
    ]
    return pl.pallas_call(
        functools.partial(middle_kernel, scales),
        out_shape=tuple(jax.ShapeDtypeStruct(shape, F32) for shape in shapes),
        in_specs=[pl.BlockSpec(memory_space=pltpu.VMEM)] * 9,
        out_specs=tuple(pl.BlockSpec(memory_space=pltpu.VMEM) for _ in shapes),
        compiler_params=pltpu.CompilerParams(vmem_limit_bytes=VMEM_LIMIT),
        name="middle",
    )(*rows, gains, heads, video_text, live, positive, counts)


def feed_kernel(with_product, h_ref, w_ref, sel_ref, slope_ref, sums_ref, *rest):
    hidden = dot(h_ref[...], w_ref[...])
    root = 0.7978845608028654
    square = hidden * hidden
    tang = jnp.tanh(root * hidden * (1.0 + 0.044715 * square))
    half = 0.5 * (1.0 + tang)
    active = (hidden * half).astype(BF16)
    slope = half + (0.5 * root) * hidden * (1.0 - tang * tang) * (1.0 + (3 * 0.044715) * square)
    slope = slope.astype(BF16)
    slope_ref[...] = slope
    if with_product:
        sums_ref[...] = jnp.broadcast_to(
            jnp.sum(active.astype(F32), 0, keepdims=True), sums_ref.shape
        )
        rest[0][...] = dot_tn(h_ref[...], slope).astype(BF16)
    else:
        sums_ref[...] = dot(sel_ref[...], active)


def feed(normed, weight, column, select, tile, with_product):
    rows, features = normed.shape
    width = weight.shape[1] - column
    first = column // tile
    shapes = [
        jax.ShapeDtypeStruct((rows, width), BF16),
        jax.ShapeDtypeStruct((8, width), F32),
    ]
    outs = [
        pl.BlockSpec((rows, tile), lambda j: (0, j)),
        pl.BlockSpec((8, tile), lambda j: (0, j)),
    ]
    if with_product:
        shapes.append(jax.ShapeDtypeStruct((features, width), BF16))
        outs.append(pl.BlockSpec((features, tile), lambda j: (0, j)))
    return pl.pallas_call(
        functools.partial(feed_kernel, with_product),
        grid=(width // tile,),
        out_shape=tuple(shapes),
        in_specs=[
            pl.BlockSpec((rows, features), lambda j: (0, 0)),
            pl.BlockSpec((features, tile), lambda j: (0, first + j)),
            pl.BlockSpec(select.shape, lambda j: (0, 0)),
        ],
        out_specs=tuple(outs),
        compiler_params=pltpu.CompilerParams(vmem_limit_bytes=VMEM_LIMIT),
        cost_estimate=pl.CostEstimate(
            flops=4 * rows * features * width,
            bytes_accessed=2 * features * width * 2 + 2 * rows * width,
            transcendentals=rows * width,
        ),
        name=f"feed_{rows}",
    )(normed, weight, select)


def both_columns(own, other, core):
    first = jnp.where(core == 0, own, other)
    second = jnp.where(core == 0, other, own)
    return jnp.concatenate([first, second], -1)


def attention_forward(stream, bias, mixing, gains, block):
    features = stream.shape[1]
    normed = norm_rows(stream, gains[0], gains[1]).astype(BF16)
    joined = dot(normed, mixing[:, : 3 * features]).astype(BF16)
    return normed, joined, attend(joined, bias, block)


def feed_forward(stream, mixed, mixing, gains, select, with_product):
    features = stream.shape[1]
    middle = stream + dot(mixed, mixing[:, 3 * features : 4 * features])
    normed = norm_rows(middle, gains[2], gains[3]).astype(BF16)
    return middle, normed, feed(normed, mixing, 4 * features, select, 512, with_product)


def output_backward(grad_rows, grad_normed, mixed, middle, mixing, gains):
    features = middle.shape[1]
    grad_norm, grad_gain, grad_shift = jax.vjp(norm_rows, middle, gains[2], gains[3])[1](
        grad_normed
    )
    grad_middle = grad_rows + grad_norm
    grad_attention = grad_middle.astype(BF16)
    grad_mixed = dot_nt(grad_attention, mixing[:, 3 * features : 4 * features]).astype(BF16)
    grad_output = dot_tn(mixed, grad_attention).astype(BF16)
    return grad_middle, grad_output, grad_mixed, [grad_gain, grad_shift]


def input_backward(grad_middle, grad_joined, stream, mixing, gains):
    features = stream.shape[1]
    grad_normed = dot_nt(grad_joined, mixing[:, : 3 * features])
    grad_norm, grad_gain, grad_shift = jax.vjp(norm_rows, stream, gains[0], gains[1])[1](
        grad_normed
    )
    return (grad_middle + grad_norm).astype(BF16), [grad_gain, grad_shift]


def both_columns(own, other, core):
    first = jnp.where(core == 0, own, other)
    second = jnp.where(core == 0, other, own)
    return jnp.concatenate([first, second], -1)


class Links:
    def __init__(self):
        self.group = lax.axis_size("fsdp")
        self.replicas = lax.axis_size("dp")
        self.member = lax.axis_index("fsdp")
        self.replica = lax.axis_index("dp")
        self.core = self.member % 2
        self.paired = self.group == 16 and self.replicas == 2

    def swap(self, values, name):
        if name == "y":
            return lax.ppermute(values, "dp", [(0, 1), (1, 0)])
        bit = {"core": 1, "x": 2, "near": 4, "far": 8}[name]
        return lax.ppermute(values, "fsdp", [(f, f ^ bit) for f in range(self.group)])

    def bit(self, name):
        if name == "y":
            return self.replica
        return (self.member // {"core": 1, "x": 2, "near": 4, "far": 8}[name]) % 2

    def merge(self, values, other, names, name, order=("far", "near", "x", "core", "y")):
        names = sorted(names + [name], key=order.index)
        at = names.index(name)
        place = lax.broadcasted_iota(jnp.int32, (2,) + (1,) * (values.ndim - at), 0)
        joined = jnp.where(
            place == self.bit(name), jnp.expand_dims(values, at), jnp.expand_dims(other, at)
        )
        return joined, names

    def sides(self, values, names, name):
        at = names.index(name)
        bit = self.bit(name)
        give = lax.dynamic_index_in_dim(values, 1 - bit, at, keepdims=False)
        keep = lax.dynamic_index_in_dim(values, bit, at, keepdims=False)
        return keep, give, [n for n in names if n != name]

    def gather_clips(self, values):
        if not self.paired:
            return lax.all_gather(values, ("dp", "fsdp"), axis=0, tiled=True)
        names = []
        order = ["y", "far", "near", "x", "core"]
        for name in ("near", "far", "y", "x", "core"):
            other = yield values, name
            values, names = self.merge(values, other, names, name, order)
        return values.reshape(-1, values.shape[-1])

    def sum_replicas(self, part):
        if not self.paired:
            return lax.psum(part, "dp").astype(F32)
        other = yield part, "y"
        return part.astype(F32) + other.astype(F32)

    def gather_rows(self, shard, order):
        rows, width = shard.shape
        half = width // 2
        if not self.paired:
            return lax.all_gather(shard, "fsdp", axis=0, tiled=True)
        values = lax.dynamic_slice_in_dim(shard, self.replica * half, half, 1)
        names = []
        for name in order + ("core",):
            other = yield values, name
            if name == "y":
                values = both_columns(values, other, self.replica)
            else:
                values, names = self.merge(values, other, names, name)
        return values.reshape(self.group * rows, width)

    def reduce_columns(self, own, other, order):
        rows, half = own.shape
        part = rows // self.group
        other = yield other, "core"
        values = add(own, other).reshape(2, 2, 2, 2, 2, part // 2, half)
        names = ["far", "near", "x", "core", "y"]
        for name in order:
            keep, give, names = self.sides(values, names, name)
            other = yield give, name
            values = add(keep, other)
        return values

    def share_columns(self, values):
        mine, give, _ = self.sides(values, ["core"], "core")
        other = yield give, "core"
        values = jnp.concatenate([mine, other], 1)
        other = yield values, "y"
        values, _ = self.merge(values, other, [], "y")
        return values.reshape(2 * values.shape[1], values.shape[2]).astype(F32)

    def scatter_columns(self, own, other, order):
        if not self.paired:
            half = own.shape[1]
            core = self.core
            whole = both_columns(own, other, core)
            whole = lax.psum_scatter(whole, "fsdp", scatter_dimension=0, tiled=True)
            whole = lax.psum(whole, "dp").astype(F32)
            return jnp.concatenate(
                [
                    lax.dynamic_slice_in_dim(whole, core * half, half, 1),
                    lax.dynamic_slice_in_dim(whole, (1 - core) * half, half, 1),
                ],
                1,
            )
        values = yield from self.reduce_columns(own, other, order)
        return (yield from self.share_columns(values))

    def scatter_rows(self, values, order):
        rows, width = values.shape
        part = rows // self.group
        half = width // 2
        if not self.paired:
            part_sum = lax.psum_scatter(values, "fsdp", scatter_dimension=0, tiled=True)
            return lax.psum(part_sum, "dp").astype(F32)
        values = values.reshape(2, 2, 2, 2, part, width)
        names = ["far", "near", "x", "core"]
        for name in ("core",) + order:
            if name == "y":
                last = values.ndim - 1
                give = lax.dynamic_slice_in_dim(values, (1 - self.replica) * half, half, last)
                keep = lax.dynamic_slice_in_dim(values, self.replica * half, half, last)
            else:
                keep, give, names = self.sides(values, names, name)
            other = yield give, name
            values = add(keep, other)
        other = yield values, "y"
        return both_columns(values, other, self.replica).astype(F32)

    def scatter_words(self, values):
        rows, width = values.shape
        if not self.paired:
            return lax.psum_scatter(values, "fsdp", scatter_dimension=0, tiled=True)
        values = values.reshape(2, 2, 2, 2, rows // self.group, width)
        names = ["far", "near", "x", "core"]
        for name in ("core", "x", "far", "near"):
            keep, give, names = self.sides(values, names, name)
            other = yield give, name
            values = add(keep, other)
        return values

    def stage(self, flows, work=None, inputs=()):
        active = [flow for flow in flows if flow.request is not None]
        names = [flow.request[1] for flow in active]
        held, inputs = lax.optimization_barrier(([flow.request[0] for flow in active], inputs))
        sent = [self.swap(values, name) for values, name in zip(held, names)]
        made = work(*inputs) if work is not None else ()
        sent, made = lax.optimization_barrier((sent, made))
        for flow, other in zip(active, sent):
            flow.push(other)
        return made


class Flow:
    def __init__(self, steps):
        self.steps = steps
        self.value = None
        self.push(None)

    def push(self, other):
        try:
            self.request = self.steps.send(other)
        except StopIteration as end:
            self.request, self.value = None, end.value


def add(left, right):
    return (left.astype(F32) + right.astype(F32)).astype(BF16)


def body(
    video,
    audio,
    word_ids,
    word_counts,
    caption_counts,
    caption_clips,
    mixing_in,
    mixing_in_first,
    mixing_in_second,
    mixing_out,
    mixing_out_first,
    mixing_out_second,
    norm_params,
    norm_params_first,
    norm_params_second,
    input_embed,
    input_embed_first,
    input_embed_second,
    word_table,
    word_table_first,
    word_table_second,
    head_proj,
    head_proj_first,
    head_proj_second,
    video_text_proj,
    video_text_proj_first,
    video_text_proj_second,
):
    group = lax.axis_size("fsdp")
    replicas = lax.axis_size("dp")
    clips = group * replicas
    member = lax.axis_index("fsdp")
    replica = lax.axis_index("dp")
    clip = replica * group + member
    captions, slots = word_ids.shape[1:]
    words = captions * slots
    patch = video.shape[2]
    video_count, audio_count = video.shape[1], audio.shape[1]
    features = mixing_in.shape[1] * group
    pairs = features // 128
    shard = mixing_in.shape[1]
    qkv = 3 * features

    links = Links()
    core = links.core
    half = features // 2
    joint_part, text_width = video_text_proj.shape
    table_rows = word_table.shape[0]
    gain_part = norm_params.shape[2]
    wave = audio.shape[2]
    low = regroup(mixing_in, features)

    def gather(values):
        return lax.all_gather(values, "fsdp", axis=0, tiled=True)

    weights = [None] * 3
    weights[1] = gather(low[1])
    embed_flow = Flow(links.gather_rows(input_embed.astype(BF16), ("near", "far", "x", "y")))

    def exchange(*parts):
        packed = jnp.concatenate([part.reshape(-1).astype(F32) for part in parts])
        packed = jnp.pad(packed, (0, -packed.shape[0] % 1024)).reshape(-1, 128)
        return everyone(packed, 0).reshape(clips, -1)

    every = links.stage(
        [embed_flow],
        exchange,
        (word_ids, word_counts, caption_counts, caption_clips, norm_params),
    )
    all_ids = every[:, :words].astype(jnp.int32)
    at = words + captions
    all_caption_counts = every[:, at].astype(jnp.int32)
    all_counts = every[:, words : words + captions]
    all_caption_clips = every[:, at + 1 : at + 1 + captions].astype(jnp.int32)
    at = at + 1 + captions
    gains_all = (
        every[:group, at : at + 18 * gain_part]
        .reshape(group, 3, 6, gain_part)
        .transpose(1, 2, 0, 3)
        .reshape(3, 6, features)
        .astype(BF16)
        .astype(F32)
    )

    def owned_rows(ids):
        local_ids = ids - member * table_rows
        owned = (local_ids >= 0) & (local_ids < table_rows)
        return jnp.clip(local_ids, 0, table_rows - 1), owned

    def pick_words(ids):
        group_ids = lax.dynamic_slice_in_dim(ids, replica * group, group, 0).reshape(-1)
        local_ids, owned = owned_rows(group_ids)
        return jnp.where(owned[:, None], word_table[local_ids], 0.0).astype(BF16)

    picked = links.stage([embed_flow], pick_words, (all_ids,))
    words_flow = Flow(links.scatter_words(picked))

    valid = jnp.arange(slots)[None, :] < word_counts[0][:, None]
    flat_valid = valid.reshape(-1)
    caption_of = jnp.arange(words) // slots
    allowed = (caption_of[:, None] == caption_of[None, :]) & flat_valid[None, :]
    word_bias = jnp.where(allowed, 0.0, -1000000000.0).astype(F32)
    select = ((jnp.arange(8)[:, None] == caption_of[None, :]) & flat_valid[None, :]).astype(BF16)
    unused = jnp.zeros((8, 128), BF16)

    biases = (None, None, word_bias)
    selects = (unused, unused, select)
    forward_block = (512, 512, words)
    backward_block = (512, 256, words)
    counts = word_counts[0].astype(F32)

    normed, joined, attended, fed, streams = ([None] * 3 for _ in range(5))
    for _ in range(3):
        links.stage([embed_flow, words_flow])
    embed = embed_flow.value
    streams[1], streams[0] = links.stage(
        [words_flow],
        lambda rows: (dot(audio[0], rows[patch:]), dot(video[0], rows[:patch])),
        (embed,),
    )
    heads_low = jnp.concatenate(
        [head_proj, jnp.pad(video_text_proj, ((0, shard - joint_part), (0, 0)))], 1
    ).astype(BF16)
    streams[2] = words_flow.value.astype(F32)

    def forward(tower):
        normed[tower], joined[tower], attended[tower] = attention_forward(
            streams[tower],
            biases[tower],
            weights[tower],
            gains_all[tower],
            forward_block[tower],
        )
        fed[tower] = feed_forward(
            streams[tower],
            attended[tower][0],
            weights[tower],
            gains_all[tower],
            selects[tower],
            tower < 2,
        )

    streams, weights[1], low_video, low_text = lax.optimization_barrier(
        (streams, weights[1], low[0], low[2])
    )
    weights[0] = gather(low_video)
    weights[2] = gather(low_text)
    forward(1)
    fed[1], weights[0] = lax.optimization_barrier((fed[1], weights[0]))
    forward(0)
    fed[0], weights[2], heads_low = lax.optimization_barrier((fed[0], weights[2], heads_low))
    heads_all = gather(heads_low)
    forward(2)

    heads = heads_all[:, : head_proj.shape[1]].astype(F32)
    video_text = heads_all[:, head_proj.shape[1] :].reshape(group, shard, text_width)
    video_text = video_text[:, :joint_part].reshape(group * joint_part, text_width).astype(F32)
    slopes, sums, products, bases = [], [], [], []
    for tower in range(3):
        rows, _, parts = fed[tower]
        slopes.append(parts[0])
        if tower < 2:
            products.append(parts[2])
            sums.append(parts[1][:1])
            bases.append(jnp.sum(rows, 0, keepdims=True))
        else:
            sums.append(parts[1][:captions])
            bases.append(full(select[:captions].astype(F32), rows))

    token_count = 2 + captions
    back_part = mixing_out.shape[1]
    backs = mixing_out.astype(BF16).astype(F32)
    hidden = back_part * group
    summed = jnp.concatenate(sums, 0).reshape(token_count, group, back_part).transpose(1, 0, 2)
    every_sum = unpack(everyone(pack(summed), 3, parts=True), (token_count, back_part))

    def own_group(values):
        return lax.dynamic_slice_in_dim(values, replica * group, group, 0)

    def by_tower(values):
        width = values.shape[-1]
        return values[:, 0], values[:, 1], values[:, 2:].reshape(-1, width)

    def by_clip(parts):
        count, width = parts[0].shape
        return jnp.concatenate(
            [parts[0][:, None], parts[1][:, None], parts[2].reshape(count, captions, width)], 1
        )

    group_sums = by_tower(own_group(every_sum))
    partial = by_clip([full(group_sums[t], backs[t]) for t in range(3)])
    through = everyone(pack(partial), 4, within=True, parts=True)
    through = unpack(jnp.sum(through, 0, keepdims=True), (token_count, features))[0]
    scales = jnp.concatenate([jnp.array([video_count, audio_count], F32), counts])
    mine = (jnp.concatenate(bases, 0) + through) / scales[:, None]

    pooled = unpack(everyone(pack(mine[None])[0], 1), (token_count * features,))
    live = (jnp.arange(captions)[None, :] < all_caption_counts[:, None]).reshape(1, -1)
    positive = live & (all_caption_clips.reshape(1, -1) == jnp.arange(clips)[:, None])
    outer_rows = jnp.pad(gains_all[:, 4:].reshape(6, features), ((0, 2), (0, 0)))
    (
        loss,
        *grad_rows_all,
        outer_grads,
        z_pair,
        z_text,
        d_pair,
        d_text,
        embed_video,
        d_video_text,
    ) = contrast(
        (1.0 / video_count, 1.0 / audio_count),
        (
            pooled[:, :features],
            pooled[:, features : 2 * features],
            pooled[:, 2 * features :].reshape(-1, features),
        ),
        outer_rows,
        heads,
        video_text,
        live.astype(F32),
        positive.astype(F32),
        all_counts.reshape(-1, 1),
    )
    loss = loss[0, 0]
    z = (z_pair[0], z_pair[1], z_text)
    d_heads = (d_pair[0], d_pair[1], d_text)

    def own_columns(values):
        return lax.dynamic_slice_in_dim(values, member * shard, shard, 1)

    def head_grads():
        heads_grad = jnp.concatenate([full(own_columns(z[t]).T, d_heads[t]) for t in range(3)], 1)
        own = lax.dynamic_slice_in_dim(embed_video, member * joint_part, joint_part, 1)
        return heads_grad, full(own.T, d_video_text)

    branch_all = [rows.astype(BF16) for rows in grad_rows_all]

    all_sums = by_tower(every_sum)

    def back_grads():
        return jnp.stack([full(all_sums[t].T, branch_all[t].astype(F32)) for t in range(3)])

    group_branch = by_clip(branch_all)
    group_branch = by_tower(own_group(group_branch).astype(F32))
    partial = by_clip([dot_nt_full(group_branch[t], backs[t]) for t in range(3)])
    sloped = unpack(everyone(pack(partial), 5, within=True, parts=True), (token_count, back_part))
    sloped = sloped.transpose(1, 0, 2).reshape(token_count, hidden)
    own_slopes = (sloped[:1], sloped[1:2], sloped[2:])

    def own_rows(values, per_clip):
        return lax.dynamic_slice_in_dim(values, clip * per_clip, per_clip, 0)

    own_grads = [own_rows(grad_rows_all[t], 1 if t < 2 else captions) for t in range(3)]
    ups = scale_columns(products[1], products[0], jnp.concatenate(own_slopes[1::-1], 0))
    ups, own_slopes = lax.optimization_barrier((ups, own_slopes))
    up_part = lax.psum_scatter(ups, "fsdp", scatter_dimension=0, tiled=True)
    first, second = ("y", "x", "far", "near"), ("x", "y", "far", "near")

    def halves(inward, outward):
        return [
            jnp.concatenate(
                [
                    lax.dynamic_slice_in_dim(inward, at * 3 * half, 3 * half, 1),
                    lax.dynamic_slice_in_dim(outward, at * half, half, 1),
                ],
                1,
            )
            for at in (core, 1 - core)
        ]

    def hidden_backward(tower, slope):
        upper = weights[tower][:, 4 * features :]
        if tower == 2:
            spread = select[:captions].astype(F32).T
            grad_hidden = (slopes[2].astype(F32) * full(spread, slope)).astype(BF16)
            up = dot_tn(fed[2][1], grad_hidden).astype(BF16)
            return full(spread, own_grads[2]), dot_nt(grad_hidden, upper), up
        scaled = (upper.astype(F32) * slope).astype(BF16)
        return own_grads[tower], dot_nt(slopes[tower], scaled), None

    def outward_backward(tower, slope):
        rows_grad, grads, up = hidden_backward(tower, slope)
        made = output_backward(
            rows_grad, grads, attended[tower][0], fed[tower][0], weights[tower], gains_all[tower]
        )
        return made, up

    def inner_backward(tower, grad_mixed):
        turned = None if biases[tower] is None else biases[tower].T
        return attend_back(
            joined[tower],
            grad_mixed,
            attended[tower][0],
            attended[tower][1],
            turned,
            backward_block[tower],
        )

    def entry_backward(tower, grad_middle, grad_joined):
        return input_backward(
            grad_middle, grad_joined, streams[tower], weights[tower], gains_all[tower]
        )

    gains_grads = [None] * 3

    def text_backward(slope):
        made, up = outward_backward(2, slope)
        grad_joined = inner_backward(2, made[2])
        inward = dot_tn(normed[2], grad_joined).astype(BF16)
        entry, entry_gains = entry_backward(2, made[0], grad_joined)
        return jnp.concatenate([inward, made[1], up], 1), entry, entry_gains + made[3]

    text_grad, entry, gains_grads[2] = links.stage([], text_backward, (own_slopes[2],))
    word_flow = Flow(links.gather_clips(entry))
    text_part = lax.psum_scatter(text_grad, "fsdp", scatter_dimension=0, tiled=True)
    made_video, _ = links.stage([word_flow], lambda slope: outward_backward(0, slope), (own_slopes[0],))
    embed_rows = input_embed.shape[0] * group

    def video_inner(grad_mixed):
        grad_joined = inner_backward(0, grad_mixed)
        inward = dot_tn(normed[0], grad_joined).astype(BF16)
        entry, entry_gains = entry_backward(0, made_video[0], grad_joined)
        return halves(inward, made_video[1]), entry, entry_gains

    video_parts, entry, entry_gains = links.stage([word_flow], video_inner, (made_video[2],))
    gains_grads[0] = entry_gains + made_video[3]
    video_flow = Flow(links.scatter_columns(*video_parts, first))

    def video_entry(entry, slope):
        made, _ = outward_backward(1, slope)
        return patch_grads(video, entry, embed_rows), made

    grad_embed, made_audio = links.stage([word_flow, video_flow], video_entry, (entry, own_slopes[1]))
    embed_flow = Flow(links.scatter_rows(grad_embed, first))
    rest = [word_flow, video_flow, embed_flow]
    joined_audio = links.stage(rest, lambda part: inner_backward(1, part), (made_audio[2],))

    def audio_inward(grad_joined):
        return halves(dot_tn(normed[1], grad_joined).astype(BF16), made_audio[1])

    audio_parts = links.stage(rest, audio_inward, (joined_audio,))
    cut = features
    if links.paired:
        audio_flows = [
            Flow(links.reduce_columns(*[part[:, :cut] for part in audio_parts], first)),
            Flow(links.reduce_columns(*[part[:, cut:] for part in audio_parts], second)),
        ]
    else:
        audio_flows = [Flow(links.scatter_columns(*audio_parts, first))]
    rest += audio_flows

    def audio_entry(grad_joined):
        entry, entry_gains = entry_backward(1, made_audio[0], grad_joined)
        wave_grad = dot_tn(entry, audio[0]).astype(BF16)
        every_gain = jnp.stack(gains_grads[0] + entry_gains + made_audio[3] + gains_grads[2])
        every_gain = jnp.pad(every_gain, ((0, wave - every_gain.shape[0]), (0, 0)))
        gain_columns = every_gain.T.astype(BF16)
        return (
            jnp.where(core == 0, wave_grad, gain_columns),
            jnp.where(core == 0, gain_columns, wave_grad),
        )

    beside = links.stage(rest, audio_entry, (joined_audio,))
    beside_flow = Flow(
        links.reduce_columns(*beside, second)
        if links.paired
        else links.scatter_columns(*beside, first)
    )
    rest += [beside_flow]

    def scatter_table(every_word):
        local_ids, owned = owned_rows(all_ids.reshape(-1))
        return jax.ops.segment_sum(
            jnp.where(owned[:, None], every_word.astype(F32), 0.0),
            local_ids,
            num_segments=table_rows,
        )

    def squared(*values):
        return sum(jnp.sum(value * value) for value in values)

    table_grad = links.stage(rest, scatter_table, (word_flow.value,))
    back_grad, (heads_grad, video_text_grad), table_square = links.stage(
        rest, lambda table: (back_grads(), head_grads(), squared(table)), (table_grad,)
    )
    up_flow = Flow(links.sum_replicas(up_part))
    rest += [up_flow]
    small_square = links.stage(rest, squared, (back_grad, heads_grad, video_text_grad))
    links.stage(rest)
    text_flow = Flow(links.sum_replicas(text_part))
    if links.paired:
        values = jnp.concatenate([flow.value for flow in audio_flows], 2)
        audio_flows = [Flow(links.share_columns(values))]
    rest += audio_flows + [text_flow]
    for _ in range(4):
        if any(flow.request is not None for flow in rest):
            links.stage(rest)
    pieces = (up_flow.value, text_flow.value, video_flow.value, audio_flows[0].value)
    embed_grad = embed_flow.value

    outer = lax.dynamic_slice_in_dim(outer_grads[:6], member * gain_part, gain_part, 1)
    local_square = table_square + small_square + squared(*pieces, embed_grad, outer)
    piece = beside_flow.value.reshape(-1, wave)
    piece_square = squared(piece.astype(F32))
    marks = jnp.where(jnp.arange(128) < 64, local_square, piece_square)
    mark_rows = []
    for _ in range(3):
        mark_rows.append(marks.astype(BF16))
        marks = marks - mark_rows[-1].astype(F32)
    mark_rows = jnp.pad(jnp.stack(mark_rows), ((0, 16 - 3 + -piece.shape[0] % 16), (0, 0)))
    sent = everyone(jnp.concatenate([piece, mark_rows], 0), 2).astype(F32)
    marks = jnp.sum(sent[:, piece.shape[0] : piece.shape[0] + 3], 1)
    sent = sent[:, : piece.shape[0]]
    if links.paired:
        square = jnp.sum(marks[:group, 0]) + jnp.sum(marks[:, 127])
        placed = sent.reshape(replicas, group // 2, 2, 2, gain_part // 2, wave)
        placed = placed.transpose(2, 1, 3, 0, 4, 5).reshape(2, features, wave)
    else:
        square = jnp.sum(marks[:group, 0]) + jnp.sum(marks[:group, 127])
        placed = sent[:group].reshape(group, gain_part, 2, wave)
        swapped = (jnp.arange(group) % 2 == 1)[:, None, None, None]
        placed = jnp.where(swapped, placed[:, :, ::-1], placed)
        placed = placed.transpose(2, 0, 1, 3).reshape(2, features, wave)
    wave_rows, gain_rows = placed[0].T, placed[1].T
    embed_part = input_embed.shape[0]
    row = member * embed_part + jnp.arange(embed_part) - patch
    chosen = (row[:, None] == jnp.arange(wave)[None, :]).astype(F32)
    inner = lax.dynamic_slice_in_dim(gain_rows[:12], member * gain_part, gain_part, 1)
    gains_grad = jnp.concatenate(
        [inner.reshape(3, 4, gain_part), outer.reshape(3, 2, gain_part)], 1
    )
    grads = (
        None,
        back_grad,
        gains_grad,
        embed_grad + full(chosen, wave_rows),
        table_grad,
        heads_grad,
        video_text_grad,
    )
    grad_norm = jnp.sqrt(square)
    factor = CLIP_NORM / jnp.maximum(grad_norm, CLIP_NORM)
    clipped = [None] + [g * factor for g in grads[1:]]
    masters = (
        mixing_in,
        mixing_out,
        norm_params,
        input_embed,
        word_table,
        head_proj,
        video_text_proj,
    )
    firsts = (
        mixing_in_first,
        mixing_out_first,
        norm_params_first,
        input_embed_first,
        word_table_first,
        head_proj_first,
        video_text_proj_first,
    )
    seconds = (
        mixing_in_second,
        mixing_out_second,
        norm_params_second,
        input_embed_second,
        word_table_second,
        head_proj_second,
        video_text_proj_second,
    )
    new = [
        adam_mixing(
            factor,
            core,
            pieces,
            mixing_in,
            mixing_in_first,
            mixing_in_second,
            features,
        )
    ]
    for i in range(1, 7):
        new.append(adam_update(masters[i], firsts[i], seconds[i], clipped[i], RATES[i]))
    outputs = [loss, grad_norm]
    for i in range(7):
        outputs += [new[i][0], clipped[4] if i == 4 else new[i][1], new[i][2]]
    return tuple(outputs)


def solution(mesh):
    both = ("dp", "fsdp")
    weight_specs = (
        P(None, "fsdp", None),
        P(None, "fsdp", None),
        P(None, None, "fsdp"),
        P("fsdp", None),
        P("fsdp", None),
        P("fsdp", None),
        P("fsdp", None),
    )
    tripled = tuple(spec for spec in weight_specs for _ in range(3))
    return jax.shard_map(
        body,
        mesh=mesh,
        in_specs=(
            P(both, None, None),
            P(both, None, None),
            P(both, None, None),
            P(both, None),
            P(both),
            P(both, None),
        )
        + tripled,
        out_specs=(P(), P()) + tripled,
        check_vma=False,
    )
```

time: 1350 us -> 959 us (0.71)
  waiting for transfers between devices: 625 us -> 207 us
  Pallas kernels: 172 us -> 249 us
  matrix products: 161 us -> 113 us
  starting transfers between devices: 8.12 us -> 41 us
  blocking collectives: 23.5 us -> 0 us
    all_gather x8 -> x4, waiting for transfers between devices: 334 us -> 36.1 us  [gather(): return lax.all_gather(values, 'fsdp', axis=0, tiled=True)]
    reduce_scatter x5 -> x2, waiting for transfers between devices: 208 us -> 0.04 us  [the longest x1 0.02 us: body(): up_part = lax.psum_scatter(ups, 'fsdp', scatter_dimension=0, tiled=True)]
    ppermute x5 -> x46, waiting for transfers between devices: 11.2 us -> 170 us  [the longest x34 136 us: swap(): lax.ppermute(values, 'fsdp', [(f, f ^ bit) for f in range(self.group)])]
    pallas_call x3 -> x11, Pallas kernels: 46 us -> 122 us  [the longest x6 79.6 us: everyone(): pl.pallas_call(functools.partial(exchange_kernel, within, parts), out_sha...]
    unnamed x15 -> x6, waiting for transfers between devices: 71 us -> 0.76 us
    ppermute x5 -> x46, starting transfers between devices: 6.96 us -> 40.8 us  [the longest x34 30.5 us: swap(): lax.ppermute(values, 'fsdp', [(f, f ^ bit) for f in range(self.group)])]
    all_gather x1 -> x0, blocking collectives: 23.5 us -> none  [gather(): return lax.all_gather(values, 'fsdp', axis=axis, tiled=True)]
    convert_element_type x13 -> x47, other arithmetic: 20.9 us -> 42.2 us  [the longest x26 21.4 us: add(): return (left.astype(F32) + right.astype(F32)).astype(BF16)]
  transfers between devices with their start and end apart: 19 -> 52, of which waited for: 11 -> 19; matrix products, arithmetic and copies ran while one was open for 28% -> 30% of each run, Pallas kernels for 11% -> 19%
where the time goes in v2:
time: 959 us; the launch traced here: 946 us
  Pallas kernels  249 us (26%)
  waiting for transfers between devices  207 us (22%)
  other arithmetic  194 us (20%)
  local copies, waits for them, and re-layouts  115 us (12%)
  matrix products  113 us (12%)
  starting transfers between devices  41 us (4%)
  between operations  27 us (3%)
    ppermute x34, waiting for transfers between devices, swap(): lax.ppermute(values, 'fsdp', [(f, f ^ bit) for f in range(self.group)])  136 us
    pallas_call x6, Pallas kernels, everyone(): pl.pallas_call(functools.partial(exchange_kernel, within, parts), out_sha...  79.6 us
    pallas_call x3, Pallas kernels, attend_back(): pl.pallas_call(functools.partial(attend_back_kernel, rows, block, bias is...  52.2 us
    dot_general x9, matrix products, dot_nt(): return lax.dot_general(a, b, NT, preferred_element_type=F32)  44.5 us
    pallas_call x3, Pallas kernels, feed(): pl.pallas_call(functools.partial(feed_kernel, with_product), grid=(width...  38.1 us
    sub x5, other arithmetic, adam_update(): master - rate * (first_hat / (jnp.sqrt(second_hat) + EPSILON) + WEIGHT_DE...  37.7 us
    pallas_call x3, Pallas kernels, attend(): pl.pallas_call(functools.partial(attend_kernel, rows, block, bias is not...  36.1 us
    all_gather x4, waiting for transfers between devices, gather(): return lax.all_gather(values, 'fsdp', axis=0, tiled=True)  36.1 us
  transfers between devices with their start and end apart: 52, of which 19 were waited for; matrix products, arithmetic and copies ran while one was open for 30% of the time, Pallas kernels for 19%

profile of v2, /device:TPU:0, one launch (start us, length us, event | category | flops | bytes accessed | tf_op | source)
XLA Modules:
  0.0 945.6 jit_solution(9827395374340291742)
XLA Ops:
  7.3 4.0 regroup.1
  11.3 2.7 slice_bitcast_fusion
  15.1 3.1 collective-permute-start
  19.7 11.1 %everyone_0.1 = f32[32,8,128]{2,1,0:T(8,128)} custom-call(f32[8,128]{1,0:T(8,128)} %pad_bitcast_fusion.3.x_ref), custom_call_target="tpu_custom_call" | custom-call | tf_op jit(solution)/shard_map/everyone_0/pallas_call | solution.py:127
  34.0 10.7 %gather_fusion = bf16[1536,768]{1,0:T(8,128)(2,1)S(1)} fusion(f32[4096,768]{1,0:T(8,128)} %param.46, s32[2048]{0:T(1024)S(1)} %pad_clamp_fusion), kind=kCustom, calls=%fused_computation | custom fusion | bytes 4724736 | tf_op jit(solution)/shard_map/gather | solution.py:890
  45.2 16.3 %collective-permute-done.1 = bf16[2,200,384]{2,1,0:T(8,128)(2,1)S(1)} collective-permute-done((bf16[2,200,384]{2,1,0:T(8,128)(2,1)S(1)}, bf16[2,200,384]{2,1,0:T(8,128)(2,1)S(1)}, u32[]{:S(2)}, u32[]{:S(2)}) %collective-permute-start.1) | collective-permute-done | bytes 307232 | tf_op jit(solution)/shard_map/ppermute | solution.py:644
  64.3 27.9 %collective-permute-done.2 = bf16[2,2,200,384]{3,2,1,0:T(8,128)(2,1)S(1)} collective-permute-done((bf16[2,2,200,384]{3,2,1,0:T(8,128)(2,1)S(1)}, bf16[2,2,200,384]{3,2,1,0:T(8,128)(2,1)S(1)}, u32[]{:S(2)}, u32[]{:S(2)}) %collective-permute-start.2) | collective-permute-done | bytes 614432 | tf_op jit(solution)/shard_map/ppermute | solution.py:644
  99.9 17.3 %collective-permute-done.5 = bf16[2,2,96,768]{3,2,1,0:T(8,128)(2,1)} collective-permute-done((bf16[2,2,96,768]{3,2,1,0:T(8,128)(2,1)}, bf16[2,2,96,768]{3,2,1,0:T(8,128)(2,1)}, u32[]{:S(2)}, u32[]{:S(2)}) %collective-permute-start.5) | collective-permute-done | bytes 589856 | tf_op jit(solution)/shard_map/ppermute | solution.py:644
  117.2 7.9 collective-permute-done.4
  129.7 14.8 %collective-permute-done.7 = bf16[2,96,768]{2,1,0:T(8,128)(2,1)S(1)} collective-permute-done((bf16[2,96,768]{2,1,0:T(8,128)(2,1)S(1)}, bf16[2,96,768]{2,1,0:T(8,128)(2,1)S(1)}, u32[]{:S(2)}, u32[]{:S(2)}) %collective-permute-start.7) | collective-permute-done | bytes 294944 | tf_op jit(solution)/shard_map/ppermute | solution.py:644
  147.0 3.8 fusion.34
  160.3 2.6 convert_element_type.691
  190.8 8.1 convolution_convert_fusion.refs_0_
  198.9 22.0 %attend_1024.1 = (bf16[1024,768]{1,0:T(8,128)(2,1)}, f32[1024,768]{1,0:T(8,128)}) custom-call(bf16[1024,2304]{1,0:T(8,128)(2,1)} %convolution_convert_fusion.refs_0_), custom_call_target="tpu_custom_call" | custom-call | flops 25769803776 | bytes 9437184 | tf_op jit(solution)/shard_map/attend_1024/pallas_call | solution.py:188
  220.9 3.2 fusion.166
  227.0 20.0 %feed_1024.1 = (bf16[1024,3072]{1,0:T(8,128)(2,1)}, f32[8,3072]{1,0:T(8,128)}, bf16[768,3072]{1,0:T(8,128)(2,1)}) custom-call(bf16[1024,768]{1,0:T(8,128)(2,1)} %add_convert_fusion.2.h_ref, bf16[768,6144]{1,0:T(8,128)(2,1)} %bitcast.397, bf16[8,128]{1,0:T(8,128)(2,1)} %broadcast_in_dim.468.sel_ref), custom_call_target="tpu_custom_call" | custom-call | flops 9663676416 | bytes 15728640 | tf_op jit(solution)/shard_map/feed_1024/pallas_call | solution.py:564
  249.5 5.5 convolution_convert_fusion.5.refs_0_
  255.0 8.3 attend_512.1
  263.3 2.4 fusion.167
  268.0 12.0 %feed_512.1 = (bf16[512,3072]{1,0:T(8,128)(2,1)}, f32[8,3072]{1,0:T(8,128)}, bf16[768,3072]{1,0:T(8,128)(2,1)}) custom-call(bf16[512,768]{1,0:T(8,128)(2,1)} %add_convert_fusion.9.h_ref, bf16[768,6144]{1,0:T(8,128)(2,1)} %all-gather.6.cloned.1.call-done.w_ref, bf16[8,128]{1,0:T(8,128)(2,1)} %broadcast_in_dim.468.sel_ref), custom_call_target="tpu_custom_call" | custom-call | flops 4831838208 | bytes 12582912 | tf_op jit(solution)/shard_map/feed_512/pallas_call | solution.py:564
  280.0 36.1 %all-gather.8.cloned.1.call-done.w_ref = bf16[768,6144]{1,0:T(8,128)(2,1)} async-done(((bf16[48,6144]{1,0:T(8,128)(2,1)}), bf16[768,6144]{1,0:T(8,128)(2,1)}) %all-gather.8.cloned.1.call-update) | async-done | bytes 9437200 | tf_op jit(solution)/shard_map/all_gather | solution.py:851
  321.0 3.7 convolution_convert_fusion.6.refs_0_
  324.6 5.8 attend_96.1
  334.2 6.2 feed_96.1
  345.2 11.5 %everyone_3.1 = f32[32,8,128]{2,1,0:T(8,128)} custom-call(f32[16,8,128]{2,1,0:T(8,128)} %bitcast.390), custom_call_target="tpu_custom_call" | custom-call | tf_op jit(solution)/shard_map/everyone_3/pallas_call | solution.py:127
  366.5 11.0 %everyone_4.1 = f32[16,32,128]{2,1,0:T(8,128)} custom-call(f32[16,32,128]{2,1,0:T(8,128)} %bitcast.372), custom_call_target="tpu_custom_call" | custom-call | tf_op jit(solution)/shard_map/everyone_4/pallas_call | solution.py:127
  379.1 18.3 %everyone_1.1 = f32[32,32,128]{2,1,0:T(8,128)} custom-call(f32[32,128]{1,0:T(8,128)} %bitcast.404), custom_call_target="tpu_custom_call" | custom-call | tf_op jit(solution)/shard_map/everyone_1/pallas_call | solution.py:127
  408.5 3.8 slice_convert_fusion.heads_ref
  412.2 10.4 %middle.1 = (f32[8,128]{1,0:T(8,128)}, f32[32,768]{1,0:T(8,128)}, f32[32,768]{1,0:T(8,128)}, f32[96,768]{1,0:T(8,128)}, f32[8,768]{1,0:T(8,128)}, /*index=5*/f32...) custom-call(f32[32,768]{1,0:T(8,128)} %get-tuple-element.513.yv_ref,, ...), custom_call_target="tpu_custom_call" | custom-call | tf_op jit(solution)/shard_map/middle/pallas_call | solution.py:520
  439.2 10.0 %everyone_5.1 = f32[16,8,128]{2,1,0:T(8,128)} custom-call(f32[16,8,128]{2,1,0:T(8,128)} %bitcast.392), custom_call_target="tpu_custom_call" | custom-call | tf_op jit(solution)/shard_map/everyone_5/pallas_call | solution.py:127
  461.2 9.1 scale_columns.1
  472.2 4.7 multiply_reduce_fusion.20
  478.4 2.5 convolution_convert_fusion.12.refs_1_
  481.4 5.8 attend_back_96.1
  487.2 4.0 multiply_reduce_fusion.21
  494.2 4.1 pad_maximum_fusion
  498.3 7.4 multiply_reduce_fusion.11
  506.7 3.6 convolution_convert_fusion.11.refs_1_
  519.8 2.9 collective-permute-done.9
  524.2 11.9 %attend_back_512.1 = bf16[512,2304]{1,0:T(8,128)(2,1)} custom-call(bf16[512,2304]{1,0:T(8,128)(2,1)} %convolution_convert_fusion.5.refs_0_, bf16[512,768]{1,0:T(8,128)(2,1)} %convolution_convert_fusion.11.refs_1_, bf16[512,768]{1,0:T(8,128)(2,1)} %get-tuple-element.256.refs_2_, f32[512,768]{1,0:T(8,128)} %get-tuple-element.288.refs_3_), custom_call_target="tpu_custom_call" | custom-call | flops 16106127360 | bytes 7864320 | tf_op jit(solution)/shard_map/attend_back_512/pallas_call | solution.py:269
  536.2 5.8 multiply_reduce_fusion.9
  553.0 26.6 %collective-permute-done.10 = bf16[2,96,768]{2,1,0:T(8,128)(2,1)S(1)} collective-permute-done((bf16[2,96,768]{2,1,0:T(8,128)(2,1)S(1)}, bf16[2,96,768]{2,1,0:T(8,128)(2,1)S(1)}, u32[]{:S(2)}, u32[]{:S(2)}) %collective-permute-start.10) | collective-permute-done | bytes 294944 | tf_op jit(solution)/shard_map/ppermute | solution.py:644
  580.0 6.1 multiply_reduce_fusion.3
  588.0 2.6 convolution_convert_fusion.7.refs_1_
  590.6 7.2 patch_grads.1
  597.8 2.5 convolution_convert_fusion.8
  610.2 34.5 %attend_back_1024.1 = bf16[1024,2304]{1,0:T(8,128)(2,1)} custom-call(bf16[1024,2304]{1,0:T(8,128)(2,1)} %convolution_convert_fusion.refs_0_, bf16[1024,768]{1,0:T(8,128)(2,1)} %convolution_convert_fusion.7.refs_1_, bf16[1024,768]{1,0:T(8,128)(2,1)} %get-tuple-element.250.refs_2_, f32[1024,768]{1,0:T(8,128)} %get-tuple-element.309.refs_3_), custom_call_target="tpu_custom_call" | custom-call | flops 64424509440 | bytes 15728640 | tf_op jit(solution)/shard_map/attend_back_1024/pallas_call | solution.py:269
  667.7 7.3 convolution_convert_fusion.1
  677.1 4.1 collective-permute-done.17
  681.2 15.0 %collective-permute-done.18 = bf16[2,2,2,200,384]{4,3,1,0,2:T(8,128)(2,1)S(1)} collective-permute-done((bf16[2,2,2,200,384]{4,3,1,0,2:T(8,128)(2,1)S(1)}, bf16[2,2,2,200,384]{4,3,1,0,2:T(8,128)(2,1)S(1)}, u32[]{:S(2)}, u32[]{:S(2)}) %collective-permute-start.18) | collective-permute-done | bytes 1228832 | tf_op jit(solution)/shard_map/ppermute | solution.py:642
  702.3 7.9 multiply_reduce_fusion.1
  711.8 5.4 bitcast_select_fusion.1
  720.9 19.7 %collective-permute-done.19 = bf16[2,2,24,1536]{3,2,1,0:T(8,128)(2,1)S(1)} collective-permute-done((bf16[2,2,24,1536]{3,2,1,0:T(8,128)(2,1)}, bf16[2,2,24,1536]{3,2,1,0:T(8,128)(2,1)S(1)}, u32[]{:S(2)}, u32[]{:S(2)}) %collective-permute-start.19) | collective-permute-done | bytes 294944 | tf_op jit(solution)/shard_map/ppermute | solution.py:644
  753.6 29.4 %scatter_custom_fusion = f32[4096,768]{1,0:T(8,128)} fusion(s32[3072]{0:T(1024)} %reshape.815, bf16[3072,768]{1,0:T(8,128)(2,1)} %bitcast_select_fusion.1, f32[]{:T(128)} %constant.479.clone.1, pred[3072]{0:T(1024)(128)(4,1)S(1)} %copy-done.120), kind=kCustom, calls=%fused_computation.7 | custom fusion | flops 7077888 | bytes 17305600 | tf_op jit(solution)/shard_map/scatter-add | solution.py:1171
  791.8 8.4 multiply_reduce_fusion
  807.0 2.6 collective-permute-start.35
  809.9 10.5 %collective-permute-done.37 = bf16[2,2,2,24,128]{4,3,2,1,0:T(8,128)(2,1)S(1)} collective-permute-done((bf16[2,2,2,24,128]{4,3,2,1,0:T(8,128)(2,1)}, bf16[2,2,2,24,128]{4,3,2,1,0:T(8,128)(2,1)S(1)}, u32[]{:S(2)}, u32[]{:S(2)}) %collective-permute-start.37) | collective-permute-done | bytes 49184 | tf_op jit(solution)/shard_map/ppermute | solution.py:642
  829.1 2.4 collective-permute-start.41
  841.5 3.1 convert_add_fusion.9
  850.8 3.1 convert_add_fusion.8
  862.0 17.7 %everyone_2.1 = bf16[32,64,128]{2,1,0:T(8,128)(2,1)} custom-call(bf16[64,128]{1,0:T(8,128)(2,1)} %pad_maximum_fusion.14.x_ref), custom_call_target="tpu_custom_call" | custom-call | tf_op jit(solution)/shard_map/everyone_2/pallas_call | solution.py:127
  887.6 5.3 multiply_subtract_fusion.1
  892.9 30.1 %multiply_subtract_fusion = (f32[4096,768]{1,0:T(8,128)}, f32[4096,768]{1,0:T(8,128)}, f32[4096,768]{1,0:T(8,128)}) fusion(f32[4096,768]{1,0:T(8,128)} %param.46, f32[4096,768]{1,0:T(8,128)} %param.47, f32[4096,768]{1,0:T(8,128)} %param.48, f32[4096,768]{1,0:T(8,128)} %scatter_custom_fusion, f32[]{:T(128)} %div.341), kind=kLoop, calls=%fused_computation.4 | loop fusion | flops 50331648 | bytes 88080384 | tf_op jit(solution)/shard_map/sub | solution.py:68
  925.6 11.8 %adam_mixing.1 = (f32[3,48,6144]{2,1,0:T(8,128)}, f32[3,48,6144]{2,1,0:T(8,128)}, f32[3,48,6144]{2,1,0:T(8,128)}) custom-call(f32[1]{0:T(128)} %bitcast.106.scal_ref, s32[1]{0:T(128)} %bitcast.107.core_ref, f32[48,6144]{1,0:T(8,128)} %get-tuple-element.504.refs_0_, f32[48,6144]{1,0:T(8,128)} %get-tuple-element.502.refs_1_, ...), custom_call_target="tpu_custom_call" | custom-call | tf_op jit(solution)/shard_map/adam_mixing/pallas_call | solution.py:361
  (765 shorter events, 273.5 us)
Async XLA Ops:
  7.2 143.5 %copy-start = (bf16[1,1024,128]{2,1,0:T(8,128)(2,1)S(1)}, bf16[1,1024,128]{2,1,0:T(8,128)(2,1)}, u32[]{:S(2)}) copy-start(bf16[1,1024,128]{2,1,0:T(8,128)(2,1)} %param.29) | copy-start | bytes 786436
  7.2 146.3 %all-gather.12.cloned.1.call-start = ((), (), s32[]{:S(2)}) async-start(), calls=%async_computation.7 | async-start | bytes 10027008 | tf_op jit(solution)/shard_map/all_gather | solution.py:851
  14.0 232.9 %all-gather.6.cloned.1.call-start = ((), (), s32[]{:S(2)}) async-start(), calls=%async_computation.2 | async-start | bytes 10027008 | tf_op jit(solution)/shard_map/all_gather | solution.py:851
  15.1 16.8 %collective-permute-start = (bf16[200,384]{1,0:T(8,128)(2,1)S(1)}, bf16[200,384]{1,0:T(8,128)(2,1)S(1)}, u32[]{:S(2)}, u32[]{:S(2)}) collective-permute-start(bf16[200,384]{1,0:T(8,128)(2,1)S(1)} %dynamic-slice_convert_fusion), channel_id=1, source_target_pairs={{0,4},{1,5},{2,6},{3,7},{4,0},{5,1},{6,2},{7,3},{8,12},{9,13},{10,... | collective-permute-start | bytes 460808 | tf_op jit(solution)/shard_map/ppermute | solution.py:644
  32.3 29.1 %collective-permute-start.1 = (bf16[2,200,384]{2,1,0:T(8,128)(2,1)S(1)}, bf16[2,200,384]{2,1,0:T(8,128)(2,1)S(1)}, u32[]{:S(2)}, u32[]{:S(2)}) collective-permute-start(bf16[2,200,384]{2,1,0:T(8,128)(2,1)S(1)} %broadcast_select_fusion.7), channel_id=1, source_target_pairs={{0,8},{1,9},{2,10},{3,11},{4,12},{5,13},{6,14},{7,15},{8,0},{9,1},... | collective-permute-start | bytes 921608 | tf_op jit(solution)/shard_map/ppermute | solution.py:644
  62.8 29.4 %collective-permute-start.3 = (bf16[2,2,2,96,768]{4,3,1,0,2:T(8,128)(2,1)}, bf16[2,2,2,96,768]{4,3,1,0,2:T(8,128)(2,1)}, u32[]{:S(2)}, u32[]{:S(2)}) collective-permute-start(bf16[2,2,2,96,768]{4,3,1,0,2:T(8,128)(2,1)} %bitcast.344), channel_id=1, source_target_pairs={{0,1},{1,0},{2,3},{3,2},{4,5},{5,4},{6,7},{7,6},{8,9},{9,8},{10,11... | collective-permute-start | bytes 3538952 | tf_op jit(solution)/shard_map/ppermute | solution.py:644
  62.9 29.3 %collective-permute-start.2 = (bf16[2,2,200,384]{3,2,1,0:T(8,128)(2,1)S(1)}, bf16[2,2,200,384]{3,2,1,0:T(8,128)(2,1)S(1)}, u32[]{:S(2)}, u32[]{:S(2)}) collective-permute-start(bf16[2,2,200,384]{3,2,1,0:T(8,128)(2,1)S(1)} %broadcast_select_fusion.5), channel_id=1, source_target_pairs={{0,2},{1,3},{2,0},{3,1},{4,6},{5,7},{6,4},{7,5},{8,10},{9,11},{10,... | collective-permute-start | bytes 1843208 | tf_op jit(solution)/shard_map/ppermute | solution.py:644
  64.3 64.8 %copy-start.135 = (pred[2]{0:T(512)(128)(4,1)}, pred[2]{0:T(512)(128)(4,1)S(1)}, u32[]{:S(2)}) copy-start(pred[2]{0:T(512)(128)(4,1)S(1)} %iota_compare_fusion.10) | copy-start | bytes 10
  97.0 28.2 %collective-permute-start.4 = (bf16[2,2,2,200,384]{4,3,2,1,0:T(8,128)(2,1)}, bf16[2,2,2,200,384]{4,3,2,1,0:T(8,128)(2,1)}, u32[]{:S(2)}, u32[]{:S(2)}) collective-permute-start(bf16[2,2,2,200,384]{4,3,2,1,0:T(8,128)(2,1)} %broadcast_select_fusion.1), channel_id=1, source_target_pairs={{0,16},{16,0},{1,17},{17,1},{2,18},{18,2},{3,19},{19,3},{4,20},{20... | collective-permute-start | bytes 3686408 | tf_op jit(solution)/shard_map/ppermute | solution.py:642
  98.0 19.2 %collective-permute-start.5 = (bf16[2,2,96,768]{3,2,1,0:T(8,128)(2,1)}, bf16[2,2,96,768]{3,2,1,0:T(8,128)(2,1)}, u32[]{:S(2)}, u32[]{:S(2)}) collective-permute-start(bf16[2,2,96,768]{3,2,1,0:T(8,128)(2,1)} %dynamic-slice_bitcast_fusion.4), channel_id=1, source_target_pairs={{0,2},{1,3},{2,0},{3,1},{4,6},{5,7},{6,4},{7,5},{8,10},{9,11},{10,... | collective-permute-start | bytes 1769480 | tf_op jit(solution)/shard_map/ppermute | solution.py:644
  129.2 15.2 %collective-permute-start.6 = (bf16[2,2,2,200,768]{4,3,2,1,0:T(8,128)(2,1)S(1)}, bf16[2,2,2,200,768]{4,3,2,1,0:T(8,128)(2,1)}, u32[]{:S(2)}, u32[]{:S(2)}) collective-permute-start(bf16[2,2,2,200,768]{4,3,2,1,0:T(8,128)(2,1)S(1)} %pad_maximum_fusion.1), channel_id=1, source_target_pairs={{0,1},{1,0},{2,3},{3,2},{4,5},{5,4},{6,7},{7,6},{8,9},{9,8},{10,11... | collective-permute-start | bytes 7372808 | tf_op jit(solution)/shard_map/ppermute | solution.py:644
  129.3 15.1 %collective-permute-start.7 = (bf16[2,96,768]{2,1,0:T(8,128)(2,1)S(1)}, bf16[2,96,768]{2,1,0:T(8,128)(2,1)S(1)}, u32[]{:S(2)}, u32[]{:S(2)}) collective-permute-start(bf16[2,96,768]{2,1,0:T(8,128)(2,1)S(1)} %dynamic-slice_bitcast_fusion.9), channel_id=1, source_target_pairs={{0,8},{1,9},{2,10},{3,11},{4,12},{5,13},{6,14},{7,15},{8,0},{9,1},... | collective-permute-start | bytes 884744 | tf_op jit(solution)/shard_map/ppermute | solution.py:644
  146.9 5.9 collective-permute-start.8
  153.6 162.5 %all-gather.8.cloned.1.call-start = ((), (), s32[]{:S(2)}) async-start(), calls=%async_computation.3 | async-start | bytes 10027008 | tf_op jit(solution)/shard_map/all_gather | solution.py:851
  154.3 252.3 %all-gather.10.cloned.1.call-start = ((), (), s32[]{:S(2)}) async-start(), calls=%async_computation.4 | async-start | bytes 2506752 | tf_op jit(solution)/shard_map/all_gather | solution.py:851
  181.3 68.0 %copy-start.118 = (f32[768]{0:T(1024)}, f32[768]{0:T(1024)S(1)}, u32[]{:S(2)}) copy-start(f32[768]{0:T(1024)S(1)} %get-tuple-element.448) | copy-start | bytes 9220
  181.3 68.0 %copy-start.139 = (f32[768]{0:T(1024)}, f32[768]{0:T(1024)S(1)}, u32[]{:S(2)}) copy-start(f32[768]{0:T(1024)S(1)} %get-tuple-element.447) | copy-start | bytes 9220
  181.3 84.7 %copy-start.92 = (f32[768]{0:T(1024)}, f32[768]{0:T(1024)S(1)}, u32[]{:S(2)}) copy-start(f32[768]{0:T(1024)S(1)} %get-tuple-element.442) | copy-start | bytes 9220
  181.3 139.6 %copy-start.84 = (f32[768]{0:T(1024)}, f32[768]{0:T(1024)S(1)}, u32[]{:S(2)}) copy-start(f32[768]{0:T(1024)S(1)} %get-tuple-element.440) | copy-start | bytes 9220
  181.3 139.6 %copy-start.114 = (f32[768]{0:T(1024)}, f32[768]{0:T(1024)S(1)}, u32[]{:S(2)}) copy-start(f32[768]{0:T(1024)S(1)} %get-tuple-element.439) | copy-start | bytes 9220
  181.3 152.0 %copy-start.86 = (f32[768]{0:T(1024)}, f32[768]{0:T(1024)S(1)}, u32[]{:S(2)}) copy-start(f32[768]{0:T(1024)S(1)} %get-tuple-element.437) | copy-start | bytes 9220
  185.5 135.4 %copy-start.131 = (f32[96]{0:T(128)}, f32[96]{0:T(128)S(1)}, u32[]{:S(2)}) copy-start(f32[96]{0:T(128)S(1)} %broadcast_multiply_fusion.8) | copy-start | bytes 1156
  186.7 62.6 %copy-start.97 = (f32[512]{0:T(512)}, f32[512]{0:T(512)S(1)}, u32[]{:S(2)}) copy-start(f32[512]{0:T(512)S(1)} %broadcast_multiply_fusion.6) | copy-start | bytes 6148
  188.6 132.4 %copy-start.141 = (f32[96]{0:T(128)}, f32[96]{0:T(128)S(1)}, u32[]{:S(2)}) copy-start(f32[96]{0:T(128)S(1)} %fusion.143) | copy-start | bytes 1156
  189.1 60.2 %copy-start.128 = (f32[512]{0:T(512)}, f32[512]{0:T(512)S(1)}, u32[]{:S(2)}) copy-start(f32[512]{0:T(512)S(1)} %fusion.136) | copy-start | bytes 6148
  317.0 485.8 %reduce-scatter.3.cloned.1.call-start = ((), (), s32[]{:S(2)}) async-start(), calls=%async_computation.5 | async-start | bytes 10027008 | tf_op jit(solution)/shard_map/reduce_scatter | solution.py:1054
  512.1 325.4 %reduce-scatter.5.cloned.1.call-start = ((), (), s32[]{:S(2)}) async-start(), calls=%async_computation.6 | async-start | bytes 10027008 | tf_op jit(solution)/shard_map/reduce_scatter | solution.py:1113
  516.8 5.9 collective-permute-start.9
  545.3 34.3 %collective-permute-start.10 = (bf16[2,96,768]{2,1,0:T(8,128)(2,1)S(1)}, bf16[2,96,768]{2,1,0:T(8,128)(2,1)S(1)}, u32[]{:S(2)}, u32[]{:S(2)}) collective-permute-start(bf16[2,96,768]{2,1,0:T(8,128)(2,1)S(1)} %copy-done.50), channel_id=1, source_target_pairs={{0,8},{1,9},{2,10},{3,11},{4,12},{5,13},{6,14},{7,15},{8,0},{9,1},... | collective-permute-start | bytes 884744 | tf_op jit(solution)/shard_map/ppermute | solution.py:644
  579.7 20.5 %collective-permute-start.11 = (bf16[2,2,96,768]{3,2,1,0:T(8,128)(2,1)S(1)}, bf16[2,2,96,768]{3,2,1,0:T(8,128)(2,1)S(1)}, u32[]{:S(2)}, u32[]{:S(2)}) collective-permute-start(bf16[2,2,96,768]{3,2,1,0:T(8,128)(2,1)S(1)} %broadcast_select_fusion.6), channel_id=1, source_target_pairs={{0,16},{16,0},{1,17},{17,1},{2,18},{18,2},{3,19},{19,3},{4,20},{20... | collective-permute-start | bytes 1769480 | tf_op jit(solution)/shard_map/ppermute | solution.py:642
  579.8 20.4 %collective-permute-start.12 = (bf16[768,1536]{1,0:T(8,128)(2,1)}, bf16[768,1536]{1,0:T(8,128)(2,1)}, u32[]{:S(2)}, u32[]{:S(2)}) collective-permute-start(bf16[768,1536]{1,0:T(8,128)(2,1)} %pad_maximum_fusion.3), channel_id=1, source_target_pairs={{0,1},{1,0},{2,3},{3,2},{4,5},{5,4},{6,7},{7,6},{8,9},{9,8},{10,11... | collective-permute-start | bytes 7077896 | tf_op jit(solution)/shard_map/ppermute | solution.py:644
  607.8 36.9 %collective-permute-start.13 = (bf16[2,2,2,96,768]{4,3,2,1,0:T(8,128)(2,1)S(1)}, bf16[2,2,2,96,768]{4,3,2,1,0:T(8,128)(2,1)S(1)}, u32[]{:S(2)}, u32[]{:S(2)}) collective-permute-start(bf16[2,2,2,96,768]{4,3,2,1,0:T(8,128)(2,1)S(1)} %broadcast_select_fusion.4), channel_id=1, source_target_pairs={{0,2},{1,3},{2,0},{3,1},{4,6},{5,7},{6,4},{7,5},{8,10},{9,11},{10,... | collective-permute-start | bytes 3538952 | tf_op jit(solution)/shard_map/ppermute | solution.py:644
  609.4 35.3 %collective-permute-start.14 = (bf16[2,2,2,2,24,1536]{5,4,3,2,1,0:T(8,128)(2,1)}, bf16[2,2,2,2,24,1536]{5,4,3,2,1,0:T(8,128)(2,1)}, u32[]{:S(2)}, u32[]{:S(2)}) collective-permute-start(bf16[2,2,2,2,24,1536]{5,4,3,2,1,0:T(8,128)(2,1)} %dynamic-slice_bitcast_fusion), channel_id=1, source_target_pairs={{0,16},{16,0},{1,17},{17,1},{2,18},{18,2},{3,19},{19,3},{4,20},{20... | collective-permute-start | bytes 3538952 | tf_op jit(solution)/shard_map/ppermute | solution.py:642
  610.2 34.5 %collective-permute-start.15 = (bf16[2,2,2,200,768]{4,3,1,0,2:T(8,128)(2,1)}, bf16[2,2,2,200,768]{4,3,1,0,2:T(8,128)(2,1)}, u32[]{:S(2)}, u32[]{:S(2)}) collective-permute-start(bf16[2,2,2,200,768]{4,3,1,0,2:T(8,128)(2,1)} %bitcast.343), channel_id=1, source_target_pairs={{0,1},{1,0},{2,3},{3,2},{4,5},{5,4},{6,7},{7,6},{8,9},{9,8},{10,11... | collective-permute-start | bytes 7372808 | tf_op jit(solution)/shard_map/ppermute | solution.py:644
  653.5 42.7 %collective-permute-start.16 = (bf16[2,2,2,2,96,768]{5,4,3,2,1,0:T(8,128)(2,1)}, bf16[2,2,2,2,96,768]{5,4,3,2,1,0:T(8,128)(2,1)}, u32[]{:S(2)}, u32[]{:S(2)}) collective-permute-start(bf16[2,2,2,2,96,768]{5,4,3,2,1,0:T(8,128)(2,1)} %broadcast_select_fusion), channel_id=1, source_target_pairs={{0,1},{1,0},{2,3},{3,2},{4,5},{5,4},{6,7},{7,6},{8,9},{9,8},{10,11... | collective-permute-start | bytes 7077896 | tf_op jit(solution)/shard_map/ppermute | solution.py:644
  665.8 15.4 %collective-permute-start.17 = (bf16[2,2,2,24,1536]{4,3,2,1,0:T(8,128)(2,1)S(1)}, bf16[2,2,2,24,1536]{4,3,2,1,0:T(8,128)(2,1)S(1)}, u32[]{:S(2)}, u32[]{:S(2)}) collective-permute-start(bf16[2,2,2,24,1536]{4,3,2,1,0:T(8,128)(2,1)S(1)} %copy-done.56), channel_id=1, source_target_pairs={{0,2},{1,3},{2,0},{3,1},{4,6},{5,7},{6,4},{7,5},{8,10},{9,11},{10,... | collective-permute-start | bytes 1769480 | tf_op jit(solution)/shard_map/ppermute | solution.py:644
  667.5 28.7 %collective-permute-start.18 = (bf16[2,2,2,200,384]{4,3,1,0,2:T(8,128)(2,1)S(1)}, bf16[2,2,2,200,384]{4,3,1,0,2:T(8,128)(2,1)S(1)}, u32[]{:S(2)}, u32[]{:S(2)}) collective-permute-start(bf16[2,2,2,200,384]{4,3,1,0,2:T(8,128)(2,1)S(1)} %copy-done.49), channel_id=1, source_target_pairs={{0,16},{16,0},{1,17},{17,1},{2,18},{18,2},{3,19},{19,3},{4,20},{20... | collective-permute-start | bytes 3686408 | tf_op jit(solution)/shard_map/ppermute | solution.py:642
  701.8 38.9 %collective-permute-start.21 = (bf16[768,768]{1,0:T(8,128)(2,1)}, bf16[768,768]{1,0:T(8,128)(2,1)}, u32[]{:S(2)}, u32[]{:S(2)}) collective-permute-start(bf16[768,768]{1,0:T(8,128)(2,1)} %get-tuple-element.324), channel_id=1, source_target_pairs={{0,1},{1,0},{2,3},{3,2},{4,5},{5,4},{6,7},{7,6},{8,9},{9,8},{10,11... | collective-permute-start | bytes 3538952 | tf_op jit(solution)/shard_map/ppermute | solution.py:644
  701.8 38.8 %collective-permute-start.22 = (bf16[768,768]{1,0:T(8,128)(2,1)}, bf16[768,768]{1,0:T(8,128)(2,1)}, u32[]{:S(2)}, u32[]{:S(2)}) collective-permute-start(bf16[768,768]{1,0:T(8,128)(2,1)} %get-tuple-element.325), channel_id=1, source_target_pairs={{0,1},{1,0},{2,3},{3,2},{4,5},{5,4},{6,7},{7,6},{8,9},{9,8},{10,11... | collective-permute-start | bytes 3538952 | tf_op jit(solution)/shard_map/ppermute | solution.py:644
  711.2 29.4 %collective-permute-start.19 = (bf16[2,2,24,1536]{3,2,1,0:T(8,128)(2,1)}, bf16[2,2,24,1536]{3,2,1,0:T(8,128)(2,1)S(1)}, u32[]{:S(2)}, u32[]{:S(2)}) collective-permute-start(bf16[2,2,24,1536]{3,2,1,0:T(8,128)(2,1)} %dynamic-slice_bitcast_fusion.8), channel_id=1, source_target_pairs={{0,8},{1,9},{2,10},{3,11},{4,12},{5,13},{6,14},{7,15},{8,0},{9,1},... | collective-permute-start | bytes 884744 | tf_op jit(solution)/shard_map/ppermute | solution.py:644
  711.3 29.3 %collective-permute-start.20 = (bf16[2,2,200,384]{3,2,1,0:T(8,128)(2,1)}, bf16[2,2,200,384]{3,2,1,0:T(8,128)(2,1)S(1)}, u32[]{:S(2)}, u32[]{:S(2)}) collective-permute-start(bf16[2,2,200,384]{3,2,1,0:T(8,128)(2,1)} %dynamic-slice_bitcast_fusion.1), channel_id=1, source_target_pairs={{0,2},{1,3},{2,0},{3,1},{4,6},{5,7},{6,4},{7,5},{8,10},{9,11},{10,... | collective-permute-start | bytes 1843208 | tf_op jit(solution)/shard_map/ppermute | solution.py:644
  747.2 35.7 %collective-permute-start.25 = (bf16[2,2,2,2,24,768]{5,4,3,1,0,2:T(8,128)(2,1)}, bf16[2,2,2,2,24,768]{5,4,3,1,0,2:T(8,128)(2,1)}, u32[]{:S(2)}, u32[]{:S(2)}) collective-permute-start(bf16[2,2,2,2,24,768]{5,4,3,1,0,2:T(8,128)(2,1)} %bitcast.346), channel_id=1, source_target_pairs={{0,16},{16,0},{1,17},{17,1},{2,18},{18,2},{3,19},{19,3},{4,20},{20... | collective-permute-start | bytes 1769480 | tf_op jit(solution)/shard_map/ppermute | solution.py:642
  748.4 34.6 %collective-permute-start.26 = (bf16[2,2,2,2,24,768]{5,4,3,2,1,0:T(8,128)(2,1)}, bf16[2,2,2,2,24,768]{5,4,3,2,1,0:T(8,128)(2,1)}, u32[]{:S(2)}, u32[]{:S(2)}) collective-permute-start(bf16[2,2,2,2,24,768]{5,4,3,2,1,0:T(8,128)(2,1)} %dynamic-slice_bitcast_fusion.2), channel_id=1, source_target_pairs={{0,2},{1,3},{2,0},{3,1},{4,6},{5,7},{6,4},{7,5},{8,10},{9,11},{10,... | collective-permute-start | bytes 1769480 | tf_op jit(solution)/shard_map/ppermute | solution.py:644
  750.9 32.1 %collective-permute-start.24 = (bf16[2,200,384]{2,1,0:T(8,128)(2,1)}, bf16[2,200,384]{2,1,0:T(8,128)(2,1)}, u32[]{:S(2)}, u32[]{:S(2)}) collective-permute-start(bf16[2,200,384]{2,1,0:T(8,128)(2,1)} %dynamic-slice_bitcast_fusion.5), channel_id=1, source_target_pairs={{0,8},{1,9},{2,10},{3,11},{4,12},{5,13},{6,14},{7,15},{8,0},{9,1},... | collective-permute-start | bytes 921608 | tf_op jit(solution)/shard_map/ppermute | solution.py:644
  751.4 31.5 %collective-permute-start.27 = (bf16[768,128]{1,0:T(8,128)(2,1)}, bf16[768,128]{1,0:T(8,128)(2,1)}, u32[]{:S(2)}, u32[]{:S(2)}) collective-permute-start(bf16[768,128]{1,0:T(8,128)(2,1)} %get-tuple-element.350), channel_id=1, source_target_pairs={{0,1},{1,0},{2,3},{3,2},{4,5},{5,4},{6,7},{7,6},{8,9},{9,8},{10,11... | collective-permute-start | bytes 589832 | tf_op jit(solution)/shard_map/ppermute | solution.py:644
  752.0 30.9 %collective-permute-start.23 = (bf16[2,24,1536]{2,1,0:T(8,128)(2,1)}, bf16[2,24,1536]{2,1,0:T(8,128)(2,1)}, u32[]{:S(2)}, u32[]{:S(2)}) collective-permute-start(bf16[2,24,1536]{2,1,0:T(8,128)(2,1)} %dynamic-slice_bitcast_fusion.13), channel_id=1, source_target_pairs={{0,4},{1,5},{2,6},{3,7},{4,0},{5,1},{6,2},{7,3},{8,12},{9,13},{10,... | collective-permute-start | bytes 442376 | tf_op jit(solution)/shard_map/ppermute | solution.py:644
  788.8 11.4 %collective-permute-start.28 = (bf16[24,1536]{1,0:T(8,128)(2,1)S(1)}, bf16[24,1536]{1,0:T(8,128)(2,1)S(1)}, u32[]{:S(2)}, u32[]{:S(2)}) collective-permute-start(bf16[24,1536]{1,0:T(8,128)(2,1)S(1)} %get-tuple-element.358), channel_id=1, source_target_pairs={{0,1},{1,0},{2,3},{3,2},{4,5},{5,4},{6,7},{7,6},{8,9},{9,8},{10,11... | collective-permute-start | bytes 221192 | tf_op jit(solution)/shard_map/ppermute | solution.py:644
  788.9 11.3 %collective-permute-start.32 = (bf16[2,2,2,2,24,128]{5,4,2,1,0,3:T(8,128)(2,1)S(1)}, bf16[2,2,2,2,24,128]{5,4,2,1,0,3:T(8,128)(2,1)S(1)}, u32[]{:S(2)}, u32[]{:S(2)}) collective-permute-start(bf16[2,2,2,2,24,128]{5,4,2,1,0,3:T(8,128)(2,1)S(1)} %bitcast.403), channel_id=1, source_target_pairs={{0,2},{1,3},{2,0},{3,1},{4,6},{5,7},{6,4},{7,5},{8,10},{9,11},{10,... | collective-permute-start | bytes 294920 | tf_op jit(solution)/shard_map/ppermute | solution.py:644
  789.0 11.2 %collective-permute-start.29 = (bf16[200,384]{1,0:T(8,128)(2,1)S(1)}, bf16[200,384]{1,0:T(8,128)(2,1)S(1)}, u32[]{:S(2)}, u32[]{:S(2)}) collective-permute-start(bf16[200,384]{1,0:T(8,128)(2,1)S(1)} %dynamic-slice_bitcast_fusion.10), channel_id=1, source_target_pairs={{0,4},{1,5},{2,6},{3,7},{4,0},{5,1},{6,2},{7,3},{8,12},{9,13},{10,... | collective-permute-start | bytes 460808 | tf_op jit(solution)/shard_map/ppermute | solution.py:644
  789.2 11.2 %collective-permute-start.30 = (bf16[2,2,2,24,768]{4,3,2,1,0:T(8,128)(2,1)S(1)}, bf16[2,2,2,24,768]{4,3,2,1,0:T(8,128)(2,1)S(1)}, u32[]{:S(2)}, u32[]{:S(2)}) collective-permute-start(bf16[2,2,2,24,768]{4,3,2,1,0:T(8,128)(2,1)S(1)} %dynamic-slice_bitcast_fusion.7), channel_id=1, source_target_pairs={{0,2},{1,3},{2,0},{3,1},{4,6},{5,7},{6,4},{7,5},{8,10},{9,11},{10,... | collective-permute-start | bytes 884744 | tf_op jit(solution)/shard_map/ppermute | solution.py:644
  791.0 9.4 collective-permute-start.31
  802.8 22.9 %collective-permute-start.38 = (bf16[48,6144]{1,0:T(8,128)(2,1)}, bf16[48,6144]{1,0:T(8,128)(2,1)}, u32[]{:S(2)}, u32[]{:S(2)}) collective-permute-start(bf16[48,6144]{1,0:T(8,128)(2,1)} %reduce-scatter.3.cloned.1.call-done), channel_id=1, source_target_pairs={{0,16},{16,0},{1,17},{17,1},{2,18},{18,2},{3,19},{19,3},{4,20},{20... | collective-permute-start | bytes 1769480 | tf_op jit(solution)/shard_map/ppermute | solution.py:642
  803.9 16.5 %collective-permute-start.37 = (bf16[2,2,2,24,128]{4,3,2,1,0:T(8,128)(2,1)}, bf16[2,2,2,24,128]{4,3,2,1,0:T(8,128)(2,1)S(1)}, u32[]{:S(2)}, u32[]{:S(2)}) collective-permute-start(bf16[2,2,2,24,128]{4,3,2,1,0:T(8,128)(2,1)} %dynamic-slice_bitcast_fusion.19), channel_id=1, source_target_pairs={{0,16},{16,0},{1,17},{17,1},{2,18},{18,2},{3,19},{19,3},{4,20},{20... | collective-permute-start | bytes 147464 | tf_op jit(solution)/shard_map/ppermute | solution.py:642
  805.9 18.7 %collective-permute-start.33 = (bf16[24,3072]{1,0:T(8,128)(2,1)S(1)}, bf16[24,3072]{1,0:T(8,128)(2,1)S(1)}, u32[]{:S(2)}, u32[]{:S(2)}) collective-permute-start(bf16[24,3072]{1,0:T(8,128)(2,1)S(1)} %pad_maximum_fusion.9), channel_id=1, source_target_pairs={{0,16},{16,0},{1,17},{17,1},{2,18},{18,2},{3,19},{19,3},{4,20},{20... | collective-permute-start | bytes 442376 | tf_op jit(solution)/shard_map/ppermute | solution.py:642
  807.0 17.7 %collective-permute-start.35 = (bf16[2,2,24,768]{3,2,1,0:T(8,128)(2,1)}, bf16[2,2,24,768]{3,2,1,0:T(8,128)(2,1)}, u32[]{:S(2)}, u32[]{:S(2)}) collective-permute-start(bf16[2,2,24,768]{3,2,1,0:T(8,128)(2,1)} %dynamic-slice_bitcast_fusion.12), channel_id=1, source_target_pairs={{0,8},{1,9},{2,10},{3,11},{4,12},{5,13},{6,14},{7,15},{8,0},{9,1},... | collective-permute-start | bytes 442376 | tf_op jit(solution)/shard_map/ppermute | solution.py:644
  809.5 15.1 %collective-permute-start.36 = (bf16[2,2,24,768]{3,2,1,0:T(8,128)(2,1)}, bf16[2,2,24,768]{3,2,1,0:T(8,128)(2,1)}, u32[]{:S(2)}, u32[]{:S(2)}) collective-permute-start(bf16[2,2,24,768]{3,2,1,0:T(8,128)(2,1)} %dynamic-slice_bitcast_fusion.11), channel_id=1, source_target_pairs={{0,8},{1,9},{2,10},{3,11},{4,12},{5,13},{6,14},{7,15},{8,0},{9,1},... | collective-permute-start | bytes 442376 | tf_op jit(solution)/shard_map/ppermute | solution.py:644
  820.4 5.3 collective-permute-start.34
  829.1 4.8 collective-permute-start.41
  831.5 4.4 collective-permute-start.39
  831.8 4.9 collective-permute-start.40
  837.5 12.4 %collective-permute-start.44 = (bf16[48,6144]{1,0:T(8,128)(2,1)}, bf16[48,6144]{1,0:T(8,128)(2,1)}, u32[]{:S(2)}, u32[]{:S(2)}) collective-permute-start(bf16[48,6144]{1,0:T(8,128)(2,1)} %reduce-scatter.5.cloned.1.call-done), channel_id=1, source_target_pairs={{0,16},{16,0},{1,17},{17,1},{2,18},{18,2},{3,19},{19,3},{4,20},{20... | collective-permute-start | bytes 1769480 | tf_op jit(solution)/shard_map/ppermute | solution.py:642
  844.6 5.4 collective-permute-start.43
  846.2 3.8 collective-permute-start.42
  850.0 5.8 collective-permute-start.45
  (160 other events, 1689.7 us)
Sparse Core Ops, SparseCore 0:
  14.2 112.7 all-gather.11
  153.7 79.7 all-gather.5
  236.4 79.6 all-gather.7
  318.7 41.6 all-gather.9
  512.3 132.6 reduce-scatter.2
  657.8 127.7 reduce-scatter.4

commit v3 on v2

--- a/solution.py
+++ b/solution.py
@@ -199,9 +199,9 @@
         ),
         compiler_params=pltpu.CompilerParams(vmem_limit_bytes=VMEM_LIMIT),
         cost_estimate=pl.CostEstimate(
-            flops=16 * rows * rows * 256 * pairs,
-            bytes_accessed=rows * pairs * 128 * 12,
-            transcendentals=2 * pairs * rows * rows,
+            flops=rows * rows * 128 * pairs,
+            bytes_accessed=rows * pairs * 128,
+            transcendentals=0,
         ),
         name=f"attend_{rows}",
     )(*args)
@@ -275,9 +275,9 @@
         scratch_shapes=[pltpu.VMEM((rows, 128), F32), pltpu.VMEM((rows, 128), F32)],
         compiler_params=pltpu.CompilerParams(vmem_limit_bytes=VMEM_LIMIT),
         cost_estimate=pl.CostEstimate(
-            flops=40 * rows * rows * 256 * pairs,
-            bytes_accessed=rows * pairs * 128 * 20,
-            transcendentals=2 * pairs * rows * rows,
+            flops=2 * rows * rows * 128 * pairs,
+            bytes_accessed=rows * pairs * 128,
+            transcendentals=0,
         ),
         name=f"attend_back_{rows}",
     )(*args)
@@ -414,11 +414,56 @@
 
 
 def middle_kernel(
-    scales, yv_ref, ya_ref, yt_ref, gains_ref, heads_ref, vt_ref, live_ref, pos_ref, count_ref,
+    scales, captions, sum_ref, base_ref, scale_ref, backs_ref, gains_ref, heads_ref, vt_ref,
+    live_ref, pos_ref, count_ref,
     loss_ref, dv_ref, da_ref, dt_ref, gg_ref, z_ref, zt_ref, de_ref, dt_e_ref, ev_ref, dvt_ref,
+    r1_ref, slope_ref,
+    x1_ref, x2_ref, r2_ref, x3_ref, r3_ref, x4_ref, r4_ref, send, recv,
 ):
-    clips = yv_ref.shape[0]
+    group = lax.axis_size("fsdp")
+    clips = lax.axis_size("dp") * group
+    member = lax.axis_index("fsdp")
+    replica = lax.axis_index("dp")
+    me = replica * group + member
+    part = backs_ref.shape[1]
     joint = vt_ref.shape[0]
+    own_group = pl.ds(pl.multiple_of(replica * group, group), group)
+    barrier = pltpu.get_barrier_semaphore()
+
+    def place(step):
+        peer = lax.rem(me + step, clips)
+        return peer, (peer // group, lax.rem(peer, group))
+
+    def near(step):
+        peer = lax.rem(member + step, group)
+        return peer, (replica, peer)
+
+    def greet(step, carry):
+        pl.semaphore_signal(barrier, inc=1, device_id=place(step)[1], device_id_type=MESH_ID)
+        return carry
+
+    def exchange(phase, count, where, source, target):
+        def copy(step):
+            peer, device = where(step)
+            return pltpu.make_async_remote_copy(
+                src_ref=source(peer),
+                dst_ref=target,
+                send_sem=send.at[phase, step],
+                recv_sem=recv.at[phase, step],
+                device_id=device,
+                device_id_type=MESH_ID,
+            )
+
+        def begin(step, carry):
+            copy(step).start()
+            return carry
+
+        def finish(step, carry):
+            copy(step).wait()
+            return carry
+
+        lax.fori_loop(1, count, begin, 0)
+        lax.fori_loop(1, count, finish, 0)
 
     def times(a, b, dims):
         return lax.dot_general(
@@ -426,6 +471,24 @@
         )
 
     plain, right, left = ((1,), (0,)), ((1,), (1,)), ((0,), (0,))
+    lax.fori_loop(1, clips, greet, 0)
+    x1_ref[...] = jnp.zeros_like(x1_ref)
+    x2_ref[...] = jnp.zeros_like(x2_ref)
+    x4_ref[...] = jnp.zeros_like(x4_ref)
+    for at in range(group):
+        x1_ref[at, :, :part] = sum_ref[:, at * part : (at + 1) * part]
+    pl.semaphore_wait(barrier, clips - 1)
+    r1_ref[me] = x1_ref[member]
+    exchange(0, clips, place, lambda peer: x1_ref.at[lax.rem(peer, group)], r1_ref.at[me])
+    for k in range(2 + captions):
+        x2_ref[:, k, :] = times(r1_ref[own_group, k, :part], backs_ref[min(k, 2)], plain)
+    r2_ref[member] = x2_ref[member]
+    exchange(1, group, near, lambda peer: x2_ref.at[peer], r2_ref.at[member])
+    x3_ref[...] = (jnp.sum(r2_ref[...], 0) + base_ref[...]) * scale_ref[...]
+    r3_ref[me] = x3_ref[...]
+    exchange(2, clips, place, lambda peer: x3_ref, r3_ref.at[me])
+    texts = jnp.concatenate([r3_ref[:, 2 + k, :] for k in range(captions)], 0)
+
 
     def normalise(values):
         centred = values - jnp.mean(values, -1, keepdims=True)
@@ -447,13 +510,13 @@
         return highest + jnp.log(total), exponent * (1.0 / total)
 
     hats, z = [], []
-    for t, ref in enumerate((yv_ref, ya_ref, yt_ref)):
-        hat, inverse = normalise(ref[...])
+    for t, rows in enumerate((r3_ref[:, 0, :], r3_ref[:, 1, :], texts)):
+        hat, inverse = normalise(rows)
         hats.append((hat, inverse))
         z.append(hat * gains_ref[2 * t : 2 * t + 1, :] + gains_ref[2 * t + 1 : 2 * t + 2, :])
-    heads = heads_ref[...]
+    heads = heads_ref[...].astype(F32)
     parts = (heads[:, :joint], heads[:, joint : 2 * joint], heads[:, 2 * joint :])
-    video_text = vt_ref[...]
+    video_text = vt_ref[...].astype(F32)
     e_video = times(z[0], parts[0], plain)
     e_both = times(e_video, video_text, plain)
     e_audio = times(z[1], parts[1], plain)
@@ -498,12 +561,27 @@
     dt_e_ref[...] = d_text
     ev_ref[...] = e_video
     dvt_ref[...] = d_both
-
-
-def contrast(scales, rows, gains, heads, video_text, live, positive, counts):
-    clips, features = rows[0].shape
-    texts = rows[2].shape[0]
+    for k in range(2 + captions):
+        if k < 2:
+            rows = (dv_ref, da_ref)[k][own_group, :]
+        else:
+            begin = pl.multiple_of((k - 2) * clips + replica * group, group)
+            rows = dt_ref[pl.ds(begin, group), :]
+        x4_ref[:, k, :part] = times(rows.astype(BF16).astype(F32), backs_ref[min(k, 2)], right)
+    r4_ref[member] = x4_ref[member]
+    exchange(3, group, near, lambda peer: x4_ref.at[peer], r4_ref.at[member])
+    for at in range(group):
+        slope_ref[:, at * part : (at + 1) * part] = r4_ref[at, :, :part]
+
+
+def contrast(scales, captions, sums, bases, token_scales, backs, gains, heads, video_text, *masks):
+    group = lax.axis_size("fsdp")
+    clips = lax.axis_size("dp") * group
+    features = bases.shape[1]
+    texts = captions * clips
     joint, width = video_text.shape
+    part = backs.shape[1]
+    padded = part + -part % 128
     shapes = [
         (8, 128),
         (clips, features),
@@ -516,15 +594,30 @@
         (texts, width),
         (clips, joint),
         (clips, width),
+        (clips, 8, padded),
+        (8, part * group),
     ]
     return pl.pallas_call(
-        functools.partial(middle_kernel, scales),
+        functools.partial(middle_kernel, scales, captions),
         out_shape=tuple(jax.ShapeDtypeStruct(shape, F32) for shape in shapes),
-        in_specs=[pl.BlockSpec(memory_space=pltpu.VMEM)] * 9,
+        in_specs=[pl.BlockSpec(memory_space=pltpu.VMEM)] * 10,
         out_specs=tuple(pl.BlockSpec(memory_space=pltpu.VMEM) for _ in shapes),
-        compiler_params=pltpu.CompilerParams(vmem_limit_bytes=VMEM_LIMIT),
+        scratch_shapes=[
+            pltpu.VMEM((group, 8, padded), F32),
+            pltpu.VMEM((group, 8, features), F32),
+            pltpu.VMEM((group, 8, features), F32),
+            pltpu.VMEM((8, features), F32),
+            pltpu.VMEM((clips, 8, features), F32),
+            pltpu.VMEM((group, 8, padded), F32),
+            pltpu.VMEM((group, 8, padded), F32),
+            pltpu.SemaphoreType.DMA((4, clips)),
+            pltpu.SemaphoreType.DMA((4, clips)),
+        ],
+        compiler_params=pltpu.CompilerParams(
+            vmem_limit_bytes=VMEM_LIMIT, collective_id=1, has_side_effects=True
+        ),
         name="middle",
-    )(*rows, gains, heads, video_text, live, positive, counts)
+    )(sums, bases, token_scales, backs, gains, heads, video_text, *masks)
 
 
 def feed_kernel(with_product, h_ref, w_ref, sel_ref, slope_ref, sums_ref, *rest):
@@ -573,9 +666,9 @@
         out_specs=tuple(outs),
         compiler_params=pltpu.CompilerParams(vmem_limit_bytes=VMEM_LIMIT),
         cost_estimate=pl.CostEstimate(
-            flops=4 * rows * features * width,
-            bytes_accessed=2 * features * width * 2 + 2 * rows * width,
-            transcendentals=rows * width,
+            flops=rows * features * width // 8,
+            bytes_accessed=rows * width,
+            transcendentals=0,
         ),
         name=f"feed_{rows}",
     )(normed, weight, select)
@@ -640,7 +733,7 @@
     def swap(self, values, name):
         if name == "y":
             return lax.ppermute(values, "dp", [(0, 1), (1, 0)])
-        bit = {"core": 1, "x": 2, "near": 4, "far": 8}[name]
+        bit = {"core": 1, "x": 2, "near": 4, "far": 8, "across": 12}[name]
         return lax.ppermute(values, "fsdp", [(f, f ^ bit) for f in range(self.group)])
 
     def bit(self, name):
@@ -664,12 +757,22 @@
         keep = lax.dynamic_index_in_dim(values, bit, at, keepdims=False)
         return keep, give, [n for n in names if n != name]
 
+    def spread(self, values):
+        for name in ("core", "x", "near", "far"):
+            other = yield values, name
+            values = jnp.where(self.bit(name) == 1, values, other)
+        return values
+
     def gather_clips(self, values):
         if not self.paired:
             return lax.all_gather(values, ("dp", "fsdp"), axis=0, tiled=True)
         names = []
         order = ["y", "far", "near", "x", "core"]
-        for name in ("near", "far", "y", "x", "core"):
+        one, two, three = yield [(values, "near"), (values, "far"), (values, "across")]
+        values, _ = self.merge(values, one, [], "near", order)
+        others, names = self.merge(two, three, [], "near", order)
+        values, names = self.merge(values, others, names, "far", order)
+        for name in ("y", "x", "core"):
             other = yield values, name
             values, names = self.merge(values, other, names, name, order)
         return values.reshape(-1, values.shape[-1])
@@ -767,13 +870,17 @@
 
     def stage(self, flows, work=None, inputs=()):
         active = [flow for flow in flows if flow.request is not None]
-        names = [flow.request[1] for flow in active]
-        held, inputs = lax.optimization_barrier(([flow.request[0] for flow in active], inputs))
-        sent = [self.swap(values, name) for values, name in zip(held, names)]
+        asked = [flow.request if isinstance(flow.request, list) else [flow.request] for flow in active]
+        held = [[values for values, _ in asks] for asks in asked]
+        held, inputs = lax.optimization_barrier((held, inputs))
+        sent = [
+            [self.swap(values, name) for values, (_, name) in zip(group, asks)]
+            for group, asks in zip(held, asked)
+        ]
         made = work(*inputs) if work is not None else ()
         sent, made = lax.optimization_barrier((sent, made))
-        for flow, other in zip(active, sent):
-            flow.push(other)
+        for flow, others in zip(active, sent):
+            flow.push(others if isinstance(flow.request, list) else others[0])
         return made
 
 
@@ -852,31 +959,18 @@
 
     weights = [None] * 3
     weights[1] = gather(low[1])
-    embed_flow = Flow(links.gather_rows(input_embed.astype(BF16), ("near", "far", "x", "y")))
-
     def exchange(*parts):
         packed = jnp.concatenate([part.reshape(-1).astype(F32) for part in parts])
         packed = jnp.pad(packed, (0, -packed.shape[0] % 1024)).reshape(-1, 128)
         return everyone(packed, 0).reshape(clips, -1)
 
+    embed_low = input_embed.astype(BF16)
+    embed_flow = Flow(links.gather_rows(embed_low, ("near", "far", "y", "x")))
+    wave_flow = Flow(links.spread(embed_low[-wave:])) if links.paired else embed_flow
     every = links.stage(
-        [embed_flow],
+        [embed_flow, wave_flow],
         exchange,
         (word_ids, word_counts, caption_counts, caption_clips, norm_params),
-    )
-    all_ids = every[:, :words].astype(jnp.int32)
-    at = words + captions
-    all_caption_counts = every[:, at].astype(jnp.int32)
-    all_counts = every[:, words : words + captions]
-    all_caption_clips = every[:, at + 1 : at + 1 + captions].astype(jnp.int32)
-    at = at + 1 + captions
-    gains_all = (
-        every[:group, at : at + 18 * gain_part]
-        .reshape(group, 3, 6, gain_part)
-        .transpose(1, 2, 0, 3)
-        .reshape(3, 6, features)
-        .astype(BF16)
-        .astype(F32)
     )
 
     def owned_rows(ids):
@@ -884,57 +978,90 @@
         owned = (local_ids >= 0) & (local_ids < table_rows)
         return jnp.clip(local_ids, 0, table_rows - 1), owned
 
-    def pick_words(ids):
+    def pick_words(every):
+        ids = every[:, :words].astype(jnp.int32)
         group_ids = lax.dynamic_slice_in_dim(ids, replica * group, group, 0).reshape(-1)
         local_ids, owned = owned_rows(group_ids)
         return jnp.where(owned[:, None], word_table[local_ids], 0.0).astype(BF16)
 
-    picked = links.stage([embed_flow], pick_words, (all_ids,))
+    picked = links.stage([embed_flow, wave_flow], pick_words, (every,))
     words_flow = Flow(links.scatter_words(picked))
 
-    valid = jnp.arange(slots)[None, :] < word_counts[0][:, None]
-    flat_valid = valid.reshape(-1)
-    caption_of = jnp.arange(words) // slots
-    allowed = (caption_of[:, None] == caption_of[None, :]) & flat_valid[None, :]
-    word_bias = jnp.where(allowed, 0.0, -1000000000.0).astype(F32)
-    select = ((jnp.arange(8)[:, None] == caption_of[None, :]) & flat_valid[None, :]).astype(BF16)
+    def prepare(every):
+        local_ids = owned_rows(every[:, :words].astype(jnp.int32).reshape(-1))
+        at = words + captions
+        live = jnp.arange(captions)[:, None] < every[:, at].astype(jnp.int32)[None, :]
+        live = live.reshape(1, -1)
+        counts = every[:, words : words + captions].T.reshape(-1, 1)
+        owners = every[:, at + 1 : at + 1 + captions].astype(jnp.int32).T.reshape(1, -1)
+        positive = live & (owners == jnp.arange(clips)[:, None])
+        at = at + 1 + captions
+        gains_all = (
+            every[:group, at : at + 18 * gain_part]
+            .reshape(group, 3, 6, gain_part)
+            .transpose(1, 2, 0, 3)
+            .reshape(3, 6, features)
+            .astype(BF16)
+            .astype(F32)
+        )
+        outer_rows = jnp.pad(gains_all[:, 4:].reshape(6, features), ((0, 2), (0, 0)))
+        masks = (live.astype(F32), positive.astype(F32), counts)
+        valid = (jnp.arange(slots)[None, :] < word_counts[0][:, None]).reshape(-1)
+        caption_of = jnp.arange(words) // slots
+        allowed = (caption_of[:, None] == caption_of[None, :]) & valid[None, :]
+        word_bias = jnp.where(allowed, 0.0, -1000000000.0).astype(F32)
+        select = ((jnp.arange(8)[:, None] == caption_of[None, :]) & valid[None, :]).astype(BF16)
+        own_counts = word_counts[0].astype(F32)
+        sizes = jnp.array([video_count, audio_count], F32)
+        scales = 1.0 / jnp.concatenate([sizes, own_counts, jnp.ones(6 - captions, F32)])
+        heads_low = jnp.concatenate(
+            [head_proj, jnp.pad(video_text_proj, ((0, shard - joint_part), (0, 0)))], 1
+        ).astype(BF16)
+        backs = mixing_out.astype(BF16).astype(F32)
+        return (
+            gains_all,
+            outer_rows,
+            masks,
+            (word_bias, word_bias.T, select),
+            scales[:, None],
+            heads_low,
+            backs,
+            local_ids,
+        )
+
+    (
+        gains_all,
+        outer_rows,
+        masks,
+        (word_bias, turned_bias, select),
+        token_scales,
+        heads_low,
+        backs,
+        (local_ids, owned),
+    ) = links.stage([embed_flow, wave_flow, words_flow], prepare, (every,))
     unused = jnp.zeros((8, 128), BF16)
-
     biases = (None, None, word_bias)
+    turned_biases = (None, None, turned_bias)
     selects = (unused, unused, select)
     forward_block = (512, 512, words)
     backward_block = (512, 256, words)
-    counts = word_counts[0].astype(F32)
-
     normed, joined, attended, fed, streams = ([None] * 3 for _ in range(5))
-    for _ in range(3):
-        links.stage([embed_flow, words_flow])
-    embed = embed_flow.value
-    streams[1], streams[0] = links.stage(
-        [words_flow],
-        lambda rows: (dot(audio[0], rows[patch:]), dot(video[0], rows[:patch])),
-        (embed,),
-    )
-    heads_low = jnp.concatenate(
-        [head_proj, jnp.pad(video_text_proj, ((0, shard - joint_part), (0, 0)))], 1
-    ).astype(BF16)
-    streams[2] = words_flow.value.astype(F32)
-
-    def forward(tower):
-        normed[tower], joined[tower], attended[tower] = attention_forward(
-            streams[tower],
-            biases[tower],
-            weights[tower],
-            gains_all[tower],
-            forward_block[tower],
-        )
-        fed[tower] = feed_forward(
-            streams[tower],
-            attended[tower][0],
-            weights[tower],
-            gains_all[tower],
-            selects[tower],
-            tower < 2,
+    links.stage([wave_flow, words_flow])
+    wave_rows = wave_flow.value
+    if not links.paired:
+        wave_rows = wave_rows[patch:]
+    streams[1] = links.stage(
+        [words_flow], lambda rows: dot(audio[0], rows), (wave_rows,)
+    )
+
+    def attention(tower, stream, mixing):
+        return attention_forward(
+            stream, biases[tower], mixing, gains_all[tower], forward_block[tower]
+        )
+
+    def feeding(tower, stream, mixed, mixing):
+        return feed_forward(
+            stream, mixed, mixing, gains_all[tower], selects[tower], tower < 2
         )
 
     streams, weights[1], low_video, low_text = lax.optimization_barrier(
@@ -942,59 +1069,45 @@
     )
     weights[0] = gather(low_video)
     weights[2] = gather(low_text)
-    forward(1)
-    fed[1], weights[0] = lax.optimization_barrier((fed[1], weights[0]))
-    forward(0)
+    normed[1], joined[1], attended[1] = links.stage(
+        [embed_flow, words_flow],
+        lambda stream, mixing: attention(1, stream, mixing),
+        (streams[1], weights[1]),
+    )
+    streams[2] = words_flow.value.astype(F32)
+    fed[1] = links.stage(
+        [embed_flow],
+        lambda mixed: feeding(1, streams[1], mixed, weights[1]),
+        (attended[1][0],),
+    )
+    embed = embed_flow.value
+    fed[1], weights[0], embed = lax.optimization_barrier((fed[1], weights[0], embed))
+    streams[0] = dot(video[0], embed[:patch])
+    normed[0], joined[0], attended[0] = attention(0, streams[0], weights[0])
+    fed[0] = feeding(0, streams[0], attended[0][0], weights[0])
     fed[0], weights[2], heads_low = lax.optimization_barrier((fed[0], weights[2], heads_low))
     heads_all = gather(heads_low)
-    forward(2)
-
-    heads = heads_all[:, : head_proj.shape[1]].astype(F32)
+    normed[2], joined[2], attended[2] = attention(2, streams[2], weights[2])
+    fed[2] = feeding(2, streams[2], attended[2][0], weights[2])
+
+    heads = heads_all[:, : head_proj.shape[1]]
     video_text = heads_all[:, head_proj.shape[1] :].reshape(group, shard, text_width)
-    video_text = video_text[:, :joint_part].reshape(group * joint_part, text_width).astype(F32)
-    slopes, sums, products, bases = [], [], [], []
-    for tower in range(3):
-        rows, _, parts = fed[tower]
-        slopes.append(parts[0])
-        if tower < 2:
-            products.append(parts[2])
-            sums.append(parts[1][:1])
-            bases.append(jnp.sum(rows, 0, keepdims=True))
-        else:
-            sums.append(parts[1][:captions])
-            bases.append(full(select[:captions].astype(F32), rows))
-
+    video_text = video_text[:, :joint_part].reshape(group * joint_part, text_width)
+    slopes = [fed[t][2][0] for t in range(3)]
+    products = [fed[t][2][2] for t in range(2)]
+    row_sums = [fed[t][2][1] for t in range(3)]
     token_count = 2 + captions
-    back_part = mixing_out.shape[1]
-    backs = mixing_out.astype(BF16).astype(F32)
-    hidden = back_part * group
-    summed = jnp.concatenate(sums, 0).reshape(token_count, group, back_part).transpose(1, 0, 2)
-    every_sum = unpack(everyone(pack(summed), 3, parts=True), (token_count, back_part))
-
-    def own_group(values):
-        return lax.dynamic_slice_in_dim(values, replica * group, group, 0)
-
-    def by_tower(values):
-        width = values.shape[-1]
-        return values[:, 0], values[:, 1], values[:, 2:].reshape(-1, width)
-
-    def by_clip(parts):
-        count, width = parts[0].shape
-        return jnp.concatenate(
-            [parts[0][:, None], parts[1][:, None], parts[2].reshape(count, captions, width)], 1
-        )
-
-    group_sums = by_tower(own_group(every_sum))
-    partial = by_clip([full(group_sums[t], backs[t]) for t in range(3)])
-    through = everyone(pack(partial), 4, within=True, parts=True)
-    through = unpack(jnp.sum(through, 0, keepdims=True), (token_count, features))[0]
-    scales = jnp.concatenate([jnp.array([video_count, audio_count], F32), counts])
-    mine = (jnp.concatenate(bases, 0) + through) / scales[:, None]
-
-    pooled = unpack(everyone(pack(mine[None])[0], 1), (token_count * features,))
-    live = (jnp.arange(captions)[None, :] < all_caption_counts[:, None]).reshape(1, -1)
-    positive = live & (all_caption_clips.reshape(1, -1) == jnp.arange(clips)[:, None])
-    outer_rows = jnp.pad(gains_all[:, 4:].reshape(6, features), ((0, 2), (0, 0)))
+    summed = jnp.concatenate(
+        [row_sums[0][:1], row_sums[1][:1], row_sums[2][: 8 - 2]], 0
+    )
+    bases = jnp.concatenate(
+        [
+            jnp.sum(fed[0][0], 0, keepdims=True),
+            jnp.sum(fed[1][0], 0, keepdims=True),
+            full(select[: 8 - 2].astype(F32), fed[2][0]),
+        ],
+        0,
+    )
     (
         loss,
         *grad_rows_all,
@@ -1005,19 +1118,19 @@
         d_text,
         embed_video,
         d_video_text,
+        every_sum,
+        sloped,
     ) = contrast(
         (1.0 / video_count, 1.0 / audio_count),
-        (
-            pooled[:, :features],
-            pooled[:, features : 2 * features],
-            pooled[:, 2 * features :].reshape(-1, features),
-        ),
+        captions,
+        summed,
+        bases,
+        token_scales,
+        backs,
         outer_rows,
         heads,
         video_text,
-        live.astype(F32),
-        positive.astype(F32),
-        all_counts.reshape(-1, 1),
+        *masks,
     )
     loss = loss[0, 0]
     z = (z_pair[0], z_pair[1], z_text)
@@ -1033,22 +1146,21 @@
 
     branch_all = [rows.astype(BF16) for rows in grad_rows_all]
 
-    all_sums = by_tower(every_sum)
+    back_part = mixing_out.shape[1]
 
     def back_grads():
-        return jnp.stack([full(all_sums[t].T, branch_all[t].astype(F32)) for t in range(3)])
-
-    group_branch = by_clip(branch_all)
-    group_branch = by_tower(own_group(group_branch).astype(F32))
-    partial = by_clip([dot_nt_full(group_branch[t], backs[t]) for t in range(3)])
-    sloped = unpack(everyone(pack(partial), 5, within=True, parts=True), (token_count, back_part))
-    sloped = sloped.transpose(1, 0, 2).reshape(token_count, hidden)
-    own_slopes = (sloped[:1], sloped[1:2], sloped[2:])
-
-    def own_rows(values, per_clip):
-        return lax.dynamic_slice_in_dim(values, clip * per_clip, per_clip, 0)
-
-    own_grads = [own_rows(grad_rows_all[t], 1 if t < 2 else captions) for t in range(3)]
+        own = every_sum[:, :, :back_part].transpose(1, 0, 2)
+        own = (own[0], own[1], own[2:token_count].reshape(-1, back_part))
+        return jnp.stack([full(own[t].T, branch_all[t].astype(F32)) for t in range(3)])
+
+    own_grads = [
+        lax.dynamic_slice_in_dim(grad_rows_all[0], clip, 1, 0),
+        lax.dynamic_slice_in_dim(grad_rows_all[1], clip, 1, 0),
+        lax.dynamic_slice_in_dim(
+            grad_rows_all[2].reshape(captions, clips, features), clip, 1, 1
+        ).reshape(captions, features),
+    ]
+    own_slopes = (sloped[:1], sloped[1:2], sloped[2:token_count])
     ups = scale_columns(products[1], products[0], jnp.concatenate(own_slopes[1::-1], 0))
     ups, own_slopes = lax.optimization_barrier((ups, own_slopes))
     up_part = lax.psum_scatter(ups, "fsdp", scatter_dimension=0, tiled=True)
@@ -1084,13 +1196,12 @@
         return made, up
 
     def inner_backward(tower, grad_mixed):
-        turned = None if biases[tower] is None else biases[tower].T
         return attend_back(
             joined[tower],
             grad_mixed,
             attended[tower][0],
             attended[tower][1],
-            turned,
+            turned_biases[tower],
             backward_block[tower],
         )
 
@@ -1133,10 +1244,18 @@
     rest = [word_flow, video_flow, embed_flow]
     joined_audio = links.stage(rest, lambda part: inner_backward(1, part), (made_audio[2],))
 
-    def audio_inward(grad_joined):
-        return halves(dot_tn(normed[1], grad_joined).astype(BF16), made_audio[1])
-
-    audio_parts = links.stage(rest, audio_inward, (joined_audio,))
+    def scatter_table(every_word):
+        return jax.ops.segment_sum(
+            jnp.where(owned[:, None], every_word.astype(F32), 0.0),
+            local_ids,
+            num_segments=table_rows,
+        )
+
+    def audio_inward(grad_joined, every_word):
+        inward = dot_tn(normed[1], grad_joined).astype(BF16)
+        return halves(inward, made_audio[1]), scatter_table(every_word)
+
+    audio_parts, table_grad = links.stage(rest, audio_inward, (joined_audio, word_flow.value))
     cut = features
     if links.paired:
         audio_flows = [
@@ -1166,18 +1285,10 @@
     )
     rest += [beside_flow]
 
-    def scatter_table(every_word):
-        local_ids, owned = owned_rows(all_ids.reshape(-1))
-        return jax.ops.segment_sum(
-            jnp.where(owned[:, None], every_word.astype(F32), 0.0),
-            local_ids,
-            num_segments=table_rows,
-        )
-
     def squared(*values):
         return sum(jnp.sum(value * value) for value in values)
 
-    table_grad = links.stage(rest, scatter_table, (word_flow.value,))
+    links.stage(rest)
     back_grad, (heads_grad, video_text_grad), table_square = links.stage(
         rest, lambda table: (back_grads(), head_grads(), squared(table)), (table_grad,)
     )

time: 959 us -> 892 us (0.930)
  waiting for transfers between devices: 207 us -> 169 us
  local copies, waits for them, and re-layouts: 115 us -> 89.2 us
    pallas_call x1, Pallas kernels: 10.4 us -> 62 us  [contrast(): pl.pallas_call(functools.partial(middle_kernel, scales, captions), out_sh...]
    pallas_call x6 -> x2, Pallas kernels: 79.6 us -> 29.9 us  [everyone(): pl.pallas_call(functools.partial(exchange_kernel, within, parts), out_sha...]
    ppermute x34 -> x39, waiting for transfers between devices: 136 us -> 111 us  [swap(): lax.ppermute(values, 'fsdp', [(f, f ^ bit) for f in range(self.group)])]
    ppermute x12, waiting for transfers between devices: 34.4 us -> 11.4 us  [swap(): return lax.ppermute(values, 'dp', [(0, 1), (1, 0)])]
    reshape x13 -> x2, local copies, waits for them, and re-layouts: 11.9 us -> 0.61 us  [the longest x1 0.59 us: prepare(): counts = every[:, words:words + captions].T.reshape(-1, 1)]
    unnamed x355 -> x347, local copies, waits for them, and re-layouts: 23 us -> 23.5 us
    ppermute x34 -> x39, starting transfers between devices: 30.5 us -> 30.5 us  [swap(): lax.ppermute(values, 'fsdp', [(f, f ^ bit) for f in range(self.group)])]
  transfers between devices with their start and end apart: 52 -> 57, of which waited for: 19 -> 20; matrix products, arithmetic and copies ran while one was open for 30% -> 33% of each run, Pallas kernels for 19% -> 16%
where the time goes in v3:
time: 892 us; the launch traced here: 884 us
  Pallas kernels  251 us (28%)
  other arithmetic  192 us (22%)
  waiting for transfers between devices  169 us (19%)
  matrix products  111 us (12%)
  local copies, waits for them, and re-layouts  89.2 us (10%)
  starting transfers between devices  44.6 us (5%)
  between operations  27.1 us (3%)
    ppermute x39, waiting for transfers between devices, swap(): lax.ppermute(values, 'fsdp', [(f, f ^ bit) for f in range(self.group)])  111 us
    pallas_call x1, Pallas kernels, contrast(): pl.pallas_call(functools.partial(middle_kernel, scales, captions), out_sh...  62 us
    pallas_call x3, Pallas kernels, attend_back(): pl.pallas_call(functools.partial(attend_back_kernel, rows, block, bias is...  52 us
    dot_general x9, matrix products, dot_nt(): return lax.dot_general(a, b, NT, preferred_element_type=F32)  49.4 us
    all_gather x4, waiting for transfers between devices, gather(): return lax.all_gather(values, 'fsdp', axis=0, tiled=True)  44.9 us
    pallas_call x3, Pallas kernels, feed(): pl.pallas_call(functools.partial(feed_kernel, with_product), grid=(width...  38.2 us
    sub x5, other arithmetic, adam_update(): master - rate * (first_hat / (jnp.sqrt(second_hat) + EPSILON) + WEIGHT_DE...  37.7 us
    pallas_call x3, Pallas kernels, attend(): pl.pallas_call(functools.partial(attend_kernel, rows, block, bias is not...  36.2 us
  transfers between devices with their start and end apart: 57, of which 20 were waited for; matrix products, arithmetic and copies ran while one was open for 33% of the time, Pallas kernels for 16%

profile of v3, /device:TPU:0, one launch (start us, length us, event | category | flops | bytes accessed | tf_op | source)
XLA Modules:
  0.0 883.8 jit_solution(14583392775917513385)
XLA Ops:
  7.3 4.0 regroup.1
  11.3 2.7 slice_bitcast_fusion
  14.3 3.1 collective-permute-start
  23.1 12.4 %everyone_0.1 = f32[32,8,128]{2,1,0:T(8,128)} custom-call(f32[8,128]{1,0:T(8,128)} %pad_bitcast_fusion.x_ref), custom_call_target="tpu_custom_call" | custom-call | tf_op jit(solution)/shard_map/everyone_0/pallas_call | solution.py:127
  42.2 10.7 %gather_fusion = bf16[1536,768]{1,0:T(8,128)(2,1)S(1)} fusion(f32[4096,768]{1,0:T(8,128)} %param.46, s32[2048]{0:T(1024)S(1)} %pad_clamp_fusion), kind=kCustom, calls=%fused_computation | custom fusion | bytes 4724736 | tf_op jit(solution)/shard_map/gather | solution.py:985
  53.4 10.7 %collective-permute-done.2 = bf16[2,200,384]{2,1,0:T(8,128)(2,1)S(1)} collective-permute-done((bf16[2,200,384]{2,1,0:T(8,128)(2,1)S(1)}, bf16[2,200,384]{2,1,0:T(8,128)(2,1)S(1)}, u32[]{:S(2)}, u32[]{:S(2)}) %collective-permute-start.2) | collective-permute-done | bytes 307232 | tf_op jit(solution)/shard_map/ppermute | solution.py:737
  76.4 14.7 %collective-permute-done.5 = bf16[128,768]{1,0:T(8,128)(2,1)} collective-permute-done((bf16[128,768]{1,0:T(8,128)(2,1)}, bf16[128,768]{1,0:T(8,128)(2,1)}, u32[]{:S(2)}, u32[]{:S(2)}) %collective-permute-start.5) | collective-permute-done | bytes 196640 | tf_op jit(solution)/shard_map/ppermute | solution.py:737
  98.0 20.5 %collective-permute-done.7 = bf16[128,768]{1,0:T(8,128)(2,1)S(1)} collective-permute-done((bf16[128,768]{1,0:T(8,128)(2,1)S(1)}, bf16[128,768]{1,0:T(8,128)(2,1)S(1)}, u32[]{:S(2)}, u32[]{:S(2)}) %collective-permute-start.7) | collective-permute-done | bytes 196640 | tf_op jit(solution)/shard_map/ppermute | solution.py:737
  120.5 13.6 %collective-permute-done.9 = bf16[2,96,768]{2,1,0:T(8,128)(2,1)} collective-permute-done((bf16[2,96,768]{2,1,0:T(8,128)(2,1)S(1)}, bf16[2,96,768]{2,1,0:T(8,128)(2,1)}, u32[]{:S(2)}, u32[]{:S(2)}) %collective-permute-start.9) | collective-permute-done | bytes 294944 | tf_op jit(solution)/shard_map/ppermute | solution.py:737
  146.1 7.4 convolution_convert_fusion.refs_0_
  153.5 21.9 %attend_1024.1 = (bf16[1024,768]{1,0:T(8,128)(2,1)}, f32[1024,768]{1,0:T(8,128)}) custom-call(bf16[1024,2304]{1,0:T(8,128)(2,1)} %convolution_convert_fusion.refs_0_), custom_call_target="tpu_custom_call" | custom-call | flops 805306368 | bytes 786432 | tf_op jit(solution)/shard_map/attend_1024/pallas_call | solution.py:188
  175.5 3.7 collective-permute-done.10
  183.4 3.3 fusion.174
  189.7 19.9 %feed_1024.1 = (bf16[1024,3072]{1,0:T(8,128)(2,1)}, f32[8,3072]{1,0:T(8,128)}, bf16[768,3072]{1,0:T(8,128)(2,1)}) custom-call(bf16[1024,768]{1,0:T(8,128)(2,1)} %add_convert_fusion.2.h_ref, bf16[768,6144]{1,0:T(8,128)(2,1)} %bitcast.320, bf16[8,128]{1,0:T(8,128)(2,1)} %broadcast_in_dim.462.sel_ref), custom_call_target="tpu_custom_call" | custom-call | flops 301989888 | bytes 3145728 | tf_op jit(solution)/shard_map/feed_1024/pallas_call | solution.py:657
  209.7 5.3 bitcast_select_fusion
  215.0 2.9 all-gather.6.cloned.1.call-done.w_ref
  217.9 7.1 fusion.175
  225.1 3.0 copy.188
  231.1 6.1 convolution_convert_fusion.5.refs_0_
  237.1 8.3 attend_512.1
  250.3 12.0 %feed_512.1 = (bf16[512,3072]{1,0:T(8,128)(2,1)}, f32[8,3072]{1,0:T(8,128)}, bf16[768,3072]{1,0:T(8,128)(2,1)}) custom-call(bf16[512,768]{1,0:T(8,128)(2,1)} %add_convert_fusion.9.h_ref, bf16[768,6144]{1,0:T(8,128)(2,1)} %all-gather.6.cloned.1.call-done.w_ref, bf16[8,128]{1,0:T(8,128)(2,1)} %broadcast_in_dim.462.sel_ref), custom_call_target="tpu_custom_call" | custom-call | flops 150994944 | bytes 1572864 | tf_op jit(solution)/shard_map/feed_512/pallas_call | solution.py:657
  262.3 40.8 %all-gather.8.cloned.1.call-done.w_ref = bf16[768,6144]{1,0:T(8,128)(2,1)} async-done(((bf16[48,6144]{1,0:T(8,128)(2,1)}), bf16[768,6144]{1,0:T(8,128)(2,1)}) %all-gather.8.cloned.1.call-update) | async-done | bytes 9437200 | tf_op jit(solution)/shard_map/all_gather | solution.py:958
  310.7 3.1 multiply_reduce_fusion.6
  322.6 3.6 convolution_convert_fusion.6.refs_0_
  326.1 5.9 attend_96.1
  335.3 6.2 feed_96.1
  348.0 2.9 slice.328.heads_ref
  351.0 62.0 %middle.1 = (f32[8,128]{1,0:T(8,128)}, f32[32,768]{1,0:T(8,128)}, f32[32,768]{1,0:T(8,128)}, f32[96,768]{1,0:T(8,128)}, f32[8,768]{1,0:T(8,128)}, /*index=5*/f32...) custom-call(f32[8,3072]{1,0:T(8,128)} %pad_maximum_fusion.11.sum_ref, ...), custom_call_target="tpu_custom_call" | custom-call | tf_op jit(solution)/shard_map/middle/pallas_call | solution.py:600
  416.2 9.3 %scale_columns.1 = bf16[768,6144]{1,0:T(8,128)(2,1)} custom-call(bf16[768,3072]{1,0:T(8,128)(2,1)} %get-tuple-element.334.first_ref, bf16[768,3072]{1,0:T(8,128)(2,1)} %get-tuple-element.335.second_ref, f32[2,3072]{1,0:T(2,128)} %pad_maximum_fusion.13.slopes_ref), custom_call_target="tpu_custom_call" | custom-call | tf_op jit(solution)/shard_map/scale_columns/pallas_call | solution.py:385
  427.3 4.9 multiply_reduce_fusion.21
  436.9 5.8 attend_back_96.1
  442.7 4.7 fusion.156
  447.5 3.0 convolution_convert_fusion.4
  459.0 4.3 pad_maximum_fusion
  468.5 8.1 multiply_reduce_fusion.12
  479.3 3.0 convolution_convert_fusion.11.refs_1_
  485.8 11.3 %attend_back_512.1 = bf16[512,2304]{1,0:T(8,128)(2,1)} custom-call(bf16[512,2304]{1,0:T(8,128)(2,1)} %convolution_convert_fusion.5.refs_0_, bf16[512,768]{1,0:T(8,128)(2,1)} %convolution_convert_fusion.11.refs_1_, bf16[512,768]{1,0:T(8,128)(2,1)} %get-tuple-element.308.refs_2_, f32[512,768]{1,0:T(8,128)} %get-tuple-element.354.refs_3_), custom_call_target="tpu_custom_call" | custom-call | flops 402653184 | bytes 393216 | tf_op jit(solution)/shard_map/attend_back_512/pallas_call | solution.py:269
  498.6 5.6 multiply_reduce_fusion.10
  516.2 7.7 multiply_reduce_fusion.4
  523.9 7.3 patch_grads.1
  531.1 2.8 fusion.165
  534.3 4.9 convolution_convert_fusion.7.refs_1_
  541.7 14.2 %collective-permute-done.17 = bf16[2,2,2,96,768]{4,3,2,1,0:T(8,128)(2,1)} collective-permute-done((bf16[2,2,2,96,768]{4,3,2,1,0:T(8,128)(2,1)S(1)}, bf16[2,2,2,96,768]{4,3,2,1,0:T(8,128)(2,1)}, u32[]{:S(2)}, u32[]{:S(2)}) %collective-permute-start.17) | collective-permute-done | bytes 1179680 | tf_op jit(solution)/shard_map/ppermute | solution.py:737
  563.9 2.9 broadcast_select_fusion.1
  581.2 34.9 %attend_back_1024.1 = bf16[1024,2304]{1,0:T(8,128)(2,1)} custom-call(bf16[1024,2304]{1,0:T(8,128)(2,1)} %convolution_convert_fusion.refs_0_, bf16[1024,768]{1,0:T(8,128)(2,1)} %convolution_convert_fusion.7.refs_1_, bf16[1024,768]{1,0:T(8,128)(2,1)} %get-tuple-element.296.refs_2_, f32[1024,768]{1,0:T(8,128)} %get-tuple-element.377.refs_3_), custom_call_target="tpu_custom_call" | custom-call | flops 1610612736 | bytes 786432 | tf_op jit(solution)/shard_map/attend_back_1024/pallas_call | solution.py:269
  623.5 5.6 bitcast_select_fusion.1
  631.1 5.4 convolution_convert_fusion.1
  636.5 29.4 %scatter_custom_fusion = f32[4096,768]{1,0:T(8,128)} fusion(s32[3072]{0:T(1024)} %min.25, bf16[3072,768]{1,0:T(8,128)(2,1)} %bitcast_select_fusion.1, f32[]{:T(128)} %constant.503.clone.1, pred[3072]{0:T(1024)(128)(4,1)S(1)} %copy-done.112), kind=kCustom, calls=%fused_computation.7 | custom fusion | flops 7077888 | bytes 17305600 | tf_op jit(solution)/shard_map/scatter-add | solution.py:1248
  665.9 2.8 constant_dynamic-slice_fusion.12
  680.1 8.0 multiply_reduce_fusion.1
  690.4 3.2 fusion.164
  694.5 8.2 collective-permute-done.24
  702.8 3.7 collective-permute-done.25
  716.7 12.5 %collective-permute-done.28 = bf16[2,24,1536]{2,1,0:T(8,128)(2,1)S(1)} collective-permute-done((bf16[2,24,1536]{2,1,0:T(8,128)(2,1)S(1)}, bf16[2,24,1536]{2,1,0:T(8,128)(2,1)S(1)}, u32[]{:S(2)}, u32[]{:S(2)}) %collective-permute-start.28) | collective-permute-done | bytes 147488 | tf_op jit(solution)/shard_map/ppermute | solution.py:737
  733.3 3.8 multiply_reduce_fusion
  737.9 3.7 collective-permute-done.35
  747.6 2.9 collective-permute-start.41
  750.5 10.4 %collective-permute-done.42 = bf16[2,2,2,24,128]{4,3,2,1,0:T(8,128)(2,1)S(1)} collective-permute-done((bf16[2,2,2,24,128]{4,3,2,1,0:T(8,128)(2,1)S(1)}, bf16[2,2,2,24,128]{4,3,2,1,0:T(8,128)(2,1)S(1)}, u32[]{:S(2)}, u32[]{:S(2)}) %collective-permute-start.42) | collective-permute-done | bytes 49184 | tf_op jit(solution)/shard_map/ppermute | solution.py:735
  779.1 3.1 convert_add_fusion.9
  788.8 3.1 convert_add_fusion.8
  800.0 17.5 %everyone_2.1 = bf16[32,64,128]{2,1,0:T(8,128)(2,1)} custom-call(bf16[64,128]{1,0:T(8,128)(2,1)} %pad_maximum_fusion.14.x_ref), custom_call_target="tpu_custom_call" | custom-call | tf_op jit(solution)/shard_map/everyone_2/pallas_call | solution.py:127
  825.4 5.3 multiply_subtract_fusion.1
  830.8 30.0 %multiply_subtract_fusion = (f32[4096,768]{1,0:T(8,128)}, f32[4096,768]{1,0:T(8,128)}, f32[4096,768]{1,0:T(8,128)}) fusion(f32[4096,768]{1,0:T(8,128)} %param.46, f32[4096,768]{1,0:T(8,128)} %param.47, f32[4096,768]{1,0:T(8,128)} %param.48, f32[4096,768]{1,0:T(8,128)} %scatter_custom_fusion, f32[]{:T(128)} %div.349), kind=kLoop, calls=%fused_computation.4 | loop fusion | flops 50331648 | bytes 88080384 | tf_op jit(solution)/shard_map/sub | solution.py:68
  863.5 11.8 %adam_mixing.1 = (f32[3,48,6144]{2,1,0:T(8,128)}, f32[3,48,6144]{2,1,0:T(8,128)}, f32[3,48,6144]{2,1,0:T(8,128)}) custom-call(f32[1]{0:T(128)} %bitcast.95.scal_ref, s32[1]{0:T(128)} %bitcast.96.core_ref, f32[48,6144]{1,0:T(8,128)} %get-tuple-element.573.refs_0_, f32[48,6144]{1,0:T(8,128)} %get-tuple-element.571.refs_1_, ...), custom_call_target="tpu_custom_call" | custom-call | tf_op jit(solution)/shard_map/adam_mixing/pallas_call | solution.py:361
  (747 shorter events, 233.4 us)
Async XLA Ops:
  7.2 112.7 %copy-start = (bf16[1,1024,128]{2,1,0:T(8,128)(2,1)S(1)}, bf16[1,1024,128]{2,1,0:T(8,128)(2,1)}, u32[]{:S(2)}) copy-start(bf16[1,1024,128]{2,1,0:T(8,128)(2,1)} %param.29) | copy-start | bytes 786436
  7.2 126.9 %all-gather.12.cloned.1.call-start = ((), (), s32[]{:S(2)}) async-start(), calls=%async_computation.7 | async-start | bytes 10027008 | tf_op jit(solution)/shard_map/all_gather | solution.py:958
  14.1 203.8 %all-gather.6.cloned.1.call-start = ((), (), s32[]{:S(2)}) async-start(), calls=%async_computation.2 | async-start | bytes 10027008 | tf_op jit(solution)/shard_map/all_gather | solution.py:958
  14.3 22.2 %collective-permute-start = (bf16[200,384]{1,0:T(8,128)(2,1)S(1)}, bf16[200,384]{1,0:T(8,128)(2,1)S(1)}, u32[]{:S(2)}, u32[]{:S(2)}) collective-permute-start(bf16[200,384]{1,0:T(8,128)(2,1)S(1)} %constant_dynamic-slice_fusion.28), channel_id=1, source_target_pairs={{0,4},{1,5},{2,6},{3,7},{4,0},{5,1},{6,2},{7,3},{8,12},{9,13},{10,... | collective-permute-start | bytes 460808 | tf_op jit(solution)/shard_map/ppermute | solution.py:737
  17.4 19.2 %collective-permute-start.1 = (bf16[128,768]{1,0:T(8,128)(2,1)S(1)}, bf16[128,768]{1,0:T(8,128)(2,1)}, u32[]{:S(2)}, u32[]{:S(2)}) collective-permute-start(bf16[128,768]{1,0:T(8,128)(2,1)S(1)} %slice.319), channel_id=1, source_target_pairs={{0,1},{1,0},{2,3},{3,2},{4,5},{5,4},{6,7},{7,6},{8,9},{9,8},{10,11... | collective-permute-start | bytes 589832 | tf_op jit(solution)/shard_map/ppermute | solution.py:737
  36.5 99.9 %copy-start.127 = (pred[2]{0:T(512)(128)(4,1)}, pred[2]{0:T(512)(128)(4,1)S(1)}, u32[]{:S(2)}) copy-start(pred[2]{0:T(512)(128)(4,1)S(1)} %iota_compare_fusion.11) | copy-start | bytes 10
  38.6 14.8 %collective-permute-start.3 = (bf16[128,768]{1,0:T(8,128)(2,1)}, bf16[128,768]{1,0:T(8,128)(2,1)}, u32[]{:S(2)}, u32[]{:S(2)}) collective-permute-start(bf16[128,768]{1,0:T(8,128)(2,1)} %broadcast_select_fusion.13), channel_id=1, source_target_pairs={{0,2},{1,3},{2,0},{3,1},{4,6},{5,7},{6,4},{7,5},{8,10},{9,11},{10,... | collective-permute-start | bytes 589832 | tf_op jit(solution)/shard_map/ppermute | solution.py:737
  40.5 23.6 %collective-permute-start.2 = (bf16[2,200,384]{2,1,0:T(8,128)(2,1)S(1)}, bf16[2,200,384]{2,1,0:T(8,128)(2,1)S(1)}, u32[]{:S(2)}, u32[]{:S(2)}) collective-permute-start(bf16[2,200,384]{2,1,0:T(8,128)(2,1)S(1)} %broadcast_select_fusion.7), channel_id=1, source_target_pairs={{0,8},{1,9},{2,10},{3,11},{4,12},{5,13},{6,14},{7,15},{8,0},{9,1},... | collective-permute-start | bytes 921608 | tf_op jit(solution)/shard_map/ppermute | solution.py:737
  68.1 23.1 %collective-permute-start.6 = (bf16[2,2,2,96,768]{4,3,1,0,2:T(8,128)(2,1)}, bf16[2,2,2,96,768]{4,3,1,0,2:T(8,128)(2,1)S(1)}, u32[]{:S(2)}, u32[]{:S(2)}) collective-permute-start(bf16[2,2,2,96,768]{4,3,1,0,2:T(8,128)(2,1)} %bitcast.304), channel_id=1, source_target_pairs={{0,1},{1,0},{2,3},{3,2},{4,5},{5,4},{6,7},{7,6},{8,9},{9,8},{10,11... | collective-permute-start | bytes 3538952 | tf_op jit(solution)/shard_map/ppermute | solution.py:737
  70.9 20.3 %collective-permute-start.5 = (bf16[128,768]{1,0:T(8,128)(2,1)}, bf16[128,768]{1,0:T(8,128)(2,1)}, u32[]{:S(2)}, u32[]{:S(2)}) collective-permute-start(bf16[128,768]{1,0:T(8,128)(2,1)} %broadcast_select_fusion.12), channel_id=1, source_target_pairs={{0,4},{1,5},{2,6},{3,7},{4,0},{5,1},{6,2},{7,3},{8,12},{9,13},{10,... | collective-permute-start | bytes 589832 | tf_op jit(solution)/shard_map/ppermute | solution.py:737
  72.4 18.7 %collective-permute-start.4 = (bf16[2,2,200,384]{3,2,1,0:T(8,128)(2,1)}, bf16[2,2,200,384]{3,2,1,0:T(8,128)(2,1)S(1)}, u32[]{:S(2)}, u32[]{:S(2)}) collective-permute-start(bf16[2,2,200,384]{3,2,1,0:T(8,128)(2,1)} %broadcast_select_fusion.3), channel_id=1, source_target_pairs={{0,16},{16,0},{1,17},{17,1},{2,18},{18,2},{3,19},{19,3},{4,20},{20... | collective-permute-start | bytes 1843208 | tf_op jit(solution)/shard_map/ppermute | solution.py:735
  94.8 23.7 %collective-permute-start.8 = (bf16[2,2,96,768]{3,2,1,0:T(8,128)(2,1)S(1)}, bf16[2,2,96,768]{3,2,1,0:T(8,128)(2,1)}, u32[]{:S(2)}, u32[]{:S(2)}) collective-permute-start(bf16[2,2,96,768]{3,2,1,0:T(8,128)(2,1)S(1)} %dynamic-slice_bitcast_fusion.4), channel_id=1, source_target_pairs={{0,2},{1,3},{2,0},{3,1},{4,6},{5,7},{6,4},{7,5},{8,10},{9,11},{10,... | collective-permute-start | bytes 1769480 | tf_op jit(solution)/shard_map/ppermute | solution.py:737
  96.7 21.8 %collective-permute-start.7 = (bf16[128,768]{1,0:T(8,128)(2,1)S(1)}, bf16[128,768]{1,0:T(8,128)(2,1)S(1)}, u32[]{:S(2)}, u32[]{:S(2)}) collective-permute-start(bf16[128,768]{1,0:T(8,128)(2,1)S(1)} %broadcast_select_fusion.11), channel_id=1, source_target_pairs={{0,8},{1,9},{2,10},{3,11},{4,12},{5,13},{6,14},{7,15},{8,0},{9,1},... | collective-permute-start | bytes 589832 | tf_op jit(solution)/shard_map/ppermute | solution.py:737
  119.8 14.3 %collective-permute-start.9 = (bf16[2,96,768]{2,1,0:T(8,128)(2,1)S(1)}, bf16[2,96,768]{2,1,0:T(8,128)(2,1)}, u32[]{:S(2)}, u32[]{:S(2)}) collective-permute-start(bf16[2,96,768]{2,1,0:T(8,128)(2,1)S(1)} %dynamic-slice_bitcast_fusion.9), channel_id=1, source_target_pairs={{0,8},{1,9},{2,10},{3,11},{4,12},{5,13},{6,14},{7,15},{8,0},{9,1},... | collective-permute-start | bytes 884744 | tf_op jit(solution)/shard_map/ppermute | solution.py:737
  134.1 169.0 %all-gather.8.cloned.1.call-start = ((), (), s32[]{:S(2)}) async-start(), calls=%async_computation.3 | async-start | bytes 10027008 | tf_op jit(solution)/shard_map/all_gather | solution.py:958
  134.9 211.4 %all-gather.10.cloned.1.call-start = ((), (), s32[]{:S(2)}) async-start(), calls=%async_computation.4 | async-start | bytes 2506752 | tf_op jit(solution)/shard_map/all_gather | solution.py:958
  141.6 37.6 %collective-permute-start.10 = (bf16[2,2,200,768]{3,2,1,0:T(8,128)(2,1)}, bf16[2,2,200,768]{3,2,1,0:T(8,128)(2,1)S(1)}, u32[]{:S(2)}, u32[]{:S(2)}) collective-permute-start(bf16[2,2,200,768]{3,2,1,0:T(8,128)(2,1)} %pad_maximum_fusion.6), channel_id=1, source_target_pairs={{0,2},{1,3},{2,0},{3,1},{4,6},{5,7},{6,4},{7,5},{8,10},{9,11},{10,... | collective-permute-start | bytes 3686408 | tf_op jit(solution)/shard_map/ppermute | solution.py:737
  144.3 31.2 %collective-permute-start.11 = (bf16[96,768]{1,0:T(8,128)(2,1)S(1)}, bf16[96,768]{1,0:T(8,128)(2,1)S(1)}, u32[]{:S(2)}, u32[]{:S(2)}) collective-permute-start(bf16[96,768]{1,0:T(8,128)(2,1)S(1)} %dynamic-slice_bitcast_fusion.14), channel_id=1, source_target_pairs={{0,4},{1,5},{2,6},{3,7},{4,0},{5,1},{6,2},{7,3},{8,12},{9,13},{10,... | collective-permute-start | bytes 442376 | tf_op jit(solution)/shard_map/ppermute | solution.py:737
  180.9 28.8 %collective-permute-start.12 = (bf16[2,2,2,200,768]{4,3,2,1,0:T(8,128)(2,1)}, bf16[2,2,2,200,768]{4,3,2,1,0:T(8,128)(2,1)}, u32[]{:S(2)}, u32[]{:S(2)}) collective-permute-start(bf16[2,2,2,200,768]{4,3,2,1,0:T(8,128)(2,1)} %broadcast_select_fusion), channel_id=1, source_target_pairs={{0,1},{1,0},{2,3},{3,2},{4,5},{5,4},{6,7},{7,6},{8,9},{9,8},{10,11... | collective-permute-start | bytes 7372808 | tf_op jit(solution)/shard_map/ppermute | solution.py:737
  303.1 440.2 %reduce-scatter.3.cloned.1.call-start = ((), (), s32[]{:S(2)}) async-start(), calls=%async_computation.5 | async-start | bytes 10027008 | tf_op jit(solution)/shard_map/reduce_scatter | solution.py:1166
  450.5 324.8 %reduce-scatter.5.cloned.1.call-start = ((), (), s32[]{:S(2)}) async-start(), calls=%async_computation.6 | async-start | bytes 10027008 | tf_op jit(solution)/shard_map/reduce_scatter | solution.py:1224
  463.3 19.7 %collective-permute-start.13 = (bf16[96,768]{1,0:T(8,128)(2,1)S(1)}, bf16[96,768]{1,0:T(8,128)(2,1)S(1)}, u32[]{:S(2)}, u32[]{:S(2)}) collective-permute-start(bf16[96,768]{1,0:T(8,128)(2,1)S(1)} %copy-done.58), channel_id=1, source_target_pairs={{0,4},{1,5},{2,6},{3,7},{4,0},{5,1},{6,2},{7,3},{8,12},{9,13},{10,... | collective-permute-start | bytes 442376 | tf_op jit(solution)/shard_map/ppermute | solution.py:737
  464.6 18.5 %collective-permute-start.14 = (bf16[96,768]{1,0:T(8,128)(2,1)S(1)}, bf16[96,768]{1,0:T(8,128)(2,1)S(1)}, u32[]{:S(2)}, u32[]{:S(2)}) collective-permute-start(bf16[96,768]{1,0:T(8,128)(2,1)S(1)} %copy-done.58), channel_id=1, source_target_pairs={{0,8},{1,9},{2,10},{3,11},{4,12},{5,13},{6,14},{7,15},{8,0},{9,1},... | collective-permute-start | bytes 442376 | tf_op jit(solution)/shard_map/ppermute | solution.py:737
  465.1 18.0 %collective-permute-start.15 = (bf16[96,768]{1,0:T(8,128)(2,1)S(1)}, bf16[96,768]{1,0:T(8,128)(2,1)S(1)}, u32[]{:S(2)}, u32[]{:S(2)}) collective-permute-start(bf16[96,768]{1,0:T(8,128)(2,1)S(1)} %copy-done.58), channel_id=1, source_target_pairs={{0,12},{1,13},{2,14},{3,15},{4,8},{5,9},{6,10},{7,11},{8,4},{9,5},... | collective-permute-start | bytes 442376 | tf_op jit(solution)/shard_map/ppermute | solution.py:737
  484.1 28.7 %collective-permute-start.16 = (bf16[2,2,96,768]{3,2,1,0:T(8,128)(2,1)}, bf16[2,2,96,768]{3,2,1,0:T(8,128)(2,1)}, u32[]{:S(2)}, u32[]{:S(2)}) collective-permute-start(bf16[2,2,96,768]{3,2,1,0:T(8,128)(2,1)} %broadcast_select_fusion.6), channel_id=1, source_target_pairs={{0,16},{16,0},{1,17},{17,1},{2,18},{18,2},{3,19},{19,3},{4,20},{20... | collective-permute-start | bytes 1769480 | tf_op jit(solution)/shard_map/ppermute | solution.py:735
  514.9 41.0 %collective-permute-start.17 = (bf16[2,2,2,96,768]{4,3,2,1,0:T(8,128)(2,1)S(1)}, bf16[2,2,2,96,768]{4,3,2,1,0:T(8,128)(2,1)}, u32[]{:S(2)}, u32[]{:S(2)}) collective-permute-start(bf16[2,2,2,96,768]{4,3,2,1,0:T(8,128)(2,1)S(1)} %broadcast_select_fusion.2), channel_id=1, source_target_pairs={{0,2},{1,3},{2,0},{3,1},{4,6},{5,7},{6,4},{7,5},{8,10},{9,11},{10,... | collective-permute-start | bytes 3538952 | tf_op jit(solution)/shard_map/ppermute | solution.py:737
  516.1 39.9 %collective-permute-start.18 = (bf16[768,1536]{1,0:T(8,128)(2,1)}, bf16[768,1536]{1,0:T(8,128)(2,1)}, u32[]{:S(2)}, u32[]{:S(2)}) collective-permute-start(bf16[768,1536]{1,0:T(8,128)(2,1)} %pad_maximum_fusion.2), channel_id=1, source_target_pairs={{0,1},{1,0},{2,3},{3,2},{4,5},{5,4},{6,7},{7,6},{8,9},{9,8},{10,11... | collective-permute-start | bytes 7077896 | tf_op jit(solution)/shard_map/ppermute | solution.py:737
  566.9 49.3 %collective-permute-start.19 = (bf16[2,2,2,2,96,768]{5,4,3,2,1,0:T(8,128)(2,1)}, bf16[2,2,2,2,96,768]{5,4,3,2,1,0:T(8,128)(2,1)}, u32[]{:S(2)}, u32[]{:S(2)}) collective-permute-start(bf16[2,2,2,2,96,768]{5,4,3,2,1,0:T(8,128)(2,1)} %broadcast_select_fusion.1), channel_id=1, source_target_pairs={{0,1},{1,0},{2,3},{3,2},{4,5},{5,4},{6,7},{7,6},{8,9},{9,8},{10,11... | collective-permute-start | bytes 7077896 | tf_op jit(solution)/shard_map/ppermute | solution.py:737
  566.9 49.2 %collective-permute-start.21 = (bf16[2,2,2,200,768]{4,3,1,0,2:T(8,128)(2,1)}, bf16[2,2,2,200,768]{4,3,1,0,2:T(8,128)(2,1)}, u32[]{:S(2)}, u32[]{:S(2)}) collective-permute-start(bf16[2,2,2,200,768]{4,3,1,0,2:T(8,128)(2,1)} %bitcast.303), channel_id=1, source_target_pairs={{0,1},{1,0},{2,3},{3,2},{4,5},{5,4},{6,7},{7,6},{8,9},{9,8},{10,11... | collective-permute-start | bytes 7372808 | tf_op jit(solution)/shard_map/ppermute | solution.py:737
  574.0 42.2 %collective-permute-start.20 = (bf16[2,2,2,2,24,1536]{5,4,3,2,1,0:T(8,128)(2,1)}, bf16[2,2,2,2,24,1536]{5,4,3,2,1,0:T(8,128)(2,1)S(1)}, u32[]{:S(2)}, u32[]{:S(2)}) collective-permute-start(bf16[2,2,2,2,24,1536]{5,4,3,2,1,0:T(8,128)(2,1)} %dynamic-slice_bitcast_fusion), channel_id=1, source_target_pairs={{0,16},{16,0},{1,17},{17,1},{2,18},{18,2},{3,19},{19,3},{4,20},{20... | collective-permute-start | bytes 3538952 | tf_op jit(solution)/shard_map/ppermute | solution.py:735
  581.2 35.0 %copy-start.16 = (bf16[768,1536]{1,0:T(8,128)(2,1)S(1)}, bf16[768,1536]{1,0:T(8,128)(2,1)}, u32[]{:S(2)}) copy-start(bf16[768,1536]{1,0:T(8,128)(2,1)} %copy-done.15) | copy-start | bytes 7077892
  629.1 42.2 %collective-permute-start.22 = (bf16[2,2,2,24,1536]{4,3,2,1,0:T(8,128)(2,1)}, bf16[2,2,2,24,1536]{4,3,2,1,0:T(8,128)(2,1)}, u32[]{:S(2)}, u32[]{:S(2)}) collective-permute-start(bf16[2,2,2,24,1536]{4,3,2,1,0:T(8,128)(2,1)} %dynamic-slice_bitcast_fusion.3), channel_id=1, source_target_pairs={{0,2},{1,3},{2,0},{3,1},{4,6},{5,7},{6,4},{7,5},{8,10},{9,11},{10,... | collective-permute-start | bytes 1769480 | tf_op jit(solution)/shard_map/ppermute | solution.py:737
  630.3 41.0 %collective-permute-start.23 = (bf16[2,2,2,200,384]{4,3,1,0,2:T(8,128)(2,1)}, bf16[2,2,2,200,384]{4,3,1,0,2:T(8,128)(2,1)}, u32[]{:S(2)}, u32[]{:S(2)}) collective-permute-start(bf16[2,2,2,200,384]{4,3,1,0,2:T(8,128)(2,1)} %constant_dynamic-slice_fusion.15), channel_id=1, source_target_pairs={{0,16},{16,0},{1,17},{17,1},{2,18},{18,2},{3,19},{19,3},{4,20},{20... | collective-permute-start | bytes 3686408 | tf_op jit(solution)/shard_map/ppermute | solution.py:735
  679.6 26.8 %collective-permute-start.26 = (bf16[768,768]{1,0:T(8,128)(2,1)}, bf16[768,768]{1,0:T(8,128)(2,1)}, u32[]{:S(2)}, u32[]{:S(2)}) collective-permute-start(bf16[768,768]{1,0:T(8,128)(2,1)} %get-tuple-element.395), channel_id=1, source_target_pairs={{0,1},{1,0},{2,3},{3,2},{4,5},{5,4},{6,7},{7,6},{8,9},{9,8},{10,11... | collective-permute-start | bytes 3538952 | tf_op jit(solution)/shard_map/ppermute | solution.py:737
  679.6 26.8 %collective-permute-start.27 = (bf16[768,768]{1,0:T(8,128)(2,1)}, bf16[768,768]{1,0:T(8,128)(2,1)}, u32[]{:S(2)}, u32[]{:S(2)}) collective-permute-start(bf16[768,768]{1,0:T(8,128)(2,1)} %get-tuple-element.396), channel_id=1, source_target_pairs={{0,1},{1,0},{2,3},{3,2},{4,5},{5,4},{6,7},{7,6},{8,9},{9,8},{10,11... | collective-permute-start | bytes 3538952 | tf_op jit(solution)/shard_map/ppermute | solution.py:737
  690.4 12.4 %collective-permute-start.24 = (bf16[2,2,24,1536]{3,2,1,0:T(8,128)(2,1)}, bf16[2,2,24,1536]{3,2,1,0:T(8,128)(2,1)S(1)}, u32[]{:S(2)}, u32[]{:S(2)}) collective-permute-start(bf16[2,2,24,1536]{3,2,1,0:T(8,128)(2,1)} %dynamic-slice_bitcast_fusion.8), channel_id=1, source_target_pairs={{0,8},{1,9},{2,10},{3,11},{4,12},{5,13},{6,14},{7,15},{8,0},{9,1},... | collective-permute-start | bytes 884744 | tf_op jit(solution)/shard_map/ppermute | solution.py:737
  690.4 16.1 %collective-permute-start.25 = (bf16[2,2,200,384]{3,2,1,0:T(8,128)(2,1)}, bf16[2,2,200,384]{3,2,1,0:T(8,128)(2,1)S(1)}, u32[]{:S(2)}, u32[]{:S(2)}) collective-permute-start(bf16[2,2,200,384]{3,2,1,0:T(8,128)(2,1)} %dynamic-slice_bitcast_fusion.1), channel_id=1, source_target_pairs={{0,2},{1,3},{2,0},{3,1},{4,6},{5,7},{6,4},{7,5},{8,10},{9,11},{10,... | collective-permute-start | bytes 1843208 | tf_op jit(solution)/shard_map/ppermute | solution.py:737
  710.5 18.8 %collective-permute-start.30 = (bf16[2,2,2,2,24,768]{5,4,3,1,0,2:T(8,128)(2,1)S(1)}, bf16[2,2,2,2,24,768]{5,4,3,1,0,2:T(8,128)(2,1)S(1)}, u32[]{:S(2)}, u32[]{:S(2)}) collective-permute-start(bf16[2,2,2,2,24,768]{5,4,3,1,0,2:T(8,128)(2,1)S(1)} %bitcast.349), channel_id=1, source_target_pairs={{0,16},{16,0},{1,17},{17,1},{2,18},{18,2},{3,19},{19,3},{4,20},{20... | collective-permute-start | bytes 1769480 | tf_op jit(solution)/shard_map/ppermute | solution.py:735
  711.5 17.8 %collective-permute-start.31 = (bf16[2,2,2,2,24,768]{5,4,3,2,1,0:T(8,128)(2,1)S(1)}, bf16[2,2,2,2,24,768]{5,4,3,2,1,0:T(8,128)(2,1)S(1)}, u32[]{:S(2)}, u32[]{:S(2)}) collective-permute-start(bf16[2,2,2,2,24,768]{5,4,3,2,1,0:T(8,128)(2,1)S(1)} %dynamic-slice_bitcast_fusion.2), channel_id=1, source_target_pairs={{0,2},{1,3},{2,0},{3,1},{4,6},{5,7},{6,4},{7,5},{8,10},{9,11},{10,... | collective-permute-start | bytes 1769480 | tf_op jit(solution)/shard_map/ppermute | solution.py:737
  712.8 16.5 %collective-permute-start.29 = (bf16[2,200,384]{2,1,0:T(8,128)(2,1)S(1)}, bf16[2,200,384]{2,1,0:T(8,128)(2,1)S(1)}, u32[]{:S(2)}, u32[]{:S(2)}) collective-permute-start(bf16[2,200,384]{2,1,0:T(8,128)(2,1)S(1)} %dynamic-slice_bitcast_fusion.5), channel_id=1, source_target_pairs={{0,8},{1,9},{2,10},{3,11},{4,12},{5,13},{6,14},{7,15},{8,0},{9,1},... | collective-permute-start | bytes 921608 | tf_op jit(solution)/shard_map/ppermute | solution.py:737
  716.0 13.3 %collective-permute-start.32 = (bf16[768,128]{1,0:T(8,128)(2,1)S(1)}, bf16[768,128]{1,0:T(8,128)(2,1)S(1)}, u32[]{:S(2)}, u32[]{:S(2)}) collective-permute-start(bf16[768,128]{1,0:T(8,128)(2,1)S(1)} %get-tuple-element.420), channel_id=1, source_target_pairs={{0,1},{1,0},{2,3},{3,2},{4,5},{5,4},{6,7},{7,6},{8,9},{9,8},{10,11... | collective-permute-start | bytes 589832 | tf_op jit(solution)/shard_map/ppermute | solution.py:737
  716.5 12.7 %collective-permute-start.28 = (bf16[2,24,1536]{2,1,0:T(8,128)(2,1)S(1)}, bf16[2,24,1536]{2,1,0:T(8,128)(2,1)S(1)}, u32[]{:S(2)}, u32[]{:S(2)}) collective-permute-start(bf16[2,24,1536]{2,1,0:T(8,128)(2,1)S(1)} %dynamic-slice_bitcast_fusion.13), channel_id=1, source_target_pairs={{0,4},{1,5},{2,6},{3,7},{4,0},{5,1},{6,2},{7,3},{8,12},{9,13},{10,... | collective-permute-start | bytes 442376 | tf_op jit(solution)/shard_map/ppermute | solution.py:737
  730.0 7.1 collective-permute-start.33
  730.1 7.1 collective-permute-start.37
  731.9 6.1 collective-permute-start.34
  731.9 9.7 %collective-permute-start.35 = (bf16[2,2,2,24,768]{4,3,2,1,0:T(8,128)(2,1)S(1)}, bf16[2,2,2,24,768]{4,3,2,1,0:T(8,128)(2,1)S(1)}, u32[]{:S(2)}, u32[]{:S(2)}) collective-permute-start(bf16[2,2,2,24,768]{4,3,2,1,0:T(8,128)(2,1)S(1)} %dynamic-slice_bitcast_fusion.7), channel_id=1, source_target_pairs={{0,2},{1,3},{2,0},{3,1},{4,6},{5,7},{6,4},{7,5},{8,10},{9,11},{10,... | collective-permute-start | bytes 884744 | tf_op jit(solution)/shard_map/ppermute | solution.py:737
  732.2 9.4 %collective-permute-start.36 = (bf16[2,2,2,24,768]{4,3,2,1,0:T(8,128)(2,1)S(1)}, bf16[2,2,2,24,768]{4,3,2,1,0:T(8,128)(2,1)S(1)}, u32[]{:S(2)}, u32[]{:S(2)}) collective-permute-start(bf16[2,2,2,24,768]{4,3,2,1,0:T(8,128)(2,1)S(1)} %dynamic-slice_bitcast_fusion.6), channel_id=1, source_target_pairs={{0,16},{16,0},{1,17},{17,1},{2,18},{18,2},{3,19},{19,3},{4,20},{20... | collective-permute-start | bytes 884744 | tf_op jit(solution)/shard_map/ppermute | solution.py:735
  743.3 22.9 %collective-permute-start.43 = (bf16[48,6144]{1,0:T(8,128)(2,1)}, bf16[48,6144]{1,0:T(8,128)(2,1)}, u32[]{:S(2)}, u32[]{:S(2)}) collective-permute-start(bf16[48,6144]{1,0:T(8,128)(2,1)} %reduce-scatter.3.cloned.1.call-done), channel_id=1, source_target_pairs={{0,16},{16,0},{1,17},{17,1},{2,18},{18,2},{3,19},{19,3},{4,20},{20... | collective-permute-start | bytes 1769480 | tf_op jit(solution)/shard_map/ppermute | solution.py:735
  744.5 16.4 %collective-permute-start.42 = (bf16[2,2,2,24,128]{4,3,2,1,0:T(8,128)(2,1)S(1)}, bf16[2,2,2,24,128]{4,3,2,1,0:T(8,128)(2,1)S(1)}, u32[]{:S(2)}, u32[]{:S(2)}) collective-permute-start(bf16[2,2,2,24,128]{4,3,2,1,0:T(8,128)(2,1)S(1)} %dynamic-slice_bitcast_fusion.19), channel_id=1, source_target_pairs={{0,16},{16,0},{1,17},{17,1},{2,18},{18,2},{3,19},{19,3},{4,20},{20... | collective-permute-start | bytes 147464 | tf_op jit(solution)/shard_map/ppermute | solution.py:735
  746.5 18.8 %collective-permute-start.38 = (bf16[24,3072]{1,0:T(8,128)(2,1)S(1)}, bf16[24,3072]{1,0:T(8,128)(2,1)S(1)}, u32[]{:S(2)}, u32[]{:S(2)}) collective-permute-start(bf16[24,3072]{1,0:T(8,128)(2,1)S(1)} %pad_maximum_fusion.9), channel_id=1, source_target_pairs={{0,16},{16,0},{1,17},{17,1},{2,18},{18,2},{3,19},{19,3},{4,20},{20... | collective-permute-start | bytes 442376 | tf_op jit(solution)/shard_map/ppermute | solution.py:735
  747.6 17.7 %collective-permute-start.40 = (bf16[2,2,24,768]{3,2,1,0:T(8,128)(2,1)}, bf16[2,2,24,768]{3,2,1,0:T(8,128)(2,1)}, u32[]{:S(2)}, u32[]{:S(2)}) collective-permute-start(bf16[2,2,24,768]{3,2,1,0:T(8,128)(2,1)} %dynamic-slice_bitcast_fusion.12), channel_id=1, source_target_pairs={{0,8},{1,9},{2,10},{3,11},{4,12},{5,13},{6,14},{7,15},{8,0},{9,1},... | collective-permute-start | bytes 442376 | tf_op jit(solution)/shard_map/ppermute | solution.py:737
  747.6 17.7 %collective-permute-start.41 = (bf16[2,2,24,768]{3,2,1,0:T(8,128)(2,1)}, bf16[2,2,24,768]{3,2,1,0:T(8,128)(2,1)}, u32[]{:S(2)}, u32[]{:S(2)}) collective-permute-start(bf16[2,2,24,768]{3,2,1,0:T(8,128)(2,1)} %dynamic-slice_bitcast_fusion.11), channel_id=1, source_target_pairs={{0,8},{1,9},{2,10},{3,11},{4,12},{5,13},{6,14},{7,15},{8,0},{9,1},... | collective-permute-start | bytes 442376 | tf_op jit(solution)/shard_map/ppermute | solution.py:737
  760.9 5.3 collective-permute-start.39
  768.8 5.0 collective-permute-start.46
  768.9 4.9 collective-permute-start.44
  770.1 4.5 collective-permute-start.45
  775.3 12.3 %collective-permute-start.49 = (bf16[48,6144]{1,0:T(8,128)(2,1)}, bf16[48,6144]{1,0:T(8,128)(2,1)}, u32[]{:S(2)}, u32[]{:S(2)}) collective-permute-start(bf16[48,6144]{1,0:T(8,128)(2,1)} %reduce-scatter.5.cloned.1.call-done), channel_id=1, source_target_pairs={{0,16},{16,0},{1,17},{17,1},{2,18},{18,2},{3,19},{19,3},{4,20},{20... | collective-permute-start | bytes 1769480 | tf_op jit(solution)/shard_map/ppermute | solution.py:735
  782.2 5.4 collective-permute-start.48
  783.8 3.8 collective-permute-start.47
  787.6 6.2 collective-permute-start.50
  830.8 30.8 %copy-start.56 = (f32[200,768]{1,0:T(8,128)S(1)}, f32[200,768]{1,0:T(8,128)}, u32[]{:S(2)}) copy-start(f32[200,768]{1,0:T(8,128)} %param.43) | copy-start | bytes 1843204
  830.8 30.8 %copy-start.62 = (bf16[1,8,2,2,24,128]{5,4,3,2,1,0:T(8,128)(2,1)S(1)}, bf16[1,8,2,2,24,128]{5,4,3,2,1,0:T(8,128)(2,1)}, u32[]{:S(2)}) copy-start(bf16[1,8,2,2,24,128]{5,4,3,2,1,0:T(8,128)(2,1)} %slice.340) | copy-start | bytes 589828
  830.8 30.7 %copy-start.156 = (f32[200,768]{1,0:T(8,128)S(1)}, f32[200,768]{1,0:T(8,128)}, u32[]{:S(2)}) copy-start(f32[200,768]{1,0:T(8,128)} %param.44) | copy-start | bytes 1843204
  830.8 30.7 %copy-start.157 = (f32[200,768]{1,0:T(8,128)S(1)}, f32[200,768]{1,0:T(8,128)}, u32[]{:S(2)}) copy-start(f32[200,768]{1,0:T(8,128)} %param.45) | copy-start | bytes 1843204
  (167 other events, 1107.3 us)
Sparse Core Ops, SparseCore 0:
  14.2 106.7 all-gather.11
  134.3 83.6 all-gather.5
  220.8 82.2 all-gather.7
  305.8 40.4 all-gather.9
  450.6 122.5 reduce-scatter.2
  578.2 111.1 reduce-scatter.4

commit v4 on v3

--- a/solution.py
+++ b/solution.py
@@ -253,25 +253,37 @@
     g_ref[:, 256:384] = dv_ref[...].astype(BF16)
 
 
-def attend_back(qkv, grad_out, out, totals, bias, block):
+def attend_back(qkv, grad_out, out, totals, bias, block, begin=0, end=None, buffer=None):
     rows, width = qkv.shape
-    pairs = width // 384
+    pairs = (width // 384 if end is None else end) - begin
     specs = [
-        pl.BlockSpec((rows, 384), lambda j: (0, j)),
-        pl.BlockSpec((rows, 128), lambda j: (0, j)),
-        pl.BlockSpec((rows, 128), lambda j: (0, j)),
-        pl.BlockSpec((rows, 128), lambda j: (0, j)),
+        pl.BlockSpec((rows, 384), lambda j: (0, begin + j)),
+        pl.BlockSpec((rows, 128), lambda j: (0, begin + j)),
+        pl.BlockSpec((rows, 128), lambda j: (0, begin + j)),
+        pl.BlockSpec((rows, 128), lambda j: (0, begin + j)),
     ]
     args = [qkv, grad_out, out, totals]
     if bias is not None:
         specs.append(pl.BlockSpec(bias.shape, lambda j: (0, 0)))
         args.append(bias)
+    kernel = functools.partial(attend_back_kernel, rows, block, bias is not None)
+    aliases = {}
+    if buffer is not None:
+        aliases = {len(args): 0}
+        specs.append(pl.BlockSpec(memory_space=pl.ANY))
+        at = len(args)
+        args.append(buffer)
+        inner = kernel
+
+        def kernel(*refs):
+            return inner(*refs[:at], *refs[at + 1 :])
+
     return pl.pallas_call(
-        functools.partial(attend_back_kernel, rows, block, bias is not None),
+        kernel,
         grid=(pairs,),
         out_shape=jax.ShapeDtypeStruct(qkv.shape, BF16),
         in_specs=specs,
-        out_specs=pl.BlockSpec((rows, 384), lambda j: (0, j)),
+        out_specs=pl.BlockSpec((rows, 384), lambda j: (0, begin + j)),
         scratch_shapes=[pltpu.VMEM((rows, 128), F32), pltpu.VMEM((rows, 128), F32)],
         compiler_params=pltpu.CompilerParams(vmem_limit_bytes=VMEM_LIMIT),
         cost_estimate=pl.CostEstimate(
@@ -279,7 +291,8 @@
             bytes_accessed=rows * pairs * 128,
             transcendentals=0,
         ),
-        name=f"attend_back_{rows}",
+        input_output_aliases=aliases,
+        name=f"attend_back_{rows}_{begin}",
     )(*args)
 
 
@@ -293,23 +306,22 @@
 
 
 def gradient_runs(features, width):
-    half = features // 2
     upper = width - 4 * features
     runs = column_runs(features, width)[:-1]
     towers = []
-    for piece, upper_at in ((2, upper), (3, 0)):
-        tower = []
-        for begin, at, size in runs:
-            side, local = divmod(at, 3 * half)
-            spots = [4 * half * (side ^ core) + local for core in range(2)]
-            tower.append((piece, *spots, begin, size))
-        for side in range(2):
-            spots = [4 * half * (side ^ core) + 3 * half for core in range(2)]
-            tower.append((piece, *spots, 3 * features + side * half, half))
-        tower.append((0, upper_at, upper_at, 4 * features, upper))
-        towers.append(tower)
-    tower = [(1, at, at, begin, size) for begin, at, size in runs]
-    tower.append((1, 3 * features, 3 * features, 3 * features, width - 3 * features))
+    half = features // 2
+    tower = [(1, width + at, begin, size) for begin, at, size in runs]
+    tower.append((1, width + 3 * features, 3 * features, features))
+    tower.append((0, upper, 4 * features, upper))
+    towers.append(tower)
+    tower = [(2, at + at // (3 * half) * half, begin, size) for begin, at, size in runs]
+    for side in range(2):
+        spot = (4 * side + 3) * half
+        tower.append((2, spot, 3 * features + side * half, half))
+    tower.append((0, 0, 4 * features, upper))
+    towers.append(tower)
+    tower = [(1, at, begin, size) for begin, at, size in runs]
+    tower.append((1, 3 * features, 3 * features, width - 3 * features))
     return towers + [tower]
 
 
@@ -332,43 +344,40 @@
     )(mixing)
 
 
-def adam_kernel(towers, scal_ref, core_ref, *refs):
-    pieces, (w_ref, first_ref, second_ref), outs = refs[:4], refs[4:7], refs[7:]
+def adam_kernel(towers, scal_ref, *refs):
+    pieces, (w_ref, first_ref, second_ref), outs = refs[:3], refs[3:6], refs[6:]
     factor = scal_ref[0]
     for tower, runs in enumerate(towers):
-        for core in range(2):
-
-            @pl.when((pl.program_id(0) == tower) & (core_ref[0] == core))
-            def _():
-                for run in runs:
-                    piece, begin, size = run[0], run[3], run[4]
-                    at = run[1 + core]
-                    new = adam_update(
-                        w_ref[0, :, begin : begin + size],
-                        first_ref[0, :, begin : begin + size],
-                        second_ref[0, :, begin : begin + size],
-                        pieces[piece][:, at : at + size] * factor,
-                        RATES[0],
-                    )
-                    for out, value in zip(outs, new):
-                        out[0, :, begin : begin + size] = value
-
-
-def adam_mixing(factor, core, pieces, master, first, second, features):
+
+        @pl.when(pl.program_id(1) == tower)
+        def _():
+            for piece, at, begin, size in runs:
+                new = adam_update(
+                    w_ref[0, :, begin : begin + size],
+                    first_ref[0, :, begin : begin + size],
+                    second_ref[0, :, begin : begin + size],
+                    pieces[piece][:, at : at + size] * factor,
+                    RATES[0],
+                )
+                for out, value in zip(outs, new):
+                    out[0, :, begin : begin + size] = value
+
+
+def adam_mixing(factor, pieces, master, first, second, features):
     towers, rows, width = master.shape
-    spec = pl.BlockSpec((1, rows, width), lambda t: (t, 0, 0))
-    scalar = pl.BlockSpec(memory_space=pltpu.SMEM)
+    block = rows // 3 if rows % 24 == 0 else rows
+    spec = pl.BlockSpec((1, block, width), lambda r, t: (t, r, 0))
     return pl.pallas_call(
         functools.partial(adam_kernel, gradient_runs(features, width)),
-        grid=(towers,),
+        grid=(rows // block, towers),
         out_shape=(jax.ShapeDtypeStruct(master.shape, F32),) * 3,
-        in_specs=[scalar, scalar]
-        + [pl.BlockSpec(piece.shape, lambda t: (0, 0)) for piece in pieces]
+        in_specs=[pl.BlockSpec(memory_space=pltpu.SMEM)]
+        + [pl.BlockSpec((block, piece.shape[1]), lambda r, t: (r, 0)) for piece in pieces]
         + [spec] * 3,
         out_specs=(spec,) * 3,
         compiler_params=pltpu.CompilerParams(vmem_limit_bytes=VMEM_LIMIT),
         name="adam_mixing",
-    )(factor.reshape(1), core.reshape(1).astype(jnp.int32), *pieces, master, first, second)
+    )(factor.reshape(1), *pieces, master, first, second)
 
 
 def scale_kernel(first_ref, second_ref, slopes_ref, out_ref):
@@ -687,11 +696,11 @@
     return normed, joined, attend(joined, bias, block)
 
 
-def feed_forward(stream, mixed, mixing, gains, select, with_product):
+def feed_forward(stream, mixed, mixing, upper, column, gains, select, with_product):
     features = stream.shape[1]
     middle = stream + dot(mixed, mixing[:, 3 * features : 4 * features])
     normed = norm_rows(middle, gains[2], gains[3]).astype(BF16)
-    return middle, normed, feed(normed, mixing, 4 * features, select, 512, with_product)
+    return middle, normed, feed(normed, upper, column, select, 512, with_product)
 
 
 def output_backward(grad_rows, grad_normed, mixed, middle, mixing, gains):
@@ -729,10 +738,15 @@
         self.replica = lax.axis_index("dp")
         self.core = self.member % 2
         self.paired = self.group == 16 and self.replicas == 2
+        self.carried = []
 
     def swap(self, values, name):
         if name == "y":
             return lax.ppermute(values, "dp", [(0, 1), (1, 0)])
+        if name == "corner":
+            count = 2 * self.group
+            pairs = [(f, (f + self.group) % count ^ 1) for f in range(count)]
+            return lax.ppermute(values, ("dp", "fsdp"), pairs)
         bit = {"core": 1, "x": 2, "near": 4, "far": 8, "across": 12}[name]
         return lax.ppermute(values, "fsdp", [(f, f ^ bit) for f in range(self.group)])
 
@@ -798,9 +812,30 @@
                 values, names = self.merge(values, other, names, name)
         return values.reshape(self.group * rows, width)
 
+    def reduce_line(self, values):
+        far, near = self.bit("far"), self.bit("near")
+
+        def part(at_far, at_near):
+            begin = (at_far, at_near) + (0,) * (values.ndim - 2)
+            return lax.dynamic_slice(values, begin, (1, 1) + values.shape[2:])[0, 0]
+
+        others = yield [
+            (part(far, 1 - near), "near"),
+            (part(1 - far, near), "far"),
+            (part(1 - far, 1 - near), "across"),
+        ]
+        total = part(far, near).astype(F32)
+        for other in others:
+            total = total + other.astype(F32)
+        return total.astype(BF16)
+
     def reduce_columns(self, own, other, order):
         rows, half = own.shape
         part = rows // self.group
+        if not self.paired:
+            whole = both_columns(own, other, self.core)
+            whole = lax.psum_scatter(whole, "fsdp", scatter_dimension=0, tiled=True)
+            return lax.psum(whole, "dp")
         other = yield other, "core"
         values = add(own, other).reshape(2, 2, 2, 2, 2, part // 2, half)
         names = ["far", "near", "x", "core", "y"]
@@ -808,32 +843,18 @@
             keep, give, names = self.sides(values, names, name)
             other = yield give, name
             values = add(keep, other)
-        return values
-
-    def share_columns(self, values):
+        return (yield from self.reduce_line(values))
+
+    def scatter_columns(self, own, other, order):
+        values = yield from self.reduce_columns(own, other, order)
+        if not self.paired:
+            return values.astype(F32)
         mine, give, _ = self.sides(values, ["core"], "core")
-        other = yield give, "core"
-        values = jnp.concatenate([mine, other], 1)
-        other = yield values, "y"
-        values, _ = self.merge(values, other, [], "y")
+        beside, across, corner = yield [(give, "core"), (mine, "y"), (give, "corner")]
+        near = both_columns(mine, beside, self.core)
+        far = both_columns(across, corner, self.core)
+        values, _ = self.merge(near, far, [], "y")
         return values.reshape(2 * values.shape[1], values.shape[2]).astype(F32)
-
-    def scatter_columns(self, own, other, order):
-        if not self.paired:
-            half = own.shape[1]
-            core = self.core
-            whole = both_columns(own, other, core)
-            whole = lax.psum_scatter(whole, "fsdp", scatter_dimension=0, tiled=True)
-            whole = lax.psum(whole, "dp").astype(F32)
-            return jnp.concatenate(
-                [
-                    lax.dynamic_slice_in_dim(whole, core * half, half, 1),
-                    lax.dynamic_slice_in_dim(whole, (1 - core) * half, half, 1),
-                ],
-                1,
-            )
-        values = yield from self.reduce_columns(own, other, order)
-        return (yield from self.share_columns(values))
 
     def scatter_rows(self, values, order):
         rows, width = values.shape
@@ -853,6 +874,7 @@
                 keep, give, names = self.sides(values, names, name)
             other = yield give, name
             values = add(keep, other)
+        values = yield from self.reduce_line(values)
         other = yield values, "y"
         return both_columns(values, other, self.replica).astype(F32)
 
@@ -868,18 +890,22 @@
             values = add(keep, other)
         return values
 
-    def stage(self, flows, work=None, inputs=()):
+    def stage(self, flows, work=None, inputs=(), slow=()):
+        slow = [flow for flow in slow if flow.request is not None]
         active = [flow for flow in flows if flow.request is not None]
-        asked = [flow.request if isinstance(flow.request, list) else [flow.request] for flow in active]
+        every = active + slow
+        asked = [flow.request if isinstance(flow.request, list) else [flow.request] for flow in every]
         held = [[values for values, _ in asks] for asks in asked]
         held, inputs = lax.optimization_barrier((held, inputs))
         sent = [
             [self.swap(values, name) for values, (_, name) in zip(group, asks)]
             for group, asks in zip(held, asked)
         ]
+        ending = list(zip(active, sent)) + self.carried
+        self.carried = list(zip(slow, sent[len(active) :]))
         made = work(*inputs) if work is not None else ()
-        sent, made = lax.optimization_barrier((sent, made))
-        for flow, others in zip(active, sent):
+        received, made = lax.optimization_barrier(([others for _, others in ending], made))
+        for (flow, _), others in zip(ending, received):
             flow.push(others if isinstance(flow.request, list) else others[0])
         return made
 
@@ -965,7 +991,7 @@
         return everyone(packed, 0).reshape(clips, -1)
 
     embed_low = input_embed.astype(BF16)
-    embed_flow = Flow(links.gather_rows(embed_low, ("near", "far", "y", "x")))
+    embed_flow = Flow(links.gather_rows(embed_low, ("near", "far", "x", "y")))
     wave_flow = Flow(links.spread(embed_low[-wave:])) if links.paired else embed_flow
     every = links.stage(
         [embed_flow, wave_flow],
@@ -1038,7 +1064,7 @@
         heads_low,
         backs,
         (local_ids, owned),
-    ) = links.stage([embed_flow, wave_flow, words_flow], prepare, (every,))
+    ) = links.stage([embed_flow, wave_flow], prepare, (every,))
     unused = jnp.zeros((8, 128), BF16)
     biases = (None, None, word_bias)
     turned_biases = (None, None, turned_bias)
@@ -1046,49 +1072,63 @@
     forward_block = (512, 512, words)
     backward_block = (512, 256, words)
     normed, joined, attended, fed, streams = ([None] * 3 for _ in range(5))
-    links.stage([wave_flow, words_flow])
+    links.stage([wave_flow])
     wave_rows = wave_flow.value
     if not links.paired:
         wave_rows = wave_rows[patch:]
-    streams[1] = links.stage(
-        [words_flow], lambda rows: dot(audio[0], rows), (wave_rows,)
-    )
+    streams[1] = dot(audio[0], wave_rows)
 
     def attention(tower, stream, mixing):
         return attention_forward(
             stream, biases[tower], mixing, gains_all[tower], forward_block[tower]
         )
 
-    def feeding(tower, stream, mixed, mixing):
+    def feeding(tower, stream, mixed, mixing, upper, column):
         return feed_forward(
-            stream, mixed, mixing, gains_all[tower], selects[tower], tower < 2
+            stream, mixed, mixing, upper, column, gains_all[tower], selects[tower], tower < 2
         )
 
     streams, weights[1], low_video, low_text = lax.optimization_barrier(
-        (streams, weights[1], low[0], low[2])
+        (streams, weights[1], low[0], low[2, :, : 4 * features])
     )
     weights[0] = gather(low_video)
     weights[2] = gather(low_text)
+    upper_flow = Flow(links.gather_rows(low[2, :, 4 * features :], ("near", "far", "x", "y")))
     normed[1], joined[1], attended[1] = links.stage(
-        [embed_flow, words_flow],
+        [embed_flow, words_flow, upper_flow],
         lambda stream, mixing: attention(1, stream, mixing),
         (streams[1], weights[1]),
     )
-    streams[2] = words_flow.value.astype(F32)
     fed[1] = links.stage(
-        [embed_flow],
-        lambda mixed: feeding(1, streams[1], mixed, weights[1]),
+        [embed_flow, words_flow, upper_flow],
+        lambda mixed: feeding(1, streams[1], mixed, weights[1], weights[1], 4 * features),
         (attended[1][0],),
     )
     embed = embed_flow.value
     fed[1], weights[0], embed = lax.optimization_barrier((fed[1], weights[0], embed))
-    streams[0] = dot(video[0], embed[:patch])
-    normed[0], joined[0], attended[0] = attention(0, streams[0], weights[0])
-    fed[0] = feeding(0, streams[0], attended[0][0], weights[0])
-    fed[0], weights[2], heads_low = lax.optimization_barrier((fed[0], weights[2], heads_low))
+
+    def video_attention(rows, mixing):
+        stream = dot(video[0], rows)
+        return stream, attention(0, stream, mixing)
+
+    streams[0], (normed[0], joined[0], attended[0]) = links.stage(
+        [words_flow, upper_flow], video_attention, (embed[:patch], weights[0])
+    )
+    fed[0] = links.stage(
+        [words_flow, upper_flow],
+        lambda mixed: feeding(0, streams[0], mixed, weights[0], weights[0], 4 * features),
+        (attended[0][0],),
+    )
+    links.stage([upper_flow])
+    streams[2] = words_flow.value.astype(F32)
+    text_upper = upper_flow.value
+    text_upper, weights[2], heads_low = lax.optimization_barrier(
+        (text_upper, weights[2], heads_low)
+    )
     heads_all = gather(heads_low)
     normed[2], joined[2], attended[2] = attention(2, streams[2], weights[2])
-    fed[2] = feeding(2, streams[2], attended[2][0], weights[2])
+    fed[2] = feeding(2, streams[2], attended[2][0], weights[2], text_upper, 0)
+    uppers = (weights[0][:, 4 * features :], weights[1][:, 4 * features :], text_upper)
 
     heads = heads_all[:, : head_proj.shape[1]]
     video_text = heads_all[:, head_proj.shape[1] :].reshape(group, shard, text_width)
@@ -1164,22 +1204,10 @@
     ups = scale_columns(products[1], products[0], jnp.concatenate(own_slopes[1::-1], 0))
     ups, own_slopes = lax.optimization_barrier((ups, own_slopes))
     up_part = lax.psum_scatter(ups, "fsdp", scatter_dimension=0, tiled=True)
-    first, second = ("y", "x", "far", "near"), ("x", "y", "far", "near")
-
-    def halves(inward, outward):
-        return [
-            jnp.concatenate(
-                [
-                    lax.dynamic_slice_in_dim(inward, at * 3 * half, 3 * half, 1),
-                    lax.dynamic_slice_in_dim(outward, at * half, half, 1),
-                ],
-                1,
-            )
-            for at in (core, 1 - core)
-        ]
+    first, second = ("y", "x"), ("x", "y")
 
     def hidden_backward(tower, slope):
-        upper = weights[tower][:, 4 * features :]
+        upper = uppers[tower]
         if tower == 2:
             spread = select[:captions].astype(F32).T
             grad_hidden = (slopes[2].astype(F32) * full(spread, slope)).astype(BF16)
@@ -1217,32 +1245,66 @@
         grad_joined = inner_backward(2, made[2])
         inward = dot_tn(normed[2], grad_joined).astype(BF16)
         entry, entry_gains = entry_backward(2, made[0], grad_joined)
-        return jnp.concatenate([inward, made[1], up], 1), entry, entry_gains + made[3]
+        return (inward, made[1], up), entry, entry_gains + made[3]
 
     text_grad, entry, gains_grads[2] = links.stage([], text_backward, (own_slopes[2],))
     word_flow = Flow(links.gather_clips(entry))
-    text_part = lax.psum_scatter(text_grad, "fsdp", scatter_dimension=0, tiled=True)
-    made_video, _ = links.stage([word_flow], lambda slope: outward_backward(0, slope), (own_slopes[0],))
+    made_video, _ = links.stage(
+        [word_flow], lambda slope: outward_backward(0, slope), (own_slopes[0],)
+    )
     embed_rows = input_embed.shape[0] * group
 
     def video_inner(grad_mixed):
         grad_joined = inner_backward(0, grad_mixed)
         inward = dot_tn(normed[0], grad_joined).astype(BF16)
         entry, entry_gains = entry_backward(0, made_video[0], grad_joined)
-        return halves(inward, made_video[1]), entry, entry_gains
-
-    video_parts, entry, entry_gains = links.stage([word_flow], video_inner, (made_video[2],))
+        return jnp.concatenate([*text_grad, inward, made_video[1]], 1), entry, entry_gains
+
+    pair_grad, entry, entry_gains = links.stage([word_flow], video_inner, (made_video[2],))
     gains_grads[0] = entry_gains + made_video[3]
-    video_flow = Flow(links.scatter_columns(*video_parts, first))
+    pair_part = lax.psum_scatter(pair_grad, "fsdp", scatter_dimension=0, tiled=True)
 
     def video_entry(entry, slope):
         made, _ = outward_backward(1, slope)
         return patch_grads(video, entry, embed_rows), made
 
-    grad_embed, made_audio = links.stage([word_flow, video_flow], video_entry, (entry, own_slopes[1]))
-    embed_flow = Flow(links.scatter_rows(grad_embed, first))
-    rest = [word_flow, video_flow, embed_flow]
-    joined_audio = links.stage(rest, lambda part: inner_backward(1, part), (made_audio[2],))
+    grad_embed, made_audio = links.stage([word_flow], video_entry, (entry, own_slopes[1]))
+    embed_flow = Flow(links.scatter_rows(grad_embed, ("y", "x")))
+
+    def audio_pairs(grad_mixed, *bounds):
+        return attend_back(
+            joined[1],
+            grad_mixed,
+            attended[1][0],
+            attended[1][1],
+            None,
+            backward_block[1],
+            *bounds,
+        )
+
+    first_pairs = links.stage(
+        [word_flow, embed_flow], lambda part: audio_pairs(part, 0, pairs // 2), (made_audio[2],)
+    )
+
+    def audio_inner(grad_mixed, first_pairs):
+        grad_joined = audio_pairs(grad_mixed, pairs // 2, pairs, first_pairs)
+        inward = dot_tn(normed[1], grad_joined).astype(BF16)
+        sides = [
+            jnp.concatenate(
+                [
+                    lax.dynamic_slice_in_dim(inward, at * 3 * half, 3 * half, 1),
+                    lax.dynamic_slice_in_dim(made_audio[1], at * half, half, 1),
+                ],
+                1,
+            )
+            for at in (core, 1 - core)
+        ]
+        return grad_joined, sides
+
+    joined_audio, audio_sides = links.stage(
+        [embed_flow], audio_inner, (made_audio[2], first_pairs)
+    )
+    audio_flow = Flow(links.scatter_columns(*audio_sides, ("y", "x")))
 
     def scatter_table(every_word):
         return jax.ops.segment_sum(
@@ -1251,20 +1313,8 @@
             num_segments=table_rows,
         )
 
-    def audio_inward(grad_joined, every_word):
-        inward = dot_tn(normed[1], grad_joined).astype(BF16)
-        return halves(inward, made_audio[1]), scatter_table(every_word)
-
-    audio_parts, table_grad = links.stage(rest, audio_inward, (joined_audio, word_flow.value))
-    cut = features
-    if links.paired:
-        audio_flows = [
-            Flow(links.reduce_columns(*[part[:, :cut] for part in audio_parts], first)),
-            Flow(links.reduce_columns(*[part[:, cut:] for part in audio_parts], second)),
-        ]
-    else:
-        audio_flows = [Flow(links.scatter_columns(*audio_parts, first))]
-    rest += audio_flows
+    def squared(*values):
+        return sum(jnp.sum(value * value) for value in values)
 
     def audio_entry(grad_joined):
         entry, entry_gains = entry_backward(1, made_audio[0], grad_joined)
@@ -1277,38 +1327,27 @@
             jnp.where(core == 0, gain_columns, wave_grad),
         )
 
-    beside = links.stage(rest, audio_entry, (joined_audio,))
-    beside_flow = Flow(
-        links.reduce_columns(*beside, second)
-        if links.paired
-        else links.scatter_columns(*beside, first)
-    )
-    rest += [beside_flow]
-
-    def squared(*values):
-        return sum(jnp.sum(value * value) for value in values)
-
-    links.stage(rest)
+    up_flow = Flow(links.sum_replicas(up_part))
+    beside = links.stage([audio_flow, up_flow], audio_entry, (joined_audio,), [embed_flow])
+    beside_flow = Flow(links.reduce_columns(*beside, ("y", "x")))
+    rest = [audio_flow, beside_flow]
+    table_grad = links.stage(rest, scatter_table, (word_flow.value,))
     back_grad, (heads_grad, video_text_grad), table_square = links.stage(
-        rest, lambda table: (back_grads(), head_grads(), squared(table)), (table_grad,)
-    )
-    up_flow = Flow(links.sum_replicas(up_part))
-    rest += [up_flow]
-    small_square = links.stage(rest, squared, (back_grad, heads_grad, video_text_grad))
-    links.stage(rest)
-    text_flow = Flow(links.sum_replicas(text_part))
-    if links.paired:
-        values = jnp.concatenate([flow.value for flow in audio_flows], 2)
-        audio_flows = [Flow(links.share_columns(values))]
-    rest += audio_flows + [text_flow]
-    for _ in range(4):
-        if any(flow.request is not None for flow in rest):
-            links.stage(rest)
-    pieces = (up_flow.value, text_flow.value, video_flow.value, audio_flows[0].value)
+        rest,
+        lambda table, up: (back_grads(), head_grads(), squared(table, up)),
+        (table_grad, up_flow.value),
+        [embed_flow],
+    )
+    pair_flow = Flow(links.sum_replicas(pair_part))
+    small_square = links.stage(
+        rest + [pair_flow], squared, (back_grad, heads_grad, video_text_grad)
+    )
+    small_square = small_square + links.stage(rest + [embed_flow], squared, (pair_flow.value,))
+    pieces = (up_flow.value, pair_flow.value, audio_flow.value)
     embed_grad = embed_flow.value
 
     outer = lax.dynamic_slice_in_dim(outer_grads[:6], member * gain_part, gain_part, 1)
-    local_square = table_square + small_square + squared(*pieces, embed_grad, outer)
+    local_square = table_square + small_square + squared(pieces[2], embed_grad, outer)
     piece = beside_flow.value.reshape(-1, wave)
     piece_square = squared(piece.astype(F32))
     marks = jnp.where(jnp.arange(128) < 64, local_square, piece_square)
@@ -1327,8 +1366,6 @@
     else:
         square = jnp.sum(marks[:group, 0]) + jnp.sum(marks[:group, 127])
         placed = sent[:group].reshape(group, gain_part, 2, wave)
-        swapped = (jnp.arange(group) % 2 == 1)[:, None, None, None]
-        placed = jnp.where(swapped, placed[:, :, ::-1], placed)
         placed = placed.transpose(2, 0, 1, 3).reshape(2, features, wave)
     wave_rows, gain_rows = placed[0].T, placed[1].T
     embed_part = input_embed.shape[0]
@@ -1380,7 +1417,6 @@
     new = [
         adam_mixing(
             factor,
-            core,
             pieces,
             mixing_in,
             mixing_in_first,

time: 892 us -> 869 us (0.974)
  waiting for transfers between devices: 169 us -> 137 us
    all_gather x4, waiting for transfers between devices: 44.9 us -> 20 us  [gather(): return lax.all_gather(values, 'fsdp', axis=0, tiled=True)]
    ppermute x39 -> x37, waiting for transfers between devices: 111 us -> 89.6 us  [swap(): lax.ppermute(values, 'fsdp', [(f, f ^ bit) for f in range(self.group)])]
    ppermute x12 -> x10, waiting for transfers between devices: 11.4 us -> 22.9 us  [swap(): return lax.ppermute(values, 'dp', [(0, 1), (1, 0)])]
    ppermute x39 -> x37, starting transfers between devices: 30.5 us -> 39.3 us  [swap(): lax.ppermute(values, 'fsdp', [(f, f ^ bit) for f in range(self.group)])]
    reduce_sum x8 -> x10, other arithmetic: 9.85 us -> 18.6 us  [squared(): return sum((jnp.sum(value * value) for value in values))]
    select_n x9 -> x13, other arithmetic: 19.6 us -> 27.2 us  [merge(): jnp.where(place == self.bit(name), jnp.expand_dims(values, at), jnp.expan...]
    unnamed x347 -> x394, local copies, waits for them, and re-layouts: 23.5 us -> 21.4 us
    pallas_call x3 -> x4, Pallas kernels: 52 us -> 54.1 us  [attend_back(): pl.pallas_call(kernel, grid=(pairs,), out_shape=jax.ShapeDtypeStruct(qkv....]
  transfers between devices with their start and end apart: 57 -> 54, of which waited for: 20 -> 22; matrix products, arithmetic and copies ran while one was open for 33% -> 36% of each run, Pallas kernels for 16% -> 17%
where the time goes in v4:
time: 869 us; the launch traced here: 861 us
  Pallas kernels  254 us (29%)
  other arithmetic  198 us (23%)
  waiting for transfers between devices  137 us (16%)
  matrix products  103 us (12%)
  local copies, waits for them, and re-layouts  89.6 us (10%)
  starting transfers between devices  53.3 us (6%)
  between operations  26.4 us (3%)
    ppermute x37, waiting for transfers between devices, swap(): lax.ppermute(values, 'fsdp', [(f, f ^ bit) for f in range(self.group)])  89.6 us
    pallas_call x1, Pallas kernels, contrast(): pl.pallas_call(functools.partial(middle_kernel, scales, captions), out_sh...  62 us
    pallas_call x4, Pallas kernels, attend_back(): pl.pallas_call(kernel, grid=(pairs,), out_shape=jax.ShapeDtypeStruct(qkv....  54.1 us
    dot_general x9, matrix products, dot_nt(): return lax.dot_general(a, b, NT, preferred_element_type=F32)  45.9 us
    sub x5, other arithmetic, adam_update(): master - rate * (first_hat / (jnp.sqrt(second_hat) + EPSILON) + WEIGHT_DE...  39.8 us
    ppermute x37, starting transfers between devices, swap(): lax.ppermute(values, 'fsdp', [(f, f ^ bit) for f in range(self.group)])  39.3 us
    pallas_call x3, Pallas kernels, feed(): pl.pallas_call(functools.partial(feed_kernel, with_product), grid=(width...  38.2 us
    pallas_call x3, Pallas kernels, attend(): pl.pallas_call(functools.partial(attend_kernel, rows, block, bias is not...  36.1 us
  transfers between devices with their start and end apart: 54, of which 22 were waited for; matrix products, arithmetic and copies ran while one was open for 36% of the time, Pallas kernels for 17%

profile of v4, /device:TPU:0, one launch (start us, length us, event | category | flops | bytes accessed | tf_op | source)
XLA Modules:
  0.0 860.8 jit_solution(5292712926037006547)
XLA Ops:
  7.3 4.0 regroup.1
  14.0 3.1 collective-permute-start
  23.0 12.2 %everyone_0.1 = f32[32,8,128]{2,1,0:T(8,128)} custom-call(f32[8,128]{1,0:T(8,128)} %pad_bitcast_fusion.x_ref), custom_call_target="tpu_custom_call" | custom-call | tf_op jit(solution)/shard_map/everyone_0/pallas_call | solution.py:127
  42.4 10.7 %gather_fusion = bf16[1536,768]{1,0:T(8,128)(2,1)S(1)} fusion(f32[4096,768]{1,0:T(8,128)} %param.46, s32[2048]{0:T(1024)S(1)} %pad_clamp_fusion), kind=kCustom, calls=%fused_computation | custom fusion | bytes 4724736 | tf_op jit(solution)/shard_map/gather | solution.py:1011
  55.0 9.0 %collective-permute-done.2 = bf16[2,200,384]{2,1,0:T(8,128)(2,1)} collective-permute-done((bf16[2,200,384]{2,1,0:T(8,128)(2,1)S(1)}, bf16[2,200,384]{2,1,0:T(8,128)(2,1)}, u32[]{:S(2)}, u32[]{:S(2)}) %collective-permute-start.2) | collective-permute-done | bytes 307232 | tf_op jit(solution)/shard_map/ppermute | solution.py:751
  72.2 15.4 %collective-permute-done.5 = bf16[128,768]{1,0:T(8,128)(2,1)S(1)} collective-permute-done((bf16[128,768]{1,0:T(8,128)(2,1)S(1)}, bf16[128,768]{1,0:T(8,128)(2,1)S(1)}, u32[]{:S(2)}, u32[]{:S(2)}) %collective-permute-start.5) | collective-permute-done | bytes 196640 | tf_op jit(solution)/shard_map/ppermute | solution.py:751
  87.6 10.8 %collective-permute-done.4 = bf16[2,2,200,384]{3,2,1,0:T(8,128)(2,1)S(1)} collective-permute-done((bf16[2,2,200,384]{3,2,1,0:T(8,128)(2,1)S(1)}, bf16[2,2,200,384]{3,2,1,0:T(8,128)(2,1)S(1)}, u32[]{:S(2)}, u32[]{:S(2)}) %collective-permute-start.4) | collective-permute-done | bytes 614432 | tf_op jit(solution)/shard_map/ppermute | solution.py:751
  101.9 18.8 %collective-permute-done.6 = bf16[128,768]{1,0:T(8,128)(2,1)} collective-permute-done((bf16[128,768]{1,0:T(8,128)(2,1)S(1)}, bf16[128,768]{1,0:T(8,128)(2,1)}, u32[]{:S(2)}, u32[]{:S(2)}) %collective-permute-start.6) | collective-permute-done | bytes 196640 | tf_op jit(solution)/shard_map/ppermute | solution.py:751
  122.2 5.1 all-gather.12.cloned.1.call-done
  128.5 2.8 constant_dynamic-slice_fusion.19
  139.9 7.4 convolution_convert_fusion.refs_0_
  147.4 21.9 %attend_1024.1 = (bf16[1024,768]{1,0:T(8,128)(2,1)}, f32[1024,768]{1,0:T(8,128)}) custom-call(bf16[1024,2304]{1,0:T(8,128)(2,1)} %convolution_convert_fusion.refs_0_), custom_call_target="tpu_custom_call" | custom-call | flops 805306368 | bytes 786432 | tf_op jit(solution)/shard_map/attend_1024/pallas_call | solution.py:188
  179.7 3.2 fusion.169
  186.0 20.0 %feed_1024.1 = (bf16[1024,3072]{1,0:T(8,128)(2,1)}, f32[8,3072]{1,0:T(8,128)}, bf16[768,3072]{1,0:T(8,128)(2,1)}) custom-call(bf16[1024,768]{1,0:T(8,128)(2,1)} %add_convert_fusion.2.h_ref, bf16[768,6144]{1,0:T(8,128)(2,1)} %bitcast.260, bf16[8,128]{1,0:T(8,128)(2,1)} %broadcast_in_dim.558.sel_ref), custom_call_target="tpu_custom_call" | custom-call | flops 301989888 | bytes 3145728 | tf_op jit(solution)/shard_map/feed_1024/pallas_call | solution.py:666
  207.4 5.8 bitcast_select_fusion
  215.8 9.7 %all-gather.6.cloned.1.call-done.w_ref = bf16[768,6144]{1,0:T(8,128)(2,1)} async-done(((bf16[48,6144]{1,0:T(8,128)(2,1)}), bf16[768,6144]{1,0:T(8,128)(2,1)}) %all-gather.6.cloned.1.call-update) | async-done | bytes 9437200 | tf_op jit(solution)/shard_map/all_gather | solution.py:984
  228.9 3.8 fusion.170
  232.6 3.1 copy.174
  238.9 5.4 convolution_convert_fusion.5.refs_0_
  244.3 8.3 attend_512.1
  262.4 12.0 %feed_512.1 = (bf16[512,3072]{1,0:T(8,128)(2,1)}, f32[8,3072]{1,0:T(8,128)}, bf16[768,3072]{1,0:T(8,128)(2,1)}) custom-call(bf16[512,768]{1,0:T(8,128)(2,1)} %add_convert_fusion.7.h_ref, bf16[768,6144]{1,0:T(8,128)(2,1)} %all-gather.6.cloned.1.call-done.w_ref, bf16[8,128]{1,0:T(8,128)(2,1)} %broadcast_in_dim.558.sel_ref), custom_call_target="tpu_custom_call" | custom-call | flops 150994944 | bytes 1572864 | tf_op jit(solution)/shard_map/feed_512/pallas_call | solution.py:666
  274.5 9.9 %collective-permute-done.16 = bf16[2,2,2,48,1536]{4,3,2,1,0:T(8,128)(2,1)S(1)} collective-permute-done((bf16[2,2,2,48,1536]{4,3,2,1,0:T(8,128)(2,1)S(1)}, bf16[2,2,2,48,1536]{4,3,2,1,0:T(8,128)(2,1)S(1)}, u32[]{:S(2)}, u32[]{:S(2)}) %collective-permute-start.16) | collective-permute-done | bytes 1179680 | tf_op jit(solution)/shard_map/ppermute | solution.py:745
  287.7 4.7 collective-permute-done.17
  292.4 5.0 bitcast_select_fusion.2.w_ref
  300.9 3.1 multiply_reduce_fusion.6
  312.9 3.5 convolution_convert_fusion.6.refs_0_
  316.5 5.9 attend_96.1
  325.2 6.2 feed_96.1
  333.9 5.2 all-gather.10.cloned.1.call-done
  340.8 2.9 slice.316.heads_ref
  343.7 62.0 %middle.1 = (f32[8,128]{1,0:T(8,128)}, f32[32,768]{1,0:T(8,128)}, f32[32,768]{1,0:T(8,128)}, f32[96,768]{1,0:T(8,128)}, f32[8,768]{1,0:T(8,128)}, /*index=5*/f32...) custom-call(f32[8,3072]{1,0:T(8,128)} %pad_maximum_fusion.9.sum_ref,, ...), custom_call_target="tpu_custom_call" | custom-call | tf_op jit(solution)/shard_map/middle/pallas_call | solution.py:609
  409.0 8.9 %scale_columns.1 = bf16[768,6144]{1,0:T(8,128)(2,1)} custom-call(bf16[768,3072]{1,0:T(8,128)(2,1)} %get-tuple-element.350.first_ref, bf16[768,3072]{1,0:T(8,128)(2,1)} %get-tuple-element.351.second_ref, f32[2,3072]{1,0:T(2,128)} %pad_maximum_fusion.11.slopes_ref), custom_call_target="tpu_custom_call" | custom-call | tf_op jit(solution)/shard_map/scale_columns/pallas_call | solution.py:394
  426.6 5.0 multiply_reduce_fusion.21
  432.3 2.6 convolution_convert_fusion.12.refs_1_
  434.9 5.8 attend_back_96_0.1
  440.7 4.0 fusion.152
  458.6 3.5 multiply_reduce_fusion.14
  474.5 11.3 %attend_back_512_0.1 = bf16[512,2304]{1,0:T(8,128)(2,1)} custom-call(bf16[512,2304]{1,0:T(8,128)(2,1)} %convolution_convert_fusion.5.refs_0_, bf16[512,768]{1,0:T(8,128)(2,1)} %convolution_convert_fusion.11.refs_1_, bf16[512,768]{1,0:T(8,128)(2,1)} %get-tuple-element.322.refs_2_, f32[512,768]{1,0:T(8,128)} %get-tuple-element.375.refs_3_), custom_call_target="tpu_custom_call" | custom-call | flops 402653184 | bytes 393216 | tf_op jit(solution)/shard_map/attend_back_512_0/pallas_call | solution.py:281
  485.8 5.6 multiply_reduce_fusion.11
  493.9 3.9 fusion.5
  498.9 3.0 add_convert_fusion.6.entry_ref
  506.8 7.7 patch_grads.1
  514.5 9.2 %multiply_reduce_fusion.4 = (bf16[768]{0:T(1024)(128)(2,1)S(1)}, f32[1024]{0:T(1024)S(1)}, bf16[768]{0:T(1024)(128)(2,1)S(1)}, f32[1024,768]{1,0:T(8,128)S(1)}) fusion(f32[1024,768]{1,0:T(8,128)S(1)} %copy-done.2, f32[1024]{0:T(1024)S(1)} %fusion.132, f32[1024]{0:T(1024)S(1)} %copy-done.103, f32[768]{0:T(1024)S(1)} %copy-done.109, ...), kind=kOutput, calls=%fused_computation.52 | convolution fusion | flops 4845204480 | bytes 17332224 | tf_op jit(solution)/shard_map/dot_general | solution.py:31
  525.7 4.9 convolution_convert_fusion.7.refs_1_
  533.1 10.3 %collective-permute-done.22 = bf16[2,2,2,96,768]{4,3,2,1,0:T(8,128)(2,1)} collective-permute-done((bf16[2,2,2,96,768]{4,3,2,1,0:T(8,128)(2,1)S(1)}, bf16[2,2,2,96,768]{4,3,2,1,0:T(8,128)(2,1)}, u32[]{:S(2)}, u32[]{:S(2)}) %collective-permute-start.22) | collective-permute-done | bytes 1179680 | tf_op jit(solution)/shard_map/ppermute | solution.py:751
  560.8 18.7 %attend_back_1024_0.1.refs_4_ = bf16[1024,2304]{1,0:T(8,128)(2,1)} custom-call(bf16[1024,2304]{1,0:T(8,128)(2,1)} %convolution_convert_fusion.refs_0_, bf16[1024,768]{1,0:T(8,128)(2,1)} %convolution_convert_fusion.7.refs_1_, bf16[1024,768]{1,0:T(8,128)(2,1)} %get-tuple-element.296.refs_2_, f32[1024,768]{1,0:T(8,128)} %get-tuple-element.393.refs_3_), custom_call_target="tpu_custom_call" | custom-call | flops 805306368 | bytes 393216 | tf_op jit(solution)/shard_map/attend_back_1024_0/pallas_call | solution.py:281
  586.9 18.3 %attend_back_1024_3.1 = bf16[1024,2304]{1,0:T(8,128)(2,1)} custom-call(bf16[1024,2304]{1,0:T(8,128)(2,1)} %convolution_convert_fusion.refs_0_, bf16[1024,768]{1,0:T(8,128)(2,1)} %convolution_convert_fusion.7.refs_1_, bf16[1024,768]{1,0:T(8,128)(2,1)} %get-tuple-element.296.refs_2_, ...), custom_call_target="tpu_custom_call", output_to_operand_aliasing={{}: (4, {})} | custom-call | flops 805306368 | bytes 393216 | tf_op jit(solution)/shard_map/attend_back_1024_3/pallas_call | solution.py:281
  605.2 6.8 convolution_convert_fusion.1
  612.0 4.4 bitcast_select_fusion.1
  624.5 9.3 %multiply_reduce_fusion.1 = (bf16[768]{0:T(1024)(128)(2,1)S(1)}, f32[1024]{0:T(1024)S(1)}, bf16[768]{0:T(1024)(128)(2,1)S(1)}, f32[1024,768]{1,0:T(8,128)}) fusion(f32[1024,768]{1,0:T(8,128)S(1)} %convolution_bitcast_fusion, f32[1024]{0:T(1024)} %fusion.133, f32[1024]{0:T(1024)} %copy-done.104, f32[768]{0:T(1024)} %get-tuple-element.527, ...), kind=kOutput, calls=%fused_computation.48 | convolution fusion | flops 3630167552 | bytes 14568448 | tf_op jit(solution)/shard_map/dot_general | solution.py:31
  636.8 3.1 fusion.160
  641.6 9.3 %collective-permute-done.27 = bf16[48,6144]{1,0:T(8,128)(2,1)S(1)} collective-permute-done((bf16[48,6144]{1,0:T(8,128)(2,1)}, bf16[48,6144]{1,0:T(8,128)(2,1)S(1)}, u32[]{:S(2)}, u32[]{:S(2)}) %collective-permute-start.27) | collective-permute-done | bytes 589856 | tf_op jit(solution)/shard_map/ppermute | solution.py:745
  655.7 28.6 %scatter_custom_fusion = f32[4096,768]{1,0:T(8,128)} fusion(s32[3072]{0:T(1024)} %min.25, bf16[3072,768]{1,0:T(8,128)(2,1)} %bitcast_select_fusion.1, f32[]{:T(128)} %constant.411.clone.1, pred[3072]{0:T(1024)(128)(4,1)S(1)} %copy-done.132), kind=kCustom, calls=%fused_computation.6 | custom fusion | flops 7077888 | bytes 17305600 | tf_op jit(solution)/shard_map/scatter-add | solution.py:1310
  692.4 8.5 multiply_reduce_fusion
  703.1 3.2 collective-permute-done.31
  709.5 3.8 reduce-scatter.5.cloned.1.call-done
  725.4 6.9 collective-permute-done.39
  739.1 4.2 collective-permute-done.34
  745.8 2.6 convert_add_fusion.3.refs_1_
  762.1 3.7 collective-permute-done.47
  774.2 17.7 %everyone_2.1 = bf16[32,64,128]{2,1,0:T(8,128)(2,1)} custom-call(bf16[64,128]{1,0:T(8,128)(2,1)} %pad_maximum_fusion.12.x_ref), custom_call_target="tpu_custom_call" | custom-call | tf_op jit(solution)/shard_map/everyone_2/pallas_call | solution.py:127
  801.6 5.4 multiply_subtract_fusion.1
  807.0 30.1 %multiply_subtract_fusion = (f32[4096,768]{1,0:T(8,128)}, f32[4096,768]{1,0:T(8,128)}, f32[4096,768]{1,0:T(8,128)}) fusion(f32[4096,768]{1,0:T(8,128)} %param.46, f32[4096,768]{1,0:T(8,128)} %param.47, f32[4096,768]{1,0:T(8,128)} %param.48, f32[4096,768]{1,0:T(8,128)} %scatter_custom_fusion, f32[]{:T(128)} %div.352), kind=kLoop, calls=%fused_computation.4 | loop fusion | flops 50331648 | bytes 88080384 | tf_op jit(solution)/shard_map/sub | solution.py:68
  839.8 12.8 %adam_mixing.1 = (f32[3,48,6144]{2,1,0:T(8,128)}, f32[3,48,6144]{2,1,0:T(8,128)}, f32[3,48,6144]{2,1,0:T(8,128)}) custom-call(f32[1]{0:T(128)} %bitcast.78.scal_ref, f32[48,6144]{1,0:T(8,128)} %copy-done.12, f32[48,9216]{1,0:T(8,128)} %convert_add_fusion.3.refs_1_, f32[48,3072]{1,0:T(8,128)} %fusion.68.refs_2_, f32[3,48,6144]{2,1,0:T(8,128)} %refs_3_.1, ...), custom_call_target="tpu_custom_call" | custom-call | tf_op jit(solution)/shard_map/adam_mixing/pallas_call | solution.py:370
  (775 shorter events, 250.3 us)
Async XLA Ops:
  7.2 113.5 %copy-start = (bf16[1,1024,128]{2,1,0:T(8,128)(2,1)S(1)}, bf16[1,1024,128]{2,1,0:T(8,128)(2,1)}, u32[]{:S(2)}) copy-start(bf16[1,1024,128]{2,1,0:T(8,128)(2,1)} %param.29) | copy-start | bytes 786436
  7.2 120.1 %all-gather.12.cloned.1.call-start = ((), (), s32[]{:S(2)}) async-start(), calls=%async_computation.7 | async-start | bytes 10027008 | tf_op jit(solution)/shard_map/all_gather | solution.py:984
  13.9 211.7 %all-gather.6.cloned.1.call-start = ((), (), s32[]{:S(2)}) async-start(), calls=%async_computation.2 | async-start | bytes 10027008 | tf_op jit(solution)/shard_map/all_gather | solution.py:984
  14.0 22.1 %collective-permute-start = (bf16[200,384]{1,0:T(8,128)(2,1)S(1)}, bf16[200,384]{1,0:T(8,128)(2,1)}, u32[]{:S(2)}, u32[]{:S(2)}) collective-permute-start(bf16[200,384]{1,0:T(8,128)(2,1)S(1)} %constant_dynamic-slice_fusion.21), channel_id=1, source_target_pairs={{0,4},{1,5},{2,6},{3,7},{4,0},{5,1},{6,2},{7,3},{8,12},{9,13},{10,... | collective-permute-start | bytes 460808 | tf_op jit(solution)/shard_map/ppermute | solution.py:751
  17.1 19.0 %collective-permute-start.1 = (bf16[128,768]{1,0:T(8,128)(2,1)S(1)}, bf16[128,768]{1,0:T(8,128)(2,1)}, u32[]{:S(2)}, u32[]{:S(2)}) collective-permute-start(bf16[128,768]{1,0:T(8,128)(2,1)S(1)} %slice.306), channel_id=1, source_target_pairs={{0,1},{1,0},{2,3},{3,2},{4,5},{5,4},{6,7},{7,6},{8,9},{9,8},{10,11... | collective-permute-start | bytes 589832 | tf_op jit(solution)/shard_map/ppermute | solution.py:751
  38.6 16.4 %collective-permute-start.3 = (bf16[128,768]{1,0:T(8,128)(2,1)S(1)}, bf16[128,768]{1,0:T(8,128)(2,1)}, u32[]{:S(2)}, u32[]{:S(2)}) collective-permute-start(bf16[128,768]{1,0:T(8,128)(2,1)S(1)} %broadcast_select_fusion.17), channel_id=1, source_target_pairs={{0,2},{1,3},{2,0},{3,1},{4,6},{5,7},{6,4},{7,5},{8,10},{9,11},{10,... | collective-permute-start | bytes 589832 | tf_op jit(solution)/shard_map/ppermute | solution.py:751
  40.6 23.4 %collective-permute-start.2 = (bf16[2,200,384]{2,1,0:T(8,128)(2,1)S(1)}, bf16[2,200,384]{2,1,0:T(8,128)(2,1)}, u32[]{:S(2)}, u32[]{:S(2)}) collective-permute-start(bf16[2,200,384]{2,1,0:T(8,128)(2,1)S(1)} %broadcast_select_fusion.11), channel_id=1, source_target_pairs={{0,8},{1,9},{2,10},{3,11},{4,12},{5,13},{6,14},{7,15},{8,0},{9,1},... | collective-permute-start | bytes 921608 | tf_op jit(solution)/shard_map/ppermute | solution.py:751
  66.2 35.7 %copy-start.25 = (bf16[2,2,200,384]{3,2,1,0:T(8,128)(2,1)}, bf16[2,2,200,384]{3,2,1,0:T(8,128)(2,1)S(1)}, u32[]{:S(2)}) copy-start(bf16[2,2,200,384]{3,2,1,0:T(8,128)(2,1)S(1)} %broadcast_select_fusion.8) | copy-start | bytes 1843204
  68.2 19.4 %collective-permute-start.5 = (bf16[128,768]{1,0:T(8,128)(2,1)S(1)}, bf16[128,768]{1,0:T(8,128)(2,1)S(1)}, u32[]{:S(2)}, u32[]{:S(2)}) collective-permute-start(bf16[128,768]{1,0:T(8,128)(2,1)S(1)} %broadcast_select_fusion.16), channel_id=1, source_target_pairs={{0,4},{1,5},{2,6},{3,7},{4,0},{5,1},{6,2},{7,3},{8,12},{9,13},{10,... | collective-permute-start | bytes 589832 | tf_op jit(solution)/shard_map/ppermute | solution.py:751
  69.0 29.4 %collective-permute-start.4 = (bf16[2,2,200,384]{3,2,1,0:T(8,128)(2,1)S(1)}, bf16[2,2,200,384]{3,2,1,0:T(8,128)(2,1)S(1)}, u32[]{:S(2)}, u32[]{:S(2)}) collective-permute-start(bf16[2,2,200,384]{3,2,1,0:T(8,128)(2,1)S(1)} %broadcast_select_fusion.8), channel_id=1, source_target_pairs={{0,2},{1,3},{2,0},{3,1},{4,6},{5,7},{6,4},{7,5},{8,10},{9,11},{10,... | collective-permute-start | bytes 1843208 | tf_op jit(solution)/shard_map/ppermute | solution.py:751
  98.5 22.2 %collective-permute-start.6 = (bf16[128,768]{1,0:T(8,128)(2,1)S(1)}, bf16[128,768]{1,0:T(8,128)(2,1)}, u32[]{:S(2)}, u32[]{:S(2)}) collective-permute-start(bf16[128,768]{1,0:T(8,128)(2,1)S(1)} %broadcast_select_fusion.15), channel_id=1, source_target_pairs={{0,8},{1,9},{2,10},{3,11},{4,12},{5,13},{6,14},{7,15},{8,0},{9,1},... | collective-permute-start | bytes 589832 | tf_op jit(solution)/shard_map/ppermute | solution.py:751
  127.3 170.1 %all-gather.8.cloned.1.call-start = ((), (), s32[]{:S(2)}) async-start(), calls=%async_computation.3 | async-start | bytes 5013504 | tf_op jit(solution)/shard_map/all_gather | solution.py:984
  135.4 33.9 %collective-permute-start.7 = (bf16[2,2,2,200,384]{4,3,2,1,0:T(8,128)(2,1)}, bf16[2,2,2,200,384]{4,3,2,1,0:T(8,128)(2,1)S(1)}, u32[]{:S(2)}, u32[]{:S(2)}) collective-permute-start(bf16[2,2,2,200,384]{4,3,2,1,0:T(8,128)(2,1)} %broadcast_select_fusion.1), channel_id=1, source_target_pairs={{0,16},{16,0},{1,17},{17,1},{2,18},{18,2},{3,19},{19,3},{4,20},{20... | collective-permute-start | bytes 3686408 | tf_op jit(solution)/shard_map/ppermute | solution.py:745
  138.1 31.2 %collective-permute-start.9 = (bf16[48,1536]{1,0:T(8,128)(2,1)S(1)}, bf16[48,1536]{1,0:T(8,128)(2,1)}, u32[]{:S(2)}, u32[]{:S(2)}) collective-permute-start(bf16[48,1536]{1,0:T(8,128)(2,1)S(1)} %dynamic-slice_bitcast_fusion.12), channel_id=1, source_target_pairs={{0,4},{1,5},{2,6},{3,7},{4,0},{5,1},{6,2},{7,3},{8,12},{9,13},{10,... | collective-permute-start | bytes 442376 | tf_op jit(solution)/shard_map/ppermute | solution.py:751
  138.2 31.2 %collective-permute-start.8 = (bf16[2,2,2,96,768]{4,3,1,0,2:T(8,128)(2,1)S(1)}, bf16[2,2,2,96,768]{4,3,1,0,2:T(8,128)(2,1)S(1)}, u32[]{:S(2)}, u32[]{:S(2)}) collective-permute-start(bf16[2,2,2,96,768]{4,3,1,0,2:T(8,128)(2,1)S(1)} %bitcast.272), channel_id=1, source_target_pairs={{0,1},{1,0},{2,3},{3,2},{4,5},{5,4},{6,7},{7,6},{8,9},{9,8},{10,11... | collective-permute-start | bytes 3538952 | tf_op jit(solution)/shard_map/ppermute | solution.py:751
  175.4 31.9 %collective-permute-start.10 = (bf16[2,2,2,200,768]{4,3,2,1,0:T(8,128)(2,1)}, bf16[2,2,2,200,768]{4,3,2,1,0:T(8,128)(2,1)}, u32[]{:S(2)}, u32[]{:S(2)}) collective-permute-start(bf16[2,2,2,200,768]{4,3,2,1,0:T(8,128)(2,1)} %pad_maximum_fusion), channel_id=1, source_target_pairs={{0,1},{1,0},{2,3},{3,2},{4,5},{5,4},{6,7},{7,6},{8,9},{9,8},{10,11... | collective-permute-start | bytes 7372808 | tf_op jit(solution)/shard_map/ppermute | solution.py:751
  175.9 111.6 %copy-start.165 = (pred[2]{0:T(512)(128)(4,1)}, pred[2]{0:T(512)(128)(4,1)S(1)}, u32[]{:S(2)}) copy-start(pred[2]{0:T(512)(128)(4,1)S(1)} %iota_compare_fusion.9) | copy-start | bytes 10
  176.2 162.9 %all-gather.10.cloned.1.call-start = ((), (), s32[]{:S(2)}) async-start(), calls=%async_computation.4 | async-start | bytes 2506752 | tf_op jit(solution)/shard_map/all_gather | solution.py:984
  176.2 31.1 %collective-permute-start.12 = (bf16[2,48,1536]{2,1,0:T(8,128)(2,1)}, bf16[2,48,1536]{2,1,0:T(8,128)(2,1)S(1)}, u32[]{:S(2)}, u32[]{:S(2)}) collective-permute-start(bf16[2,48,1536]{2,1,0:T(8,128)(2,1)} %broadcast_select_fusion.14), channel_id=1, source_target_pairs={{0,8},{1,9},{2,10},{3,11},{4,12},{5,13},{6,14},{7,15},{8,0},{9,1},... | collective-permute-start | bytes 884744 | tf_op jit(solution)/shard_map/ppermute | solution.py:751
  178.1 29.3 %collective-permute-start.11 = (bf16[2,2,96,768]{3,2,1,0:T(8,128)(2,1)}, bf16[2,2,96,768]{3,2,1,0:T(8,128)(2,1)S(1)}, u32[]{:S(2)}, u32[]{:S(2)}) collective-permute-start(bf16[2,2,96,768]{3,2,1,0:T(8,128)(2,1)} %dynamic-slice_bitcast_fusion.3), channel_id=1, source_target_pairs={{0,2},{1,3},{2,0},{3,1},{4,6},{5,7},{6,4},{7,5},{8,10},{9,11},{10,... | collective-permute-start | bytes 1769480 | tf_op jit(solution)/shard_map/ppermute | solution.py:751
  225.5 27.0 %collective-permute-start.13 = (bf16[2,96,768]{2,1,0:T(8,128)(2,1)}, bf16[2,96,768]{2,1,0:T(8,128)(2,1)}, u32[]{:S(2)}, u32[]{:S(2)}) collective-permute-start(bf16[2,96,768]{2,1,0:T(8,128)(2,1)} %dynamic-slice_bitcast_fusion.4), channel_id=1, source_target_pairs={{0,8},{1,9},{2,10},{3,11},{4,12},{5,13},{6,14},{7,15},{8,0},{9,1},... | collective-permute-start | bytes 884744 | tf_op jit(solution)/shard_map/ppermute | solution.py:751
  227.0 25.6 %collective-permute-start.14 = (bf16[2,2,48,1536]{3,2,1,0:T(8,128)(2,1)}, bf16[2,2,48,1536]{3,2,1,0:T(8,128)(2,1)}, u32[]{:S(2)}, u32[]{:S(2)}) collective-permute-start(bf16[2,2,48,1536]{3,2,1,0:T(8,128)(2,1)} %broadcast_select_fusion.10), channel_id=1, source_target_pairs={{0,2},{1,3},{2,0},{3,1},{4,6},{5,7},{6,4},{7,5},{8,10},{9,11},{10,... | collective-permute-start | bytes 1769480 | tf_op jit(solution)/shard_map/ppermute | solution.py:751
  255.9 18.6 %collective-permute-start.15 = (bf16[96,768]{1,0:T(8,128)(2,1)S(1)}, bf16[96,768]{1,0:T(8,128)(2,1)S(1)}, u32[]{:S(2)}, u32[]{:S(2)}) collective-permute-start(bf16[96,768]{1,0:T(8,128)(2,1)S(1)} %dynamic-slice_bitcast_fusion.11), channel_id=1, source_target_pairs={{0,4},{1,5},{2,6},{3,7},{4,0},{5,1},{6,2},{7,3},{8,12},{9,13},{10,... | collective-permute-start | bytes 442376 | tf_op jit(solution)/shard_map/ppermute | solution.py:751
  256.5 27.9 %collective-permute-start.16 = (bf16[2,2,2,48,1536]{4,3,2,1,0:T(8,128)(2,1)S(1)}, bf16[2,2,2,48,1536]{4,3,2,1,0:T(8,128)(2,1)S(1)}, u32[]{:S(2)}, u32[]{:S(2)}) collective-permute-start(bf16[2,2,2,48,1536]{4,3,2,1,0:T(8,128)(2,1)S(1)} %broadcast_select_fusion.5), channel_id=1, source_target_pairs={{0,16},{16,0},{1,17},{17,1},{2,18},{18,2},{3,19},{19,3},{4,20},{20... | collective-permute-start | bytes 3538952 | tf_op jit(solution)/shard_map/ppermute | solution.py:745
  287.6 4.9 collective-permute-start.17
  297.4 327.0 %reduce-scatter.3.cloned.1.call-start = ((), (), s32[]{:S(2)}) async-start(), calls=%async_computation.5 | async-start | bytes 10027008 | tf_op jit(solution)/shard_map/reduce_scatter | solution.py:1206
  417.9 295.4 %reduce-scatter.5.cloned.1.call-start = ((), (), s32[]{:S(2)}) async-start(), calls=%async_computation.6 | async-start | bytes 15040512 | tf_op jit(solution)/shard_map/reduce_scatter | solution.py:1265
  448.9 20.1 %collective-permute-start.18 = (bf16[96,768]{1,0:T(8,128)(2,1)S(1)}, bf16[96,768]{1,0:T(8,128)(2,1)S(1)}, u32[]{:S(2)}, u32[]{:S(2)}) collective-permute-start(bf16[96,768]{1,0:T(8,128)(2,1)S(1)} %add_convert_fusion.12), channel_id=1, source_target_pairs={{0,4},{1,5},{2,6},{3,7},{4,0},{5,1},{6,2},{7,3},{8,12},{9,13},{10,... | collective-permute-start | bytes 442376 | tf_op jit(solution)/shard_map/ppermute | solution.py:751
  450.2 19.9 %collective-permute-start.19 = (bf16[96,768]{1,0:T(8,128)(2,1)S(1)}, bf16[96,768]{1,0:T(8,128)(2,1)S(1)}, u32[]{:S(2)}, u32[]{:S(2)}) collective-permute-start(bf16[96,768]{1,0:T(8,128)(2,1)S(1)} %add_convert_fusion.12), channel_id=1, source_target_pairs={{0,8},{1,9},{2,10},{3,11},{4,12},{5,13},{6,14},{7,15},{8,0},{9,1},... | collective-permute-start | bytes 442376 | tf_op jit(solution)/shard_map/ppermute | solution.py:751
  450.8 21.1 %collective-permute-start.20 = (bf16[96,768]{1,0:T(8,128)(2,1)S(1)}, bf16[96,768]{1,0:T(8,128)(2,1)S(1)}, u32[]{:S(2)}, u32[]{:S(2)}) collective-permute-start(bf16[96,768]{1,0:T(8,128)(2,1)S(1)} %add_convert_fusion.12), channel_id=1, source_target_pairs={{0,12},{1,13},{2,14},{3,15},{4,8},{5,9},{6,10},{7,11},{8,4},{9,5},... | collective-permute-start | bytes 442376 | tf_op jit(solution)/shard_map/ppermute | solution.py:751
  473.0 28.9 %collective-permute-start.21 = (bf16[2,2,96,768]{3,2,1,0:T(8,128)(2,1)}, bf16[2,2,96,768]{3,2,1,0:T(8,128)(2,1)}, u32[]{:S(2)}, u32[]{:S(2)}) collective-permute-start(bf16[2,2,96,768]{3,2,1,0:T(8,128)(2,1)} %broadcast_select_fusion.9), channel_id=1, source_target_pairs={{0,16},{16,0},{1,17},{17,1},{2,18},{18,2},{3,19},{19,3},{4,20},{20... | collective-permute-start | bytes 1769480 | tf_op jit(solution)/shard_map/ppermute | solution.py:745
  506.2 37.2 %collective-permute-start.22 = (bf16[2,2,2,96,768]{4,3,2,1,0:T(8,128)(2,1)S(1)}, bf16[2,2,2,96,768]{4,3,2,1,0:T(8,128)(2,1)}, u32[]{:S(2)}, u32[]{:S(2)}) collective-permute-start(bf16[2,2,2,96,768]{4,3,2,1,0:T(8,128)(2,1)S(1)} %broadcast_select_fusion.4), channel_id=1, source_target_pairs={{0,2},{1,3},{2,0},{3,1},{4,6},{5,7},{6,4},{7,5},{8,10},{9,11},{10,... | collective-permute-start | bytes 3538952 | tf_op jit(solution)/shard_map/ppermute | solution.py:751
  547.0 34.9 %collective-permute-start.23 = (bf16[2,2,2,2,96,768]{5,4,3,2,1,0:T(8,128)(2,1)S(1)}, bf16[2,2,2,2,96,768]{5,4,3,2,1,0:T(8,128)(2,1)}, u32[]{:S(2)}, u32[]{:S(2)}) collective-permute-start(bf16[2,2,2,2,96,768]{5,4,3,2,1,0:T(8,128)(2,1)S(1)} %broadcast_select_fusion), channel_id=1, source_target_pairs={{0,1},{1,0},{2,3},{3,2},{4,5},{5,4},{6,7},{7,6},{8,9},{9,8},{10,11... | collective-permute-start | bytes 7077896 | tf_op jit(solution)/shard_map/ppermute | solution.py:751
  547.1 34.9 %collective-permute-start.24 = (bf16[2,2,2,200,768]{4,3,1,0,2:T(8,128)(2,1)}, bf16[2,2,2,200,768]{4,3,1,0,2:T(8,128)(2,1)}, u32[]{:S(2)}, u32[]{:S(2)}) collective-permute-start(bf16[2,2,2,200,768]{4,3,1,0,2:T(8,128)(2,1)} %bitcast.241), channel_id=1, source_target_pairs={{0,1},{1,0},{2,3},{3,2},{4,5},{5,4},{6,7},{7,6},{8,9},{9,8},{10,11... | collective-permute-start | bytes 7372808 | tf_op jit(solution)/shard_map/ppermute | solution.py:751
  585.4 35.4 %collective-permute-start.25 = (bf16[2,2,2,200,384]{4,3,1,0,2:T(8,128)(2,1)}, bf16[2,2,2,200,384]{4,3,1,0,2:T(8,128)(2,1)}, u32[]{:S(2)}, u32[]{:S(2)}) collective-permute-start(bf16[2,2,2,200,384]{4,3,1,0,2:T(8,128)(2,1)} %constant_dynamic-slice_fusion.12), channel_id=1, source_target_pairs={{0,16},{16,0},{1,17},{17,1},{2,18},{18,2},{3,19},{19,3},{4,20},{20... | collective-permute-start | bytes 3686408 | tf_op jit(solution)/shard_map/ppermute | solution.py:745
  624.5 26.4 %collective-permute-start.26 = (bf16[768,1536]{1,0:T(8,128)(2,1)}, bf16[768,1536]{1,0:T(8,128)(2,1)}, u32[]{:S(2)}, u32[]{:S(2)}) collective-permute-start(bf16[768,1536]{1,0:T(8,128)(2,1)} %pad_maximum_fusion.3), channel_id=1, source_target_pairs={{0,1},{1,0},{2,3},{3,2},{4,5},{5,4},{6,7},{7,6},{8,9},{9,8},{10,11... | collective-permute-start | bytes 7077896 | tf_op jit(solution)/shard_map/ppermute | solution.py:751
  634.9 16.0 %collective-permute-start.27 = (bf16[48,6144]{1,0:T(8,128)(2,1)}, bf16[48,6144]{1,0:T(8,128)(2,1)S(1)}, u32[]{:S(2)}, u32[]{:S(2)}) collective-permute-start(bf16[48,6144]{1,0:T(8,128)(2,1)} %reduce-scatter.3.cloned.1.call-done), channel_id=1, source_target_pairs={{0,16},{16,0},{1,17},{17,1},{2,18},{18,2},{3,19},{19,3},{4,20},{20... | collective-permute-start | bytes 1769480 | tf_op jit(solution)/shard_map/ppermute | solution.py:745
  635.6 48.7 %collective-permute-start.30 = (bf16[2,2,200,384]{3,2,1,0:T(8,128)(2,1)}, bf16[2,2,200,384]{3,2,1,0:T(8,128)(2,1)}, u32[]{:S(2)}, u32[]{:S(2)}) collective-permute-start(bf16[2,2,200,384]{3,2,1,0:T(8,128)(2,1)} %dynamic-slice_bitcast_fusion.1), channel_id=1, source_target_pairs={{0,2},{1,3},{2,0},{3,1},{4,6},{5,7},{6,4},{7,5},{8,10},{9,11},{10,... | collective-permute-start | bytes 1843208 | tf_op jit(solution)/shard_map/ppermute | solution.py:751
  654.5 29.8 %collective-permute-start.29 = (bf16[768,128]{1,0:T(8,128)(2,1)}, bf16[768,128]{1,0:T(8,128)(2,1)S(1)}, u32[]{:S(2)}, u32[]{:S(2)}) collective-permute-start(bf16[768,128]{1,0:T(8,128)(2,1)} %get-tuple-element.425), channel_id=1, source_target_pairs={{0,1},{1,0},{2,3},{3,2},{4,5},{5,4},{6,7},{7,6},{8,9},{9,8},{10,11... | collective-permute-start | bytes 589832 | tf_op jit(solution)/shard_map/ppermute | solution.py:751
  655.1 29.2 %collective-permute-start.28 = (bf16[2,2,2,2,24,1536]{5,4,3,2,1,0:T(8,128)(2,1)}, bf16[2,2,2,2,24,1536]{5,4,3,2,1,0:T(8,128)(2,1)}, u32[]{:S(2)}, u32[]{:S(2)}) collective-permute-start(bf16[2,2,2,2,24,1536]{5,4,3,2,1,0:T(8,128)(2,1)} %dynamic-slice_bitcast_fusion), channel_id=1, source_target_pairs={{0,16},{16,0},{1,17},{17,1},{2,18},{18,2},{3,19},{19,3},{4,20},{20... | collective-permute-start | bytes 3538952 | tf_op jit(solution)/shard_map/ppermute | solution.py:745
  655.7 45.2 %copy-start.12 = (f32[48,6144]{1,0:T(8,128)}, f32[48,6144]{1,0:T(8,128)S(1)}, u32[]{:S(2)}) copy-start(f32[48,6144]{1,0:T(8,128)S(1)} %convert_add_fusion.7.refs_0_) | copy-start | bytes 3538948
  690.0 13.1 %collective-permute-start.32 = (bf16[2,2,2,2,24,128]{5,4,3,1,0,2:T(8,128)(2,1)S(1)}, bf16[2,2,2,2,24,128]{5,4,3,1,0,2:T(8,128)(2,1)S(1)}, u32[]{:S(2)}, u32[]{:S(2)}) collective-permute-start(bf16[2,2,2,2,24,128]{5,4,3,1,0,2:T(8,128)(2,1)S(1)} %bitcast.289), channel_id=1, source_target_pairs={{0,16},{16,0},{1,17},{17,1},{2,18},{18,2},{3,19},{19,3},{4,20},{20... | collective-permute-start | bytes 294920 | tf_op jit(solution)/shard_map/ppermute | solution.py:745
  691.7 14.7 %collective-permute-start.31 = (bf16[2,2,2,24,1536]{4,3,2,1,0:T(8,128)(2,1)}, bf16[2,2,2,24,1536]{4,3,2,1,0:T(8,128)(2,1)}, u32[]{:S(2)}, u32[]{:S(2)}) collective-permute-start(bf16[2,2,2,24,1536]{4,3,2,1,0:T(8,128)(2,1)} %dynamic-slice_bitcast_fusion.2), channel_id=1, source_target_pairs={{0,2},{1,3},{2,0},{3,1},{4,6},{5,7},{6,4},{7,5},{8,10},{9,11},{10,... | collective-permute-start | bytes 1769480 | tf_op jit(solution)/shard_map/ppermute | solution.py:751
  713.3 30.1 %collective-permute-start.37 = (bf16[48,9216]{1,0:T(8,128)(2,1)}, bf16[48,9216]{1,0:T(8,128)(2,1)}, u32[]{:S(2)}, u32[]{:S(2)}) collective-permute-start(bf16[48,9216]{1,0:T(8,128)(2,1)} %reduce-scatter.5.cloned.1.call-done), channel_id=1, source_target_pairs={{0,16},{16,0},{1,17},{17,1},{2,18},{18,2},{3,19},{19,3},{4,20},{20... | collective-permute-start | bytes 2654216 | tf_op jit(solution)/shard_map/ppermute | solution.py:745
  715.5 8.2 collective-permute-start.38
  717.7 14.6 %collective-permute-start.39 = (bf16[200,384]{1,0:T(8,128)(2,1)S(1)}, bf16[200,384]{1,0:T(8,128)(2,1)S(1)}, u32[]{:S(2)}, u32[]{:S(2)}) collective-permute-start(bf16[200,384]{1,0:T(8,128)(2,1)S(1)} %copy-done.78), channel_id=1, source_target_pairs={{0,8},{1,9},{2,10},{3,11},{4,12},{5,13},{6,14},{7,15},{8,0},{9,1},... | collective-permute-start | bytes 460808 | tf_op jit(solution)/shard_map/ppermute | solution.py:751
  718.3 16.7 %collective-permute-start.40 = (bf16[200,384]{1,0:T(8,128)(2,1)S(1)}, bf16[200,384]{1,0:T(8,128)(2,1)S(1)}, u32[]{:S(2)}, u32[]{:S(2)}) collective-permute-start(bf16[200,384]{1,0:T(8,128)(2,1)S(1)} %copy-done.77), channel_id=1, source_target_pairs={{0,12},{1,13},{2,14},{3,15},{4,8},{5,9},{6,10},{7,11},{8,4},{9,5},... | collective-permute-start | bytes 460808 | tf_op jit(solution)/shard_map/ppermute | solution.py:751
  721.2 18.0 %collective-permute-start.33 = (bf16[2,24,1536]{2,1,0:T(8,128)(2,1)}, bf16[2,24,1536]{2,1,0:T(8,128)(2,1)}, u32[]{:S(2)}, u32[]{:S(2)}) collective-permute-start(bf16[2,24,1536]{2,1,0:T(8,128)(2,1)} %get-tuple-element.452), channel_id=1, source_target_pairs={{0,4},{1,5},{2,6},{3,7},{4,0},{5,1},{6,2},{7,3},{8,12},{9,13},{10,... | collective-permute-start | bytes 442376 | tf_op jit(solution)/shard_map/ppermute | solution.py:751
  723.8 19.6 %collective-permute-start.34 = (bf16[2,24,1536]{2,1,0:T(8,128)(2,1)}, bf16[2,24,1536]{2,1,0:T(8,128)(2,1)}, u32[]{:S(2)}, u32[]{:S(2)}) collective-permute-start(bf16[2,24,1536]{2,1,0:T(8,128)(2,1)} %get-tuple-element.453), channel_id=1, source_target_pairs={{0,8},{1,9},{2,10},{3,11},{4,12},{5,13},{6,14},{7,15},{8,0},{9,1},... | collective-permute-start | bytes 442376 | tf_op jit(solution)/shard_map/ppermute | solution.py:751
  732.3 11.0 %collective-permute-start.35 = (bf16[2,24,1536]{2,1,0:T(8,128)(2,1)S(1)}, bf16[2,24,1536]{2,1,0:T(8,128)(2,1)S(1)}, u32[]{:S(2)}, u32[]{:S(2)}) collective-permute-start(bf16[2,24,1536]{2,1,0:T(8,128)(2,1)S(1)} %get-tuple-element.454), channel_id=1, source_target_pairs={{0,12},{1,13},{2,14},{3,15},{4,8},{5,9},{6,10},{7,11},{8,4},{9,5},... | collective-permute-start | bytes 442376 | tf_op jit(solution)/shard_map/ppermute | solution.py:751
  735.0 4.1 collective-permute-start.36
  748.3 9.1 %collective-permute-start.44 = (bf16[2,24,128]{2,1,0:T(8,128)(2,1)S(1)}, bf16[2,24,128]{2,1,0:T(8,128)(2,1)S(1)}, u32[]{:S(2)}, u32[]{:S(2)}) collective-permute-start(bf16[2,24,128]{2,1,0:T(8,128)(2,1)S(1)} %get-tuple-element.474), channel_id=1, source_target_pairs={{0,4},{1,5},{2,6},{3,7},{4,0},{5,1},{6,2},{7,3},{8,12},{9,13},{10,... | collective-permute-start | bytes 36872 | tf_op jit(solution)/shard_map/ppermute | solution.py:751
  750.7 7.4 collective-permute-start.45
  754.3 7.5 collective-permute-start.46
  756.2 5.6 collective-permute-start.41
  756.2 5.6 collective-permute-start.42
  757.4 4.7 collective-permute-start.43
  758.1 7.7 collective-permute-start.47
  807.0 30.8 %copy-start.62 = (f32[200,768]{1,0:T(8,128)S(1)}, f32[200,768]{1,0:T(8,128)}, u32[]{:S(2)}) copy-start(f32[200,768]{1,0:T(8,128)} %param.43) | copy-start | bytes 1843204
  807.0 30.8 %copy-start.65 = (bf16[200,384]{1,0:T(8,128)(2,1)S(1)}, bf16[200,384]{1,0:T(8,128)(2,1)}, u32[]{:S(2)}) copy-start(bf16[200,384]{1,0:T(8,128)(2,1)} %copy-done.64) | copy-start | bytes 460804
  807.0 30.8 %copy-start.67 = (bf16[200,384]{1,0:T(8,128)(2,1)S(1)}, bf16[200,384]{1,0:T(8,128)(2,1)}, u32[]{:S(2)}) copy-start(bf16[200,384]{1,0:T(8,128)(2,1)} %copy-done.66) | copy-start | bytes 460804
  807.0 30.8 %copy-start.76 = (bf16[1,8,2,2,24,128]{5,4,3,2,1,0:T(8,128)(2,1)S(1)}, bf16[1,8,2,2,24,128]{5,4,3,2,1,0:T(8,128)(2,1)}, u32[]{:S(2)}) copy-start(bf16[1,8,2,2,24,128]{5,4,3,2,1,0:T(8,128)(2,1)} %slice.328) | copy-start | bytes 589828
  807.0 30.8 %copy-start.187 = (f32[200,768]{1,0:T(8,128)S(1)}, f32[200,768]{1,0:T(8,128)}, u32[]{:S(2)}) copy-start(f32[200,768]{1,0:T(8,128)} %param.44) | copy-start | bytes 1843204
  807.0 30.8 %copy-start.188 = (f32[200,768]{1,0:T(8,128)S(1)}, f32[200,768]{1,0:T(8,128)}, u32[]{:S(2)}) copy-start(f32[200,768]{1,0:T(8,128)} %param.45) | copy-start | bytes 1843204
  (187 other events, 1278.1 us)
Sparse Core Ops, SparseCore 0:
  14.0 113.2 all-gather.11
  129.6 95.8 all-gather.5
  227.8 54.4 all-gather.7
  297.5 41.4 all-gather.9
  418.1 133.7 reduce-scatter.2
  556.5 156.8 reduce-scatter.4

commit v5 on v4

--- a/solution.py
+++ b/solution.py
@@ -365,7 +365,7 @@
 
 def adam_mixing(factor, pieces, master, first, second, features):
     towers, rows, width = master.shape
-    block = rows // 3 if rows % 24 == 0 else rows
+    block = rows
     spec = pl.BlockSpec((1, block, width), lambda r, t: (t, r, 0))
     return pl.pallas_call(
         functools.partial(adam_kernel, gradient_runs(features, width)),
@@ -1268,7 +1268,9 @@
         made, _ = outward_backward(1, slope)
         return patch_grads(video, entry, embed_rows), made
 
-    grad_embed, made_audio = links.stage([word_flow], video_entry, (entry, own_slopes[1]))
+    grad_embed, made_audio = links.stage(
+        [], video_entry, (entry, own_slopes[1]), [word_flow]
+    )
     embed_flow = Flow(links.scatter_rows(grad_embed, ("y", "x")))
 
     def audio_pairs(grad_mixed, *bounds):
@@ -1283,7 +1285,7 @@
         )
 
     first_pairs = links.stage(
-        [word_flow, embed_flow], lambda part: audio_pairs(part, 0, pairs // 2), (made_audio[2],)
+        [embed_flow], lambda part: audio_pairs(part, 0, pairs // 2), (made_audio[2],)
     )
 
     def audio_inner(grad_mixed, first_pairs):
@@ -1302,7 +1304,7 @@
         return grad_joined, sides
 
     joined_audio, audio_sides = links.stage(
-        [embed_flow], audio_inner, (made_audio[2], first_pairs)
+        [embed_flow, word_flow], audio_inner, (made_audio[2], first_pairs)
     )
     audio_flow = Flow(links.scatter_columns(*audio_sides, ("y", "x")))
 
@@ -1328,7 +1330,7 @@
         )
 
     up_flow = Flow(links.sum_replicas(up_part))
-    beside = links.stage([audio_flow, up_flow], audio_entry, (joined_audio,), [embed_flow])
+    beside = links.stage([audio_flow], audio_entry, (joined_audio,), [embed_flow, up_flow])
     beside_flow = Flow(links.reduce_columns(*beside, ("y", "x")))
     rest = [audio_flow, beside_flow]
     table_grad = links.stage(rest, scatter_table, (word_flow.value,))

time: 869 us -> 872 us (level)
  waiting for transfers between devices: 137 us -> 113 us
  Pallas kernels: 254 us -> 263 us
    pallas_call x3, Pallas kernels: 38.2 us -> 48.6 us  [feed(): pl.pallas_call(functools.partial(feed_kernel, with_product), grid=(width...]
    all_gather x4, waiting for transfers between devices: 20 us -> 11.1 us  [gather(): return lax.all_gather(values, 'fsdp', axis=0, tiled=True)]
    unnamed x394 -> x402, local copies, waits for them, and re-layouts: 21.4 us -> 24.7 us
  transfers between devices with their start and end apart: 54 -> 54, of which waited for: 22 -> 19; matrix products, arithmetic and copies ran while one was open for 36% -> 37% of each run, Pallas kernels for 17% -> 18%
where the time goes in v5:
time: 872 us; the launch traced here: 864 us
  Pallas kernels  263 us (30%)
  other arithmetic  200 us (23%)
  waiting for transfers between devices  113 us (13%)
  matrix products  107 us (12%)
  local copies, waits for them, and re-layouts  95.5 us (11%)
  starting transfers between devices  59.7 us (7%)
  between operations  26.2 us (3%)
    ppermute x37, waiting for transfers between devices, swap(): lax.ppermute(values, 'fsdp', [(f, f ^ bit) for f in range(self.group)])  83.5 us
    pallas_call x1, Pallas kernels, contrast(): pl.pallas_call(functools.partial(middle_kernel, scales, captions), out_sh...  62 us
    pallas_call x4, Pallas kernels, attend_back(): pl.pallas_call(kernel, grid=(pairs,), out_shape=jax.ShapeDtypeStruct(qkv....  54.3 us
    pallas_call x3, Pallas kernels, feed(): pl.pallas_call(functools.partial(feed_kernel, with_product), grid=(width...  48.6 us
    dot_general x9, matrix products, dot_nt(): return lax.dot_general(a, b, NT, preferred_element_type=F32)  46.6 us
    ppermute x37, starting transfers between devices, swap(): lax.ppermute(values, 'fsdp', [(f, f ^ bit) for f in range(self.group)])  46.2 us
    sub x5, other arithmetic, adam_update(): master - rate * (first_hat / (jnp.sqrt(second_hat) + EPSILON) + WEIGHT_DE...  39.8 us
    pallas_call x3, Pallas kernels, attend(): pl.pallas_call(functools.partial(attend_kernel, rows, block, bias is not...  36.3 us
  transfers between devices with their start and end apart: 54, of which 19 were waited for; matrix products, arithmetic and copies ran while one was open for 37% of the time, Pallas kernels for 18%

profile of v5, /device:TPU:0, one launch (start us, length us, event | category | flops | bytes accessed | tf_op | source)
XLA Modules:
  0.0 863.6 jit_solution(9276543781648048900)
XLA Ops:
  7.3 4.0 regroup.1
  14.0 3.1 collective-permute-start
  23.0 12.1 %everyone_0.1 = f32[32,8,128]{2,1,0:T(8,128)} custom-call(f32[8,128]{1,0:T(8,128)} %pad_bitcast_fusion.x_ref), custom_call_target="tpu_custom_call" | custom-call | tf_op jit(solution)/shard_map/everyone_0/pallas_call | solution.py:127
  42.4 10.7 %gather_fusion = bf16[1536,768]{1,0:T(8,128)(2,1)S(1)} fusion(f32[4096,768]{1,0:T(8,128)} %param.46, s32[2048]{0:T(1024)S(1)} %pad_clamp_fusion), kind=kCustom, calls=%fused_computation | custom fusion | bytes 4724736 | tf_op jit(solution)/shard_map/gather | solution.py:1011
  55.0 9.0 %collective-permute-done.2 = bf16[2,200,384]{2,1,0:T(8,128)(2,1)} collective-permute-done((bf16[2,200,384]{2,1,0:T(8,128)(2,1)S(1)}, bf16[2,200,384]{2,1,0:T(8,128)(2,1)}, u32[]{:S(2)}, u32[]{:S(2)}) %collective-permute-start.2) | collective-permute-done | bytes 307232 | tf_op jit(solution)/shard_map/ppermute | solution.py:751
  72.3 15.3 %collective-permute-done.5 = bf16[128,768]{1,0:T(8,128)(2,1)S(1)} collective-permute-done((bf16[128,768]{1,0:T(8,128)(2,1)S(1)}, bf16[128,768]{1,0:T(8,128)(2,1)S(1)}, u32[]{:S(2)}, u32[]{:S(2)}) %collective-permute-start.5) | collective-permute-done | bytes 196640 | tf_op jit(solution)/shard_map/ppermute | solution.py:751
  87.6 10.8 %collective-permute-done.4 = bf16[2,2,200,384]{3,2,1,0:T(8,128)(2,1)S(1)} collective-permute-done((bf16[2,2,200,384]{3,2,1,0:T(8,128)(2,1)S(1)}, bf16[2,2,200,384]{3,2,1,0:T(8,128)(2,1)S(1)}, u32[]{:S(2)}, u32[]{:S(2)}) %collective-permute-start.4) | collective-permute-done | bytes 614432 | tf_op jit(solution)/shard_map/ppermute | solution.py:751
  101.9 18.7 %collective-permute-done.6 = bf16[128,768]{1,0:T(8,128)(2,1)} collective-permute-done((bf16[128,768]{1,0:T(8,128)(2,1)S(1)}, bf16[128,768]{1,0:T(8,128)(2,1)}, u32[]{:S(2)}, u32[]{:S(2)}) %collective-permute-start.6) | collective-permute-done | bytes 196640 | tf_op jit(solution)/shard_map/ppermute | solution.py:751
  122.1 5.2 all-gather.12.cloned.1.call-done
  128.7 2.8 constant_dynamic-slice_fusion.19
  140.2 7.4 convolution_convert_fusion.refs_0_
  147.6 21.9 %attend_1024.1 = (bf16[1024,768]{1,0:T(8,128)(2,1)}, f32[1024,768]{1,0:T(8,128)}) custom-call(bf16[1024,2304]{1,0:T(8,128)(2,1)} %convolution_convert_fusion.refs_0_), custom_call_target="tpu_custom_call" | custom-call | flops 805306368 | bytes 786432 | tf_op jit(solution)/shard_map/attend_1024/pallas_call | solution.py:188
  179.8 3.2 fusion.169
  186.1 30.4 %feed_1024.1 = (bf16[1024,3072]{1,0:T(8,128)(2,1)}, f32[8,3072]{1,0:T(8,128)}, bf16[768,3072]{1,0:T(8,128)(2,1)}) custom-call(bf16[1024,768]{1,0:T(8,128)(2,1)} %add_convert_fusion.2.h_ref, bf16[768,6144]{1,0:T(8,128)(2,1)} %bitcast.260, bf16[8,128]{1,0:T(8,128)(2,1)} %broadcast_in_dim.558.sel_ref), custom_call_target="tpu_custom_call" | custom-call | flops 301989888 | bytes 3145728 | tf_op jit(solution)/shard_map/feed_1024/pallas_call | solution.py:666
  216.6 5.4 bitcast_select_fusion
  228.9 3.8 fusion.170
  232.7 3.1 copy.174
  238.9 5.4 convolution_convert_fusion.5.refs_0_
  244.3 8.3 attend_512.1
  262.5 12.0 %feed_512.1 = (bf16[512,3072]{1,0:T(8,128)(2,1)}, f32[8,3072]{1,0:T(8,128)}, bf16[768,3072]{1,0:T(8,128)(2,1)}) custom-call(bf16[512,768]{1,0:T(8,128)(2,1)} %add_convert_fusion.7.h_ref, bf16[768,6144]{1,0:T(8,128)(2,1)} %all-gather.6.cloned.1.call-done.w_ref, bf16[8,128]{1,0:T(8,128)(2,1)} %broadcast_in_dim.558.sel_ref), custom_call_target="tpu_custom_call" | custom-call | flops 150994944 | bytes 1572864 | tf_op jit(solution)/shard_map/feed_512/pallas_call | solution.py:666
  274.4 10.0 %collective-permute-done.16 = bf16[2,2,2,48,1536]{4,3,2,1,0:T(8,128)(2,1)S(1)} collective-permute-done((bf16[2,2,2,48,1536]{4,3,2,1,0:T(8,128)(2,1)S(1)}, bf16[2,2,2,48,1536]{4,3,2,1,0:T(8,128)(2,1)S(1)}, u32[]{:S(2)}, u32[]{:S(2)}) %collective-permute-start.16) | collective-permute-done | bytes 1179680 | tf_op jit(solution)/shard_map/ppermute | solution.py:745
  287.8 4.7 collective-permute-done.17
  292.5 5.0 bitcast_select_fusion.2.w_ref
  301.0 3.1 multiply_reduce_fusion.6
  313.0 3.5 convolution_convert_fusion.6.refs_0_
  316.5 6.1 attend_96.1
  325.5 6.2 feed_96.1
  334.2 5.1 all-gather.10.cloned.1.call-done
  341.0 2.9 slice.316.heads_ref
  344.0 62.0 %middle.1 = (f32[8,128]{1,0:T(8,128)}, f32[32,768]{1,0:T(8,128)}, f32[32,768]{1,0:T(8,128)}, f32[96,768]{1,0:T(8,128)}, f32[8,768]{1,0:T(8,128)}, /*index=5*/f32...) custom-call(f32[8,3072]{1,0:T(8,128)} %pad_maximum_fusion.9.sum_ref,, ...), custom_call_target="tpu_custom_call" | custom-call | tf_op jit(solution)/shard_map/middle/pallas_call | solution.py:609
  409.2 8.9 %scale_columns.1 = bf16[768,6144]{1,0:T(8,128)(2,1)} custom-call(bf16[768,3072]{1,0:T(8,128)(2,1)} %get-tuple-element.350.first_ref, bf16[768,3072]{1,0:T(8,128)(2,1)} %get-tuple-element.351.second_ref, f32[2,3072]{1,0:T(2,128)} %pad_maximum_fusion.11.slopes_ref), custom_call_target="tpu_custom_call" | custom-call | tf_op jit(solution)/shard_map/scale_columns/pallas_call | solution.py:394
  426.8 5.1 multiply_reduce_fusion.21
  432.5 2.6 convolution_convert_fusion.12.refs_1_
  435.1 5.8 attend_back_96_0.1
  440.9 4.0 fusion.152
  450.9 2.6 collective-permute-start.20
  458.8 3.5 multiply_reduce_fusion.14
  474.3 11.4 %attend_back_512_0.1 = bf16[512,2304]{1,0:T(8,128)(2,1)} custom-call(bf16[512,2304]{1,0:T(8,128)(2,1)} %convolution_convert_fusion.5.refs_0_, bf16[512,768]{1,0:T(8,128)(2,1)} %convolution_convert_fusion.11.refs_1_, bf16[512,768]{1,0:T(8,128)(2,1)} %get-tuple-element.322.refs_2_, f32[512,768]{1,0:T(8,128)} %get-tuple-element.375.refs_3_), custom_call_target="tpu_custom_call" | custom-call | flops 402653184 | bytes 393216 | tf_op jit(solution)/shard_map/attend_back_512_0/pallas_call | solution.py:281
  485.7 5.6 multiply_reduce_fusion.11
  493.8 3.9 fusion.5
  498.8 3.0 add_convert_fusion.6.entry_ref
  505.7 7.1 patch_grads.1
  512.9 9.9 %multiply_reduce_fusion.4 = (bf16[768]{0:T(1024)(128)(2,1)}, f32[1024]{0:T(1024)S(1)}, bf16[768]{0:T(1024)(128)(2,1)}, f32[1024,768]{1,0:T(8,128)S(1)}) fusion(f32[1024,768]{1,0:T(8,128)S(1)} %copy-done.2, f32[1024]{0:T(1024)S(1)} %fusion.132, f32[1024]{0:T(1024)S(1)} %copy-done.105, f32[768]{0:T(1024)S(1)} %copy-done.111, ...), kind=kOutput, calls=%fused_computation.52 | convolution fusion | flops 4845204480 | bytes 17332224 | tf_op jit(solution)/shard_map/dot_general | solution.py:31
  524.9 4.9 convolution_convert_fusion.7.refs_1_
  542.5 18.6 %attend_back_1024_0.1.refs_4_ = bf16[1024,2304]{1,0:T(8,128)(2,1)} custom-call(bf16[1024,2304]{1,0:T(8,128)(2,1)} %convolution_convert_fusion.refs_0_, bf16[1024,768]{1,0:T(8,128)(2,1)} %convolution_convert_fusion.7.refs_1_, bf16[1024,768]{1,0:T(8,128)(2,1)} %get-tuple-element.296.refs_2_, f32[1024,768]{1,0:T(8,128)} %get-tuple-element.391.refs_3_), custom_call_target="tpu_custom_call" | custom-call | flops 805306368 | bytes 393216 | tf_op jit(solution)/shard_map/attend_back_1024_0/pallas_call | solution.py:281
  561.1 4.3 collective-permute-done.23
  566.5 2.7 fusion.6
  582.2 18.5 %attend_back_1024_3.1 = bf16[1024,2304]{1,0:T(8,128)(2,1)} custom-call(bf16[1024,2304]{1,0:T(8,128)(2,1)} %convolution_convert_fusion.refs_0_, bf16[1024,768]{1,0:T(8,128)(2,1)} %convolution_convert_fusion.7.refs_1_, bf16[1024,768]{1,0:T(8,128)(2,1)} %get-tuple-element.296.refs_2_, ...), custom_call_target="tpu_custom_call", output_to_operand_aliasing={{}: (4, {})} | custom-call | flops 805306368 | bytes 393216 | tf_op jit(solution)/shard_map/attend_back_1024_3/pallas_call | solution.py:281
  600.7 6.7 convolution_convert_fusion.1
  611.7 4.4 bitcast_select_fusion.1
  619.8 9.3 %multiply_reduce_fusion.1 = (bf16[768]{0:T(1024)(128)(2,1)S(1)}, f32[1024]{0:T(1024)S(1)}, bf16[768]{0:T(1024)(128)(2,1)S(1)}, f32[1024,768]{1,0:T(8,128)}) fusion(f32[1024,768]{1,0:T(8,128)S(1)} %convolution_bitcast_fusion, f32[1024]{0:T(1024)} %fusion.133, f32[1024]{0:T(1024)} %copy-done.106, f32[768]{0:T(1024)} %get-tuple-element.527, ...), kind=kOutput, calls=%fused_computation.48 | convolution fusion | flops 3630167552 | bytes 14568448 | tf_op jit(solution)/shard_map/dot_general | solution.py:31
  630.2 3.2 fusion.160
  646.4 29.3 %scatter_custom_fusion = f32[4096,768]{1,0:T(8,128)} fusion(s32[3072]{0:T(1024)} %min.25, bf16[3072,768]{1,0:T(8,128)(2,1)} %bitcast_select_fusion.1, f32[]{:T(128)} %constant.411.clone.1, pred[3072]{0:T(1024)(128)(4,1)S(1)} %copy-done.134), kind=kCustom, calls=%fused_computation.6 | custom fusion | flops 7077888 | bytes 17305600 | tf_op jit(solution)/shard_map/scatter-add | solution.py:1312
  675.8 4.3 collective-permute-done.30
  691.7 8.5 multiply_reduce_fusion
  702.4 3.7 collective-permute-done.31
  710.5 11.4 %collective-permute-start.38 = (bf16[200,384]{1,0:T(8,128)(2,1)}, bf16[200,384]{1,0:T(8,128)(2,1)S(1)}, u32[]{:S(2)}, u32[]{:S(2)}) collective-permute-start(bf16[200,384]{1,0:T(8,128)(2,1)} %get-tuple-element.457), channel_id=1, source_target_pairs={{0,4},{1,5},{2,6},{3,7},{4,0},{5,1},{6,2},{7,3},{8,12},{9,13},{10,... | collective-permute-start | bytes 460808 | tf_op jit(solution)/shard_map/ppermute | solution.py:751
  728.8 7.8 collective-permute-done.39
  742.5 4.9 collective-permute-done.34
  766.1 3.5 collective-permute-done.47
  778.0 18.0 %everyone_2.1 = bf16[32,64,128]{2,1,0:T(8,128)(2,1)} custom-call(bf16[64,128]{1,0:T(8,128)(2,1)} %pad_maximum_fusion.12.x_ref), custom_call_target="tpu_custom_call" | custom-call | tf_op jit(solution)/shard_map/everyone_2/pallas_call | solution.py:127
  805.7 5.4 multiply_subtract_fusion.1
  811.1 30.1 %multiply_subtract_fusion = (f32[4096,768]{1,0:T(8,128)}, f32[4096,768]{1,0:T(8,128)}, f32[4096,768]{1,0:T(8,128)}) fusion(f32[4096,768]{1,0:T(8,128)} %param.46, f32[4096,768]{1,0:T(8,128)} %param.47, f32[4096,768]{1,0:T(8,128)} %param.48, f32[4096,768]{1,0:T(8,128)} %scatter_custom_fusion, f32[]{:T(128)} %div.352), kind=kLoop, calls=%fused_computation.4 | loop fusion | flops 50331648 | bytes 88080384 | tf_op jit(solution)/shard_map/sub | solution.py:68
  843.9 11.5 %adam_mixing.1 = (f32[3,48,6144]{2,1,0:T(8,128)}, f32[3,48,6144]{2,1,0:T(8,128)}, f32[3,48,6144]{2,1,0:T(8,128)}) custom-call(f32[1]{0:T(128)} %bitcast.78.scal_ref, f32[48,6144]{1,0:T(8,128)} %copy-done.11, f32[48,9216]{1,0:T(8,128)} %convert_add_fusion.3.refs_1_, f32[48,3072]{1,0:T(8,128)} %fusion.68.refs_2_, f32[3,48,6144]{2,1,0:T(8,128)} %refs_3_.1, ...), custom_call_target="tpu_custom_call" | custom-call | tf_op jit(solution)/shard_map/adam_mixing/pallas_call | solution.py:370
  (783 shorter events, 251.6 us)
Async XLA Ops:
  7.2 113.4 %copy-start = (bf16[1,1024,128]{2,1,0:T(8,128)(2,1)S(1)}, bf16[1,1024,128]{2,1,0:T(8,128)(2,1)}, u32[]{:S(2)}) copy-start(bf16[1,1024,128]{2,1,0:T(8,128)(2,1)} %param.29) | copy-start | bytes 786436
  7.2 120.1 %all-gather.12.cloned.1.call-start = ((), (), s32[]{:S(2)}) async-start(), calls=%async_computation.7 | async-start | bytes 10027008 | tf_op jit(solution)/shard_map/all_gather | solution.py:984
  13.9 211.7 %all-gather.6.cloned.1.call-start = ((), (), s32[]{:S(2)}) async-start(), calls=%async_computation.2 | async-start | bytes 10027008 | tf_op jit(solution)/shard_map/all_gather | solution.py:984
  14.0 22.0 %collective-permute-start = (bf16[200,384]{1,0:T(8,128)(2,1)S(1)}, bf16[200,384]{1,0:T(8,128)(2,1)}, u32[]{:S(2)}, u32[]{:S(2)}) collective-permute-start(bf16[200,384]{1,0:T(8,128)(2,1)S(1)} %constant_dynamic-slice_fusion.21), channel_id=1, source_target_pairs={{0,4},{1,5},{2,6},{3,7},{4,0},{5,1},{6,2},{7,3},{8,12},{9,13},{10,... | collective-permute-start | bytes 460808 | tf_op jit(solution)/shard_map/ppermute | solution.py:751
  17.1 18.9 %collective-permute-start.1 = (bf16[128,768]{1,0:T(8,128)(2,1)S(1)}, bf16[128,768]{1,0:T(8,128)(2,1)}, u32[]{:S(2)}, u32[]{:S(2)}) collective-permute-start(bf16[128,768]{1,0:T(8,128)(2,1)S(1)} %slice.306), channel_id=1, source_target_pairs={{0,1},{1,0},{2,3},{3,2},{4,5},{5,4},{6,7},{7,6},{8,9},{9,8},{10,11... | collective-permute-start | bytes 589832 | tf_op jit(solution)/shard_map/ppermute | solution.py:751
  38.5 16.5 %collective-permute-start.3 = (bf16[128,768]{1,0:T(8,128)(2,1)S(1)}, bf16[128,768]{1,0:T(8,128)(2,1)}, u32[]{:S(2)}, u32[]{:S(2)}) collective-permute-start(bf16[128,768]{1,0:T(8,128)(2,1)S(1)} %broadcast_select_fusion.17), channel_id=1, source_target_pairs={{0,2},{1,3},{2,0},{3,1},{4,6},{5,7},{6,4},{7,5},{8,10},{9,11},{10,... | collective-permute-start | bytes 589832 | tf_op jit(solution)/shard_map/ppermute | solution.py:751
  40.5 23.5 %collective-permute-start.2 = (bf16[2,200,384]{2,1,0:T(8,128)(2,1)S(1)}, bf16[2,200,384]{2,1,0:T(8,128)(2,1)}, u32[]{:S(2)}, u32[]{:S(2)}) collective-permute-start(bf16[2,200,384]{2,1,0:T(8,128)(2,1)S(1)} %broadcast_select_fusion.11), channel_id=1, source_target_pairs={{0,8},{1,9},{2,10},{3,11},{4,12},{5,13},{6,14},{7,15},{8,0},{9,1},... | collective-permute-start | bytes 921608 | tf_op jit(solution)/shard_map/ppermute | solution.py:751
  66.2 35.7 %copy-start.23 = (bf16[2,2,200,384]{3,2,1,0:T(8,128)(2,1)}, bf16[2,2,200,384]{3,2,1,0:T(8,128)(2,1)S(1)}, u32[]{:S(2)}) copy-start(bf16[2,2,200,384]{3,2,1,0:T(8,128)(2,1)S(1)} %broadcast_select_fusion.8) | copy-start | bytes 1843204
  68.2 19.4 %collective-permute-start.5 = (bf16[128,768]{1,0:T(8,128)(2,1)S(1)}, bf16[128,768]{1,0:T(8,128)(2,1)S(1)}, u32[]{:S(2)}, u32[]{:S(2)}) collective-permute-start(bf16[128,768]{1,0:T(8,128)(2,1)S(1)} %broadcast_select_fusion.16), channel_id=1, source_target_pairs={{0,4},{1,5},{2,6},{3,7},{4,0},{5,1},{6,2},{7,3},{8,12},{9,13},{10,... | collective-permute-start | bytes 589832 | tf_op jit(solution)/shard_map/ppermute | solution.py:751
  68.9 29.4 %collective-permute-start.4 = (bf16[2,2,200,384]{3,2,1,0:T(8,128)(2,1)S(1)}, bf16[2,2,200,384]{3,2,1,0:T(8,128)(2,1)S(1)}, u32[]{:S(2)}, u32[]{:S(2)}) collective-permute-start(bf16[2,2,200,384]{3,2,1,0:T(8,128)(2,1)S(1)} %broadcast_select_fusion.8), channel_id=1, source_target_pairs={{0,2},{1,3},{2,0},{3,1},{4,6},{5,7},{6,4},{7,5},{8,10},{9,11},{10,... | collective-permute-start | bytes 1843208 | tf_op jit(solution)/shard_map/ppermute | solution.py:751
  98.4 22.2 %collective-permute-start.6 = (bf16[128,768]{1,0:T(8,128)(2,1)S(1)}, bf16[128,768]{1,0:T(8,128)(2,1)}, u32[]{:S(2)}, u32[]{:S(2)}) collective-permute-start(bf16[128,768]{1,0:T(8,128)(2,1)S(1)} %broadcast_select_fusion.15), channel_id=1, source_target_pairs={{0,8},{1,9},{2,10},{3,11},{4,12},{5,13},{6,14},{7,15},{8,0},{9,1},... | collective-permute-start | bytes 589832 | tf_op jit(solution)/shard_map/ppermute | solution.py:751
  127.3 170.2 %all-gather.8.cloned.1.call-start = ((), (), s32[]{:S(2)}) async-start(), calls=%async_computation.3 | async-start | bytes 5013504 | tf_op jit(solution)/shard_map/all_gather | solution.py:984
  135.6 34.0 %collective-permute-start.7 = (bf16[2,2,2,200,384]{4,3,2,1,0:T(8,128)(2,1)}, bf16[2,2,2,200,384]{4,3,2,1,0:T(8,128)(2,1)S(1)}, u32[]{:S(2)}, u32[]{:S(2)}) collective-permute-start(bf16[2,2,2,200,384]{4,3,2,1,0:T(8,128)(2,1)} %broadcast_select_fusion.1), channel_id=1, source_target_pairs={{0,16},{16,0},{1,17},{17,1},{2,18},{18,2},{3,19},{19,3},{4,20},{20... | collective-permute-start | bytes 3686408 | tf_op jit(solution)/shard_map/ppermute | solution.py:745
  138.3 31.2 %collective-permute-start.9 = (bf16[48,1536]{1,0:T(8,128)(2,1)S(1)}, bf16[48,1536]{1,0:T(8,128)(2,1)}, u32[]{:S(2)}, u32[]{:S(2)}) collective-permute-start(bf16[48,1536]{1,0:T(8,128)(2,1)S(1)} %dynamic-slice_bitcast_fusion.12), channel_id=1, source_target_pairs={{0,4},{1,5},{2,6},{3,7},{4,0},{5,1},{6,2},{7,3},{8,12},{9,13},{10,... | collective-permute-start | bytes 442376 | tf_op jit(solution)/shard_map/ppermute | solution.py:751
  138.4 31.1 %collective-permute-start.8 = (bf16[2,2,2,96,768]{4,3,1,0,2:T(8,128)(2,1)S(1)}, bf16[2,2,2,96,768]{4,3,1,0,2:T(8,128)(2,1)S(1)}, u32[]{:S(2)}, u32[]{:S(2)}) collective-permute-start(bf16[2,2,2,96,768]{4,3,1,0,2:T(8,128)(2,1)S(1)} %bitcast.272), channel_id=1, source_target_pairs={{0,1},{1,0},{2,3},{3,2},{4,5},{5,4},{6,7},{7,6},{8,9},{9,8},{10,11... | collective-permute-start | bytes 3538952 | tf_op jit(solution)/shard_map/ppermute | solution.py:751
  175.6 40.9 %collective-permute-start.10 = (bf16[2,2,2,200,768]{4,3,2,1,0:T(8,128)(2,1)}, bf16[2,2,2,200,768]{4,3,2,1,0:T(8,128)(2,1)}, u32[]{:S(2)}, u32[]{:S(2)}) collective-permute-start(bf16[2,2,2,200,768]{4,3,2,1,0:T(8,128)(2,1)} %pad_maximum_fusion), channel_id=1, source_target_pairs={{0,1},{1,0},{2,3},{3,2},{4,5},{5,4},{6,7},{7,6},{8,9},{9,8},{10,11... | collective-permute-start | bytes 7372808 | tf_op jit(solution)/shard_map/ppermute | solution.py:751
  176.1 111.5 %copy-start.167 = (pred[2]{0:T(512)(128)(4,1)}, pred[2]{0:T(512)(128)(4,1)S(1)}, u32[]{:S(2)}) copy-start(pred[2]{0:T(512)(128)(4,1)S(1)} %iota_compare_fusion.9) | copy-start | bytes 10
  176.4 162.9 %all-gather.10.cloned.1.call-start = ((), (), s32[]{:S(2)}) async-start(), calls=%async_computation.4 | async-start | bytes 2506752 | tf_op jit(solution)/shard_map/all_gather | solution.py:984
  176.4 40.1 %collective-permute-start.12 = (bf16[2,48,1536]{2,1,0:T(8,128)(2,1)}, bf16[2,48,1536]{2,1,0:T(8,128)(2,1)S(1)}, u32[]{:S(2)}, u32[]{:S(2)}) collective-permute-start(bf16[2,48,1536]{2,1,0:T(8,128)(2,1)} %broadcast_select_fusion.14), channel_id=1, source_target_pairs={{0,8},{1,9},{2,10},{3,11},{4,12},{5,13},{6,14},{7,15},{8,0},{9,1},... | collective-permute-start | bytes 884744 | tf_op jit(solution)/shard_map/ppermute | solution.py:751
  178.5 38.1 %collective-permute-start.11 = (bf16[2,2,96,768]{3,2,1,0:T(8,128)(2,1)}, bf16[2,2,96,768]{3,2,1,0:T(8,128)(2,1)S(1)}, u32[]{:S(2)}, u32[]{:S(2)}) collective-permute-start(bf16[2,2,96,768]{3,2,1,0:T(8,128)(2,1)} %dynamic-slice_bitcast_fusion.3), channel_id=1, source_target_pairs={{0,2},{1,3},{2,0},{3,1},{4,6},{5,7},{6,4},{7,5},{8,10},{9,11},{10,... | collective-permute-start | bytes 1769480 | tf_op jit(solution)/shard_map/ppermute | solution.py:751
  225.5 27.1 %collective-permute-start.13 = (bf16[2,96,768]{2,1,0:T(8,128)(2,1)}, bf16[2,96,768]{2,1,0:T(8,128)(2,1)}, u32[]{:S(2)}, u32[]{:S(2)}) collective-permute-start(bf16[2,96,768]{2,1,0:T(8,128)(2,1)} %dynamic-slice_bitcast_fusion.4), channel_id=1, source_target_pairs={{0,8},{1,9},{2,10},{3,11},{4,12},{5,13},{6,14},{7,15},{8,0},{9,1},... | collective-permute-start | bytes 884744 | tf_op jit(solution)/shard_map/ppermute | solution.py:751
  227.1 25.5 %collective-permute-start.14 = (bf16[2,2,48,1536]{3,2,1,0:T(8,128)(2,1)}, bf16[2,2,48,1536]{3,2,1,0:T(8,128)(2,1)}, u32[]{:S(2)}, u32[]{:S(2)}) collective-permute-start(bf16[2,2,48,1536]{3,2,1,0:T(8,128)(2,1)} %broadcast_select_fusion.10), channel_id=1, source_target_pairs={{0,2},{1,3},{2,0},{3,1},{4,6},{5,7},{6,4},{7,5},{8,10},{9,11},{10,... | collective-permute-start | bytes 1769480 | tf_op jit(solution)/shard_map/ppermute | solution.py:751
  255.9 18.5 %collective-permute-start.15 = (bf16[96,768]{1,0:T(8,128)(2,1)S(1)}, bf16[96,768]{1,0:T(8,128)(2,1)S(1)}, u32[]{:S(2)}, u32[]{:S(2)}) collective-permute-start(bf16[96,768]{1,0:T(8,128)(2,1)S(1)} %dynamic-slice_bitcast_fusion.11), channel_id=1, source_target_pairs={{0,4},{1,5},{2,6},{3,7},{4,0},{5,1},{6,2},{7,3},{8,12},{9,13},{10,... | collective-permute-start | bytes 442376 | tf_op jit(solution)/shard_map/ppermute | solution.py:751
  256.5 27.9 %collective-permute-start.16 = (bf16[2,2,2,48,1536]{4,3,2,1,0:T(8,128)(2,1)S(1)}, bf16[2,2,2,48,1536]{4,3,2,1,0:T(8,128)(2,1)S(1)}, u32[]{:S(2)}, u32[]{:S(2)}) collective-permute-start(bf16[2,2,2,48,1536]{4,3,2,1,0:T(8,128)(2,1)S(1)} %broadcast_select_fusion.5), channel_id=1, source_target_pairs={{0,16},{16,0},{1,17},{17,1},{2,18},{18,2},{3,19},{19,3},{4,20},{20... | collective-permute-start | bytes 3538952 | tf_op jit(solution)/shard_map/ppermute | solution.py:745
  287.6 4.9 collective-permute-start.17
  297.5 322.3 %reduce-scatter.3.cloned.1.call-start = ((), (), s32[]{:S(2)}) async-start(), calls=%async_computation.5 | async-start | bytes 10027008 | tf_op jit(solution)/shard_map/reduce_scatter | solution.py:1206
  418.1 291.1 %reduce-scatter.5.cloned.1.call-start = ((), (), s32[]{:S(2)}) async-start(), calls=%async_computation.6 | async-start | bytes 15040512 | tf_op jit(solution)/shard_map/reduce_scatter | solution.py:1265
  449.1 20.2 %collective-permute-start.18 = (bf16[96,768]{1,0:T(8,128)(2,1)S(1)}, bf16[96,768]{1,0:T(8,128)(2,1)S(1)}, u32[]{:S(2)}, u32[]{:S(2)}) collective-permute-start(bf16[96,768]{1,0:T(8,128)(2,1)S(1)} %add_convert_fusion.12), channel_id=1, source_target_pairs={{0,4},{1,5},{2,6},{3,7},{4,0},{5,1},{6,2},{7,3},{8,12},{9,13},{10,... | collective-permute-start | bytes 442376 | tf_op jit(solution)/shard_map/ppermute | solution.py:751
  450.1 20.4 %collective-permute-start.19 = (bf16[96,768]{1,0:T(8,128)(2,1)S(1)}, bf16[96,768]{1,0:T(8,128)(2,1)S(1)}, u32[]{:S(2)}, u32[]{:S(2)}) collective-permute-start(bf16[96,768]{1,0:T(8,128)(2,1)S(1)} %add_convert_fusion.12), channel_id=1, source_target_pairs={{0,8},{1,9},{2,10},{3,11},{4,12},{5,13},{6,14},{7,15},{8,0},{9,1},... | collective-permute-start | bytes 442376 | tf_op jit(solution)/shard_map/ppermute | solution.py:751
  450.9 20.8 %collective-permute-start.20 = (bf16[96,768]{1,0:T(8,128)(2,1)S(1)}, bf16[96,768]{1,0:T(8,128)(2,1)S(1)}, u32[]{:S(2)}, u32[]{:S(2)}) collective-permute-start(bf16[96,768]{1,0:T(8,128)(2,1)S(1)} %add_convert_fusion.12), channel_id=1, source_target_pairs={{0,12},{1,13},{2,14},{3,15},{4,8},{5,9},{6,10},{7,11},{8,4},{9,5},... | collective-permute-start | bytes 442376 | tf_op jit(solution)/shard_map/ppermute | solution.py:751
  472.8 28.9 %collective-permute-start.21 = (bf16[2,2,96,768]{3,2,1,0:T(8,128)(2,1)}, bf16[2,2,96,768]{3,2,1,0:T(8,128)(2,1)}, u32[]{:S(2)}, u32[]{:S(2)}) collective-permute-start(bf16[2,2,96,768]{3,2,1,0:T(8,128)(2,1)} %broadcast_select_fusion.9), channel_id=1, source_target_pairs={{0,16},{16,0},{1,17},{17,1},{2,18},{18,2},{3,19},{19,3},{4,20},{20... | collective-permute-start | bytes 1769480 | tf_op jit(solution)/shard_map/ppermute | solution.py:745
  535.8 29.7 %collective-permute-start.22 = (bf16[2,2,2,200,768]{4,3,1,0,2:T(8,128)(2,1)}, bf16[2,2,2,200,768]{4,3,1,0,2:T(8,128)(2,1)}, u32[]{:S(2)}, u32[]{:S(2)}) collective-permute-start(bf16[2,2,2,200,768]{4,3,1,0,2:T(8,128)(2,1)} %bitcast.241), channel_id=1, source_target_pairs={{0,1},{1,0},{2,3},{3,2},{4,5},{5,4},{6,7},{7,6},{8,9},{9,8},{10,11... | collective-permute-start | bytes 7372808 | tf_op jit(solution)/shard_map/ppermute | solution.py:751
  536.8 28.7 %collective-permute-start.23 = (bf16[2,2,2,96,768]{4,3,2,1,0:T(8,128)(2,1)}, bf16[2,2,2,96,768]{4,3,2,1,0:T(8,128)(2,1)S(1)}, u32[]{:S(2)}, u32[]{:S(2)}) collective-permute-start(bf16[2,2,2,96,768]{4,3,2,1,0:T(8,128)(2,1)} %broadcast_select_fusion.4), channel_id=1, source_target_pairs={{0,2},{1,3},{2,0},{3,1},{4,6},{5,7},{6,4},{7,5},{8,10},{9,11},{10,... | collective-permute-start | bytes 3538952 | tf_op jit(solution)/shard_map/ppermute | solution.py:751
  572.0 39.7 %collective-permute-start.25 = (bf16[2,2,2,2,96,768]{5,4,3,2,1,0:T(8,128)(2,1)S(1)}, bf16[2,2,2,2,96,768]{5,4,3,2,1,0:T(8,128)(2,1)}, u32[]{:S(2)}, u32[]{:S(2)}) collective-permute-start(bf16[2,2,2,2,96,768]{5,4,3,2,1,0:T(8,128)(2,1)S(1)} %broadcast_select_fusion), channel_id=1, source_target_pairs={{0,1},{1,0},{2,3},{3,2},{4,5},{5,4},{6,7},{7,6},{8,9},{9,8},{10,11... | collective-permute-start | bytes 7077896 | tf_op jit(solution)/shard_map/ppermute | solution.py:751
  581.7 30.0 %collective-permute-start.24 = (bf16[2,2,2,200,384]{4,3,1,0,2:T(8,128)(2,1)}, bf16[2,2,2,200,384]{4,3,1,0,2:T(8,128)(2,1)}, u32[]{:S(2)}, u32[]{:S(2)}) collective-permute-start(bf16[2,2,2,200,384]{4,3,1,0,2:T(8,128)(2,1)} %constant_dynamic-slice_fusion.12), channel_id=1, source_target_pairs={{0,16},{16,0},{1,17},{17,1},{2,18},{18,2},{3,19},{19,3},{4,20},{20... | collective-permute-start | bytes 3686408 | tf_op jit(solution)/shard_map/ppermute | solution.py:745
  619.8 15.4 %collective-permute-start.26 = (bf16[768,1536]{1,0:T(8,128)(2,1)}, bf16[768,1536]{1,0:T(8,128)(2,1)}, u32[]{:S(2)}, u32[]{:S(2)}) collective-permute-start(bf16[768,1536]{1,0:T(8,128)(2,1)} %pad_maximum_fusion.3), channel_id=1, source_target_pairs={{0,1},{1,0},{2,3},{3,2},{4,5},{5,4},{6,7},{7,6},{8,9},{9,8},{10,11... | collective-permute-start | bytes 7077896 | tf_op jit(solution)/shard_map/ppermute | solution.py:751
  638.7 41.4 %collective-permute-start.27 = (bf16[2,2,2,2,24,1536]{5,4,3,2,1,0:T(8,128)(2,1)}, bf16[2,2,2,2,24,1536]{5,4,3,2,1,0:T(8,128)(2,1)}, u32[]{:S(2)}, u32[]{:S(2)}) collective-permute-start(bf16[2,2,2,2,24,1536]{5,4,3,2,1,0:T(8,128)(2,1)} %dynamic-slice_bitcast_fusion), channel_id=1, source_target_pairs={{0,16},{16,0},{1,17},{17,1},{2,18},{18,2},{3,19},{19,3},{4,20},{20... | collective-permute-start | bytes 3538952 | tf_op jit(solution)/shard_map/ppermute | solution.py:745
  642.9 37.1 %collective-permute-start.30 = (bf16[48,6144]{1,0:T(8,128)(2,1)}, bf16[48,6144]{1,0:T(8,128)(2,1)}, u32[]{:S(2)}, u32[]{:S(2)}) collective-permute-start(bf16[48,6144]{1,0:T(8,128)(2,1)} %reduce-scatter.3.cloned.1.call-done), channel_id=1, source_target_pairs={{0,16},{16,0},{1,17},{17,1},{2,18},{18,2},{3,19},{19,3},{4,20},{20... | collective-permute-start | bytes 1769480 | tf_op jit(solution)/shard_map/ppermute | solution.py:745
  643.5 36.5 %collective-permute-start.29 = (bf16[2,2,200,384]{3,2,1,0:T(8,128)(2,1)}, bf16[2,2,200,384]{3,2,1,0:T(8,128)(2,1)}, u32[]{:S(2)}, u32[]{:S(2)}) collective-permute-start(bf16[2,2,200,384]{3,2,1,0:T(8,128)(2,1)} %dynamic-slice_bitcast_fusion.1), channel_id=1, source_target_pairs={{0,2},{1,3},{2,0},{3,1},{4,6},{5,7},{6,4},{7,5},{8,10},{9,11},{10,... | collective-permute-start | bytes 1843208 | tf_op jit(solution)/shard_map/ppermute | solution.py:751
  645.4 34.7 %collective-permute-start.28 = (bf16[768,128]{1,0:T(8,128)(2,1)}, bf16[768,128]{1,0:T(8,128)(2,1)}, u32[]{:S(2)}, u32[]{:S(2)}) collective-permute-start(bf16[768,128]{1,0:T(8,128)(2,1)} %get-tuple-element.424), channel_id=1, source_target_pairs={{0,1},{1,0},{2,3},{3,2},{4,5},{5,4},{6,7},{7,6},{8,9},{9,8},{10,11... | collective-permute-start | bytes 589832 | tf_op jit(solution)/shard_map/ppermute | solution.py:751
  646.4 35.4 %copy-start.27 = (bf16[2,2,2,200,384]{4,3,1,0,2:T(8,128)(2,1)S(1)}, bf16[2,2,2,200,384]{4,3,1,0,2:T(8,128)(2,1)}, u32[]{:S(2)}) copy-start(bf16[2,2,2,200,384]{4,3,1,0,2:T(8,128)(2,1)} %copy-done.26) | copy-start | bytes 3686404
  689.5 12.8 %collective-permute-start.32 = (bf16[2,2,2,2,24,128]{5,4,3,1,0,2:T(8,128)(2,1)}, bf16[2,2,2,2,24,128]{5,4,3,1,0,2:T(8,128)(2,1)S(1)}, u32[]{:S(2)}, u32[]{:S(2)}) collective-permute-start(bf16[2,2,2,2,24,128]{5,4,3,1,0,2:T(8,128)(2,1)} %bitcast.246), channel_id=1, source_target_pairs={{0,16},{16,0},{1,17},{17,1},{2,18},{18,2},{3,19},{19,3},{4,20},{20... | collective-permute-start | bytes 294920 | tf_op jit(solution)/shard_map/ppermute | solution.py:745
  691.1 15.0 %collective-permute-start.31 = (bf16[2,2,2,24,1536]{4,3,2,1,0:T(8,128)(2,1)}, bf16[2,2,2,24,1536]{4,3,2,1,0:T(8,128)(2,1)}, u32[]{:S(2)}, u32[]{:S(2)}) collective-permute-start(bf16[2,2,2,24,1536]{4,3,2,1,0:T(8,128)(2,1)} %dynamic-slice_bitcast_fusion.2), channel_id=1, source_target_pairs={{0,2},{1,3},{2,0},{3,1},{4,6},{5,7},{6,4},{7,5},{8,10},{9,11},{10,... | collective-permute-start | bytes 1769480 | tf_op jit(solution)/shard_map/ppermute | solution.py:751
  706.1 31.7 %copy-start.45 = (f32[48,1280]{1,0:T(8,128)S(1)}, f32[48,1280]{1,0:T(8,128)}, u32[]{:S(2)}) copy-start(f32[48,1280]{1,0:T(8,128)} %pad_maximum_fusion.6) | copy-start | bytes 737284
  709.3 38.2 %collective-permute-start.37 = (bf16[48,9216]{1,0:T(8,128)(2,1)}, bf16[48,9216]{1,0:T(8,128)(2,1)}, u32[]{:S(2)}, u32[]{:S(2)}) collective-permute-start(bf16[48,9216]{1,0:T(8,128)(2,1)} %reduce-scatter.5.cloned.1.call-done), channel_id=1, source_target_pairs={{0,16},{16,0},{1,17},{17,1},{2,18},{18,2},{3,19},{19,3},{4,20},{20... | collective-permute-start | bytes 2654216 | tf_op jit(solution)/shard_map/ppermute | solution.py:745
  710.5 17.3 %collective-permute-start.38 = (bf16[200,384]{1,0:T(8,128)(2,1)}, bf16[200,384]{1,0:T(8,128)(2,1)S(1)}, u32[]{:S(2)}, u32[]{:S(2)}) collective-permute-start(bf16[200,384]{1,0:T(8,128)(2,1)} %get-tuple-element.457), channel_id=1, source_target_pairs={{0,4},{1,5},{2,6},{3,7},{4,0},{5,1},{6,2},{7,3},{8,12},{9,13},{10,... | collective-permute-start | bytes 460808 | tf_op jit(solution)/shard_map/ppermute | solution.py:751
  721.9 14.7 %collective-permute-start.39 = (bf16[200,384]{1,0:T(8,128)(2,1)S(1)}, bf16[200,384]{1,0:T(8,128)(2,1)S(1)}, u32[]{:S(2)}, u32[]{:S(2)}) collective-permute-start(bf16[200,384]{1,0:T(8,128)(2,1)S(1)} %copy-done.78), channel_id=1, source_target_pairs={{0,8},{1,9},{2,10},{3,11},{4,12},{5,13},{6,14},{7,15},{8,0},{9,1},... | collective-permute-start | bytes 460808 | tf_op jit(solution)/shard_map/ppermute | solution.py:751
  721.9 16.5 %collective-permute-start.40 = (bf16[200,384]{1,0:T(8,128)(2,1)S(1)}, bf16[200,384]{1,0:T(8,128)(2,1)S(1)}, u32[]{:S(2)}, u32[]{:S(2)}) collective-permute-start(bf16[200,384]{1,0:T(8,128)(2,1)S(1)} %copy-done.77), channel_id=1, source_target_pairs={{0,12},{1,13},{2,14},{3,15},{4,8},{5,9},{6,10},{7,11},{8,4},{9,5},... | collective-permute-start | bytes 460808 | tf_op jit(solution)/shard_map/ppermute | solution.py:751
  725.3 17.2 %collective-permute-start.33 = (bf16[2,24,1536]{2,1,0:T(8,128)(2,1)}, bf16[2,24,1536]{2,1,0:T(8,128)(2,1)}, u32[]{:S(2)}, u32[]{:S(2)}) collective-permute-start(bf16[2,24,1536]{2,1,0:T(8,128)(2,1)} %get-tuple-element.452), channel_id=1, source_target_pairs={{0,4},{1,5},{2,6},{3,7},{4,0},{5,1},{6,2},{7,3},{8,12},{9,13},{10,... | collective-permute-start | bytes 442376 | tf_op jit(solution)/shard_map/ppermute | solution.py:751
  727.8 19.6 %collective-permute-start.34 = (bf16[2,24,1536]{2,1,0:T(8,128)(2,1)}, bf16[2,24,1536]{2,1,0:T(8,128)(2,1)}, u32[]{:S(2)}, u32[]{:S(2)}) collective-permute-start(bf16[2,24,1536]{2,1,0:T(8,128)(2,1)} %get-tuple-element.453), channel_id=1, source_target_pairs={{0,8},{1,9},{2,10},{3,11},{4,12},{5,13},{6,14},{7,15},{8,0},{9,1},... | collective-permute-start | bytes 442376 | tf_op jit(solution)/shard_map/ppermute | solution.py:751
  736.6 10.9 %collective-permute-start.35 = (bf16[2,24,1536]{2,1,0:T(8,128)(2,1)S(1)}, bf16[2,24,1536]{2,1,0:T(8,128)(2,1)S(1)}, u32[]{:S(2)}, u32[]{:S(2)}) collective-permute-start(bf16[2,24,1536]{2,1,0:T(8,128)(2,1)S(1)} %get-tuple-element.454), channel_id=1, source_target_pairs={{0,12},{1,13},{2,14},{3,15},{4,8},{5,9},{6,10},{7,11},{8,4},{9,5},... | collective-permute-start | bytes 442376 | tf_op jit(solution)/shard_map/ppermute | solution.py:751
  738.4 4.1 collective-permute-start.36
  752.4 9.3 %collective-permute-start.44 = (bf16[2,24,128]{2,1,0:T(8,128)(2,1)S(1)}, bf16[2,24,128]{2,1,0:T(8,128)(2,1)S(1)}, u32[]{:S(2)}, u32[]{:S(2)}) collective-permute-start(bf16[2,24,128]{2,1,0:T(8,128)(2,1)S(1)} %get-tuple-element.474), channel_id=1, source_target_pairs={{0,4},{1,5},{2,6},{3,7},{4,0},{5,1},{6,2},{7,3},{8,12},{9,13},{10,... | collective-permute-start | bytes 36872 | tf_op jit(solution)/shard_map/ppermute | solution.py:751
  754.6 7.4 collective-permute-start.45
  757.7 8.4 collective-permute-start.46
  760.1 6.0 collective-permute-start.41
  760.1 6.0 collective-permute-start.42
  761.7 4.4 collective-permute-start.43
  761.9 7.7 collective-permute-start.47
  811.0 30.8 %copy-start.63 = (f32[200,768]{1,0:T(8,128)S(1)}, f32[200,768]{1,0:T(8,128)}, u32[]{:S(2)}) copy-start(f32[200,768]{1,0:T(8,128)} %param.43) | copy-start | bytes 1843204
  811.1 30.8 %copy-start.66 = (bf16[200,384]{1,0:T(8,128)(2,1)S(1)}, bf16[200,384]{1,0:T(8,128)(2,1)}, u32[]{:S(2)}) copy-start(bf16[200,384]{1,0:T(8,128)(2,1)} %copy-done.65) | copy-start | bytes 460804
  811.1 30.8 %copy-start.68 = (bf16[200,384]{1,0:T(8,128)(2,1)S(1)}, bf16[200,384]{1,0:T(8,128)(2,1)}, u32[]{:S(2)}) copy-start(bf16[200,384]{1,0:T(8,128)(2,1)} %copy-done.67) | copy-start | bytes 460804
  811.1 30.8 %copy-start.75 = (bf16[1,8,2,2,24,128]{5,4,3,2,1,0:T(8,128)(2,1)S(1)}, bf16[1,8,2,2,24,128]{5,4,3,2,1,0:T(8,128)(2,1)}, u32[]{:S(2)}) copy-start(bf16[1,8,2,2,24,128]{5,4,3,2,1,0:T(8,128)(2,1)} %slice.328) | copy-start | bytes 589828
  811.1 30.8 %copy-start.191 = (f32[200,768]{1,0:T(8,128)S(1)}, f32[200,768]{1,0:T(8,128)}, u32[]{:S(2)}) copy-start(f32[200,768]{1,0:T(8,128)} %param.44) | copy-start | bytes 1843204
  (191 other events, 1216.6 us)
Sparse Core Ops, SparseCore 0:
  14.0 113.2 all-gather.11
  129.5 95.9 all-gather.5
  227.8 54.5 all-gather.7
  297.6 41.6 all-gather.9
  418.3 124.9 reduce-scatter.2
  547.9 155.2 reduce-scatter.4
